TPU v7x, 32 devices: a whole 2x2x4 slice. The times are simulated.
32 devices in a mesh: dp: 8 (over y, x, core), tensor: 4 (over z).
Axes of the slice: x: 2, y: 2, z: 4, core: 2. Of those that a mesh axis runs over, the one named last changes fastest.
Arguments:
- layer_input: float32 [8192, 1536], P(('dp', 'tensor')), may hold values from -6 to 6
- segment_ids: int32 [8192], P('dp'), may hold values from 0 to 23, as said below
- attn_gain: float32 [1536], replicated, may hold values from 0.25 to 1.75
- query_weight: float32 [1536, 1536], P('dp', 'tensor'), may hold values from -0.15625 to 0.15625
- key_weight: float32 [1536, 1536], P('dp', 'tensor'), may hold values from -0.15625 to 0.15625
- value_weight: float32 [1536, 1536], P('dp', 'tensor'), may hold values from -0.15625 to 0.15625
- forget_weight: float32 [1536, 24], P('dp', 'tensor'), may hold values from -0.15625 to 0.15625
- forget_bias: float32 [24], replicated, may hold values from 0 to 6
- output_weight: float32 [1536, 1536], P('dp', 'tensor'), may hold values from -0.4375 to 0.4375
- feed_gain: float32 [1536], replicated, may hold values from 0.25 to 1.75
- gate_weight: float32 [1536, 4096], P('dp', 'tensor'), may hold values from -0.15625 to 0.15625
- up_weight: float32 [1536, 4096], P('dp', 'tensor'), may hold values from -0.15625 to 0.15625
- down_weight: float32 [1536, 4096], P('dp', 'tensor'), may hold values from -0.1875 to 0.1875
- output_cotangent: float32 [8192, 1536], P(('dp', 'tensor')), may hold values from -6 to 6
Outputs:
- layer_output: float32 [8192, 1536], P(('dp', 'tensor'))
- input_grad: float32 [8192, 1536], P(('dp', 'tensor'))
- attn_gain_grad: float32 [1536], replicated
- query_grad: float32 [1536, 1536], P('dp', 'tensor')
- key_grad: float32 [1536, 1536], P('dp', 'tensor')
- value_grad: float32 [1536, 1536], P('dp', 'tensor')
- forget_grad: float32 [1536, 24], P('dp', 'tensor')
- bias_grad: float32 [24], replicated
- output_grad: float32 [1536, 1536], P('dp', 'tensor')
- feed_gain_grad: float32 [1536], replicated
- gate_grad: float32 [1536, 4096], P('dp', 'tensor')
- up_grad: float32 [1536, 4096], P('dp', 'tensor')
- down_grad: float32 [1536, 4096], P('dp', 'tensor')
Inputs may be any that keep to these rules, and one draw needn't show every extreme that they name: `segment_ids`: each sequence of 1024 tokens holds three documents and begins a new number; numbers never fall and rise by one at each document start. The middle document has exactly 800 tokens, the first 60 to 164 tokens, the last the rest.
All inputs are finite; a program needn't handle non-finite values.
Results may differ from a plain program's by a relative error of at most 0.014.
Values may be sent and summed in bfloat16 or wider, within the bound.
No kernel may reach another device: no remote copies, remote signals or barrier semaphores. Data moves between devices by JAX's collectives and lax.ppermute only.
A program may use at most 192 MiB of HBM per device.

v0:
```python
from functools import partial

import jax
import jax.numpy as jnp
from jax import lax
from jax.sharding import PartitionSpec as P

LEN = 1024


epsilon = 1e-06


def norm_rows(rows, gain):
    return rows * lax.rsqrt(jnp.mean(rows * rows, axis=-1, keepdims=True) + epsilon) * gain


def right_product(left, right):
    return lax.dot_general(
        left, right, (((1,), (1,)), ((), ())), preferred_element_type=jnp.float32
    )


def token_product(left, right):
    return lax.dot_general(
        left, right, (((0,), (0,)), ((), ())), preferred_element_type=jnp.float32
    )


def block_scores(query_block, keys, decays, segment, begin, scale):
    span = query_block.shape[0]
    length = keys.shape[0]
    place = jnp.arange(length, dtype=jnp.int32)
    raw = jnp.einsum("ihd,jhd->hij", query_block, keys, preferred_element_type=jnp.float32)
    scores = raw * scale + decays[:, begin : begin + span, None] - decays[:, None, :]
    allowed = (place[None, :] <= place[begin : begin + span, None]) & (
        segment[begin : begin + span, None] == segment[None, :]
    )
    return jnp.where(allowed[None], scores, -1e30)


def attend_forward(pack, scale):
    queries, keys, values, decays, segment = pack
    length = queries.shape[0]
    span = min(512, length)
    outputs = []
    logsums = []
    for begin in range(0, length, span):
        scores = block_scores(queries[begin : begin + span], keys, decays, segment, begin, scale)
        highest = jnp.max(scores, axis=-1, keepdims=True)
        powers = jnp.exp(scores - highest)
        totals = jnp.sum(powers, axis=-1, keepdims=True)
        shares = (powers / totals).astype(jnp.bfloat16)
        mixed = jnp.einsum("hij,jhd->ihd", shares, values, preferred_element_type=jnp.float32)
        outputs.append(mixed.astype(jnp.bfloat16))
        logsums.append((highest + jnp.log(totals))[:, :, 0])
    return (jnp.concatenate(outputs, axis=0), jnp.concatenate(logsums, axis=1))


def attend_backward(pack, scale):
    queries, keys, values, decays, segment, logsums, mixed_back = pack
    length = queries.shape[0]
    span = min(512, length)
    key_total = jnp.zeros(keys.shape, jnp.float32)
    value_total = jnp.zeros(values.shape, jnp.float32)
    column_total = jnp.zeros(decays.shape, jnp.float32)
    query_parts = []
    row_parts = []
    for begin in range(0, length, span):
        query_block = queries[begin : begin + span]
        scores = block_scores(query_block, keys, decays, segment, begin, scale)
        shares = jnp.exp(scores - logsums[:, begin : begin + span, None])
        grad_block = mixed_back[begin : begin + span]
        value_total = value_total + jnp.einsum(
            "hij,ihd->jhd",
            shares.astype(jnp.bfloat16),
            grad_block,
            preferred_element_type=jnp.float32,
        )
        share_grad = jnp.einsum(
            "ihd,jhd->hij", grad_block, values, preferred_element_type=jnp.float32
        )
        delta = jnp.sum(shares * share_grad, axis=-1, keepdims=True)
        score_grad = shares * (share_grad - delta)
        score_low = (score_grad * scale).astype(jnp.bfloat16)
        query_parts.append(
            jnp.einsum("hij,jhd->ihd", score_low, keys, preferred_element_type=jnp.float32)
        )
        key_total = key_total + jnp.einsum(
            "hij,ihd->jhd", score_low, query_block, preferred_element_type=jnp.float32
        )
        row_parts.append(jnp.sum(score_grad, axis=-1))
        column_total = column_total + jnp.sum(score_grad, axis=1)
    decay_grad = jnp.concatenate(row_parts, axis=1) - column_total
    return (jnp.concatenate(query_parts, axis=0), key_total, value_total, decay_grad)


def per_device(
    layer_input,
    segment_ids,
    attn_gain,
    query_weight,
    key_weight,
    value_weight,
    forget_weight,
    forget_bias,
    output_weight,
    feed_gain,
    gate_weight,
    up_weight,
    down_weight,
    output_cotangent,
):
    lowered = (
        query_weight.astype(jnp.bfloat16),
        key_weight.astype(jnp.bfloat16),
        value_weight.astype(jnp.bfloat16),
        forget_weight.astype(jnp.bfloat16),
        output_weight.astype(jnp.bfloat16),
        gate_weight.astype(jnp.bfloat16),
        up_weight.astype(jnp.bfloat16),
        down_weight.astype(jnp.bfloat16),
    )
    w_query, w_key, w_value, w_forget, w_output, w_gate, w_up, w_down = (
        lax.all_gather(lowered[0], "dp", axis=0, tiled=True),
        lax.all_gather(lowered[1], "dp", axis=0, tiled=True),
        lax.all_gather(lowered[2], "dp", axis=0, tiled=True),
        lax.all_gather(lowered[3], "dp", axis=0, tiled=True),
        lax.all_gather(lowered[4], "dp", axis=0, tiled=True),
        lax.all_gather(lowered[5], "dp", axis=0, tiled=True),
        lax.all_gather(lowered[6], "dp", axis=0, tiled=True),
        lax.all_gather(lowered[7], "dp", axis=0, tiled=True),
    )
    heads_local = w_forget.shape[1]
    head_size = w_query.shape[1] // heads_local
    scale = head_size ** (-0.5)
    total_rows = segment_ids.shape[0]
    length = LEN
    sequences = total_rows // length
    local_rows = layer_input.shape[0]
    bias_local = lax.dynamic_slice_in_dim(
        forget_bias, lax.axis_index("tensor") * heads_local, heads_local
    )
    attn_normed = lax.all_gather(
        norm_rows(layer_input, attn_gain).astype(jnp.bfloat16), "tensor", axis=0, tiled=True
    )
    queries = jnp.dot(attn_normed, w_query, preferred_element_type=jnp.float32).astype(jnp.bfloat16)
    keys = jnp.dot(attn_normed, w_key, preferred_element_type=jnp.float32).astype(jnp.bfloat16)
    values = jnp.dot(attn_normed, w_value, preferred_element_type=jnp.float32).astype(jnp.bfloat16)
    logits = jnp.dot(attn_normed, w_forget, preferred_element_type=jnp.float32) + bias_local
    logdecay = -jax.nn.softplus(-logits)
    decays = jnp.cumsum(logdecay.reshape(sequences, length, heads_local), axis=1).transpose(0, 2, 1)
    segments = segment_ids.reshape(sequences, length)

    def split_heads(tensor):
        return tensor.reshape(sequences, length, heads_local, head_size)

    mixed, logsums = lax.map(
        partial(attend_forward, scale=scale),
        (split_heads(queries), split_heads(keys), split_heads(values), decays, segments),
    )
    mixed = mixed.reshape(total_rows, heads_local * head_size)
    middle = layer_input + lax.psum_scatter(
        right_product(
            lax.slice_in_dim(mixed, 0, local_rows * lax.axis_size("tensor"), axis=0), w_output
        ),
        "tensor",
        scatter_dimension=0,
        tiled=True,
    )
    feed_normed = lax.all_gather(
        norm_rows(middle, feed_gain).astype(jnp.bfloat16), "tensor", axis=0, tiled=True
    )
    gate = jnp.dot(feed_normed, w_gate, preferred_element_type=jnp.float32)
    up = jnp.dot(feed_normed, w_up, preferred_element_type=jnp.float32)
    gate_sigmoid = jax.nn.sigmoid(gate)
    gate_silu = gate * gate_sigmoid
    hidden = (gate_silu * up).astype(jnp.bfloat16)
    layer_output = middle + lax.psum_scatter(
        right_product(
            lax.slice_in_dim(hidden, 0, local_rows * lax.axis_size("tensor"), axis=0), w_down
        ).astype(jnp.bfloat16),
        "tensor",
        scatter_dimension=0,
        tiled=True,
    ).astype(jnp.float32)
    w_query, w_key, w_value, w_forget, w_output, w_gate, w_up, w_down = (
        lax.all_gather(lowered[0], "dp", axis=0, tiled=True),
        lax.all_gather(lowered[1], "dp", axis=0, tiled=True),
        lax.all_gather(lowered[2], "dp", axis=0, tiled=True),
        lax.all_gather(lowered[3], "dp", axis=0, tiled=True),
        lax.all_gather(lowered[4], "dp", axis=0, tiled=True),
        lax.all_gather(lowered[5], "dp", axis=0, tiled=True),
        lax.all_gather(lowered[6], "dp", axis=0, tiled=True),
        lax.all_gather(lowered[7], "dp", axis=0, tiled=True),
    )
    cot_low = lax.all_gather(output_cotangent.astype(jnp.bfloat16), "tensor", axis=0, tiled=True)
    hidden_grad = jnp.dot(cot_low, w_down, preferred_element_type=jnp.float32)
    down_grad = token_product(cot_low, hidden)
    gate_back = (hidden_grad * up * gate_sigmoid * (1.0 + gate * (1.0 - gate_sigmoid))).astype(
        jnp.bfloat16
    )
    up_back = (hidden_grad * gate_silu).astype(jnp.bfloat16)
    gate_grad = token_product(feed_normed, gate_back)
    up_grad = token_product(feed_normed, up_back)
    feed_normed_grad = lax.psum_scatter(
        right_product(
            lax.slice_in_dim(gate_back, 0, local_rows * lax.axis_size("tensor"), axis=0), w_gate
        )
        + right_product(
            lax.slice_in_dim(up_back, 0, local_rows * lax.axis_size("tensor"), axis=0), w_up
        ),
        "tensor",
        scatter_dimension=0,
        tiled=True,
    )
    unused_feed, feed_pull = jax.vjp(norm_rows, middle, feed_gain)
    middle_part, feed_gain_part = feed_pull(feed_normed_grad)
    middle_grad = output_cotangent + middle_part
    middle_low = lax.all_gather(middle_grad.astype(jnp.bfloat16), "tensor", axis=0, tiled=True)
    mixed_back = jnp.dot(middle_low, w_output, preferred_element_type=jnp.float32).astype(
        jnp.bfloat16
    )
    output_grad = token_product(middle_low, mixed)
    query_rows, key_rows, value_rows, decay_grad = lax.map(
        partial(attend_backward, scale=scale),
        (
            split_heads(queries),
            split_heads(keys),
            split_heads(values),
            decays,
            segments,
            logsums,
            split_heads(mixed_back),
        ),
    )
    query_back = query_rows.reshape(total_rows, heads_local * head_size).astype(jnp.bfloat16)
    key_back = key_rows.reshape(total_rows, heads_local * head_size).astype(jnp.bfloat16)
    value_back = value_rows.reshape(total_rows, heads_local * head_size).astype(jnp.bfloat16)
    later_sums = jnp.flip(jnp.cumsum(jnp.flip(decay_grad, axis=2), axis=2), axis=2)
    later_sums = later_sums.transpose(0, 2, 1).reshape(total_rows, heads_local)
    logit_back = (later_sums * jax.nn.sigmoid(-logits)).astype(jnp.bfloat16)
    attn_normed_grad = lax.psum_scatter(
        right_product(
            lax.slice_in_dim(query_back, 0, local_rows * lax.axis_size("tensor"), axis=0), w_query
        )
        + right_product(
            lax.slice_in_dim(key_back, 0, local_rows * lax.axis_size("tensor"), axis=0), w_key
        )
        + right_product(
            lax.slice_in_dim(value_back, 0, local_rows * lax.axis_size("tensor"), axis=0), w_value
        )
        + right_product(logit_back, w_forget),
        "tensor",
        scatter_dimension=0,
        tiled=True,
    )
    unused_attn, attn_pull = jax.vjp(norm_rows, layer_input, attn_gain)
    input_part, attn_gain_part = attn_pull(attn_normed_grad)
    input_grad = middle_grad + input_part
    query_grad = token_product(attn_normed, query_back)
    key_grad = token_product(attn_normed, key_back)
    value_grad = token_product(attn_normed, value_back)
    forget_grad = token_product(attn_normed, logit_back)
    bias_part = jnp.sum(logit_back.astype(jnp.float32), axis=0)
    bias_full = lax.dynamic_update_slice_in_dim(
        jnp.zeros(forget_bias.shape, jnp.float32),
        bias_part,
        lax.axis_index("tensor") * heads_local,
        0,
    )
    (
        query_shard,
        key_shard,
        value_shard,
        forget_shard,
        output_shard,
        gate_shard,
        up_shard,
        down_shard,
    ) = (
        lax.psum_scatter(query_grad, "dp", scatter_dimension=0, tiled=True),
        lax.psum_scatter(key_grad, "dp", scatter_dimension=0, tiled=True),
        lax.psum_scatter(value_grad, "dp", scatter_dimension=0, tiled=True),
        lax.psum_scatter(forget_grad, "dp", scatter_dimension=0, tiled=True),
        lax.psum_scatter(output_grad, "dp", scatter_dimension=0, tiled=True),
        lax.psum_scatter(gate_grad, "dp", scatter_dimension=0, tiled=True),
        lax.psum_scatter(up_grad, "dp", scatter_dimension=0, tiled=True),
        lax.psum_scatter(down_grad, "dp", scatter_dimension=0, tiled=True),
    )
    attn_gain_grad, feed_gain_grad, bias_grad = lax.psum(
        (attn_gain_part, feed_gain_part, bias_full), ("dp", "tensor")
    )
    return (
        layer_output,
        input_grad,
        attn_gain_grad,
        query_shard,
        key_shard,
        value_shard,
        forget_shard,
        bias_grad,
        output_shard,
        feed_gain_grad,
        gate_shard,
        up_shard,
        down_shard,
    )


def solution(mesh):
    in_specs = (
        P(("dp", "tensor"), None),
        P("dp"),
        P(),
        P("dp", "tensor"),
        P("dp", "tensor"),
        P("dp", "tensor"),
        P("dp", "tensor"),
        P(),
        P("dp", "tensor"),
        P(),
        P("dp", "tensor"),
        P("dp", "tensor"),
        P("dp", "tensor"),
        P(("dp", "tensor"), None),
    )
    out_specs = (
        P(("dp", "tensor"), None),
        P(("dp", "tensor"), None),
        P(),
        P("dp", "tensor"),
        P("dp", "tensor"),
        P("dp", "tensor"),
        P("dp", "tensor"),
        P(),
        P("dp", "tensor"),
        P(),
        P("dp", "tensor"),
        P("dp", "tensor"),
        P("dp", "tensor"),
    )
    return jax.shard_map(
        per_device, mesh=mesh, in_specs=in_specs, out_specs=out_specs, check_vma=False
    )
```

profile of v0, /device:TPU:0, one launch (start us, length us, event | category | flops | bytes accessed | tf_op | source)
XLA Modules:
  0.0 1422.8 jit_solution(4262104393257930933)
XLA Ops:
  10.1 2.5 multiply_convert_fusion.10
  15.8 10.5 all-gather
  28.4 50.6 %all-gather.13.cloned.1.call-done = bf16[1024,1536]{1,0:T(8,128)(2,1)} async-done(((bf16[256,1536]{1,0:T(8,128)(2,1)}), bf16[1024,1536]{1,0:T(8,128)(2,1)}) %all-gather.13.cloned.1.call-update) | async-done | bytes 3145744 | tf_op jit(solution)/shard_map/all_gather | solution.py:144
  79.0 2.9 convolution_add_fusion.1
  86.9 17.3 %all-gather.17.cloned.1.call-done = bf16[1536,384]{1,0:T(8,128)(2,1)} async-done(((bf16[192,384]{1,0:T(8,128)(2,1)}), bf16[1536,384]{1,0:T(8,128)(2,1)}) %all-gather.17.cloned.1.call-update) | async-done | bytes 1179664 | tf_op jit(solution)/shard_map/all_gather | solution.py:125
  104.2 2.7 convolution_convert_fusion.3
  107.8 23.0 %all-gather.19.cloned.1.call-done = bf16[1536,384]{1,0:T(8,128)(2,1)} async-done(((bf16[192,384]{1,0:T(8,128)(2,1)}), bf16[1536,384]{1,0:T(8,128)(2,1)}) %all-gather.19.cloned.1.call-update) | async-done | bytes 1179664 | tf_op jit(solution)/shard_map/all_gather | solution.py:126
  130.8 2.8 convolution_convert_fusion.2
  133.6 3.6 fusion.64
  137.2 4.5 copy-done
  141.7 3.4 fusion.4
  145.2 12.0 all-gather.15.cloned.1.call-done
  157.2 2.8 convolution_convert_fusion.4
  162.4 3.8 fusion.43
  166.3 3.5 fusion.63
  169.8 2.8 fusion.5
  174.6 3.3 fusion.44
  178.0 5.6 all-gather.21.cloned.1.call-done
  183.6 5.8 fusion.65
  191.4 108.9 %reduce-scatter.17.cloned.1.call-done = f32[256,1536]{1,0:T(8,128)} async-done(((f32[1024,1536]{1,0:T(8,128)}), f32[256,1536]{1,0:T(8,128)}) %reduce-scatter.17.cloned.1.call-update) | async-done | bytes 1572880 | tf_op jit(solution)/shard_map/reduce_scatter | solution.py:163
  308.4 27.3 %all-gather.27.cloned.1.call-done = bf16[1536,1024]{1,0:T(8,128)(2,1)} async-done(((bf16[192,1024]{1,0:T(8,128)(2,1)}), bf16[1536,1024]{1,0:T(8,128)(2,1)}) %all-gather.27.cloned.1.call-update) | async-done | bytes 3145744 | tf_op jit(solution)/shard_map/all_gather | solution.py:131
  335.7 65.7 %all-gather.23.cloned.1.call-done = bf16[1024,1536]{1,0:T(8,128)(2,1)} async-done(((bf16[256,1536]{1,0:T(8,128)(2,1)}), bf16[1024,1536]{1,0:T(8,128)(2,1)}) %all-gather.23.cloned.1.call-update) | async-done | bytes 3145744 | tf_op jit(solution)/shard_map/all_gather | solution.py:171
  401.3 8.2 fusion.67
  409.6 25.2 %all-gather.25.cloned.1.call-done = bf16[1536,1024]{1,0:T(8,128)(2,1)} async-done(((bf16[192,1024]{1,0:T(8,128)(2,1)}), bf16[1536,1024]{1,0:T(8,128)(2,1)}) %all-gather.25.cloned.1.call-update) | async-done | bytes 3145744 | tf_op jit(solution)/shard_map/all_gather | solution.py:130
  434.8 8.3 fusion.66
  443.1 57.2 %all-gather.31.cloned.1.call-done = bf16[1024,1536]{1,0:T(8,128)(2,1)} async-done(((bf16[256,1536]{1,0:T(8,128)(2,1)}), bf16[1024,1536]{1,0:T(8,128)(2,1)}) %all-gather.31.cloned.1.call-update) | async-done | bytes 3145744 | tf_op jit(solution)/shard_map/all_gather | solution.py:197
  500.3 32.9 %all-gather.29.cloned.1.call-done = bf16[1536,1024]{1,0:T(8,128)(2,1)} async-done(((bf16[192,1024]{1,0:T(8,128)(2,1)}), bf16[1536,1024]{1,0:T(8,128)(2,1)}) %all-gather.29.cloned.1.call-update) | async-done | bytes 3145744 | tf_op jit(solution)/shard_map/all_gather | solution.py:132
  533.2 11.5 multiply_convert_fusion.2
  544.7 3.5 fusion.68
  548.2 5.7 convolution_add_fusion
  553.9 7.7 convolution_convert_fusion
  561.7 103.1 %reduce-scatter.21.cloned.1.call-done = f32[256,1536]{1,0:T(8,128)} async-done(((f32[1024,1536]{1,0:T(8,128)}), f32[256,1536]{1,0:T(8,128)}) %reduce-scatter.21.cloned.1.call-update) | async-done | bytes 1572880 | tf_op jit(solution)/shard_map/reduce_scatter | solution.py:206
  667.7 60.2 %reduce-scatter.19.cloned.1.call-done = bf16[256,1536]{1,0:T(8,128)(2,1)} async-done(((bf16[1024,1536]{1,0:T(8,128)(2,1)}), bf16[256,1536]{1,0:T(8,128)(2,1)}) %reduce-scatter.19.cloned.1.call-update) | async-done | bytes 786448 | tf_op jit(solution)/shard_map/reduce_scatter | solution.py:179
  727.9 4.0 fusion.57
  733.5 62.1 %all-gather.33.cloned.1.call-done = bf16[1024,1536]{1,0:T(8,128)(2,1)} async-done(((bf16[256,1536]{1,0:T(8,128)(2,1)}), bf16[1024,1536]{1,0:T(8,128)(2,1)}) %all-gather.33.cloned.1.call-update) | async-done | bytes 3145744 | tf_op jit(solution)/shard_map/all_gather | solution.py:220
  795.6 3.6 convolution_convert_fusion.1
  799.3 6.2 fusion.12
  805.5 20.2 %fusion.54 = (f32[6,1024]{1,0:T(8,128)}, f32[6,512]{1,0:T(8,128)}, f32[6,512,1024]{2,1,0:T(8,128)}) fusion(f32[6,512,1024]{2,1,0:T(8,128)} %copy-done.2, f32[6,512]{1,0:T(8,128)S(1)} %log_add_fusion, bf16[512,6,64]{0,2,1:T(8,128)(2,1)S(1)} %bitcast.160, bf16[1024,6,64]{0,2,1:T(8,128)(2,1)} %bitcast.171), kind=kOutput, calls=%fused_computation.108 | convolution fusion | flops 827321344 | bytes 26394624 | tf_op jit(solution)/shard_map/while/body/eval_jaxpr/sub | solution.py:84
  825.7 19.3 %fusion.55 = (f32[6,1024]{1,0:T(8,128)S(1)}, f32[6,512]{1,0:T(8,128)S(1)}, f32[6,512,1024]{2,1,0:T(8,128)}) fusion(f32[6,512,1024]{2,1,0:T(8,128)} %copy-done, f32[6,512]{1,0:T(8,128)S(1)} %log_add_fusion.1, bf16[512,6,64]{0,2,1:T(8,128)(2,1)S(1)} %bitcast.157, bf16[1024,6,64]{0,2,1:T(8,128)(2,1)} %bitcast.172), kind=kOutput, calls=%fused_computation.109 | convolution fusion | flops 827321344 | bytes 26394624 | tf_op jit(solution)/shard_map/while/body/eval_jaxpr/sub | solution.py:84
  845.0 7.5 fusion.41
  852.6 7.1 fusion.23
  859.7 3.3 add_convert_fusion
  867.9 7.5 fusion.42
  875.4 7.0 add_convert_fusion.1
  885.5 3.7 fusion.71
  892.9 3.7 add_add_fusion
  896.9 8.6 convolution_bitcast_fusion
  905.5 6.6 copy.38
  912.2 8.7 fusion.78
  921.0 8.7 fusion.77
  929.8 5.4 fusion.76
  935.5 4.5 fusion.72
  940.0 4.4 fusion.74
  944.6 4.4 fusion.73
  950.9 80.1 %reduce-scatter.23.cloned.1.call-done = f32[256,1536]{1,0:T(8,128)} async-done(((f32[1024,1536]{1,0:T(8,128)}), f32[256,1536]{1,0:T(8,128)}) %reduce-scatter.23.cloned.1.call-update) | async-done | bytes 1572880 | tf_op jit(solution)/shard_map/reduce_scatter | solution.py:243
  1032.9 41.4 %all-reduce = (f32[1536]{0:T(1024)}, f32[24]{0:T(128)}, f32[1536]{0:T(1024)}) all-reduce(f32[1536]{0:T(1024)S(1)} %get-tuple-element.118, f32[24]{0:T(128)S(1)} %dynamic_update_slice.18, f32[1536]{0:T(1024)S(1)} %copy-done.41), channel_id=1, replica_groups=mesh['dp'=8,'tensor'=4] {'dp','tensor'}, use_global_device_ids=true, to_apply=%region_23.24 | all-reduce | flops 3096 | bytes 24768 | tf_op jit(solution)/shard_map/psum | solution.py:291
  1074.4 2.9 fusion.30
  1077.3 20.4 %reduce-scatter.39.cloned.1.call-done = f32[192,1024]{1,0:T(8,128)} async-done(((f32[1536,1024]{1,0:T(8,128)}), f32[192,1024]{1,0:T(8,128)}) %reduce-scatter.39.cloned.1.call-update) | async-done | bytes 786448
  1097.7 66.0 %reduce-scatter.35.cloned.1.call-done = f32[192,1024]{1,0:T(8,128)} async-done(((f32[1536,1024]{1,0:T(8,128)}), f32[192,1024]{1,0:T(8,128)}) %reduce-scatter.35.cloned.1.call-update) | async-done | bytes 786448 | tf_op jit(solution)/shard_map/reduce_scatter | solution.py:288
  1163.7 65.7 %reduce-scatter.33.cloned.1.call-done = f32[192,1024]{1,0:T(8,128)} async-done(((f32[1536,1024]{1,0:T(8,128)}), f32[192,1024]{1,0:T(8,128)}) %reduce-scatter.33.cloned.1.call-update) | async-done | bytes 786448 | tf_op jit(solution)/shard_map/reduce_scatter | solution.py:287
  1229.4 46.7 %reduce-scatter.31.cloned.1.call-done = f32[192,384]{1,0:T(8,128)} async-done(((f32[1536,384]{1,0:T(8,128)}), f32[192,384]{1,0:T(8,128)}) %reduce-scatter.31.cloned.1.call-update) | async-done | bytes 294928 | tf_op jit(solution)/shard_map/reduce_scatter | solution.py:286
  1276.1 46.5 %reduce-scatter.25.cloned.1.call-done = f32[192,384]{1,0:T(8,128)} async-done(((f32[1536,384]{1,0:T(8,128)}), f32[192,384]{1,0:T(8,128)}) %reduce-scatter.25.cloned.1.call-update) | async-done | bytes 294928 | tf_op jit(solution)/shard_map/reduce_scatter | solution.py:282
  1322.6 46.8 %reduce-scatter.29.cloned.1.call-done = f32[192,384]{1,0:T(8,128)} async-done(((f32[1536,384]{1,0:T(8,128)}), f32[192,384]{1,0:T(8,128)}) %reduce-scatter.29.cloned.1.call-update) | async-done | bytes 294928 | tf_op jit(solution)/shard_map/reduce_scatter | solution.py:284
  1369.4 46.5 %reduce-scatter.27.cloned.1.call-done = f32[192,384]{1,0:T(8,128)} async-done(((f32[1536,384]{1,0:T(8,128)}), f32[192,384]{1,0:T(8,128)}) %reduce-scatter.27.cloned.1.call-update) | async-done | bytes 294928 | tf_op jit(solution)/shard_map/reduce_scatter | solution.py:283
  (233 shorter events, 49.1 us)
Async XLA Ops:
  7.2 5.5 copy-start.26
  7.2 6.3 copy-start.27
  7.2 7.0 copy-start.28
  7.2 7.8 copy-start.29
  7.2 71.8 %all-gather.13.cloned.1.call-start = ((), (), s32[]{:S(2)}) async-start(), calls=%async_computation.12 | async-start | bytes 3932160 | tf_op jit(solution)/shard_map/all_gather | solution.py:144
  9.5 6.2 copy-start.51
  9.5 6.3 copy-start.45
  9.5 16.9 %copy-start.55 = (f32[24]{0:T(128)S(1)}, f32[24]{0:T(128)}, u32[]{:S(2)}) copy-start(f32[24]{0:T(128)} %param.21) | copy-start | bytes 292
  12.6 91.6 %all-gather.17.cloned.1.call-start = ((), (), s32[]{:S(2)}) async-start(), calls=%async_computation.14 | async-start | bytes 1327104 | tf_op jit(solution)/shard_map/all_gather | solution.py:125
  13.4 117.4 %all-gather.19.cloned.1.call-start = ((), (), s32[]{:S(2)}) async-start(), calls=%async_computation.15 | async-start | bytes 1327104 | tf_op jit(solution)/shard_map/all_gather | solution.py:126
  14.2 143.0 %all-gather.15.cloned.1.call-start = ((), (), s32[]{:S(2)}) async-start(), calls=%async_computation.13 | async-start | bytes 1327104 | tf_op jit(solution)/shard_map/all_gather | solution.py:127
  14.9 168.7 %all-gather.21.cloned.1.call-start = ((), (), s32[]{:S(2)}) async-start(), calls=%async_computation.16 | async-start | bytes 1327104 | tf_op jit(solution)/shard_map/all_gather | solution.py:129
  15.7 284.6 %reduce-scatter.17.cloned.1.call-start = ((), (), s32[]{:S(2)}) async-start(), calls=%async_computation.17 | async-start | bytes 7864320 | tf_op jit(solution)/shard_map/reduce_scatter | solution.py:163
  26.5 55.5 %copy-start.30 = (bf16[1536,6]{0,1:T(8,128)(2,1)}, bf16[1536,6]{0,1:T(8,128)(2,1)S(1)}, u32[]{:S(2)}) copy-start(bf16[1536,6]{0,1:T(8,128)(2,1)S(1)} %reshape.302) | copy-start | bytes 55300
  79.0 25.2 %copy-start.5 = (bf16[1024,1536]{1,0:T(8,128)(2,1)S(1)}, bf16[1024,1536]{1,0:T(8,128)(2,1)}, u32[]{:S(2)}) copy-start(bf16[1024,1536]{1,0:T(8,128)(2,1)} %all-gather.13.cloned.1.call-done) | copy-start | bytes 9437188
  137.2 4.5 copy-start
  137.2 22.8 %copy-start.37 = (f32[6,512]{1,0:T(8,128)}, f32[6,512]{1,0:T(8,128)S(1)}, u32[]{:S(2)}) copy-start(f32[6,512]{1,0:T(8,128)S(1)} %get-tuple-element.145) | copy-start | bytes 36868
  157.2 5.2 copy-start.1
  157.2 5.2 copy-start.38
  160.0 12.6 copy-start.56
  162.4 3.8 copy-start.14
  162.4 3.9 copy-start.17
  162.4 3.9 copy-start.22
  162.4 3.9 copy-start.34
  162.4 3.9 copy-start.46
  169.8 4.5 copy-start.2
  169.8 4.7 copy-start.39
  178.0 11.4 copy-start.10
  189.4 110.9 %copy-start.3 = (f32[256,1536]{1,0:T(8,128)S(1)}, f32[256,1536]{1,0:T(8,128)}, u32[]{:S(2)}) copy-start(f32[256,1536]{1,0:T(8,128)} %param.14) | copy-start | bytes 4718596
  189.4 112.6 %copy-start.36 = (f32[1536]{0:T(1024)S(1)}, f32[1536]{0:T(1024)}, u32[]{:S(2)}) copy-start(f32[1536]{0:T(1024)} %param.23) | copy-start | bytes 18436
  189.4 146.2 %all-gather.27.cloned.1.call-start = ((), (), s32[]{:S(2)}) async-start(), calls=%async_computation.20 | async-start | bytes 3538944 | tf_op jit(solution)/shard_map/all_gather | solution.py:131
  191.4 210.0 %all-gather.23.cloned.1.call-start = ((), (), s32[]{:S(2)}) async-start(), calls=%async_computation.18 | async-start | bytes 3932160 | tf_op jit(solution)/shard_map/all_gather | solution.py:171
  303.1 131.7 %all-gather.25.cloned.1.call-start = ((), (), s32[]{:S(2)}) async-start(), calls=%async_computation.19 | async-start | bytes 3538944 | tf_op jit(solution)/shard_map/all_gather | solution.py:130
  305.1 195.2 %all-gather.31.cloned.1.call-start = ((), (), s32[]{:S(2)}) async-start(), calls=%async_computation.23 | async-start | bytes 3932160 | tf_op jit(solution)/shard_map/all_gather | solution.py:197
  306.2 227.0 %all-gather.29.cloned.1.call-start = ((), (), s32[]{:S(2)}) async-start(), calls=%async_computation.21 | async-start | bytes 3538944 | tf_op jit(solution)/shard_map/all_gather | solution.py:132
  308.2 356.6 %reduce-scatter.21.cloned.1.call-start = ((), (), s32[]{:S(2)}) async-start(), calls=%async_computation.24 | async-start | bytes 7864320 | tf_op jit(solution)/shard_map/reduce_scatter | solution.py:206
  533.2 11.5 copy-start.54
  553.9 174.0 %reduce-scatter.19.cloned.1.call-start = ((), (), s32[]{:S(2)}) async-start(), calls=%async_computation.22 | async-start | bytes 3932160 | tf_op jit(solution)/shard_map/reduce_scatter | solution.py:179
  561.6 234.0 %all-gather.33.cloned.1.call-start = ((), (), s32[]{:S(2)}) async-start(), calls=%async_computation.25 | async-start | bytes 3932160 | tf_op jit(solution)/shard_map/all_gather | solution.py:220
  731.9 217.3 %reduce-scatter.37.cloned.1.call-start = ((), (), s32[]{:S(2)}) async-start(), calls=%async_computation.33 | async-start | bytes 884736
  825.7 19.3 %copy-start.15 = (bf16[1024,384]{0,1:T(8,128)(2,1)S(1)}, bf16[1024,384]{0,1:T(8,128)(2,1)}, u32[]{:S(2)}) copy-start(bf16[1024,384]{0,1:T(8,128)(2,1)} %copy-done.13) | copy-start | bytes 2359300
  845.0 14.6 %slice-start = ((s8[12582912]{0:T(1024)(128)(4,1)}), s8[4194304]{0:T(1024)(128)(4,1)S(1)}, s32[]{:S(2)}) async-start(s8[12582912]{0:T(1024)(128)(4,1)} %bitcast.141), calls=%async_computation.35 | async-start | bytes 8388608
  845.0 14.6 %slice-start.1 = ((s8[12582912]{0:T(1024)(128)(4,1)}), s8[4194304]{0:T(1024)(128)(4,1)S(1)}, s32[]{:S(2)}) async-start(s8[12582912]{0:T(1024)(128)(4,1)} %bitcast.141), calls=%async_computation.36 | async-start | bytes 8388608
  852.6 7.1 slice-start.2
  859.7 7.6 copy-start.25
  867.9 7.5 copy-start.7
  867.9 7.5 copy-start.18
  875.4 7.0 copy-start.6
  884.3 146.7 %reduce-scatter.23.cloned.1.call-start = ((), (), s32[]{:S(2)}) async-start(), calls=%async_computation.26 | async-start | bytes 7864320 | tf_op jit(solution)/shard_map/reduce_scatter | solution.py:243
  885.5 5.6 copy-start.11
  896.7 201.1 %reduce-scatter.39.cloned.1.call-start = ((), (), s32[]{:S(2)}) async-start(), calls=%async_computation.34 | async-start | bytes 7077888
  912.2 251.5 %reduce-scatter.35.cloned.1.call-start = ((), (), s32[]{:S(2)}) async-start(), calls=%async_computation.32 | async-start | bytes 7077888 | tf_op jit(solution)/shard_map/reduce_scatter | solution.py:288
  921.0 308.5 %reduce-scatter.33.cloned.1.call-start = ((), (), s32[]{:S(2)}) async-start(), calls=%async_computation.31 | async-start | bytes 7077888 | tf_op jit(solution)/shard_map/reduce_scatter | solution.py:287
  929.7 346.4 %reduce-scatter.31.cloned.1.call-start = ((), (), s32[]{:S(2)}) async-start(), calls=%async_computation.30 | async-start | bytes 2654208 | tf_op jit(solution)/shard_map/reduce_scatter | solution.py:286
  935.2 387.4 %reduce-scatter.25.cloned.1.call-start = ((), (), s32[]{:S(2)}) async-start(), calls=%async_computation.27 | async-start | bytes 2654208 | tf_op jit(solution)/shard_map/reduce_scatter | solution.py:282
  940.0 429.4 %reduce-scatter.29.cloned.1.call-start = ((), (), s32[]{:S(2)}) async-start(), calls=%async_computation.29 | async-start | bytes 2654208 | tf_op jit(solution)/shard_map/reduce_scatter | solution.py:284
  944.5 4.5 copy-start.52
  944.5 86.5 %copy-start.35 = (f32[1536]{0:T(1024)S(1)}, f32[1536]{0:T(1024)}, u32[]{:S(2)}) copy-start(f32[1536]{0:T(1024)} %param.16) | copy-start | bytes 18436
  944.5 86.5 %copy-start.44 = (f32[256]{0:T(256)S(1)}, f32[256]{0:T(256)}, u32[]{:S(2)}) copy-start(f32[256]{0:T(256)} %copy-done.43) | copy-start | bytes 3076
  944.5 471.3 %reduce-scatter.27.cloned.1.call-start = ((), (), s32[]{:S(2)}) async-start(), calls=%async_computation.28 | async-start | bytes 2654208 | tf_op jit(solution)/shard_map/reduce_scatter | solution.py:283
  948.9 82.1 %copy-start.4 = (f32[256,1536]{1,0:T(8,128)S(1)}, f32[256,1536]{1,0:T(8,128)}, u32[]{:S(2)}) copy-start(f32[256,1536]{1,0:T(8,128)} %param.14) | copy-start | bytes 4718596
  948.9 84.0 %copy-start.41 = (f32[1536]{0:T(1024)S(1)}, f32[1536]{0:T(1024)}, u32[]{:S(2)}) copy-start(f32[1536]{0:T(1024)} %get-tuple-element.116) | copy-start | bytes 18436
  948.9 125.4 %copy-start.50 = (f32[256]{0:T(256)S(1)}, f32[256]{0:T(256)}, u32[]{:S(2)}) copy-start(f32[256]{0:T(256)} %copy-done.49) | copy-start | bytes 3076
  1031.0 43.3 %copy-start.8 = (f32[256,1536]{1,0:T(8,128)S(1)}, f32[256,1536]{1,0:T(8,128)}, u32[]{:S(2)}) copy-start(f32[256,1536]{1,0:T(8,128)} %reduce-scatter.23.cloned.1.call-done) | copy-start | bytes 4718596
  (21 other events, 52.4 us)
Sparse Core Ops, SparseCore 0:
  12.7 66.1 all-gather.12
  81.4 22.7 all-gather.16
  106.7 24.0 all-gather.18
  133.1 24.0 all-gather.14
  159.5 24.0 all-gather.20
  189.5 110.7 reduce-scatter.16
  302.8 32.8 all-gather.26
  337.8 63.4 all-gather.22
  403.8 30.9 all-gather.24
  436.8 63.4 all-gather.30
  502.2 30.9 all-gather.28
  554.0 110.7 reduce-scatter.20
  667.1 60.7 reduce-scatter.18
  732.1 63.5 all-gather.32
  884.4 33.6 reduce-scatter.36
  920.2 110.7 reduce-scatter.22
  1034.8 62.8 reduce-scatter.38
  1101.9 61.7 reduce-scatter.34
  1167.7 61.7 reduce-scatter.32
  1233.5 42.4 reduce-scatter.30
  1280.0 42.5 reduce-scatter.24
  1326.9 42.4 reduce-scatter.28
  1373.3 42.5 reduce-scatter.26
where the time goes:
time: 1430 us; the launch traced here: 1420 us
  waiting for transfers between devices  1070 us (75%)
  matrix products  215 us (15%)
  blocking collectives  51.9 us (4%)
  other arithmetic  44 us (3%)
  local copies, waits for them, and re-layouts  24.4 us (2%)
  between operations  15.3 us (1%)
    reduce_scatter x1, waiting for transfers between devices, per_device(): lax.psum_scatter(right_product(lax.slice_in_dim(mixed, 0, local_rows * la...  109 us
    reduce_scatter x1, waiting for transfers between devices, per_device(): lax.psum_scatter(right_product(lax.slice_in_dim(gate_back, 0, local_rows...  103 us
    reduce_scatter x1, waiting for transfers between devices, per_device(): lax.psum_scatter(right_product(lax.slice_in_dim(query_back, 0, local_rows...  80.1 us
    reduce_scatter x1, waiting for transfers between devices, per_device(): lax.psum_scatter(up_grad, 'dp', scatter_dimension=0, tiled=True)  66 us
    reduce_scatter x1, waiting for transfers between devices, per_device(): lax.psum_scatter(gate_grad, 'dp', scatter_dimension=0, tiled=True)  65.7 us
    all_gather x1, waiting for transfers between devices, per_device(): lax.all_gather(norm_rows(middle, feed_gain).astype(jnp.bfloat16), 'tensor...  65.7 us
    all_gather x1, waiting for transfers between devices, per_device(): lax.all_gather(middle_grad.astype(jnp.bfloat16), 'tensor', axis=0, tiled=...  62.1 us
    reduce_scatter x1, waiting for transfers between devices, per_device(): lax.psum_scatter(right_product(lax.slice_in_dim(hidden, 0, local_rows * l...  60.2 us
  transfers between devices with their start and end apart: 23, of which 22 were waited for; matrix products, arithmetic and copies ran while one was open for 10% of the time, Pallas kernels for 0%

commit v1 on v0

v1 whole, which is shorter than its diff:
```python
import functools

import jax
import jax.numpy as jnp
from jax import lax
from jax.experimental import pallas as pl
from jax.experimental.pallas import tpu as pltpu
from jax.sharding import PartitionSpec as P

F32 = jnp.float32
BF = jnp.bfloat16
NT = (((1,), (1,)), ((), ()))
NN = (((1,), (0,)), ((), ()))
TN = (((0,), (0,)), ((), ()))
BOTH = ("dp", "tensor")
EPS = 1e-6


def dotf(a, b, dn):
    return lax.dot_general(a, b, dn, preferred_element_type=F32)


def split3(x):
    a=x.astype(BF); r=x-a.astype(F32); b=r.astype(BF); c=(r-b.astype(F32)).astype(BF)
    return a,b,c

def fwd_kernel(heads, qb, x_ref, logit_ref, segc_ref, segr_ref, mixed_ref, rows_ref, dcol_ref, lse_sc, drow_sc):
    T=x_ref.shape[0]; W=heads*64
    logits=logit_ref[...]
    ld=-(jnp.maximum(-logits,0.0)+jnp.log1p(jnp.exp(-jnp.abs(logits))))
    ri=lax.broadcasted_iota(jnp.int32,(128,128),0); ci=lax.broadcasted_iota(jnp.int32,(128,128),1)
    tri=(ri>=ci).astype(BF)
    carry=jnp.zeros((1,128),F32)
    for b in range(T//128):
        blk=ld[b*128:(b+1)*128]
        a,bb,c=split3(blk)
        pre=dotf(tri,a,NN)+dotf(tri,bb,NN)+dotf(tri,c,NN)+carry
        dcol_ref[b*128:(b+1)*128,:]=pre
        drow_sc[:,b*128:(b+1)*128]=pre.T
        carry=pre[127:128]
    lane=lax.broadcasted_iota(jnp.int32,(1,128),1)
    rq=lax.broadcasted_iota(jnp.int32,(qb,qb),0); cq=lax.broadcasted_iota(jnp.int32,(qb,qb),1)
    causal=rq>=cq
    for pr in range(heads//2):
        c0=pr*128
        for b in range(T//qb):
            r0=b*qb; L=r0+qb
            q=x_ref[r0:L,c0:c0+128].astype(F32)*0.125
            k=x_ref[0:L,W+c0:W+c0+128]
            v=x_ref[0:L,2*W+c0:2*W+c0+128]
            same=segc_ref[r0:L,:]==segr_ref[:,0:L]
            outs=[]
            for hh in range(2):
                h=2*pr+hh
                qm=jnp.where((lane>=64) if hh else (lane<64),q,0.0).astype(BF)
                s=dotf(qm,k,NT)
                s=s+dcol_ref[r0:L,h:h+1]-drow_sc[h:h+1,0:L]
                s=jnp.where(same,s,-1e30)
                sd=jnp.where(causal,s[:,r0:],-1e30)
                s=sd if b==0 else jnp.concatenate([s[:,:r0],sd],axis=1)
                m=jnp.max(s,axis=1,keepdims=True)
                p=jnp.exp(s-m)
                l=jnp.sum(p,axis=1,keepdims=True)
                o=dotf(p.astype(BF),v,NN)/l
                outs.append(o)
                lse_sc[r0:L,h:h+1]=m+jnp.log(l)
            mixed_ref[r0:L,c0:c0+128]=jnp.where(lane<64,outs[0],outs[1]).astype(BF)
    rows_ref[0:8,:]=drow_sc[0:8,:]
    for b in range(T//128):
        rows_ref[8:16,b*128:(b+1)*128]=lse_sc[b*128:(b+1)*128,:].T[0:8]

def attn_fwd(qkv, logits, segc, segr, heads=6, qb=256):
    T=qkv.shape[0]
    return pl.pallas_call(functools.partial(fwd_kernel,heads,qb),
        out_shape=(jax.ShapeDtypeStruct((T,heads*64),BF),jax.ShapeDtypeStruct((16,T),F32),jax.ShapeDtypeStruct((T,128),F32)),
        scratch_shapes=[pltpu.VMEM((T,128),F32),pltpu.VMEM((128,T),F32)],
        compiler_params=pltpu.CompilerParams(vmem_limit_bytes=60*1024*1024),
        cost_estimate=pl.CostEstimate(flops=3*10**9,bytes_accessed=4*10**6,transcendentals=4*10**6),
        name="attend_fwd")(qkv,logits,segc,segr)

def bwd_kernel(heads, kb, x_ref, mixed_ref, mb_ref, rows_ref, dcol_ref, segc_ref, segr_ref, grad_ref, drow_ref, dq_sc, rs_sc):
    T=x_ref.shape[0]; W=heads*64
    lane=lax.broadcasted_iota(jnp.int32,(1,128),1)
    rq=lax.broadcasted_iota(jnp.int32,(kb,kb),0); cq=lax.broadcasted_iota(jnp.int32,(kb,kb),1)
    causal=rq<=cq
    for pr in range(heads//2):
        c0=pr*128
        prod=mb_ref[:,c0:c0+128].astype(F32)*mixed_ref[:,c0:c0+128].astype(F32)
        rr=lax.broadcasted_iota(jnp.int32,(8,128),0); ll=lax.broadcasted_iota(jnp.int32,(8,128),1)
        sel=((ll//64)==rr).astype(BF)
        a,b_,c_=split3(prod)
        delta=dotf(sel,a,NT)+dotf(sel,b_,NT)+dotf(sel,c_,NT)
        for b in range(T//kb):
            k0=b*kb
            k=x_ref[k0:k0+kb,W+c0:W+c0+128]
            v=x_ref[k0:k0+kb,2*W+c0:2*W+c0+128]
            q=x_ref[k0:T,c0:c0+128]
            do=mb_ref[k0:T,c0:c0+128]
            same=segc_ref[k0:k0+kb,:]==segr_ref[:,k0:T]
            dks=[];dvs=[];dqs=[]
            for hh in range(2):
                h=2*pr+hh
                msk=(lane>=64) if hh else (lane<64)
                km=jnp.where(msk,k.astype(F32)*0.125,0.0).astype(BF)
                vm=jnp.where(msk,v.astype(F32),0.0).astype(BF)
                s=dotf(km,q,NT)
                r=rows_ref[h:h+1,k0:T]-rows_ref[8+h:9+h,k0:T]
                s=s+r-dcol_ref[k0:k0+kb,h:h+1]
                s=jnp.where(same,s,-1e30)
                sd=jnp.where(causal,s[:,:kb],-1e30)
                s=sd if k0+kb==T else jnp.concatenate([sd,s[:,kb:]],axis=1)
                p=jnp.exp(s)
                dvs.append(dotf(p.astype(BF),do,NN))
                dp=dotf(vm,do,NT)
                ds=p*(dp-delta[hh:hh+1,k0:T])
                dsl=(ds*0.125).astype(BF)
                dks.append(dotf(dsl,q,NN))
                dqs.append(dotf(dsl,k,TN))
                cs=jnp.sum(ds,axis=1,keepdims=True)
                rs_=jnp.sum(ds,axis=0,keepdims=True)
                rs_sc[k0:k0+kb,h:h+1]=cs
                if b==0: drow_ref[h:h+1,:]=rs_
                else: drow_ref[h:h+1,k0:T]+=rs_
            grad_ref[k0:k0+kb,W+c0:W+c0+128]=jnp.where(lane<64,dks[0],dks[1]).astype(BF)
            grad_ref[k0:k0+kb,2*W+c0:2*W+c0+128]=jnp.where(lane<64,dvs[0],dvs[1]).astype(BF)
            dq=jnp.where(lane<64,dqs[0],dqs[1])
            if b==0: dq_sc[...]=dq
            else: dq_sc[k0:T,:]+=dq
        grad_ref[:,c0:c0+128]=dq_sc[...].astype(BF)
    for b in range(T//128):
        drow_ref[:,b*128:(b+1)*128]=drow_ref[:,b*128:(b+1)*128]-rs_sc[b*128:(b+1)*128,:].T[0:8]

def attn_bwd(qkv, mixed, mb, rows, dcol, segc, segr, heads=6, kb=256):
    T=qkv.shape[0]
    return pl.pallas_call(functools.partial(bwd_kernel,heads,kb),
        out_shape=(jax.ShapeDtypeStruct((T,3*heads*64),BF),jax.ShapeDtypeStruct((8,T),F32)),
        scratch_shapes=[pltpu.VMEM((T,128),F32),pltpu.VMEM((T,128),F32)],
        compiler_params=pltpu.CompilerParams(vmem_limit_bytes=60*1024*1024),
        cost_estimate=pl.CostEstimate(flops=8*10**9,bytes_accessed=8*10**6,transcendentals=4*10**6),
        name="attend_bwd")(qkv,mixed,mb,rows,dcol,segc,segr)


class Layout:
    def __init__(self, dp, tensor):
        self.groups = [[core + 2 * i for i in range(dp // 2)] for core in range(2)]
        self.core = [(d, d ^ 1) for d in range(dp)]
        self.pair = [(z, z ^ 1) for z in range(tensor)]
        flat = lambda d, z: d * tensor + z
        devices = [(d, z) for d in range(dp) for z in range(tensor)]
        away = [(d, z) for d, z in devices if (d & 1) != (z >> 1)]
        near = [(d, z) for d, z in devices if (d & 1) == (z >> 1)]
        self.move = [(flat(d, z), flat(d ^ 1, z ^ 2)) for d, z in away]
        self.pair_near = [(flat(d, z), flat(d, z ^ 1)) for d, z in near]
        self.pair_away = [(flat(d, z), flat(d, z ^ 1)) for d, z in away]
        even = [(d, z) for d, z in devices if d & 1 == 0]
        odd = [(d, z) for d, z in devices if d & 1 == 1]
        self.even_far = [(flat(d, z), flat(d + 1, z ^ 2)) for d, z in even]
        self.odd_far = [(flat(d, z), flat(d, z ^ 2)) for d, z in odd]
        self.odd_even = [(flat(d, z), flat(d - 1, z)) for d, z in odd]
        self.back_even_far = [(b, a) for a, b in self.even_far]
        self.back_odd_even = [(b, a) for a, b in self.odd_even]


def cat(*parts):
    return jnp.concatenate(parts, axis=0)


def gather_weight(lay, w, odd):
    a = lax.ppermute(w, BOTH, lay.even_far)
    b = lax.ppermute(w, BOTH, lay.odd_far)
    c = lax.ppermute(w, BOTH, lay.odd_even)
    rows = jnp.where(odd, cat(a, b), cat(w, c))
    return lax.all_gather(rows, "dp", axis=0, tiled=True, axis_index_groups=lay.groups)


def scatter_grad(lay, g, odd):
    r = lax.psum_scatter(
        g, "dp", scatter_dimension=0, tiled=True, axis_index_groups=lay.groups
    )
    half = r.shape[0] // 2
    low, high = r[:half], r[half:]
    a = lax.ppermute(low, BOTH, lay.back_even_far)
    b = lax.ppermute(high, BOTH, lay.odd_far)
    c = lax.ppermute(high, BOTH, lay.back_odd_even)
    return jnp.where(odd, c, low).astype(F32) + jnp.where(odd, b, a).astype(F32)


def gather_pair(lay, x):
    z = lax.ppermute(x, "tensor", lay.pair)
    near = cat(x, z)
    return cat(near, lax.ppermute(near, "dp", lay.core))


def scatter_pair(lay, part):
    half = part.shape[0] // 2
    quarter = half // 2
    got = lax.ppermute(part[half:], "dp", lay.core)
    mine = part[:half].astype(F32) + got.astype(F32)
    got = lax.ppermute(mine[quarter:].astype(BF), "tensor", lay.pair)
    return mine[:quarter] + got.astype(F32)


def gather_sequence(lay, x, odd, zodd, away):
    moved = lax.ppermute(x, BOTH, lay.move)
    near = lax.ppermute(x, BOTH, lay.pair_near)
    far = lax.ppermute(moved, BOTH, lay.pair_away)
    mine = jnp.where(away, moved, x)
    other = jnp.where(away, far, near)
    half = jnp.where(zodd, cat(other, mine), cat(mine, other))
    got = lax.ppermute(half, "dp", lay.core)
    return jnp.where(odd, cat(got, half), cat(half, got))


def scatter_sequence(lay, part, odd, zodd, away):
    half = part.shape[0] // 2
    quarter = half // 2
    first, second = part[:half], part[half:]
    got = lax.ppermute(jnp.where(odd, first, second), "dp", lay.core)
    mine = jnp.where(odd, second, first).astype(F32) + got.astype(F32)
    first, second = mine[:quarter], mine[quarter:]
    got = lax.ppermute(jnp.where(zodd, first, second).astype(BF), "tensor", lay.pair)
    mine = jnp.where(zodd, second, first) + got.astype(F32)
    got = lax.ppermute(mine.astype(BF), BOTH, lay.move)
    return jnp.where(away, got.astype(F32), mine)


def inverse_rms(rows):
    return lax.rsqrt(jnp.mean(rows * rows, axis=-1, keepdims=True) + EPS)


def norm_back(rows, gain, grad):
    r = inverse_rms(rows)
    xhat = rows * r
    scaled = grad * gain
    back = r * (scaled - xhat * jnp.mean(scaled * xhat, axis=-1, keepdims=True))
    return back, jnp.sum(grad * xhat, axis=0)


def per_device(
    layer_input,
    segment_ids,
    attn_gain,
    query_weight,
    key_weight,
    value_weight,
    forget_weight,
    forget_bias,
    output_weight,
    feed_gain,
    gate_weight,
    up_weight,
    down_weight,
    output_cotangent,
):
    lay = Layout(lax.axis_size("dp"), lax.axis_size("tensor"))
    z = lax.axis_index("tensor")
    odd = (lax.axis_index("dp") & 1) == 1
    zodd = (z & 1) == 1
    away = odd != (z >= 2)
    quarter = jnp.where(odd, z ^ 2, z)
    heads = forget_weight.shape[1]
    width = query_weight.shape[1]
    hidden_width = gate_weight.shape[1]
    forget_pad = jnp.pad(forget_weight, ((0, 0), (0, 128 - heads)))

    normed = (layer_input * inverse_rms(layer_input) * attn_gain).astype(BF)
    w_attn_local = jnp.concatenate(
        [query_weight, key_weight, value_weight, forget_pad, output_weight], axis=1
    ).astype(BF)
    w_feed_local = jnp.concatenate([gate_weight, up_weight, down_weight], axis=1).astype(BF)
    w_attn = gather_weight(lay, w_attn_local, odd)
    w_feed = gather_weight(lay, w_feed_local, odd)
    w_qkv = w_attn[:, : 3 * width]
    w_forget = w_attn[:, 3 * width : 3 * width + 128]
    w_output = w_attn[:, 3 * width + 128 :]
    w_gate = w_feed[:, :hidden_width]
    w_up = w_feed[:, hidden_width : 2 * hidden_width]
    w_down = w_feed[:, 2 * hidden_width :]

    segment = jnp.where(away, lax.ppermute(segment_ids, "dp", lay.core), segment_ids)
    bias = jnp.pad(
        lax.dynamic_slice_in_dim(forget_bias, quarter * heads, heads), (0, 128 - heads)
    )

    attn_normed = gather_sequence(lay, normed, odd, zodd, away)
    qkv = dotf(attn_normed, w_qkv, NN).astype(BF)
    logits = dotf(attn_normed, w_forget, NN) + bias
    segc, segr = segment[:, None], segment[None, :]
    mixed, rows, dcol = attn_fwd(qkv, logits, segc, segr, heads)
    branch = scatter_sequence(lay, dotf(mixed, w_output, NT).astype(BF), odd, zodd, away)
    middle = layer_input + branch

    feed_normed = gather_pair(lay, (middle * inverse_rms(middle) * feed_gain).astype(BF))
    cot_low = gather_pair(lay, output_cotangent.astype(BF))
    gate = dotf(feed_normed, w_gate, NN)
    up = dotf(feed_normed, w_up, NN)
    sig = jax.nn.sigmoid(gate)
    silu = gate * sig
    hidden = (silu * up).astype(BF)
    hidden_grad = dotf(cot_low, w_down, NN)
    gate_back = (hidden_grad * up * sig * (1.0 + gate * (1.0 - sig))).astype(BF)
    up_back = (hidden_grad * silu).astype(BF)
    feed_part = (dotf(gate_back, w_gate, NT) + dotf(up_back, w_up, NT)).astype(BF)
    feed_normed_grad = scatter_pair(lay, feed_part)
    layer_output = middle + scatter_pair(lay, dotf(hidden, w_down, NT).astype(BF))
    feed_grads = jnp.concatenate(
        [
            dotf(feed_normed, gate_back, TN).astype(BF),
            dotf(feed_normed, up_back, TN).astype(BF),
            dotf(cot_low, hidden, TN).astype(BF),
        ],
        axis=1,
    )
    feed_shard = scatter_grad(lay, feed_grads, odd)

    middle_part, feed_gain_part = norm_back(middle, feed_gain, feed_normed_grad)
    middle_grad = output_cotangent + middle_part
    middle_low = gather_sequence(lay, middle_grad.astype(BF), odd, zodd, away)
    mixed_back = dotf(middle_low, w_output, NN).astype(BF)
    grads, decay_grad = attn_bwd(qkv, mixed, mixed_back, rows, dcol, segc, segr, heads)
    later = jnp.dot(
        decay_grad,
        jnp.tril(jnp.ones((decay_grad.shape[1],) * 2, F32)),
        precision=lax.Precision.HIGHEST,
    )
    logit_back = (jnp.pad(later.T, ((0, 0), (0, 120))) * jax.nn.sigmoid(-logits)).astype(BF)
    lane = jnp.arange(128)[None, :]
    logit_back = jnp.where(lane < heads, logit_back, 0)
    attn_part = (
        dotf(grads, w_qkv, NT) + dotf(logit_back, w_forget, NT)
    ).astype(BF)
    attn_normed_grad = scatter_sequence(lay, attn_part, odd, zodd, away)
    attn_grads = jnp.concatenate(
        [
            dotf(attn_normed, grads, TN).astype(BF),
            dotf(attn_normed, logit_back, TN).astype(BF),
            dotf(middle_low, mixed, TN).astype(BF),
        ],
        axis=1,
    )
    attn_shard = scatter_grad(lay, attn_grads, odd)
    input_part, attn_gain_part = norm_back(layer_input, attn_gain, attn_normed_grad)
    input_grad = middle_grad + input_part

    bias_part = jnp.sum(logit_back[:, :heads].astype(F32), axis=0)
    bias_full = lax.dynamic_update_slice_in_dim(
        jnp.zeros(forget_bias.shape, F32), bias_part, quarter * heads, 0
    )
    n = attn_gain.shape[0]
    small = lax.psum(cat(attn_gain_part, feed_gain_part, bias_full), BOTH)
    return (
        layer_output,
        input_grad,
        small[:n],
        attn_shard[:, :width],
        attn_shard[:, width : 2 * width],
        attn_shard[:, 2 * width : 3 * width],
        attn_shard[:, 3 * width : 3 * width + heads],
        small[2 * n :],
        attn_shard[:, 3 * width + 128 :],
        small[n : 2 * n],
        feed_shard[:, :hidden_width],
        feed_shard[:, hidden_width : 2 * hidden_width],
        feed_shard[:, 2 * hidden_width :],
    )


def solution(mesh):
    tokens = P(("dp", "tensor"), None)
    weight = P("dp", "tensor")
    in_specs = (
        tokens, P("dp"), P(), weight, weight, weight, weight, P(), weight, P(), weight, weight, weight, tokens,
    )
    out_specs = (
        tokens, tokens, P(), weight, weight, weight, weight, P(), weight, P(), weight, weight, weight,
    )
    return jax.shard_map(
        per_device, mesh=mesh, in_specs=in_specs, out_specs=out_specs, check_vma=False
    )
```

time: 1430 us -> 694 us (0.49)
  waiting for transfers between devices: 1070 us -> 222 us
  starting transfers between devices: 1.6 us -> 162 us
  matrix products: 215 us -> 92.9 us
  Pallas kernels: 0 us -> 32.3 us
  local copies, waits for them, and re-layouts: 24.4 us -> 53.4 us
    reduce_scatter x10 -> x0, waiting for transfers between devices: 670 us -> none  [the longest x1 109 us: per_device(): lax.psum_scatter(right_product(lax.slice_in_dim(mixed, 0, local_rows * la...]
    all_gather x11 -> x2, waiting for transfers between devices: 379 us -> 0.01 us  [gather_weight(): lax.all_gather(rows, 'dp', axis=0, tiled=True, axis_index_groups=lay.groups)]
    ppermute x0 -> x35, waiting for transfers between devices: none -> 165 us  [the longest x2 37.2 us: gather_pair(): z = lax.ppermute(x, 'tensor', lay.pair)]
    ppermute x0 -> x35, starting transfers between devices: none -> 162 us  [the longest x2 57.5 us: gather_sequence(): got = lax.ppermute(half, 'dp', lay.core)]
    dot_general x33 -> x19, matrix products: 174 us -> 92.9 us  [the longest x18 88.3 us: dotf(): return lax.dot_general(a, b, dn, preferred_element_type=F32)]
    sub x2 -> x0, matrix products: 39.5 us -> none  [attend_backward(): score_grad = shares * (share_grad - delta)]
    unnamed x25 -> x6, waiting for transfers between devices: 20.8 us -> 56.6 us
    pallas_call x0 -> x2, Pallas kernels: none -> 32.3 us  [the longest x1 17.6 us: attn_bwd(): pl.pallas_call(functools.partial(bwd_kernel, heads, kb), out_shape=(jax.S...]
  transfers between devices with their start and end apart: 23 -> 39, of which waited for: 22 -> 16; matrix products, arithmetic and copies ran while one was open for 10% -> 17% of each run, Pallas kernels for 0% -> 2%
where the time goes in v1:
time: 694 us; the launch traced here: 688 us
  waiting for transfers between devices  222 us (32%)
  starting transfers between devices  162 us (23%)
  matrix products  92.9 us (13%)
  blocking collectives  64.8 us (9%)
  local copies, waits for them, and re-layouts  53.4 us (8%)
  other arithmetic  45.8 us (7%)
  Pallas kernels  32.3 us (5%)
  between operations  15 us (2%)
    dot_general x18, matrix products, dotf(): return lax.dot_general(a, b, dn, preferred_element_type=F32)  88.3 us
    psum x1, blocking collectives, per_device(): small = lax.psum(cat(attn_gain_part, feed_gain_part, bias_full), BOTH)  64.8 us
    ppermute x2, starting transfers between devices, gather_sequence(): got = lax.ppermute(half, 'dp', lay.core)  57.5 us
    unnamed x6, waiting for transfers between devices  56.6 us
    ppermute x2, waiting for transfers between devices, gather_pair(): z = lax.ppermute(x, 'tensor', lay.pair)  37.2 us
    ppermute x2, waiting for transfers between devices, scatter_sequence(): lax.ppermute(jnp.where(zodd, first, second).astype(BF), 'tensor', lay.pair)  36.6 us
    unnamed x99, local copies, waits for them, and re-layouts  34.2 us
    ppermute x2, starting transfers between devices, scatter_grad(): c = lax.ppermute(high, BOTH, lay.back_odd_even)  32.4 us
  transfers between devices with their start and end apart: 39, of which 16 were waited for; matrix products, arithmetic and copies ran while one was open for 17% of the time, Pallas kernels for 2%

profile of v1, /device:TPU:0, one launch (start us, length us, event | category | flops | bytes accessed | tf_op | source)
XLA Modules:
  0.0 688.1 jit_solution(15491243838408523821)
XLA Ops:
  12.9 6.6 collective-permute-start.4
  20.8 10.9 %collective-permute-done.4 = bf16[192,1664]{1,0:T(8,128)(2,1)S(1)} collective-permute-done((bf16[192,1664]{1,0:T(8,128)(2,1)S(1)}, bf16[192,1664]{1,0:T(8,128)(2,1)S(1)}, u32[]{:S(2)}, u32[]{:S(2)}) %collective-permute-start.4) | collective-permute-done | bytes 639008 | tf_op jit(solution)/shard_map/ppermute | solution.py:169
  31.8 2.4 maximum_select_fusion.5
  36.8 1.7 collective-permute-start.14
  38.5 19.6 %collective-permute-start.13 = (bf16[192,3072]{1,0:T(8,128)(2,1)}, bf16[192,3072]{1,0:T(8,128)(2,1)}, u32[]{:S(2)}, u32[]{:S(2)}) collective-permute-start(bf16[192,3072]{1,0:T(8,128)(2,1)} %pad_maximum_fusion.8), channel_id=1, source_target_pairs={{0,6},{1,7},{2,4},{3,5},{8,14},{9,15},{10,12},{11,13},{16,22},{17,... | collective-permute-start | bytes 3538952 | tf_op jit(solution)/shard_map/ppermute | solution.py:169
  62.3 3.4 collective-permute-start.2
  67.2 16.6 %collective-permute-done.13 = bf16[192,3072]{1,0:T(8,128)(2,1)} collective-permute-done((bf16[192,3072]{1,0:T(8,128)(2,1)}, bf16[192,3072]{1,0:T(8,128)(2,1)}, u32[]{:S(2)}, u32[]{:S(2)}) %collective-permute-start.13) | collective-permute-done | bytes 1179680 | tf_op jit(solution)/shard_map/ppermute | solution.py:169
  83.8 8.3 %maximum_select_fusion.2 = bf16[384,3072]{1,0:T(8,128)(2,1)} fusion(bf16[192,3072]{1,0:T(8,128)(2,1)} %collective-permute-done.14, bf16[192,3072]{1,0:T(8,128)(2,1)} %collective-permute-done.13, bf16[192,3072]{1,0:T(8,128)(2,1)} %collective-permute-done.15, bf16[192,1024]{1,0:T(8,128)(2,1)S(1)} %convert.39, bf16[192,1024]{1,0:T(8,128)(2,1)S(1)} %convert.38, ...), kind=kLoop, calls=%fused_computation.42 | loop fusion | flops 15335424 | bytes 7077889 | tf_op jit(solution)/shard_map/jit(_where)/select_n | solution.py:172
  92.9 3.0 collective-permute-done.2
  96.6 42.4 %collective-permute-start.3 = (bf16[512,1536]{1,0:T(8,128)(2,1)S(1)}, bf16[512,1536]{1,0:T(8,128)(2,1)}, u32[]{:S(2)}, u32[]{:S(2)}) collective-permute-start(bf16[512,1536]{1,0:T(8,128)(2,1)S(1)} %maximum_select_fusion.3), channel_id=1, source_target_pairs={{0,4},{4,0},{8,12},{12,8},{16,20},{20,16},{24,28},{28,24},{1,5},{5... | collective-permute-start | bytes 4718600 | tf_op jit(solution)/shard_map/ppermute | solution.py:210
  139.1 2.7 collective-permute-done.7
  142.9 4.3 convolution_add_fusion.logit_ref
  147.7 7.6 %convolution_convert_fusion.2.x_ref = bf16[1024,1152]{1,0:T(8,128)(2,1)} fusion(bf16[1536,1664]{1,0:T(8,128)(2,1)S(1)} %copy-done.25, bf16[512,1536]{1,0:T(8,128)(2,1)S(1)} %maximum_select_fusion.3, bf16[512,1536]{1,0:T(8,128)(2,1)} %collective-permute-done.3, pred[]{:T(512)S(6)} %eq.6), kind=kOutput, calls=%fused_computation.14 | convolution fusion | flops 3639214080 | bytes 9043969 | tf_op jit(solution)/shard_map/dot_general | solution.py:20
  155.3 14.7 %attend_fwd.1 = (bf16[1024,384]{1,0:T(8,128)(2,1)}, f32[16,1024]{1,0:T(8,128)}, f32[1024,128]{1,0:T(8,128)}) custom-call(bf16[1024,1152]{1,0:T(8,128)(2,1)} %convolution_convert_fusion.2.x_ref, f32[1024,128]{1,0:T(8,128)} %convolution_add_fusion.logit_ref, s32[1024,1]{1,0:T(8,128)} %copy.75.segc_ref, s32[1,1024]{1,0:T(1,128)} %bitcast.20), custom_call_target="tpu_custom_call" | custom-call | flops 3000000000 | bytes 4000000 | tf_op jit(solution)/shard_map/attend_fwd/pallas_call | solution.py:74
  170.0 3.3 convolution_convert_fusion.1
  173.8 3.2 collective-permute-done.8
  178.9 18.6 %collective-permute-done.9 = bf16[256,1536]{1,0:T(8,128)(2,1)S(1)} collective-permute-done((bf16[256,1536]{1,0:T(8,128)(2,1)S(1)}, bf16[256,1536]{1,0:T(8,128)(2,1)S(1)}, u32[]{:S(2)}, u32[]{:S(2)}) %collective-permute-start.9) | collective-permute-done | bytes 786464 | tf_op jit(solution)/shard_map/ppermute | solution.py:221
  200.5 19.4 %collective-permute-done.11 = bf16[256,1536]{1,0:T(8,128)(2,1)S(1)} collective-permute-done((bf16[256,1536]{1,0:T(8,128)(2,1)S(1)}, bf16[256,1536]{1,0:T(8,128)(2,1)S(1)}, u32[]{:S(2)}, u32[]{:S(2)}) %collective-permute-start.11) | collective-permute-done | bytes 786464 | tf_op jit(solution)/shard_map/ppermute | solution.py:189
  220.7 10.9 %collective-permute-start.12 = (bf16[512,1536]{1,0:T(8,128)(2,1)S(1)}, bf16[512,1536]{1,0:T(8,128)(2,1)}, u32[]{:S(2)}, u32[]{:S(2)}) collective-permute-start(bf16[512,1536]{1,0:T(8,128)(2,1)S(1)} %pad_maximum_fusion.4), channel_id=1, source_target_pairs={{0,4},{4,0},{8,12},{12,8},{16,20},{20,16},{24,28},{28,24},{1,5},{5... | collective-permute-start | bytes 4718600 | tf_op jit(solution)/shard_map/ppermute | solution.py:191
  231.7 1.7 collective-permute-start.18
  233.4 17.8 %collective-permute-done.18 = bf16[256,1536]{1,0:T(8,128)(2,1)S(1)} collective-permute-done((bf16[256,1536]{1,0:T(8,128)(2,1)S(1)}, bf16[256,1536]{1,0:T(8,128)(2,1)S(1)}, u32[]{:S(2)}, u32[]{:S(2)}) %collective-permute-start.18) | collective-permute-done | bytes 786464 | tf_op jit(solution)/shard_map/ppermute | solution.py:189
  252.8 6.4 fusion.13
  259.2 6.9 %fusion.9 = f32[1024,1024]{1,0:T(8,128)} fusion(bf16[1536,3072]{1,0:T(8,128)(2,1)S(1)} %copy-done.30, bf16[512,1536]{1,0:T(8,128)(2,1)} %collective-permute-done.12, bf16[256,1536]{1,0:T(8,128)(2,1)S(1)} %copy-done.15, bf16[256,1536]{1,0:T(8,128)(2,1)S(1)} %copy-done.5), kind=kOutput, calls=%fused_computation.35 | convolution fusion | flops 3230662656 | bytes 10485760 | tf_op jit(solution)/shard_map/dot_general | solution.py:20
  266.1 9.7 %multiply_convert_fusion = (bf16[1024,1024]{1,0:T(8,128)(2,1)}, bf16[1024,1024]{1,0:T(8,128)(2,1)}, bf16[1024,1024]{1,0:T(8,128)(2,1)}) fusion(f32[1024,1024]{1,0:T(8,128)S(1)} %fusion.13, f32[1024,1024]{1,0:T(8,128)} %fusion.9, bf16[1536,3072]{1,0:T(8,128)(2,1)S(1)} %copy-done.30, bf16[512,1536]{1,0:T(8,128)(2,1)} %collective-permute-done.19, ...), kind=kOutput, calls=%fused_computation.8 | convolution fusion | flops 3246391296 | bytes 20971520 | tf_op jit(solution)/shard_map/dot_general | solution.py:20
  275.8 5.2 fusion.11
  281.1 3.8 add_convert_fusion.1
  286.4 3.7 convolution_convert_fusion.6
  291.3 1.7 collective-permute-start.21
  294.3 1.7 collective-permute-start.17
  296.0 15.7 %collective-permute-done.21 = bf16[256,1536]{1,0:T(8,128)(2,1)S(1)} collective-permute-done((bf16[256,1536]{1,0:T(8,128)(2,1)S(1)}, bf16[256,1536]{1,0:T(8,128)(2,1)S(1)}, u32[]{:S(2)}, u32[]{:S(2)}) %collective-permute-start.21) | collective-permute-done | bytes 786464 | tf_op jit(solution)/shard_map/ppermute | solution.py:199
  312.4 15.4 %collective-permute-done.17 = bf16[256,1536]{1,0:T(8,128)(2,1)S(1)} collective-permute-done((bf16[256,1536]{1,0:T(8,128)(2,1)S(1)}, bf16[256,1536]{1,0:T(8,128)(2,1)S(1)}, u32[]{:S(2)}, u32[]{:S(2)}) %collective-permute-start.17) | collective-permute-done | bytes 786464 | tf_op jit(solution)/shard_map/ppermute | solution.py:199
  327.7 2.4 fusion.32
  330.9 3.5 collective-permute-start.24
  335.6 16.5 %collective-permute-done.24 = bf16[256,1536]{1,0:T(8,128)(2,1)S(1)} collective-permute-done((bf16[256,1536]{1,0:T(8,128)(2,1)S(1)}, bf16[256,1536]{1,0:T(8,128)(2,1)S(1)}, u32[]{:S(2)}, u32[]{:S(2)}) %collective-permute-start.24) | collective-permute-done | bytes 786464 | tf_op jit(solution)/shard_map/ppermute | solution.py:205
  352.8 15.1 %collective-permute-start.25 = (bf16[512,1536]{1,0:T(8,128)(2,1)S(1)}, bf16[512,1536]{1,0:T(8,128)(2,1)S(1)}, u32[]{:S(2)}, u32[]{:S(2)}) collective-permute-start(bf16[512,1536]{1,0:T(8,128)(2,1)S(1)} %maximum_select_fusion.4), channel_id=1, source_target_pairs={{0,4},{4,0},{8,12},{12,8},{16,20},{20,16},{24,28},{28,24},{1,5},{5... | collective-permute-start | bytes 4718600 | tf_op jit(solution)/shard_map/ppermute | solution.py:210
  367.9 3.0 collective-permute-done.25
  370.9 4.5 convolution_convert_fusion.9.mb_ref
  375.5 17.6 %attend_bwd.1 = (bf16[1024,1152]{1,0:T(8,128)(2,1)}, f32[8,1024]{1,0:T(8,128)}) custom-call(bf16[1024,1152]{1,0:T(8,128)(2,1)} %convolution_convert_fusion.2.x_ref, bf16[1024,384]{1,0:T(8,128)(2,1)} %get-tuple-element.18.mixed_ref, bf16[1024,384]{1,0:T(8,128)(2,1)} %convolution_convert_fusion.9.mb_ref, f32[16,1024]{1,0:T(8,128)} %get-tuple-element.19.rows_ref, ...), custom_call_target="tpu_custom_call" | custom-call | flops 8000000000 | bytes 8000000 | tf_op jit(solution)/shard_map/attend_bwd/pallas_call | solution.py:135
  393.0 4.5 fusion
  397.8 1.8 convolution_convert_fusion.7
  399.6 3.1 convolution_convert_fusion.8
  402.7 5.8 convolution_convert_fusion
  408.5 2.8 pad_maximum_fusion.1
  411.3 7.5 %copy.99 = bf16[1536,1664]{1,0:T(8,128)(2,1)} copy(bf16[1536,1664]{0,1:T(8,128)(2,1)} %pad_maximum_fusion.1) | data formatting | bytes 10223616
  420.2 5.7 convolution_convert_fusion.3
  425.9 5.1 convolution_convert_fusion.4
  431.0 4.9 convolution_convert_fusion.5
  435.9 4.9 pad_maximum_fusion
  440.8 12.7 %copy.101 = bf16[1536,3072]{1,0:T(8,128)(2,1)} copy(bf16[1536,3072]{0,1:T(8,128)(2,1)} %pad_maximum_fusion) | data formatting | bytes 18874368
  453.6 2.1 fusion.20
  456.9 4.5 add_convert_fusion
  461.7 3.3 collective-permute-done.26
  465.8 1.9 collective-permute-start.27
  467.7 18.1 %collective-permute-done.27 = bf16[256,1536]{1,0:T(8,128)(2,1)S(1)} collective-permute-done((bf16[256,1536]{1,0:T(8,128)(2,1)S(1)}, bf16[256,1536]{1,0:T(8,128)(2,1)S(1)}, u32[]{:S(2)}, u32[]{:S(2)}) %collective-permute-start.27) | collective-permute-done | bytes 786464 | tf_op jit(solution)/shard_map/ppermute | solution.py:221
  489.0 1.8 multiply_reduce_fusion.1
  490.8 2.8 multiply_add_fusion
  495.6 27.4 %collective-permute-start.29 = (bf16[192,1664]{1,0:T(8,128)(2,1)S(1)}, bf16[192,1664]{1,0:T(8,128)(2,1)}, u32[]{:S(2)}, u32[]{:S(2)}) collective-permute-start(bf16[192,1664]{1,0:T(8,128)(2,1)S(1)} %get-tuple-element.99), channel_id=1, source_target_pairs={{0,4},{1,5},{2,6},{3,7},{8,12},{9,13},{10,14},{11,15},{16,20},{17,... | collective-permute-start | bytes 1916936 | tf_op jit(solution)/shard_map/ppermute | solution.py:184
  524.3 56.6 %reduce-scatter.9.cloned.1.call-done = bf16[384,3072]{1,0:T(8,128)(2,1)} async-done(((bf16[1536,3072]{1,0:T(8,128)(2,1)}), bf16[384,3072]{1,0:T(8,128)(2,1)}) %reduce-scatter.9.cloned.1.call-update) | async-done | bytes 2359312
  580.9 3.1 fusion.34
  585.7 5.1 collective-permute-start.32
  592.0 64.8 %psum.7 = f32[3096]{0:T(1024)S(1)} all-reduce(f32[3096]{0:T(1024)S(1)} %pad_maximum_fusion.9), channel_id=1, replica_groups=mesh['dp'=8,'tensor'=4] {'dp','tensor'}, use_global_device_ids=true, to_apply=%region_7.8 | all-reduce | flops 3096 | bytes 24768 | tf_op jit(solution)/shard_map/psum | solution.py:350
  670.4 2.5 copy.89
  672.9 2.5 copy.85
  675.4 2.1 convert_add_fusion
  (213 shorter events, 63.9 us)
Async XLA Ops:
  7.2 135.7 %all-gather.3.cloned.1.call-start = ((), (), s32[]{:S(2)}) async-start(), calls=%async_computation.2 | async-start | bytes 6389760 | tf_op jit(solution)/shard_map/all_gather | solution.py:173
  10.1 24.2 %copy-start.12 = (f32[192,1024]{1,0:T(8,128)S(1)}, f32[192,1024]{1,0:T(8,128)}, u32[]{:S(2)}) copy-start(f32[192,1024]{1,0:T(8,128)} %param.26) | copy-start | bytes 2359300
  12.2 8.7 %collective-permute-start.5 = (bf16[192,1664]{1,0:T(8,128)(2,1)S(1)}, bf16[192,1664]{1,0:T(8,128)(2,1)S(1)}, u32[]{:S(2)}, u32[]{:S(2)}) collective-permute-start(bf16[192,1664]{1,0:T(8,128)(2,1)S(1)} %convert_dynamic-update-slice_fusion), channel_id=1, source_target_pairs={{4,6},{5,7},{6,4},{7,5},{12,14},{13,15},{14,12},{15,13},{20,22},{2... | collective-permute-start | bytes 1916936 | tf_op jit(solution)/shard_map/ppermute | solution.py:170
  12.9 18.9 %collective-permute-start.4 = (bf16[192,1664]{1,0:T(8,128)(2,1)S(1)}, bf16[192,1664]{1,0:T(8,128)(2,1)S(1)}, u32[]{:S(2)}, u32[]{:S(2)}) collective-permute-start(bf16[192,1664]{1,0:T(8,128)(2,1)S(1)} %convert_dynamic-update-slice_fusion), channel_id=1, source_target_pairs={{0,6},{1,7},{2,4},{3,5},{8,14},{9,15},{10,12},{11,13},{16,22},{17,... | collective-permute-start | bytes 1916936 | tf_op jit(solution)/shard_map/ppermute | solution.py:169
  19.5 12.3 %collective-permute-start.6 = (bf16[192,1664]{1,0:T(8,128)(2,1)S(1)}, bf16[192,1664]{1,0:T(8,128)(2,1)}, u32[]{:S(2)}, u32[]{:S(2)}) collective-permute-start(bf16[192,1664]{1,0:T(8,128)(2,1)S(1)} %convert_dynamic-update-slice_fusion), channel_id=1, source_target_pairs={{4,0},{5,1},{6,2},{7,3},{12,8},{13,9},{14,10},{15,11},{20,16},{21,... | collective-permute-start | bytes 1916936 | tf_op jit(solution)/shard_map/ppermute | solution.py:171
  20.8 13.5 %copy-start.13 = (f32[192,1024]{1,0:T(8,128)S(1)}, f32[192,1024]{1,0:T(8,128)}, u32[]{:S(2)}) copy-start(f32[192,1024]{1,0:T(8,128)} %param.25) | copy-start | bytes 2359300
  34.2 25.2 %copy-start = (f32[256,1536]{1,0:T(8,128)S(1)}, f32[256,1536]{1,0:T(8,128)}, u32[]{:S(2)}) copy-start(f32[256,1536]{1,0:T(8,128)} %param.14) | copy-start | bytes 4718596
  34.2 218.5 %all-gather.5.cloned.1.call-start = ((), (), s32[]{:S(2)}) async-start(), calls=%async_computation.3 | async-start | bytes 11796480 | tf_op jit(solution)/shard_map/all_gather | solution.py:173
  34.4 25.3 %copy-start.22 = (f32[1536]{0:T(1024)S(1)}, f32[1536]{0:T(1024)}, u32[]{:S(2)}) copy-start(f32[1536]{0:T(1024)} %param.16) | copy-start | bytes 18436
  36.8 30.4 %collective-permute-start.14 = (bf16[192,3072]{1,0:T(8,128)(2,1)}, bf16[192,3072]{1,0:T(8,128)(2,1)}, u32[]{:S(2)}, u32[]{:S(2)}) collective-permute-start(bf16[192,3072]{1,0:T(8,128)(2,1)} %pad_maximum_fusion.8), channel_id=1, source_target_pairs={{4,6},{5,7},{6,4},{7,5},{12,14},{13,15},{14,12},{15,13},{20,22},{2... | collective-permute-start | bytes 3538952 | tf_op jit(solution)/shard_map/ppermute | solution.py:170
  38.5 45.3 %collective-permute-start.13 = (bf16[192,3072]{1,0:T(8,128)(2,1)}, bf16[192,3072]{1,0:T(8,128)(2,1)}, u32[]{:S(2)}, u32[]{:S(2)}) collective-permute-start(bf16[192,3072]{1,0:T(8,128)(2,1)} %pad_maximum_fusion.8), channel_id=1, source_target_pairs={{0,6},{1,7},{2,4},{3,5},{8,14},{9,15},{10,12},{11,13},{16,22},{17,... | collective-permute-start | bytes 3538952 | tf_op jit(solution)/shard_map/ppermute | solution.py:169
  58.1 25.7 %collective-permute-start.15 = (bf16[192,3072]{1,0:T(8,128)(2,1)}, bf16[192,3072]{1,0:T(8,128)(2,1)}, u32[]{:S(2)}, u32[]{:S(2)}) collective-permute-start(bf16[192,3072]{1,0:T(8,128)(2,1)} %pad_maximum_fusion.8), channel_id=1, source_target_pairs={{4,0},{5,1},{6,2},{7,3},{12,8},{13,9},{14,10},{15,11},{20,16},{21,... | collective-permute-start | bytes 3538952 | tf_op jit(solution)/shard_map/ppermute | solution.py:171
  59.6 32.9 %copy-start.26 = (f32[256]{0:T(256)}, f32[256]{0:T(256)S(1)}, u32[]{:S(2)}) copy-start(f32[256]{0:T(256)S(1)} %add_rsqrt_fusion.1) | copy-start | bytes 3076
  60.7 4.9 collective-permute-start
  62.3 33.5 %collective-permute-start.2 = (bf16[256,1536]{1,0:T(8,128)(2,1)}, bf16[256,1536]{1,0:T(8,128)(2,1)S(1)}, u32[]{:S(2)}, u32[]{:S(2)}) collective-permute-start(bf16[256,1536]{1,0:T(8,128)(2,1)} %multiply_convert_fusion.4), channel_id=1, source_target_pairs={{0,1},{1,0},{6,7},{7,6},{8,9},{9,8},{14,15},{15,14},{16,17},{17,16... | collective-permute-start | bytes 2359304 | tf_op jit(solution)/shard_map/ppermute | solution.py:205
  65.7 30.2 %collective-permute-start.1 = (bf16[256,1536]{1,0:T(8,128)(2,1)}, bf16[256,1536]{1,0:T(8,128)(2,1)}, u32[]{:S(2)}, u32[]{:S(2)}) collective-permute-start(bf16[256,1536]{1,0:T(8,128)(2,1)} %collective-permute-done), channel_id=1, source_target_pairs={{2,3},{3,2},{4,5},{5,4},{10,11},{11,10},{12,13},{13,12},{18,19},{1... | collective-permute-start | bytes 2359304 | tf_op jit(solution)/shard_map/ppermute | solution.py:206
  92.2 401.4 %reduce-scatter.7.cloned.1.call-start = ((), (), s32[]{:S(2)}) async-start(), calls=%async_computation.4 | async-start | bytes 6389760
  92.8 46.1 %copy-start.29 = (s32[1024]{0:T(1024)S(1)}, s32[1024]{0:T(1024)}, u32[]{:S(2)}) copy-start(s32[1024]{0:T(1024)} %param.15) | copy-start | bytes 12292
  92.9 46.2 %copy-start.33 = (f32[24]{0:T(128)S(1)}, f32[24]{0:T(128)}, u32[]{:S(2)}) copy-start(f32[24]{0:T(128)} %param.21) | copy-start | bytes 292
  96.5 50.6 %copy-start.10 = (bf16[512,1536]{1,0:T(8,128)(2,1)}, bf16[512,1536]{1,0:T(8,128)(2,1)S(1)}, u32[]{:S(2)}) copy-start(bf16[512,1536]{1,0:T(8,128)(2,1)S(1)} %maximum_select_fusion.3) | copy-start | bytes 4718596
  96.6 46.3 %collective-permute-start.3 = (bf16[512,1536]{1,0:T(8,128)(2,1)S(1)}, bf16[512,1536]{1,0:T(8,128)(2,1)}, u32[]{:S(2)}, u32[]{:S(2)}) collective-permute-start(bf16[512,1536]{1,0:T(8,128)(2,1)S(1)} %maximum_select_fusion.3), channel_id=1, source_target_pairs={{0,4},{4,0},{8,12},{12,8},{16,20},{20,16},{24,28},{28,24},{1,5},{5... | collective-permute-start | bytes 4718600 | tf_op jit(solution)/shard_map/ppermute | solution.py:210
  138.9 2.9 collective-permute-start.7
  141.8 5.3 copy-start.28
  173.5 3.5 collective-permute-start.8
  177.7 19.7 %collective-permute-start.9 = (bf16[256,1536]{1,0:T(8,128)(2,1)S(1)}, bf16[256,1536]{1,0:T(8,128)(2,1)S(1)}, u32[]{:S(2)}, u32[]{:S(2)}) collective-permute-start(bf16[256,1536]{1,0:T(8,128)(2,1)S(1)} %select_convert_fusion.1), channel_id=1, source_target_pairs={{0,1},{1,0},{2,3},{3,2},{4,5},{5,4},{6,7},{7,6},{8,9},{9,8},{10,11... | collective-permute-start | bytes 2359304 | tf_op jit(solution)/shard_map/ppermute | solution.py:221
  197.8 0.7 collective-permute-start.10
  199.1 32.5 %copy-start.3 = (f32[256,1536]{1,0:T(8,128)S(1)}, f32[256,1536]{1,0:T(8,128)}, u32[]{:S(2)}) copy-start(f32[256,1536]{1,0:T(8,128)} %param.27) | copy-start | bytes 4718596
  199.4 53.2 %copy-start.4 = (bf16[256,1536]{1,0:T(8,128)(2,1)}, bf16[256,1536]{1,0:T(8,128)(2,1)S(1)}, u32[]{:S(2)}) copy-start(bf16[256,1536]{1,0:T(8,128)(2,1)S(1)} %multiply_convert_fusion.3) | copy-start | bytes 2359300
  199.4 20.5 %collective-permute-start.11 = (bf16[256,1536]{1,0:T(8,128)(2,1)S(1)}, bf16[256,1536]{1,0:T(8,128)(2,1)S(1)}, u32[]{:S(2)}, u32[]{:S(2)}) collective-permute-start(bf16[256,1536]{1,0:T(8,128)(2,1)S(1)} %multiply_convert_fusion.3), channel_id=1, source_target_pairs={{0,1},{1,0},{2,3},{3,2},{4,5},{5,4},{6,7},{7,6},{8,9},{9,8},{10,11... | collective-permute-start | bytes 2359304 | tf_op jit(solution)/shard_map/ppermute | solution.py:189
  220.7 32.0 %collective-permute-start.12 = (bf16[512,1536]{1,0:T(8,128)(2,1)S(1)}, bf16[512,1536]{1,0:T(8,128)(2,1)}, u32[]{:S(2)}, u32[]{:S(2)}) collective-permute-start(bf16[512,1536]{1,0:T(8,128)(2,1)S(1)} %pad_maximum_fusion.4), channel_id=1, source_target_pairs={{0,4},{4,0},{8,12},{12,8},{16,20},{20,16},{24,28},{28,24},{1,5},{5... | collective-permute-start | bytes 4718600 | tf_op jit(solution)/shard_map/ppermute | solution.py:191
  231.7 20.9 %copy-start.7 = (bf16[256,1536]{1,0:T(8,128)(2,1)}, bf16[256,1536]{1,0:T(8,128)(2,1)S(1)}, u32[]{:S(2)}) copy-start(bf16[256,1536]{1,0:T(8,128)(2,1)S(1)} %convert_element_type.156) | copy-start | bytes 2359300
  231.7 19.5 %collective-permute-start.18 = (bf16[256,1536]{1,0:T(8,128)(2,1)S(1)}, bf16[256,1536]{1,0:T(8,128)(2,1)S(1)}, u32[]{:S(2)}, u32[]{:S(2)}) collective-permute-start(bf16[256,1536]{1,0:T(8,128)(2,1)S(1)} %convert_element_type.156), channel_id=1, source_target_pairs={{0,1},{1,0},{2,3},{3,2},{4,5},{5,4},{6,7},{7,6},{8,9},{9,8},{10,11... | collective-permute-start | bytes 2359304 | tf_op jit(solution)/shard_map/ppermute | solution.py:189
  252.6 13.5 %collective-permute-start.19 = (bf16[512,1536]{1,0:T(8,128)(2,1)}, bf16[512,1536]{1,0:T(8,128)(2,1)}, u32[]{:S(2)}, u32[]{:S(2)}) collective-permute-start(bf16[512,1536]{1,0:T(8,128)(2,1)} %pad_maximum_fusion.5), channel_id=1, source_target_pairs={{0,4},{4,0},{8,12},{12,8},{16,20},{20,16},{24,28},{28,24},{1,5},{5... | collective-permute-start | bytes 4718600 | tf_op jit(solution)/shard_map/ppermute | solution.py:191
  252.7 6.4 copy-start.5
  252.7 6.4 copy-start.15
  252.8 6.4 copy-start.30
  259.2 6.9 %copy-start.8 = (bf16[256,1536]{1,0:T(8,128)(2,1)S(1)}, bf16[256,1536]{1,0:T(8,128)(2,1)}, u32[]{:S(2)}) copy-start(bf16[256,1536]{1,0:T(8,128)(2,1)} %copy-done.7) | copy-start | bytes 2359300
  259.2 6.9 %copy-start.18 = (bf16[256,1536]{1,0:T(8,128)(2,1)S(1)}, bf16[256,1536]{1,0:T(8,128)(2,1)}, u32[]{:S(2)}) copy-start(bf16[256,1536]{1,0:T(8,128)(2,1)} %copy-done.17) | copy-start | bytes 2359300
  275.8 5.2 copy-start.36
  285.0 5.8 collective-permute-start.20
  290.3 3.5 collective-permute-start.16
  291.3 20.5 %collective-permute-start.21 = (bf16[256,1536]{1,0:T(8,128)(2,1)S(1)}, bf16[256,1536]{1,0:T(8,128)(2,1)S(1)}, u32[]{:S(2)}, u32[]{:S(2)}) collective-permute-start(bf16[256,1536]{1,0:T(8,128)(2,1)S(1)} %slice.255), channel_id=1, source_target_pairs={{0,1},{1,0},{2,3},{3,2},{4,5},{5,4},{6,7},{7,6},{8,9},{9,8},{10,11... | collective-permute-start | bytes 2359304 | tf_op jit(solution)/shard_map/ppermute | solution.py:199
  294.3 33.4 %collective-permute-start.17 = (bf16[256,1536]{1,0:T(8,128)(2,1)S(1)}, bf16[256,1536]{1,0:T(8,128)(2,1)S(1)}, u32[]{:S(2)}, u32[]{:S(2)}) collective-permute-start(bf16[256,1536]{1,0:T(8,128)(2,1)S(1)} %slice.256), channel_id=1, source_target_pairs={{0,1},{1,0},{2,3},{3,2},{4,5},{5,4},{6,7},{7,6},{8,9},{9,8},{10,11... | collective-permute-start | bytes 2359304 | tf_op jit(solution)/shard_map/ppermute | solution.py:199
  330.1 4.3 collective-permute-start.22
  330.9 21.2 %collective-permute-start.24 = (bf16[256,1536]{1,0:T(8,128)(2,1)S(1)}, bf16[256,1536]{1,0:T(8,128)(2,1)S(1)}, u32[]{:S(2)}, u32[]{:S(2)}) collective-permute-start(bf16[256,1536]{1,0:T(8,128)(2,1)S(1)} %get-tuple-element.81), channel_id=1, source_target_pairs={{0,1},{1,0},{6,7},{7,6},{8,9},{9,8},{14,15},{15,14},{16,17},{17,16... | collective-permute-start | bytes 2359304 | tf_op jit(solution)/shard_map/ppermute | solution.py:205
  334.4 17.7 %collective-permute-start.23 = (bf16[256,1536]{1,0:T(8,128)(2,1)S(1)}, bf16[256,1536]{1,0:T(8,128)(2,1)S(1)}, u32[]{:S(2)}, u32[]{:S(2)}) collective-permute-start(bf16[256,1536]{1,0:T(8,128)(2,1)S(1)} %collective-permute-done.22), channel_id=1, source_target_pairs={{2,3},{3,2},{4,5},{5,4},{10,11},{11,10},{12,13},{13,12},{18,19},{1... | collective-permute-start | bytes 2359304 | tf_op jit(solution)/shard_map/ppermute | solution.py:206
  352.8 18.1 %collective-permute-start.25 = (bf16[512,1536]{1,0:T(8,128)(2,1)S(1)}, bf16[512,1536]{1,0:T(8,128)(2,1)S(1)}, u32[]{:S(2)}, u32[]{:S(2)}) collective-permute-start(bf16[512,1536]{1,0:T(8,128)(2,1)S(1)} %maximum_select_fusion.4), channel_id=1, source_target_pairs={{0,4},{4,0},{8,12},{12,8},{16,20},{20,16},{24,28},{28,24},{1,5},{5... | collective-permute-start | bytes 4718600 | tf_op jit(solution)/shard_map/ppermute | solution.py:210
  418.9 7.0 %copy-start.6 = (bf16[256,1536]{1,0:T(8,128)(2,1)S(1)}, bf16[256,1536]{1,0:T(8,128)(2,1)}, u32[]{:S(2)}) copy-start(bf16[256,1536]{1,0:T(8,128)(2,1)} %copy-done.4) | copy-start | bytes 2359300
  418.9 7.0 %copy-start.16 = (bf16[256,1536]{1,0:T(8,128)(2,1)S(1)}, bf16[256,1536]{1,0:T(8,128)(2,1)}, u32[]{:S(2)}) copy-start(bf16[256,1536]{1,0:T(8,128)(2,1)} %copy-done.14) | copy-start | bytes 2359300
  418.9 162.0 %reduce-scatter.9.cloned.1.call-start = ((), (), s32[]{:S(2)}) async-start(), calls=%async_computation.5 | async-start | bytes 11796480
  420.2 5.7 copy-start.37
  461.6 3.5 collective-permute-start.26
  465.8 23.2 %copy-start.1 = (f32[256,1536]{1,0:T(8,128)S(1)}, f32[256,1536]{1,0:T(8,128)}, u32[]{:S(2)}) copy-start(f32[256,1536]{1,0:T(8,128)} %param.14) | copy-start | bytes 4718596
  465.8 23.2 %copy-start.23 = (f32[1536]{0:T(1024)S(1)}, f32[1536]{0:T(1024)}, u32[]{:S(2)}) copy-start(f32[1536]{0:T(1024)} %param.16) | copy-start | bytes 18436
  465.8 23.2 %copy-start.27 = (f32[256]{0:T(256)S(1)}, f32[256]{0:T(256)}, u32[]{:S(2)}) copy-start(f32[256]{0:T(256)} %copy-done.26) | copy-start | bytes 3076
  465.8 19.9 %collective-permute-start.27 = (bf16[256,1536]{1,0:T(8,128)(2,1)S(1)}, bf16[256,1536]{1,0:T(8,128)(2,1)S(1)}, u32[]{:S(2)}, u32[]{:S(2)}) collective-permute-start(bf16[256,1536]{1,0:T(8,128)(2,1)S(1)} %select_convert_fusion), channel_id=1, source_target_pairs={{0,1},{1,0},{2,3},{3,2},{4,5},{5,4},{6,7},{7,6},{8,9},{9,8},{10,11... | collective-permute-start | bytes 2359304 | tf_op jit(solution)/shard_map/ppermute | solution.py:221
  487.0 1.9 collective-permute-start.28
  494.9 95.8 %collective-permute-start.30 = (bf16[192,1664]{1,0:T(8,128)(2,1)S(1)}, bf16[192,1664]{1,0:T(8,128)(2,1)S(1)}, u32[]{:S(2)}, u32[]{:S(2)}) collective-permute-start(bf16[192,1664]{1,0:T(8,128)(2,1)S(1)} %get-tuple-element.99), channel_id=1, source_target_pairs={{4,6},{5,7},{6,4},{7,5},{12,14},{13,15},{14,12},{15,13},{20,22},{2... | collective-permute-start | bytes 1916936 | tf_op jit(solution)/shard_map/ppermute | solution.py:183
  495.6 165.5 %collective-permute-start.29 = (bf16[192,1664]{1,0:T(8,128)(2,1)S(1)}, bf16[192,1664]{1,0:T(8,128)(2,1)}, u32[]{:S(2)}, u32[]{:S(2)}) collective-permute-start(bf16[192,1664]{1,0:T(8,128)(2,1)S(1)} %get-tuple-element.99), channel_id=1, source_target_pairs={{0,4},{1,5},{2,6},{3,7},{8,12},{9,13},{10,14},{11,15},{16,20},{17,... | collective-permute-start | bytes 1916936 | tf_op jit(solution)/shard_map/ppermute | solution.py:184
  523.0 136.7 %collective-permute-start.31 = (bf16[192,1664]{1,0:T(8,128)(2,1)S(1)}, bf16[192,1664]{1,0:T(8,128)(2,1)}, u32[]{:S(2)}, u32[]{:S(2)}) collective-permute-start(bf16[192,1664]{1,0:T(8,128)(2,1)S(1)} %get-tuple-element.98), channel_id=1, source_target_pairs={{6,0},{7,1},{4,2},{5,3},{14,8},{15,9},{12,10},{13,11},{22,16},{23,... | collective-permute-start | bytes 1916936 | tf_op jit(solution)/shard_map/ppermute | solution.py:182
  584.0 84.7 %collective-permute-start.33 = (bf16[192,3072]{1,0:T(8,128)(2,1)}, bf16[192,3072]{1,0:T(8,128)(2,1)}, u32[]{:S(2)}, u32[]{:S(2)}) collective-permute-start(bf16[192,3072]{1,0:T(8,128)(2,1)} %get-tuple-element.92), channel_id=1, source_target_pairs={{4,6},{5,7},{6,4},{7,5},{12,14},{13,15},{14,12},{15,13},{20,22},{2... | collective-permute-start | bytes 3538952 | tf_op jit(solution)/shard_map/ppermute | solution.py:183
  585.7 87.3 %collective-permute-start.32 = (bf16[192,3072]{1,0:T(8,128)(2,1)}, bf16[192,3072]{1,0:T(8,128)(2,1)}, u32[]{:S(2)}, u32[]{:S(2)}) collective-permute-start(bf16[192,3072]{1,0:T(8,128)(2,1)} %get-tuple-element.92), channel_id=1, source_target_pairs={{0,4},{1,5},{2,6},{3,7},{8,12},{9,13},{10,14},{11,15},{16,20},{17,... | collective-permute-start | bytes 3538952 | tf_op jit(solution)/shard_map/ppermute | solution.py:184
  590.7 66.7 %copy-start.20 = (bf16[192,1664]{1,0:T(8,128)(2,1)}, bf16[192,1664]{1,0:T(8,128)(2,1)S(1)}, u32[]{:S(2)}) copy-start(bf16[192,1664]{1,0:T(8,128)(2,1)S(1)} %collective-permute-done.30) | copy-start | bytes 1916932
  590.7 79.6 %collective-permute-start.34 = (bf16[192,3072]{1,0:T(8,128)(2,1)}, bf16[192,3072]{1,0:T(8,128)(2,1)}, u32[]{:S(2)}, u32[]{:S(2)}) collective-permute-start(bf16[192,3072]{1,0:T(8,128)(2,1)} %get-tuple-element.91), channel_id=1, source_target_pairs={{6,0},{7,1},{4,2},{5,3},{14,8},{15,9},{12,10},{13,11},{22,16},{23,... | collective-permute-start | bytes 3538952 | tf_op jit(solution)/shard_map/ppermute | solution.py:182
  (18 other events, 51.1 us)
Sparse Core Ops, SparseCore 0:
  34.3 75.3 all-gather.2
  111.6 118.7 all-gather.4
  419.0 63.7 reduce-scatter.6
  485.8 95.0 reduce-scatter.8

commit v2 on v1

v2 whole, which is shorter than its diff:
```python
import functools

import jax
import jax.numpy as jnp
from jax import lax
from jax.experimental import pallas as pl
from jax.experimental.pallas import tpu as pltpu
from jax.sharding import PartitionSpec as P

F32 = jnp.float32
BF = jnp.bfloat16
NT = (((1,), (1,)), ((), ()))
NN = (((1,), (0,)), ((), ()))
TN = (((0,), (0,)), ((), ()))
BOTH = ("dp", "tensor")
EPS = 1e-6


def dotf(a, b, dn):
    return lax.dot_general(a, b, dn, preferred_element_type=F32)


VMEM_LIMIT = 60 * 1024 * 1024


def split3(x):
    a = x.astype(BF)
    r = x - a.astype(F32)
    b = r.astype(BF)
    return a, b, (r - b.astype(F32)).astype(BF)


def exact_dot(left, right, dims):
    return sum(dotf(left, part, dims) for part in split3(right))


def column_of(row):
    parts = [
        jnp.broadcast_to(row[:, i : i + 128], (128, 128)).T[:, :1]
        for i in range(0, row.shape[1], 128)
    ]
    return jnp.concatenate(parts, axis=0)


def attend_kernel(
    heads, span, x_ref, w_ref, bias_ref, seg_ref, qkv_ref, mixed_ref, branch_ref, rows_ref, decay_ref, closed_ref, stat_ref, drow_ref
):
    length = x_ref.shape[0]
    width = heads * 64
    x = x_ref[...]
    qkv_ref[...] = dotf(x, w_ref[:, : 3 * width], NN).astype(BF)
    logits = dotf(x, w_ref[:, 3 * width : 3 * width + 128], NN) + bias_ref[...]
    small = jnp.exp(-jnp.abs(logits))
    log_decay = -(jnp.maximum(-logits, 0.0) + jnp.log1p(small))
    closed_ref[...] = jnp.where(logits >= 0, small, 1.0) / (1.0 + small)
    i = lax.broadcasted_iota(jnp.int32, (128, 128), 0)
    j = lax.broadcasted_iota(jnp.int32, (128, 128), 1)
    below = (i >= j).astype(BF)
    carry = jnp.zeros((1, 128), F32)
    for b in range(0, length, 128):
        total = exact_dot(below, log_decay[b : b + 128], NN) + carry
        decay_ref[b : b + 128, :] = total
        drow_ref[:, b : b + 128] = total.T
        carry = total[127:128]
    lane = lax.broadcasted_iota(jnp.int32, (1, 128), 1)
    i = lax.broadcasted_iota(jnp.int32, (span, span), 0)
    j = lax.broadcasted_iota(jnp.int32, (span, span), 1)
    causal = i >= j
    seg = seg_ref[...]
    for pair in range(heads // 2):
        at = pair * 128
        for begin in range(0, length, span):
            end = begin + span
            q = qkv_ref[begin:end, at : at + 128].astype(F32) * 0.125
            k = qkv_ref[:end, width + at : width + at + 128]
            v = qkv_ref[:end, 2 * width + at : 2 * width + at + 128]
            same = column_of(seg[:, begin:end]) == seg[:, :end]
            outs = []
            for side in range(2):
                h = 2 * pair + side
                own = (lane >= 64) if side else (lane < 64)
                s = dotf(jnp.where(own, q, 0.0).astype(BF), k, NT)
                s = s + decay_ref[begin:end, h : h + 1] - drow_ref[h : h + 1, :end]
                s = jnp.where(same, s, -1e30)
                last = jnp.where(causal, s[:, begin:], -1e30)
                s = jnp.concatenate([s[:, :begin], last], axis=1) if begin else last
                highest = jnp.max(s, axis=1, keepdims=True)
                p = jnp.exp(s - highest)
                total = jnp.sum(p, axis=1, keepdims=True)
                outs.append(dotf(p.astype(BF), v, NN) / total)
                stat_ref[begin:end, h : h + 1] = highest + jnp.log(total)
            mixed_ref[begin:end, at : at + 128] = jnp.where(lane < 64, *outs).astype(BF)
    rows_ref[0:8, :] = drow_ref[0:8, :]
    for b in range(0, length, 128):
        rows_ref[8:16, b : b + 128] = stat_ref[b : b + 128, :].T[0:8]
    branch_ref[...] = dotf(mixed_ref[...], w_ref[:, 3 * width + 128 :], NT).astype(BF)


def attend(x, w, bias, seg, heads):
    length, features = x.shape
    width = heads * 64
    return pl.pallas_call(
        functools.partial(attend_kernel, heads, 256),
        out_shape=(
            jax.ShapeDtypeStruct((length, 3 * width), BF),
            jax.ShapeDtypeStruct((length, width), BF),
            jax.ShapeDtypeStruct((length, features), BF),
            jax.ShapeDtypeStruct((16, length), F32),
            jax.ShapeDtypeStruct((length, 128), F32),
            jax.ShapeDtypeStruct((length, 128), F32),
        ),
        scratch_shapes=[pltpu.VMEM((length, 128), F32), pltpu.VMEM((128, length), F32)],
        compiler_params=pltpu.CompilerParams(vmem_limit_bytes=VMEM_LIMIT),
        cost_estimate=pl.CostEstimate(
            flops=12 * 10**9, bytes_accessed=2 * 10**7, transcendentals=5 * 10**6
        ),
        name="attend",
    )(x, w, bias, seg)


def attend_back_kernel(
    heads, span, m_ref, w_ref, qkv_ref, mixed_ref, rows_ref, decay_ref, closed_ref, seg_ref, grad_ref, part_ref, bias_ref, mb_ref, dq_ref, sums_ref, drow_ref
):
    length = m_ref.shape[0]
    width = heads * 64
    mb_ref[...] = dotf(m_ref[...], w_ref[:, 3 * width + 128 :], NN).astype(BF)
    lane = lax.broadcasted_iota(jnp.int32, (1, 128), 1)
    i = lax.broadcasted_iota(jnp.int32, (span, span), 0)
    j = lax.broadcasted_iota(jnp.int32, (span, span), 1)
    causal = i <= j
    seg = seg_ref[...]
    sums_ref[...] = jnp.zeros_like(sums_ref)
    drow_ref[...] = jnp.zeros_like(drow_ref)
    side_row = lax.broadcasted_iota(jnp.int32, (8, 128), 0)
    side_lane = lax.broadcasted_iota(jnp.int32, (8, 128), 1)
    chosen = ((side_lane // 64) == side_row).astype(BF)
    for pair in range(heads // 2):
        at = pair * 128
        own_product = mb_ref[:, at : at + 128].astype(F32) * mixed_ref[:, at : at + 128].astype(F32)
        delta = exact_dot(chosen, own_product, NT)
        for begin in range(0, length, span):
            end = begin + span
            k = qkv_ref[begin:end, width + at : width + at + 128]
            v = qkv_ref[begin:end, 2 * width + at : 2 * width + at + 128]
            q = qkv_ref[begin:, at : at + 128]
            mb = mb_ref[begin:, at : at + 128]
            same = column_of(seg[:, begin:end]) == seg[:, begin:]
            dks, dvs, dqs = [], [], []
            for side in range(2):
                h = 2 * pair + side
                own = (lane >= 64) if side else (lane < 64)
                own_k = jnp.where(own, k.astype(F32) * 0.125, 0.0).astype(BF)
                own_v = jnp.where(own, v.astype(F32), 0.0).astype(BF)
                s = dotf(own_k, q, NT)
                s = s + (rows_ref[h : h + 1, begin:] - rows_ref[8 + h : 9 + h, begin:])
                s = jnp.where(same, s - decay_ref[begin:end, h : h + 1], -1e30)
                first = jnp.where(causal, s[:, :span], -1e30)
                s = jnp.concatenate([first, s[:, span:]], axis=1) if end < length else first
                p = jnp.exp(s)
                dvs.append(dotf(p.astype(BF), mb, NN))
                ds = p * (dotf(own_v, mb, NT) - delta[side : side + 1, begin:])
                ds_low = (ds * 0.125).astype(BF)
                dks.append(dotf(ds_low, q, NN))
                dqs.append(dotf(ds_low, k, TN))
                sums_ref[begin:end, h : h + 1] = jnp.sum(ds, axis=1, keepdims=True)
                drow_ref[h : h + 1, begin:] += jnp.sum(ds, axis=0, keepdims=True)
            k_at, v_at = width + at, 2 * width + at
            grad_ref[begin:end, k_at : k_at + 128] = jnp.where(lane < 64, *dks).astype(BF)
            grad_ref[begin:end, v_at : v_at + 128] = jnp.where(lane < 64, *dvs).astype(BF)
            dq = jnp.where(lane < 64, *dqs)
            if begin:
                dq_ref[begin:, :] += dq
            else:
                dq_ref[...] = dq
        grad_ref[:, at : at + 128] = dq_ref[...].astype(BF)
    i = lax.broadcasted_iota(jnp.int32, (128, 128), 0)
    j = lax.broadcasted_iota(jnp.int32, (128, 128), 1)
    above = (i <= j).astype(BF)
    carry = jnp.zeros((1, 128), F32)
    bias = jnp.zeros((1, 128), F32)
    blank = jnp.zeros((120, 128), F32)
    for b in reversed(range(0, length, 128)):
        row_sum = jnp.concatenate([drow_ref[:, b : b + 128], blank], axis=0).T
        total = exact_dot(above, row_sum - sums_ref[b : b + 128, :], NN) + carry
        carry = total[0:1]
        back = (closed_ref[b : b + 128, :] * total).astype(BF)
        grad_ref[b : b + 128, 3 * width :] = back
        bias = bias + jnp.sum(back.astype(F32), axis=0, keepdims=True)
    bias_ref[...] = jnp.broadcast_to(bias, bias_ref.shape)
    part_ref[...] = dotf(grad_ref[...], w_ref[:, : 3 * width + 128], NT).astype(BF)


def attend_back(m, w, qkv, mixed, rows, decay, closed, seg, heads):
    length, features = m.shape
    width = heads * 64
    return pl.pallas_call(
        functools.partial(attend_back_kernel, heads, 256),
        out_shape=(
            jax.ShapeDtypeStruct((length, 3 * width + 128), BF),
            jax.ShapeDtypeStruct((length, features), BF),
            jax.ShapeDtypeStruct((8, 128), F32),
        ),
        scratch_shapes=[
            pltpu.VMEM((length, width), BF),
            pltpu.VMEM((length, 128), F32),
            pltpu.VMEM((length, 128), F32),
            pltpu.VMEM((8, length), F32),
        ],
        compiler_params=pltpu.CompilerParams(vmem_limit_bytes=VMEM_LIMIT),
        cost_estimate=pl.CostEstimate(
            flops=20 * 10**9, bytes_accessed=2 * 10**7, transcendentals=5 * 10**6
        ),
        name="attend_back",
    )(m, w, qkv, mixed, rows, decay, closed, seg)


def feed_kernel(x_ref, c_ref, wg_ref, wu_ref, wd_ref, hidden_ref, gb_ref, ub_ref, part_ref, total_ref):
    step = pl.program_id(0)
    x = x_ref[...]
    wg, wu = wg_ref[...], wu_ref[...]
    gate = dotf(x, wg, NN)
    up = dotf(x, wu, NN)
    back = dotf(c_ref[...], wd_ref[...], NN)
    sig = 1.0 / (1.0 + jnp.exp(-gate))
    silu = gate * sig
    hidden_ref[...] = (silu * up).astype(BF)
    gb = (back * up * sig * (1.0 + gate * (1.0 - sig))).astype(BF)
    ub = (back * silu).astype(BF)
    gb_ref[...] = gb
    ub_ref[...] = ub
    part = dotf(gb, wg, NT) + dotf(ub, wu, NT)

    @pl.when(step == 0)
    def _():
        total_ref[...] = part

    @pl.when(step > 0)
    def _():
        total_ref[...] += part

    @pl.when(step == pl.num_programs(0) - 1)
    def _():
        part_ref[...] = total_ref[...].astype(BF)


def feed(x, c, w, block=256):
    length, features = x.shape
    width = w.shape[1] // 3
    steps = width // block
    whole = pl.BlockSpec((length, features), lambda i: (0, 0))
    tall = lambda k: pl.BlockSpec((features, block), lambda i: (0, i + k * steps))
    out = pl.BlockSpec((length, block), lambda i: (0, i))
    return pl.pallas_call(
        feed_kernel,
        grid=(steps,),
        in_specs=[whole, whole, tall(0), tall(1), tall(2)],
        out_specs=[out, out, out, whole],
        out_shape=[jax.ShapeDtypeStruct((length, width), BF)] * 3
        + [jax.ShapeDtypeStruct((length, features), BF)],
        scratch_shapes=[pltpu.VMEM((length, features), F32)],
        compiler_params=pltpu.CompilerParams(vmem_limit_bytes=VMEM_LIMIT),
        cost_estimate=pl.CostEstimate(
            flops=16 * 10**9, bytes_accessed=25 * 10**6, transcendentals=10**6
        ),
        name="feed",
    )(x, c, w, w, w)


def weight_grad_kernel(steps, left, right, *refs):
    ins, out_ref = refs[:-1], refs[-1]
    step = pl.program_id(0)
    begin = 0
    for lhs, rhs, count in zip(left, right, steps):

        @pl.when((step >= begin) & (step < begin + count))
        def _():
            out_ref[...] = dotf(ins[lhs][...], ins[rhs][...], TN).astype(BF)

        begin += count


def weight_grad(lefts, rights, uses, block, name):
    length, features = lefts[0].shape
    counts = [rights[r].shape[1] // block for _, r in uses]
    starts = [sum(counts[:n]) for n in range(len(counts))]
    in_specs = [pl.BlockSpec((length, features), lambda i: (0, 0)) for _ in lefts]
    for n in range(len(rights)):
        in_specs.append(
            pl.BlockSpec(
                (length, block),
                lambda i, n=n: (0, jnp.clip(i - starts[n], 0, counts[n] - 1)),
            )
        )
    return pl.pallas_call(
        functools.partial(
            weight_grad_kernel,
            counts,
            [left for left, _ in uses],
            [len(lefts) + r for _, r in uses],
        ),
        grid=(sum(counts),),
        in_specs=in_specs,
        out_specs=pl.BlockSpec((features, block), lambda i: (0, i)),
        out_shape=jax.ShapeDtypeStruct((features, sum(counts) * block), BF),
        compiler_params=pltpu.CompilerParams(vmem_limit_bytes=VMEM_LIMIT),
        cost_estimate=pl.CostEstimate(
            flops=2 * length * features * sum(counts) * block,
            bytes_accessed=2 * features * (2 * length + sum(counts) * block),
            transcendentals=0,
        ),
        name=name,
    )(*lefts, *rights)
def attend_grads_kernel(x_ref, m_ref, grad_ref, mixed_ref, part_ref, out_ref, gain_ref):
    inner = grad_ref.shape[1]
    out_ref[:, :inner] = dotf(x_ref[...], grad_ref[...], TN).astype(BF)
    out_ref[:, inner:] = dotf(m_ref[...], mixed_ref[...], TN).astype(BF)
    total = jnp.zeros((8, gain_ref.shape[1]), F32)
    for b in range(0, x_ref.shape[0], 8):
        rows = slice(b, b + 8)
        total = total + x_ref[rows, :].astype(F32) * part_ref[rows, :].astype(F32)
    gain_ref[...] = jnp.broadcast_to(jnp.sum(total, axis=0, keepdims=True), gain_ref.shape)


def attend_grads(x, m, grads, mixed, part):
    length, features = x.shape
    columns = grads.shape[1] + mixed.shape[1]
    return pl.pallas_call(
        attend_grads_kernel,
        out_shape=(
            jax.ShapeDtypeStruct((features, columns), BF),
            jax.ShapeDtypeStruct((8, features), F32),
        ),
        compiler_params=pltpu.CompilerParams(vmem_limit_bytes=VMEM_LIMIT),
        cost_estimate=pl.CostEstimate(
            flops=2 * length * features * columns, bytes_accessed=2 * 10**7, transcendentals=0
        ),
        name="attend_grads",
    )(x, m, grads, mixed, part)


def finish_kernel(widths, odd_ref, low_ref, high_ref, a_ref, b_ref, c_ref, *out_refs):
    odd = odd_ref[0] == 1

    def put(first_ref, second_ref):
        begin = 0
        for width, out_ref in zip(widths, out_refs):
            first = first_ref[:, begin : begin + width].astype(F32)
            out_ref[...] = first + second_ref[:, begin : begin + width].astype(F32)
            begin += width

    @pl.when(odd)
    def _():
        put(c_ref, b_ref)

    @pl.when(jnp.logical_not(odd))
    def _():
        put(low_ref, a_ref)


def finish(odd, low, high, a, b, c, widths):
    rows = low.shape[0]
    return pl.pallas_call(
        functools.partial(finish_kernel, widths),
        in_specs=[pl.BlockSpec(memory_space=pltpu.SMEM)]
        + [pl.BlockSpec(memory_space=pltpu.VMEM)] * 5,
        out_shape=[jax.ShapeDtypeStruct((rows, width), F32) for width in widths],
        compiler_params=pltpu.CompilerParams(vmem_limit_bytes=VMEM_LIMIT),
        cost_estimate=pl.CostEstimate(flops=10**6, bytes_accessed=8 * 10**6, transcendentals=0),
        name="finish",
    )(odd, low, high, a, b, c)


class Layout:
    def __init__(self, dp, tensor):
        self.groups = [[core + 2 * i for i in range(dp // 2)] for core in range(2)]
        self.core = [(d, d ^ 1) for d in range(dp)]
        self.pair = [(z, z ^ 1) for z in range(tensor)]
        flat = lambda d, z: d * tensor + z
        devices = [(d, z) for d in range(dp) for z in range(tensor)]
        away = [(d, z) for d, z in devices if (d & 1) != (z >> 1)]
        near = [(d, z) for d, z in devices if (d & 1) == (z >> 1)]
        self.move = [(flat(d, z), flat(d ^ 1, z ^ 2)) for d, z in away]
        self.pair_near = [(flat(d, z), flat(d, z ^ 1)) for d, z in near]
        self.pair_away = [(flat(d, z), flat(d, z ^ 1)) for d, z in away]
        even = [(d, z) for d, z in devices if d & 1 == 0]
        odd = [(d, z) for d, z in devices if d & 1 == 1]
        self.even_far = [(flat(d, z), flat(d + 1, z ^ 2)) for d, z in even]
        self.odd_far = [(flat(d, z), flat(d, z ^ 2)) for d, z in odd]
        self.odd_even = [(flat(d, z), flat(d - 1, z)) for d, z in odd]
        self.back_even_far = [(b, a) for a, b in self.even_far]
        self.back_odd_even = [(b, a) for a, b in self.odd_even]


def cat(*parts):
    return jnp.concatenate(parts, axis=0)


def after(x, *deps):
    return lax.optimization_barrier((x, *deps))[0]


def swap_weight(lay, w, odd):
    a = lax.ppermute(w, BOTH, lay.even_far)
    b = lax.ppermute(w, BOTH, lay.odd_far)
    c = lax.ppermute(w, BOTH, lay.odd_even)
    return jnp.where(odd, cat(a, b), cat(w, c))


def gather_rows(lay, rows):
    return lax.all_gather(rows, "dp", axis=0, tiled=True, axis_index_groups=lay.groups)


def scatter_rows(lay, g):
    return lax.psum_scatter(
        g, "dp", scatter_dimension=0, tiled=True, axis_index_groups=lay.groups
    )


def share_grad(lay, r, odd, widths):
    half = r.shape[0] // 2
    low, high = r[:half], r[half:]
    a = lax.ppermute(low, BOTH, lay.back_even_far)
    b = lax.ppermute(high, BOTH, lay.odd_far)
    c = lax.ppermute(high, BOTH, lay.back_odd_even)
    return finish(odd.astype(jnp.int32).reshape(1), low, high, a, b, c, widths)


def gather_pair(lay, x):
    z = lax.ppermute(x, "tensor", lay.pair)
    near = cat(x, z)
    return cat(near, lax.ppermute(near, "dp", lay.core))


def scatter_pair_first(lay, part):
    half = part.shape[0] // 2
    got = lax.ppermute(part[half:], "dp", lay.core)
    return part[:half].astype(F32) + got.astype(F32)


def scatter_pair_second(lay, mine):
    quarter = mine.shape[0] // 2
    got = lax.ppermute(mine[quarter:].astype(BF), "tensor", lay.pair)
    return mine[:quarter] + got.astype(F32)


def gather_sequence(lay, x, odd, zodd, away):
    moved = lax.ppermute(x, BOTH, lay.move)
    near = lax.ppermute(x, BOTH, lay.pair_near)
    far = lax.ppermute(moved, BOTH, lay.pair_away)
    mine = jnp.where(away, moved, x)
    other = jnp.where(away, far, near)
    half = jnp.where(zodd, cat(other, mine), cat(mine, other))
    got = lax.ppermute(half, "dp", lay.core)
    return jnp.where(odd, cat(got, half), cat(half, got)), moved


def scatter_sequence(lay, part, odd, zodd, away):
    half = part.shape[0] // 2
    quarter = half // 2
    first, second = part[:half], part[half:]
    got = lax.ppermute(jnp.where(odd, first, second), "dp", lay.core)
    mine = jnp.where(odd, second, first).astype(F32) + got.astype(F32)
    first, second = mine[:quarter], mine[quarter:]
    got = lax.ppermute(jnp.where(zodd, first, second).astype(BF), "tensor", lay.pair)
    mine = jnp.where(zodd, second, first) + got.astype(F32)
    got = lax.ppermute(mine.astype(BF), BOTH, lay.move)
    return jnp.where(away, got.astype(F32), mine)


def sum_all(x, axis):
    size = lax.axis_size(axis)
    step = 1
    while step < size:
        x = x + lax.ppermute(x, axis, [(i, i ^ step) for i in range(size)])
        step *= 2
    return x


def inverse_rms(rows):
    return lax.rsqrt(jnp.mean(rows * rows, axis=-1, keepdims=True) + EPS)


def norm_back(rows, gain, grad):
    r = inverse_rms(rows)
    xhat = rows * r
    scaled = grad * gain
    return r * (scaled - xhat * jnp.mean(scaled * xhat, axis=-1, keepdims=True))


def per_device(
    layer_input,
    segment_ids,
    attn_gain,
    query_weight,
    key_weight,
    value_weight,
    forget_weight,
    forget_bias,
    output_weight,
    feed_gain,
    gate_weight,
    up_weight,
    down_weight,
    output_cotangent,
):
    lay = Layout(lax.axis_size("dp"), lax.axis_size("tensor"))
    z = lax.axis_index("tensor")
    odd = (lax.axis_index("dp") & 1) == 1
    zodd = (z & 1) == 1
    away = odd != (z >= 2)
    quarter = jnp.where(odd, z ^ 2, z)
    heads = forget_weight.shape[1]
    width = query_weight.shape[1]
    hidden_width = gate_weight.shape[1]
    features = layer_input.shape[1]
    forget_pad = jnp.pad(forget_weight, ((0, 0), (0, 128 - heads)))

    w_attn_local = jnp.concatenate(
        [query_weight, key_weight, value_weight, forget_pad, output_weight], axis=1
    ).astype(BF)
    attn_rows = swap_weight(lay, w_attn_local, odd)
    w_attn = gather_rows(lay, attn_rows)

    normed = (layer_input * inverse_rms(layer_input) * attn_gain).astype(BF)
    attn_normed, moved = gather_sequence(lay, after(normed, attn_rows), odd, zodd, away)
    segment = jnp.where(away, lax.ppermute(segment_ids, "dp", lay.core), segment_ids)
    seg_row = segment[None, :]
    bias = jnp.pad(
        lax.dynamic_slice_in_dim(forget_bias, quarter * heads, heads), (0, 128 - heads)
    )[None, :]

    w_feed_local = jnp.concatenate([gate_weight, up_weight, down_weight], axis=1).astype(BF)
    feed_rows = swap_weight(lay, after(w_feed_local, moved), odd)
    w_feed = gather_rows(lay, after(feed_rows, w_attn))
    cot_low = gather_pair(lay, after(output_cotangent.astype(BF), feed_rows))

    qkv, mixed, branch_part, rows, decay, closed = attend(
        attn_normed, w_attn, bias, seg_row, heads
    )
    branch = scatter_sequence(lay, after(branch_part, cot_low), odd, zodd, away)
    middle = layer_input + branch

    feed_normed = gather_pair(lay, (middle * inverse_rms(middle) * feed_gain).astype(BF))
    hidden, gate_back, up_back, feed_part = feed(feed_normed, cot_low, w_feed, 512)
    feed_sum = scatter_pair_first(lay, feed_part)
    ready = after(hidden, feed_sum)
    feed_grads = weight_grad(
        [feed_normed, cot_low],
        [gate_back, up_back, ready],
        [(0, 0), (0, 1), (1, 2)],
        512,
        "feed_grads",
    )
    feed_scattered = scatter_rows(lay, feed_grads)
    feed_normed_grad = after(scatter_pair_second(lay, feed_sum), feed_grads)

    middle_grad = output_cotangent + norm_back(middle, feed_gain, feed_normed_grad)
    middle_local = middle_grad.astype(BF)
    middle_low, _ = gather_sequence(lay, middle_local, odd, zodd, away)
    w_down = w_feed[:, 2 * hidden_width :]
    down_part = dotf(after(hidden, middle_local), w_down, NT).astype(BF)
    feed_gain_part = jnp.sum(
        after(feed_part, middle_local).astype(F32) * feed_normed.astype(F32), axis=0
    )
    feed_gain_part = feed_gain_part / feed_gain

    grads, attn_part, bias_part = attend_back(
        middle_low, w_attn, qkv, mixed, rows, decay, closed, seg_row, heads
    )
    down_sum = scatter_pair_first(lay, after(down_part, middle_low))
    layer_output = middle + scatter_pair_second(lay, down_sum)
    attn_grads, attn_gain_part = attend_grads(
        attn_normed, middle_low, after(grads, layer_output), mixed, attn_part
    )
    attn_scattered = scatter_rows(lay, after(attn_grads, feed_scattered))
    attn_gain_part = attn_gain_part[0] / attn_gain
    attn_normed_grad = scatter_sequence(lay, after(attn_part, attn_grads), odd, zodd, away)
    input_grad = middle_grad + norm_back(layer_input, attn_gain, attn_normed_grad)

    bias_full = lax.dynamic_update_slice_in_dim(
        jnp.zeros(forget_bias.shape, F32), bias_part[0, :heads], quarter * heads, 0
    )
    packed = cat(attn_gain_part, feed_gain_part, bias_full)
    size = packed.shape[0]
    packed = jnp.pad(packed, (0, -size % 1024)).reshape(-1, 128)
    packed = after(packed, input_grad)
    small = sum_all(sum_all(packed, "dp"), "tensor").reshape(-1)

    gate_shard, up_shard, down_shard = share_grad(
        lay, after(feed_scattered, small), odd, [hidden_width] * 3
    )
    query_shard, key_shard, value_shard, forget_shard, output_shard = share_grad(
        lay, after(attn_scattered, gate_shard), odd, [width, width, width, 128, width]
    )
    return (
        layer_output,
        input_grad,
        small[:features],
        query_shard,
        key_shard,
        value_shard,
        forget_shard[:, :heads],
        small[2 * features : size],
        output_shard,
        small[features : 2 * features],
        gate_shard,
        up_shard,
        down_shard,
    )


def solution(mesh):
    tokens = P(("dp", "tensor"), None)
    weight = P("dp", "tensor")
    in_specs = (
        tokens, P("dp"), P(), weight, weight, weight, weight, P(), weight, P(), weight, weight, weight, tokens,
    )
    out_specs = (
        tokens, tokens, P(), weight, weight, weight, weight, P(), weight, P(), weight, weight, weight,
    )
    return jax.shard_map(
        per_device, mesh=mesh, in_specs=in_specs, out_specs=out_specs, check_vma=False
    )
```

time: 694 us -> 604 us (0.87)
  matrix products: 92.9 us -> 5.61 us
  Pallas kernels: 32.3 us -> 113 us
  blocking collectives: 64.8 us -> 0 us
  local copies, waits for them, and re-layouts: 53.4 us -> 23.3 us
  starting transfers between devices: 162 us -> 171 us
    dot_general x18 -> x1, matrix products: 88.3 us -> 5.61 us  [dotf(): return lax.dot_general(a, b, dn, preferred_element_type=F32)]
    pallas_call x2 -> x7, Pallas kernels: 32.3 us -> 113 us  [the longest x1 26.7 us: attend_back(): pl.pallas_call(functools.partial(attend_back_kernel, heads, 256), out_sha...]
    psum x1 -> x0, blocking collectives: 64.8 us -> none  [per_device(): small = lax.psum(cat(attn_gain_part, feed_gain_part, bias_full), BOTH)]
    ppermute x16 -> x21, waiting for transfers between devices: 59.5 us -> 117 us  [the longest x2 49.1 us: share_grad(): a = lax.ppermute(low, BOTH, lay.back_even_far)]
    unnamed x6 -> x4, waiting for transfers between devices: 56.6 us -> 0.07 us
    ppermute x2, starting transfers between devices: 57.5 us -> 15.6 us  [gather_sequence(): got = lax.ppermute(half, 'dp', lay.core)]
    ppermute x16 -> x21, starting transfers between devices: 73 us -> 109 us  [the longest x2 47.3 us: swap_weight(): a = lax.ppermute(w, BOTH, lay.even_far)]
    unnamed x99 -> x66, local copies, waits for them, and re-layouts: 34.2 us -> 11.4 us
  transfers between devices with their start and end apart: 39 -> 44, of which waited for: 16 -> 22; matrix products, arithmetic and copies ran while one was open for 17% -> 10% of each run, Pallas kernels for 2% -> 11%
where the time goes in v2:
time: 604 us; the launch traced here: 593 us
  waiting for transfers between devices  216 us (36%)
  starting transfers between devices  171 us (28%)
  Pallas kernels  113 us (19%)
  other arithmetic  48.6 us (8%)
  local copies, waits for them, and re-layouts  23.3 us (4%)
  between operations  14.7 us (2%)
    ppermute x2, waiting for transfers between devices, share_grad(): a = lax.ppermute(low, BOTH, lay.back_even_far)  49.1 us
    ppermute x2, starting transfers between devices, swap_weight(): a = lax.ppermute(w, BOTH, lay.even_far)  47.3 us
    ppermute x2, waiting for transfers between devices, scatter_sequence(): lax.ppermute(jnp.where(zodd, first, second).astype(BF), 'tensor', lay.pair)  37.4 us
    ppermute x2, waiting for transfers between devices, swap_weight(): a = lax.ppermute(w, BOTH, lay.even_far)  30.1 us
    ppermute x2, waiting for transfers between devices, gather_pair(): z = lax.ppermute(x, 'tensor', lay.pair)  28.8 us
    pallas_call x1, Pallas kernels, attend_back(): pl.pallas_call(functools.partial(attend_back_kernel, heads, 256), out_sha...  26.7 us
    pallas_call x1, Pallas kernels, feed(): pl.pallas_call(feed_kernel, grid=(steps,), in_specs=[whole, whole, tall(0...  26.2 us
    ppermute x5, starting transfers between devices, sum_all(): x = x + lax.ppermute(x, axis, [(i, i ^ step) for i in range(size)])  24.6 us
  transfers between devices with their start and end apart: 44, of which 22 were waited for; matrix products, arithmetic and copies ran while one was open for 10% of the time, Pallas kernels for 11%

profile of v2, /device:TPU:0, one launch (start us, length us, event | category | flops | bytes accessed | tf_op | source)
XLA Modules:
  0.0 592.7 jit_solution(2895126889889415851)
XLA Ops:
  11.9 6.6 %collective-permute-start = (bf16[192,1664]{1,0:T(8,128)(2,1)S(1)}, bf16[192,1664]{1,0:T(8,128)(2,1)S(1)}, u32[]{:S(2)}, u32[]{:S(2)}) collective-permute-start(bf16[192,1664]{1,0:T(8,128)(2,1)S(1)} %convert_dynamic-update-slice_fusion), channel_id=1, source_target_pairs={{0,6},{1,7},{2,4},{3,5},{8,14},{9,15},{10,12},{11,13},{16,22},{17,... | collective-permute-start | bytes 1916936 | tf_op jit(solution)/shard_map/ppermute | solution.py:403
  19.8 10.9 %collective-permute-done = bf16[192,1664]{1,0:T(8,128)(2,1)S(1)} collective-permute-done((bf16[192,1664]{1,0:T(8,128)(2,1)S(1)}, bf16[192,1664]{1,0:T(8,128)(2,1)S(1)}, u32[]{:S(2)}, u32[]{:S(2)}) %collective-permute-start) | collective-permute-done | bytes 639008 | tf_op jit(solution)/shard_map/ppermute | solution.py:403
  30.8 2.5 maximum_select_fusion.5
  35.1 1.7 collective-permute-start.3
  37.1 1.8 collective-permute-start.9
  38.9 40.6 %collective-permute-start.8 = (bf16[192,3072]{1,0:T(8,128)(2,1)S(1)}, bf16[192,3072]{1,0:T(8,128)(2,1)}, u32[]{:S(2)}, u32[]{:S(2)}) collective-permute-start(bf16[192,3072]{1,0:T(8,128)(2,1)S(1)} %pad_maximum_fusion.3), channel_id=1, source_target_pairs={{0,6},{1,7},{2,4},{3,5},{8,14},{9,15},{10,12},{11,13},{16,22},{17,... | collective-permute-start | bytes 3538952 | tf_op jit(solution)/shard_map/ppermute | solution.py:403
  80.8 1.5 convert_element_type.88
  82.3 1.9 collective-permute-start.5
  84.2 1.5 collective-permute-start.4
  85.8 19.1 %collective-permute-done.8 = bf16[192,3072]{1,0:T(8,128)(2,1)} collective-permute-done((bf16[192,3072]{1,0:T(8,128)(2,1)S(1)}, bf16[192,3072]{1,0:T(8,128)(2,1)}, u32[]{:S(2)}, u32[]{:S(2)}) %collective-permute-start.8) | collective-permute-done | bytes 1179680 | tf_op jit(solution)/shard_map/ppermute | solution.py:403
  104.9 3.4 maximum_select_fusion.2
  110.2 17.4 %collective-permute-start.11 = (bf16[256,1536]{1,0:T(8,128)(2,1)S(1)}, bf16[256,1536]{1,0:T(8,128)(2,1)S(1)}, u32[]{:S(2)}, u32[]{:S(2)}) collective-permute-start(bf16[256,1536]{1,0:T(8,128)(2,1)S(1)} %convert_element_type.88), channel_id=1, source_target_pairs={{0,1},{1,0},{2,3},{3,2},{4,5},{5,4},{6,7},{7,6},{8,9},{9,8},{10,11... | collective-permute-start | bytes 2359304 | tf_op jit(solution)/shard_map/ppermute | solution.py:429
  128.8 1.8 maximum_select_fusion.3
  130.6 3.3 collective-permute-start.6
  133.9 10.2 %collective-permute-done.11 = bf16[256,1536]{1,0:T(8,128)(2,1)S(1)} collective-permute-done((bf16[256,1536]{1,0:T(8,128)(2,1)S(1)}, bf16[256,1536]{1,0:T(8,128)(2,1)S(1)}, u32[]{:S(2)}, u32[]{:S(2)}) %collective-permute-start.11) | collective-permute-done | bytes 786464 | tf_op jit(solution)/shard_map/ppermute | solution.py:429
  145.3 3.0 collective-permute-start.12
  148.9 2.3 collective-permute-done.7
  153.7 4.8 maximum_select_fusion.x_ref
  158.5 2.7 constant_dynamic-update-slice_fusion.c_ref.refs_1_
  161.2 23.7 %attend.1 = (bf16[1024,1152]{1,0:T(8,128)(2,1)}, bf16[1024,384]{1,0:T(8,128)(2,1)}, bf16[1024,1536]{1,0:T(8,128)(2,1)}, f32[16,1024]{1,0:T(8,128)}, f32[1024,128]{1,0:T(8,128)}, /*index=5*/f32[1024,128]{1,0:T(8,128)}) custom-call(bf16[1024,1536]{1,0:T(8,128)(2,1)} %maximum_select_fusion.x_ref, bf16[1536,1664]{1,0:T(8,128)(2,1)} %all-gather.3.cloned.1.call-done.w_ref, ...), custom_call_target="tpu_custom_call" | custom-call | flops 12000000000 | bytes 20000000 | tf_op jit(solution)/shard_map/attend/pallas_call | solution.py:102
  184.9 2.2 broadcast_select_fusion.1
  187.3 3.3 collective-permute-done.13
  192.5 18.4 %collective-permute-done.14 = bf16[256,1536]{1,0:T(8,128)(2,1)S(1)} collective-permute-done((bf16[256,1536]{1,0:T(8,128)(2,1)S(1)}, bf16[256,1536]{1,0:T(8,128)(2,1)S(1)}, u32[]{:S(2)}, u32[]{:S(2)}) %collective-permute-start.14) | collective-permute-done | bytes 786464 | tf_op jit(solution)/shard_map/ppermute | solution.py:464
  214.1 18.7 %collective-permute-done.16 = bf16[256,1536]{1,0:T(8,128)(2,1)S(1)} collective-permute-done((bf16[256,1536]{1,0:T(8,128)(2,1)S(1)}, bf16[256,1536]{1,0:T(8,128)(2,1)S(1)}, u32[]{:S(2)}, u32[]{:S(2)}) %collective-permute-start.16) | collective-permute-done | bytes 786464 | tf_op jit(solution)/shard_map/ppermute | solution.py:429
  232.9 12.9 %collective-permute-start.17 = (bf16[512,1536]{1,0:T(8,128)(2,1)S(1)}, bf16[512,1536]{1,0:T(8,128)(2,1)S(1)}, u32[]{:S(2)}, u32[]{:S(2)}) collective-permute-start(bf16[512,1536]{1,0:T(8,128)(2,1)S(1)} %pad_maximum_fusion.2), channel_id=1, source_target_pairs={{0,4},{4,0},{8,12},{12,8},{16,20},{20,16},{24,28},{28,24},{1,5},{5... | collective-permute-start | bytes 4718600 | tf_op jit(solution)/shard_map/ppermute | solution.py:431
  245.8 3.0 collective-permute-done.17
  250.0 1.8 pad_maximum_fusion.x_ref.refs_0_
  251.9 26.2 %feed.1 = (bf16[1024,1024]{1,0:T(8,128)(2,1)}, bf16[1024,1024]{1,0:T(8,128)(2,1)}, bf16[1024,1024]{1,0:T(8,128)(2,1)}, bf16[1024,1536]{1,0:T(8,128)(2,1)}) custom-call(bf16[1024,1536]{1,0:T(8,128)(2,1)} %pad_maximum_fusion.x_ref.refs_0_, bf16[1024,1536]{1,0:T(8,128)(2,1)} %constant_dynamic-update-slice_fusion.c_ref.refs_1_, ...), custom_call_target="tpu_custom_call" | custom-call | flops 16000000000 | bytes 25000000 | tf_op jit(solution)/shard_map/feed/pallas_call | solution.py:253
  278.1 1.7 slice.94
  280.2 3.0 collective-permute-done.18
  283.2 2.2 convert_add_fusion.2
  285.4 16.6 %feed_grads.1 = bf16[1536,3072]{1,0:T(8,128)(2,1)} custom-call(bf16[1024,1536]{1,0:T(8,128)(2,1)} %pad_maximum_fusion.x_ref.refs_0_, bf16[1024,1536]{1,0:T(8,128)(2,1)} %constant_dynamic-update-slice_fusion.c_ref.refs_1_, bf16[1024,1024]{1,0:T(8,128)(2,1)} %get-tuple-element.60.refs_2_, bf16[1024,1024]{1,0:T(8,128)(2,1)} %get-tuple-element.61.refs_3_, ...), custom_call_target="tpu_custom_call" | custom-call | flops 9663676416 | bytes 15728640 | tf_op jit(solution)/shard_map/feed_grads/pallas_call | solution.py:294
  302.0 1.5 slice.169
  304.0 19.4 %collective-permute-done.19 = bf16[256,1536]{1,0:T(8,128)(2,1)S(1)} collective-permute-done((bf16[256,1536]{1,0:T(8,128)(2,1)S(1)}, bf16[256,1536]{1,0:T(8,128)(2,1)S(1)}, u32[]{:S(2)}, u32[]{:S(2)}) %collective-permute-start.19) | collective-permute-done | bytes 786464 | tf_op jit(solution)/shard_map/ppermute | solution.py:442
  323.4 1.8 slice_add_fusion.1
  326.6 1.6 fusion.5
  328.9 2.2 collective-permute-start.22
  331.9 19.3 %collective-permute-done.22 = bf16[256,1536]{1,0:T(8,128)(2,1)S(1)} collective-permute-done((bf16[256,1536]{1,0:T(8,128)(2,1)S(1)}, bf16[256,1536]{1,0:T(8,128)(2,1)S(1)}, u32[]{:S(2)}, u32[]{:S(2)}) %collective-permute-start.22) | collective-permute-done | bytes 786464 | tf_op jit(solution)/shard_map/ppermute | solution.py:448
  351.9 12.3 %collective-permute-start.23 = (bf16[512,1536]{1,0:T(8,128)(2,1)S(1)}, bf16[512,1536]{1,0:T(8,128)(2,1)S(1)}, u32[]{:S(2)}, u32[]{:S(2)}) collective-permute-start(bf16[512,1536]{1,0:T(8,128)(2,1)S(1)} %maximum_select_fusion.4), channel_id=1, source_target_pairs={{0,4},{4,0},{8,12},{12,8},{16,20},{20,16},{24,28},{28,24},{1,5},{5... | collective-permute-start | bytes 4718600 | tf_op jit(solution)/shard_map/ppermute | solution.py:453
  364.3 5.6 convolution_convert_fusion
  369.9 2.4 maximum_select_fusion.1.m_ref
  373.5 3.0 collective-permute-done.24
  377.0 1.6 copy-done.7
  379.5 1.6 collective-permute-start.25
  381.1 26.7 %attend_back.1 = (bf16[1024,1280]{1,0:T(8,128)(2,1)}, bf16[1024,1536]{1,0:T(8,128)(2,1)}, f32[8,128]{1,0:T(8,128)}) custom-call(bf16[1024,1536]{1,0:T(8,128)(2,1)} %maximum_select_fusion.1.m_ref, bf16[1536,1664]{1,0:T(8,128)(2,1)} %all-gather.3.cloned.1.call-done.w_ref, bf16[1024,1152]{1,0:T(8,128)(2,1)} %get-tuple-element.66.qkv_ref, ...), custom_call_target="tpu_custom_call" | custom-call | flops 20000000000 | bytes 20000000 | tf_op jit(solution)/shard_map/attend_back/pallas_call | solution.py:196
  407.8 3.1 fusion.1
  410.9 13.0 %attend_grads.1 = (bf16[1536,1664]{1,0:T(8,128)(2,1)}, f32[8,1536]{1,0:T(8,128)}) custom-call(bf16[1024,1536]{1,0:T(8,128)(2,1)} %maximum_select_fusion.x_ref, bf16[1024,1536]{1,0:T(8,128)(2,1)} %maximum_select_fusion.1.m_ref, bf16[1024,1280]{1,0:T(8,128)(2,1)} %get-tuple-element.73.grad_ref, bf16[1024,384]{1,0:T(8,128)(2,1)} %get-tuple-element.67.mixed_ref, ...), custom_call_target="tpu_custom_call" | custom-call | flops 5234491392 | bytes 20000000 | tf_op jit(solution)/shard_map/attend_grads/pallas_call | solution.py:327
  424.0 2.2 broadcast_select_fusion
  426.4 3.3 collective-permute-done.26
  431.1 19.0 %collective-permute-done.27 = bf16[256,1536]{1,0:T(8,128)(2,1)S(1)} collective-permute-done((bf16[256,1536]{1,0:T(8,128)(2,1)S(1)}, bf16[256,1536]{1,0:T(8,128)(2,1)S(1)}, u32[]{:S(2)}, u32[]{:S(2)}) %collective-permute-start.27) | collective-permute-done | bytes 786464 | tf_op jit(solution)/shard_map/ppermute | solution.py:464
  456.1 1.7 multiply_add_fusion
  457.7 20.3 %collective-permute-start.29 = (f32[32,128]{1,0:T(8,128)S(1)}, f32[32,128]{1,0:T(8,128)S(1)}, u32[]{:S(2)}, u32[]{:S(2)}) collective-permute-start(f32[32,128]{1,0:T(8,128)S(1)} %fusion.3), channel_id=1, source_target_pairs={{0,4},{4,0},{8,12},{12,8},{16,20},{20,16},{24,28},{28,24},{1,5},{5... | collective-permute-start | bytes 49160 | tf_op jit(solution)/shard_map/ppermute | solution.py:474
  480.4 2.6 collective-permute-done.30
  484.5 2.3 collective-permute-done.31
  486.7 3.7 collective-permute-done.32
  491.8 3.4 collective-permute-done.33
  496.6 1.7 collective-permute-start.35
  498.3 7.6 %collective-permute-start.36 = (bf16[192,3072]{1,0:T(8,128)(2,1)S(1)}, bf16[192,3072]{1,0:T(8,128)(2,1)}, u32[]{:S(2)}, u32[]{:S(2)}) collective-permute-start(bf16[192,3072]{1,0:T(8,128)(2,1)S(1)} %get-tuple-element.123.high_ref), channel_id=1, source_target_pairs={{0,4},{1,5},{2,6},{3,7},{8,12},{9,13},{10,14},{11,15},{16,20},{17,... | collective-permute-start | bytes 3538952 | tf_op jit(solution)/shard_map/ppermute | solution.py:424
  505.9 33.0 %collective-permute-done.34.a_ref = bf16[192,3072]{1,0:T(8,128)(2,1)} collective-permute-done((bf16[192,3072]{1,0:T(8,128)(2,1)S(1)}, bf16[192,3072]{1,0:T(8,128)(2,1)}, u32[]{:S(2)}, u32[]{:S(2)}) %collective-permute-start.34) | collective-permute-done | bytes 1179680 | tf_op jit(solution)/shard_map/ppermute | solution.py:422
  538.9 4.3 finish.2
  546.7 15.7 %collective-permute-start.39 = (bf16[192,1664]{1,0:T(8,128)(2,1)S(1)}, bf16[192,1664]{1,0:T(8,128)(2,1)S(1)}, u32[]{:S(2)}, u32[]{:S(2)}) collective-permute-start(bf16[192,1664]{1,0:T(8,128)(2,1)S(1)} %get-tuple-element.125.high_ref), channel_id=1, source_target_pairs={{0,4},{1,5},{2,6},{3,7},{8,12},{9,13},{10,14},{11,15},{16,20},{17,... | collective-permute-start | bytes 1916936 | tf_op jit(solution)/shard_map/ppermute | solution.py:424
  563.5 16.1 %collective-permute-done.37.a_ref = bf16[192,1664]{1,0:T(8,128)(2,1)S(1)} collective-permute-done((bf16[192,1664]{1,0:T(8,128)(2,1)S(1)}, bf16[192,1664]{1,0:T(8,128)(2,1)S(1)}, u32[]{:S(2)}, u32[]{:S(2)}) %collective-permute-start.37) | collective-permute-done | bytes 639008 | tf_op jit(solution)/shard_map/ppermute | solution.py:422
  581.4 3.0 finish.3
  584.4 1.6 copy.30
  (174 shorter events, 50.9 us)
Async XLA Ops:
  7.2 4.0 copy-start.25
  7.2 101.7 %all-gather.3.cloned.1.call-start = ((), (), s32[]{:S(2)}) async-start(), calls=%async_computation.2 | async-start | bytes 6389760 | tf_op jit(solution)/shard_map/all_gather | solution.py:410
  11.2 8.7 %collective-permute-start.1 = (bf16[192,1664]{1,0:T(8,128)(2,1)S(1)}, bf16[192,1664]{1,0:T(8,128)(2,1)S(1)}, u32[]{:S(2)}, u32[]{:S(2)}) collective-permute-start(bf16[192,1664]{1,0:T(8,128)(2,1)S(1)} %convert_dynamic-update-slice_fusion), channel_id=1, source_target_pairs={{4,6},{5,7},{6,4},{7,5},{12,14},{13,15},{14,12},{15,13},{20,22},{2... | collective-permute-start | bytes 1916936 | tf_op jit(solution)/shard_map/ppermute | solution.py:404
  11.9 18.9 %collective-permute-start = (bf16[192,1664]{1,0:T(8,128)(2,1)S(1)}, bf16[192,1664]{1,0:T(8,128)(2,1)S(1)}, u32[]{:S(2)}, u32[]{:S(2)}) collective-permute-start(bf16[192,1664]{1,0:T(8,128)(2,1)S(1)} %convert_dynamic-update-slice_fusion), channel_id=1, source_target_pairs={{0,6},{1,7},{2,4},{3,5},{8,14},{9,15},{10,12},{11,13},{16,22},{17,... | collective-permute-start | bytes 1916936 | tf_op jit(solution)/shard_map/ppermute | solution.py:403
  18.5 12.3 %collective-permute-start.2 = (bf16[192,1664]{1,0:T(8,128)(2,1)S(1)}, bf16[192,1664]{1,0:T(8,128)(2,1)}, u32[]{:S(2)}, u32[]{:S(2)}) collective-permute-start(bf16[192,1664]{1,0:T(8,128)(2,1)S(1)} %convert_dynamic-update-slice_fusion), channel_id=1, source_target_pairs={{4,0},{5,1},{6,2},{7,3},{12,8},{13,9},{14,10},{15,11},{20,16},{21,... | collective-permute-start | bytes 1916936 | tf_op jit(solution)/shard_map/ppermute | solution.py:405
  30.8 2.6 copy-start
  33.4 218.5 %all-gather.5.cloned.1.call-start = ((), (), s32[]{:S(2)}) async-start(), calls=%async_computation.3 | async-start | bytes 11796480 | tf_op jit(solution)/shard_map/all_gather | solution.py:410
  33.6 3.2 copy-start.19
  34.0 2.8 copy-start.20
  35.1 2.0 collective-permute-start.3
  37.1 48.7 %collective-permute-start.9 = (bf16[192,3072]{1,0:T(8,128)(2,1)S(1)}, bf16[192,3072]{1,0:T(8,128)(2,1)}, u32[]{:S(2)}, u32[]{:S(2)}) collective-permute-start(bf16[192,3072]{1,0:T(8,128)(2,1)S(1)} %pad_maximum_fusion.3), channel_id=1, source_target_pairs={{4,6},{5,7},{6,4},{7,5},{12,14},{13,15},{14,12},{15,13},{20,22},{2... | collective-permute-start | bytes 3538952 | tf_op jit(solution)/shard_map/ppermute | solution.py:404
  38.9 66.0 %collective-permute-start.8 = (bf16[192,3072]{1,0:T(8,128)(2,1)S(1)}, bf16[192,3072]{1,0:T(8,128)(2,1)}, u32[]{:S(2)}, u32[]{:S(2)}) collective-permute-start(bf16[192,3072]{1,0:T(8,128)(2,1)S(1)} %pad_maximum_fusion.3), channel_id=1, source_target_pairs={{0,6},{1,7},{2,4},{3,5},{8,14},{9,15},{10,12},{11,13},{16,22},{17,... | collective-permute-start | bytes 3538952 | tf_op jit(solution)/shard_map/ppermute | solution.py:403
  79.5 25.4 %collective-permute-start.10 = (bf16[192,3072]{1,0:T(8,128)(2,1)S(1)}, bf16[192,3072]{1,0:T(8,128)(2,1)}, u32[]{:S(2)}, u32[]{:S(2)}) collective-permute-start(bf16[192,3072]{1,0:T(8,128)(2,1)S(1)} %pad_maximum_fusion.3), channel_id=1, source_target_pairs={{4,0},{5,1},{6,2},{7,3},{12,8},{13,9},{14,10},{15,11},{20,16},{21,... | collective-permute-start | bytes 3538952 | tf_op jit(solution)/shard_map/ppermute | solution.py:405
  82.3 45.3 %collective-permute-start.5 = (bf16[256,1536]{1,0:T(8,128)(2,1)}, bf16[256,1536]{1,0:T(8,128)(2,1)}, u32[]{:S(2)}, u32[]{:S(2)}) collective-permute-start(bf16[256,1536]{1,0:T(8,128)(2,1)} %multiply_convert_fusion.1), channel_id=1, source_target_pairs={{0,1},{1,0},{6,7},{7,6},{8,9},{9,8},{14,15},{15,14},{16,17},{17,16... | collective-permute-start | bytes 2359304 | tf_op jit(solution)/shard_map/ppermute | solution.py:448
  84.2 43.4 %collective-permute-start.4 = (bf16[256,1536]{1,0:T(8,128)(2,1)}, bf16[256,1536]{1,0:T(8,128)(2,1)}, u32[]{:S(2)}, u32[]{:S(2)}) collective-permute-start(bf16[256,1536]{1,0:T(8,128)(2,1)} %collective-permute-done.3), channel_id=1, source_target_pairs={{2,3},{3,2},{4,5},{5,4},{10,11},{11,10},{12,13},{13,12},{18,19},{1... | collective-permute-start | bytes 2359304 | tf_op jit(solution)/shard_map/ppermute | solution.py:449
  108.9 315.0 %reduce-scatter.3.cloned.1.call-start = ((), (), s32[]{:S(2)}) async-start(), calls=%async_computation.4 | async-start | bytes 11796480 | tf_op jit(solution)/shard_map/reduce_scatter | solution.py:414
  110.2 33.8 %collective-permute-start.11 = (bf16[256,1536]{1,0:T(8,128)(2,1)S(1)}, bf16[256,1536]{1,0:T(8,128)(2,1)S(1)}, u32[]{:S(2)}, u32[]{:S(2)}) collective-permute-start(bf16[256,1536]{1,0:T(8,128)(2,1)S(1)} %convert_element_type.88), channel_id=1, source_target_pairs={{0,1},{1,0},{2,3},{3,2},{4,5},{5,4},{6,7},{7,6},{8,9},{9,8},{10,11... | collective-permute-start | bytes 2359304 | tf_op jit(solution)/shard_map/ppermute | solution.py:429
  130.6 17.7 %copy-start.28 = (s32[1024]{0:T(1024)S(1)}, s32[1024]{0:T(1024)}, u32[]{:S(2)}) copy-start(s32[1024]{0:T(1024)} %param.15) | copy-start | bytes 12292
  130.6 17.7 %copy-start.29 = (f32[24]{0:T(128)S(1)}, f32[24]{0:T(128)}, u32[]{:S(2)}) copy-start(f32[24]{0:T(128)} %param.21) | copy-start | bytes 292
  130.6 23.1 %collective-permute-start.6 = (bf16[512,1536]{1,0:T(8,128)(2,1)}, bf16[512,1536]{1,0:T(8,128)(2,1)}, u32[]{:S(2)}, u32[]{:S(2)}) collective-permute-start(bf16[512,1536]{1,0:T(8,128)(2,1)} %maximum_select_fusion.3), channel_id=1, source_target_pairs={{0,4},{4,0},{8,12},{12,8},{16,20},{20,16},{24,28},{28,24},{1,5},{5... | collective-permute-start | bytes 4718600 | tf_op jit(solution)/shard_map/ppermute | solution.py:453
  145.3 13.2 %collective-permute-start.12 = (bf16[512,1536]{1,0:T(8,128)(2,1)}, bf16[512,1536]{1,0:T(8,128)(2,1)}, u32[]{:S(2)}, u32[]{:S(2)}) collective-permute-start(bf16[512,1536]{1,0:T(8,128)(2,1)} %pad_maximum_fusion.1), channel_id=1, source_target_pairs={{0,4},{4,0},{8,12},{12,8},{16,20},{20,16},{24,28},{28,24},{1,5},{5... | collective-permute-start | bytes 4718600 | tf_op jit(solution)/shard_map/ppermute | solution.py:431
  148.3 2.9 collective-permute-start.7
  184.9 5.7 copy-start.6
  187.1 3.5 collective-permute-start.13
  191.3 19.7 %collective-permute-start.14 = (bf16[256,1536]{1,0:T(8,128)(2,1)S(1)}, bf16[256,1536]{1,0:T(8,128)(2,1)S(1)}, u32[]{:S(2)}, u32[]{:S(2)}) collective-permute-start(bf16[256,1536]{1,0:T(8,128)(2,1)S(1)} %select_convert_fusion.1), channel_id=1, source_target_pairs={{0,1},{1,0},{2,3},{3,2},{4,5},{5,4},{6,7},{7,6},{8,9},{9,8},{10,11... | collective-permute-start | bytes 2359304 | tf_op jit(solution)/shard_map/ppermute | solution.py:464
  211.3 0.7 collective-permute-start.15
  212.9 36.0 %copy-start.3 = (bf16[256,1536]{1,0:T(8,128)(2,1)}, bf16[256,1536]{1,0:T(8,128)(2,1)S(1)}, u32[]{:S(2)}) copy-start(bf16[256,1536]{1,0:T(8,128)(2,1)S(1)} %multiply_convert_fusion) | copy-start | bytes 2359300
  212.9 19.9 %collective-permute-start.16 = (bf16[256,1536]{1,0:T(8,128)(2,1)S(1)}, bf16[256,1536]{1,0:T(8,128)(2,1)S(1)}, u32[]{:S(2)}, u32[]{:S(2)}) collective-permute-start(bf16[256,1536]{1,0:T(8,128)(2,1)S(1)} %multiply_convert_fusion), channel_id=1, source_target_pairs={{0,1},{1,0},{2,3},{3,2},{4,5},{5,4},{6,7},{7,6},{8,9},{9,8},{10,11... | collective-permute-start | bytes 2359304 | tf_op jit(solution)/shard_map/ppermute | solution.py:429
  232.8 16.0 %copy-start.8 = (bf16[256,1536]{1,0:T(8,128)(2,1)}, bf16[256,1536]{1,0:T(8,128)(2,1)S(1)}, u32[]{:S(2)}) copy-start(bf16[256,1536]{1,0:T(8,128)(2,1)S(1)} %collective-permute-done.16) | copy-start | bytes 2359300
  232.9 15.9 %collective-permute-start.17 = (bf16[512,1536]{1,0:T(8,128)(2,1)S(1)}, bf16[512,1536]{1,0:T(8,128)(2,1)S(1)}, u32[]{:S(2)}, u32[]{:S(2)}) collective-permute-start(bf16[512,1536]{1,0:T(8,128)(2,1)S(1)} %pad_maximum_fusion.2), channel_id=1, source_target_pairs={{0,4},{4,0},{8,12},{12,8},{16,20},{20,16},{24,28},{28,24},{1,5},{5... | collective-permute-start | bytes 4718600 | tf_op jit(solution)/shard_map/ppermute | solution.py:431
  278.1 5.2 copy-start.1
  279.7 3.5 collective-permute-start.18
  302.0 241.3 %reduce-scatter.5.cloned.1.call-start = ((), (), s32[]{:S(2)}) async-start(), calls=%async_computation.5 | async-start | bytes 6389760 | tf_op jit(solution)/shard_map/reduce_scatter | solution.py:414
  303.5 19.9 %collective-permute-start.19 = (bf16[256,1536]{1,0:T(8,128)(2,1)S(1)}, bf16[256,1536]{1,0:T(8,128)(2,1)S(1)}, u32[]{:S(2)}, u32[]{:S(2)}) collective-permute-start(bf16[256,1536]{1,0:T(8,128)(2,1)S(1)} %slice.169), channel_id=1, source_target_pairs={{0,1},{1,0},{2,3},{3,2},{4,5},{5,4},{6,7},{7,6},{8,9},{9,8},{10,11... | collective-permute-start | bytes 2359304 | tf_op jit(solution)/shard_map/ppermute | solution.py:442
  328.2 2.9 collective-permute-start.20
  328.9 22.3 %collective-permute-start.22 = (bf16[256,1536]{1,0:T(8,128)(2,1)S(1)}, bf16[256,1536]{1,0:T(8,128)(2,1)S(1)}, u32[]{:S(2)}, u32[]{:S(2)}) collective-permute-start(bf16[256,1536]{1,0:T(8,128)(2,1)S(1)} %get-tuple-element.119), channel_id=1, source_target_pairs={{0,1},{1,0},{6,7},{7,6},{8,9},{9,8},{14,15},{15,14},{16,17},{17,16... | collective-permute-start | bytes 2359304 | tf_op jit(solution)/shard_map/ppermute | solution.py:448
  331.1 20.1 %collective-permute-start.21 = (bf16[256,1536]{1,0:T(8,128)(2,1)S(1)}, bf16[256,1536]{1,0:T(8,128)(2,1)S(1)}, u32[]{:S(2)}, u32[]{:S(2)}) collective-permute-start(bf16[256,1536]{1,0:T(8,128)(2,1)S(1)} %collective-permute-done.20), channel_id=1, source_target_pairs={{2,3},{3,2},{4,5},{5,4},{10,11},{11,10},{12,13},{13,12},{18,19},{1... | collective-permute-start | bytes 2359304 | tf_op jit(solution)/shard_map/ppermute | solution.py:449
  351.3 13.0 %copy-start.30 = (bf16[1024,1024]{1,0:T(8,128)(2,1)S(1)}, bf16[1024,1024]{1,0:T(8,128)(2,1)}, u32[]{:S(2)}) copy-start(bf16[1024,1024]{1,0:T(8,128)(2,1)} %get-tuple-element.64.refs_4_) | copy-start | bytes 6291460
  351.9 18.0 %collective-permute-start.23 = (bf16[512,1536]{1,0:T(8,128)(2,1)S(1)}, bf16[512,1536]{1,0:T(8,128)(2,1)S(1)}, u32[]{:S(2)}, u32[]{:S(2)}) collective-permute-start(bf16[512,1536]{1,0:T(8,128)(2,1)S(1)} %maximum_select_fusion.4), channel_id=1, source_target_pairs={{0,4},{4,0},{8,12},{12,8},{16,20},{20,16},{24,28},{28,24},{1,5},{5... | collective-permute-start | bytes 4718600 | tf_op jit(solution)/shard_map/ppermute | solution.py:453
  372.5 4.0 collective-permute-start.24
  379.5 28.3 %collective-permute-start.25 = (bf16[256,1536]{1,0:T(8,128)(2,1)}, bf16[256,1536]{1,0:T(8,128)(2,1)}, u32[]{:S(2)}, u32[]{:S(2)}) collective-permute-start(bf16[256,1536]{1,0:T(8,128)(2,1)} %slice.168), channel_id=1, source_target_pairs={{0,1},{1,0},{2,3},{3,2},{4,5},{5,4},{6,7},{7,6},{8,9},{9,8},{10,11... | collective-permute-start | bytes 2359304 | tf_op jit(solution)/shard_map/ppermute | solution.py:442
  424.0 5.7 copy-start.5
  426.2 3.5 collective-permute-start.26
  430.4 20.9 %copy-start.4 = (bf16[256,1536]{1,0:T(8,128)(2,1)S(1)}, bf16[256,1536]{1,0:T(8,128)(2,1)}, u32[]{:S(2)}) copy-start(bf16[256,1536]{1,0:T(8,128)(2,1)} %copy-done.3) | copy-start | bytes 2359300
  430.4 20.9 %copy-start.9 = (bf16[256,1536]{1,0:T(8,128)(2,1)S(1)}, bf16[256,1536]{1,0:T(8,128)(2,1)}, u32[]{:S(2)}) copy-start(bf16[256,1536]{1,0:T(8,128)(2,1)} %copy-done.8) | copy-start | bytes 2359300
  430.4 20.9 %copy-start.13 = (bf16[512,1536]{1,0:T(8,128)(2,1)S(1)}, bf16[512,1536]{1,0:T(8,128)(2,1)}, u32[]{:S(2)}) copy-start(bf16[512,1536]{1,0:T(8,128)(2,1)} %copy-done.12) | copy-start | bytes 4718596
  430.4 19.6 %collective-permute-start.27 = (bf16[256,1536]{1,0:T(8,128)(2,1)S(1)}, bf16[256,1536]{1,0:T(8,128)(2,1)S(1)}, u32[]{:S(2)}, u32[]{:S(2)}) collective-permute-start(bf16[256,1536]{1,0:T(8,128)(2,1)S(1)} %select_convert_fusion), channel_id=1, source_target_pairs={{0,1},{1,0},{2,3},{3,2},{4,5},{5,4},{6,7},{7,6},{8,9},{9,8},{10,11... | collective-permute-start | bytes 2359304 | tf_op jit(solution)/shard_map/ppermute | solution.py:464
  450.5 4.2 collective-permute-start.28
  456.1 39.0 %copy-start.18 = (bf16[384,3072]{1,0:T(8,128)(2,1)S(1)}, bf16[384,3072]{1,0:T(8,128)(2,1)}, u32[]{:S(2)}) copy-start(bf16[384,3072]{1,0:T(8,128)(2,1)} %reduce-scatter.3.cloned.1.call-done) | copy-start | bytes 7077892
  457.7 21.2 %collective-permute-start.29 = (f32[32,128]{1,0:T(8,128)S(1)}, f32[32,128]{1,0:T(8,128)S(1)}, u32[]{:S(2)}, u32[]{:S(2)}) collective-permute-start(f32[32,128]{1,0:T(8,128)S(1)} %fusion.3), channel_id=1, source_target_pairs={{0,4},{4,0},{8,12},{12,8},{16,20},{20,16},{24,28},{28,24},{1,5},{5... | collective-permute-start | bytes 49160 | tf_op jit(solution)/shard_map/ppermute | solution.py:474
  478.9 4.1 collective-permute-start.30
  483.0 3.7 collective-permute-start.31
  486.7 3.7 collective-permute-start.32
  490.5 4.6 collective-permute-start.33
  495.3 43.7 %copy-start.14 = (bf16[192,3072]{1,0:T(8,128)(2,1)}, bf16[192,3072]{1,0:T(8,128)(2,1)S(1)}, u32[]{:S(2)}) copy-start(bf16[192,3072]{1,0:T(8,128)(2,1)S(1)} %get-tuple-element.123.high_ref) | copy-start | bytes 3538948
  495.3 43.7 %copy-start.15 = (bf16[192,3072]{1,0:T(8,128)(2,1)}, bf16[192,3072]{1,0:T(8,128)(2,1)S(1)}, u32[]{:S(2)}) copy-start(bf16[192,3072]{1,0:T(8,128)(2,1)S(1)} %get-tuple-element.124.low_ref) | copy-start | bytes 3538948
  495.3 43.6 %collective-permute-start.34 = (bf16[192,3072]{1,0:T(8,128)(2,1)S(1)}, bf16[192,3072]{1,0:T(8,128)(2,1)}, u32[]{:S(2)}, u32[]{:S(2)}) collective-permute-start(bf16[192,3072]{1,0:T(8,128)(2,1)S(1)} %get-tuple-element.124.low_ref), channel_id=1, source_target_pairs={{6,0},{7,1},{4,2},{5,3},{14,8},{15,9},{12,10},{13,11},{22,16},{23,... | collective-permute-start | bytes 3538952 | tf_op jit(solution)/shard_map/ppermute | solution.py:422
  496.6 42.3 %collective-permute-start.35 = (bf16[192,3072]{1,0:T(8,128)(2,1)S(1)}, bf16[192,3072]{1,0:T(8,128)(2,1)}, u32[]{:S(2)}, u32[]{:S(2)}) collective-permute-start(bf16[192,3072]{1,0:T(8,128)(2,1)S(1)} %get-tuple-element.123.high_ref), channel_id=1, source_target_pairs={{4,6},{5,7},{6,4},{7,5},{12,14},{13,15},{14,12},{15,13},{20,22},{2... | collective-permute-start | bytes 3538952 | tf_op jit(solution)/shard_map/ppermute | solution.py:423
  498.3 40.6 %collective-permute-start.36 = (bf16[192,3072]{1,0:T(8,128)(2,1)S(1)}, bf16[192,3072]{1,0:T(8,128)(2,1)}, u32[]{:S(2)}, u32[]{:S(2)}) collective-permute-start(bf16[192,3072]{1,0:T(8,128)(2,1)S(1)} %get-tuple-element.123.high_ref), channel_id=1, source_target_pairs={{0,4},{1,5},{2,6},{3,7},{8,12},{9,13},{10,14},{11,15},{16,20},{17,... | collective-permute-start | bytes 3538952 | tf_op jit(solution)/shard_map/ppermute | solution.py:424
  544.6 34.9 %copy-start.16 = (bf16[192,1664]{1,0:T(8,128)(2,1)}, bf16[192,1664]{1,0:T(8,128)(2,1)S(1)}, u32[]{:S(2)}) copy-start(bf16[192,1664]{1,0:T(8,128)(2,1)S(1)} %get-tuple-element.125.high_ref) | copy-start | bytes 1916932
  544.7 34.9 %copy-start.17 = (bf16[192,1664]{1,0:T(8,128)(2,1)}, bf16[192,1664]{1,0:T(8,128)(2,1)S(1)}, u32[]{:S(2)}) copy-start(bf16[192,1664]{1,0:T(8,128)(2,1)S(1)} %get-tuple-element.126.low_ref) | copy-start | bytes 1916932
  544.7 34.8 %collective-permute-start.37 = (bf16[192,1664]{1,0:T(8,128)(2,1)S(1)}, bf16[192,1664]{1,0:T(8,128)(2,1)S(1)}, u32[]{:S(2)}, u32[]{:S(2)}) collective-permute-start(bf16[192,1664]{1,0:T(8,128)(2,1)S(1)} %get-tuple-element.126.low_ref), channel_id=1, source_target_pairs={{6,0},{7,1},{4,2},{5,3},{14,8},{15,9},{12,10},{13,11},{22,16},{23,... | collective-permute-start | bytes 1916936 | tf_op jit(solution)/shard_map/ppermute | solution.py:422
  546.0 33.6 %collective-permute-start.38 = (bf16[192,1664]{1,0:T(8,128)(2,1)S(1)}, bf16[192,1664]{1,0:T(8,128)(2,1)S(1)}, u32[]{:S(2)}, u32[]{:S(2)}) collective-permute-start(bf16[192,1664]{1,0:T(8,128)(2,1)S(1)} %get-tuple-element.125.high_ref), channel_id=1, source_target_pairs={{4,6},{5,7},{6,4},{7,5},{12,14},{13,15},{14,12},{15,13},{20,22},{2... | collective-permute-start | bytes 1916936 | tf_op jit(solution)/shard_map/ppermute | solution.py:423
  546.7 32.8 %collective-permute-start.39 = (bf16[192,1664]{1,0:T(8,128)(2,1)S(1)}, bf16[192,1664]{1,0:T(8,128)(2,1)S(1)}, u32[]{:S(2)}, u32[]{:S(2)}) collective-permute-start(bf16[192,1664]{1,0:T(8,128)(2,1)S(1)} %get-tuple-element.125.high_ref), channel_id=1, source_target_pairs={{0,4},{1,5},{2,6},{3,7},{8,12},{9,13},{10,14},{11,15},{16,20},{17,... | collective-permute-start | bytes 1916936 | tf_op jit(solution)/shard_map/ppermute | solution.py:424
  (11 other events, 14.2 us)
Sparse Core Ops, SparseCore 0:
  33.5 75.3 all-gather.2
  110.7 112.3 all-gather.4
  302.1 96.9 reduce-scatter.2
  424.1 62.5 reduce-scatter.4

commit v3 on v2

--- a/solution.py
+++ b/solution.py
@@ -42,11 +42,25 @@
     return jnp.concatenate(parts, axis=0)
 
 
+def starts(place_ref, block):
+    odd, zodd = place_ref[0], place_ref[1]
+    return [
+        pl.multiple_of(
+            ((1 - odd if k >> 1 else odd) * 2 + (1 - zodd if k & 1 else zodd)) * block, block
+        )
+        for k in range(4)
+    ]
+
+
 def attend_kernel(
-    heads, span, x_ref, w_ref, bias_ref, seg_ref, qkv_ref, mixed_ref, branch_ref, rows_ref, decay_ref, closed_ref, stat_ref, drow_ref
+    heads, span, place_ref, x0_ref, x1_ref, x2_ref, x3_ref, w_ref, bias_ref, seg_ref, x_ref, qkv_ref, mixed_ref, keep_ref, send_ref, rows_ref, decay_ref, closed_ref, stat_ref, drow_ref, own_ref
 ):
     length = x_ref.shape[0]
+    block = length // 4
     width = heads * 64
+    places = starts(place_ref, block)
+    for at, part_ref in zip(places, (x0_ref, x1_ref, x2_ref, x3_ref)):
+        x_ref[pl.ds(at, block), :] = part_ref[...]
     x = x_ref[...]
     qkv_ref[...] = dotf(x, w_ref[:, : 3 * width], NN).astype(BF)
     logits = dotf(x, w_ref[:, 3 * width : 3 * width + 128], NN) + bias_ref[...]
@@ -93,36 +107,58 @@
     rows_ref[0:8, :] = drow_ref[0:8, :]
     for b in range(0, length, 128):
         rows_ref[8:16, b : b + 128] = stat_ref[b : b + 128, :].T[0:8]
-    branch_ref[...] = dotf(mixed_ref[...], w_ref[:, 3 * width + 128 :], NT).astype(BF)
-
-
-def attend(x, w, bias, seg, heads):
-    length, features = x.shape
+    for n, at in enumerate(places):
+        own_ref[n * block : (n + 1) * block, :] = mixed_ref[pl.ds(at, block), :]
+    branch = dotf(own_ref[...], w_ref[:, 3 * width + 128 :], NT)
+    keep_ref[...] = branch[: 2 * block].astype(BF)
+    send_ref[...] = branch[2 * block :].astype(BF)
+
+
+def in_memory(scalars, arrays):
+    return [pl.BlockSpec(memory_space=pltpu.SMEM)] * scalars + [
+        pl.BlockSpec(memory_space=pltpu.VMEM)
+    ] * arrays
+
+
+def attend(place, xs, w, bias, seg, heads):
+    block, features = xs[0].shape
+    length = 4 * block
     width = heads * 64
     return pl.pallas_call(
         functools.partial(attend_kernel, heads, 256),
+        in_specs=in_memory(1, 7),
         out_shape=(
+            jax.ShapeDtypeStruct((length, features), BF),
             jax.ShapeDtypeStruct((length, 3 * width), BF),
             jax.ShapeDtypeStruct((length, width), BF),
-            jax.ShapeDtypeStruct((length, features), BF),
+            jax.ShapeDtypeStruct((length // 2, features), BF),
+            jax.ShapeDtypeStruct((length // 2, features), BF),
             jax.ShapeDtypeStruct((16, length), F32),
             jax.ShapeDtypeStruct((length, 128), F32),
             jax.ShapeDtypeStruct((length, 128), F32),
         ),
-        scratch_shapes=[pltpu.VMEM((length, 128), F32), pltpu.VMEM((128, length), F32)],
+        scratch_shapes=[
+            pltpu.VMEM((length, 128), F32),
+            pltpu.VMEM((128, length), F32),
+            pltpu.VMEM((length, width), BF),
+        ],
         compiler_params=pltpu.CompilerParams(vmem_limit_bytes=VMEM_LIMIT),
         cost_estimate=pl.CostEstimate(
             flops=12 * 10**9, bytes_accessed=2 * 10**7, transcendentals=5 * 10**6
         ),
         name="attend",
-    )(x, w, bias, seg)
+    )(place, *xs, w, bias, seg)
 
 
 def attend_back_kernel(
-    heads, span, m_ref, w_ref, qkv_ref, mixed_ref, rows_ref, decay_ref, closed_ref, seg_ref, grad_ref, part_ref, bias_ref, mb_ref, dq_ref, sums_ref, drow_ref
+    heads, span, place_ref, m0_ref, m1_ref, m2_ref, m3_ref, w_ref, qkv_ref, mixed_ref, rows_ref, decay_ref, closed_ref, seg_ref, m_ref, grad_ref, keep_ref, send_ref, bias_ref, mb_ref, dq_ref, sums_ref, drow_ref, own_ref
 ):
     length = m_ref.shape[0]
+    block = length // 4
     width = heads * 64
+    places = starts(place_ref, block)
+    for at, part_ref in zip(places, (m0_ref, m1_ref, m2_ref, m3_ref)):
+        m_ref[pl.ds(at, block), :] = part_ref[...]
     mb_ref[...] = dotf(m_ref[...], w_ref[:, 3 * width + 128 :], NN).astype(BF)
     lane = lax.broadcasted_iota(jnp.int32, (1, 128), 1)
     i = lax.broadcasted_iota(jnp.int32, (span, span), 0)
@@ -187,17 +223,25 @@
         grad_ref[b : b + 128, 3 * width :] = back
         bias = bias + jnp.sum(back.astype(F32), axis=0, keepdims=True)
     bias_ref[...] = jnp.broadcast_to(bias, bias_ref.shape)
-    part_ref[...] = dotf(grad_ref[...], w_ref[:, : 3 * width + 128], NT).astype(BF)
-
-
-def attend_back(m, w, qkv, mixed, rows, decay, closed, seg, heads):
-    length, features = m.shape
+    for n, at in enumerate(places):
+        own_ref[n * block : (n + 1) * block, :] = grad_ref[pl.ds(at, block), :]
+    part = dotf(own_ref[...], w_ref[:, : 3 * width + 128], NT)
+    keep_ref[...] = part[: 2 * block].astype(BF)
+    send_ref[...] = part[2 * block :].astype(BF)
+
+
+def attend_back(place, ms, w, qkv, mixed, rows, decay, closed, seg, heads):
+    block, features = ms[0].shape
+    length = 4 * block
     width = heads * 64
     return pl.pallas_call(
         functools.partial(attend_back_kernel, heads, 256),
+        in_specs=in_memory(1, 11),
         out_shape=(
+            jax.ShapeDtypeStruct((length, features), BF),
             jax.ShapeDtypeStruct((length, 3 * width + 128), BF),
-            jax.ShapeDtypeStruct((length, features), BF),
+            jax.ShapeDtypeStruct((length // 2, features), BF),
+            jax.ShapeDtypeStruct((length // 2, features), BF),
             jax.ShapeDtypeStruct((8, 128), F32),
         ),
         scratch_shapes=[
@@ -205,17 +249,28 @@
             pltpu.VMEM((length, 128), F32),
             pltpu.VMEM((length, 128), F32),
             pltpu.VMEM((8, length), F32),
+            pltpu.VMEM((length, 3 * width + 128), BF),
         ],
         compiler_params=pltpu.CompilerParams(vmem_limit_bytes=VMEM_LIMIT),
         cost_estimate=pl.CostEstimate(
-            flops=20 * 10**9, bytes_accessed=2 * 10**7, transcendentals=5 * 10**6
+            flops=150 * 10**9, bytes_accessed=2 * 10**7, transcendentals=5 * 10**6
         ),
         name="attend_back",
-    )(m, w, qkv, mixed, rows, decay, closed, seg)
-
-
-def feed_kernel(x_ref, c_ref, wg_ref, wu_ref, wd_ref, hidden_ref, gb_ref, ub_ref, part_ref, total_ref):
+    )(place, *ms, w, qkv, mixed, rows, decay, closed, seg)
+
+
+def feed_kernel(*refs):
+    x_parts, c_parts = refs[:4], refs[4:8]
+    wg_ref, wu_ref, wd_ref, hidden_ref, gb_ref, ub_ref, x_ref, c_ref, keep_ref, send_ref, total_ref = refs[8:]
     step = pl.program_id(0)
+    block = x_ref.shape[0] // 4
+
+    @pl.when(step == 0)
+    def _():
+        for n in range(4):
+            x_ref[n * block : (n + 1) * block, :] = x_parts[n][...]
+            c_ref[n * block : (n + 1) * block, :] = c_parts[n][...]
+
     x = x_ref[...]
     wg, wu = wg_ref[...], wu_ref[...]
     gate = dotf(x, wg, NN)
@@ -240,30 +295,35 @@
 
     @pl.when(step == pl.num_programs(0) - 1)
     def _():
-        part_ref[...] = total_ref[...].astype(BF)
-
-
-def feed(x, c, w, block=256):
-    length, features = x.shape
+        keep_ref[...] = total_ref[: 2 * block].astype(BF)
+        send_ref[...] = total_ref[2 * block :].astype(BF)
+
+
+def feed(xs, cs, w, block=256):
+    rows, features = xs[0].shape
+    length = 4 * rows
     width = w.shape[1] // 3
     steps = width // block
+    part = pl.BlockSpec((rows, features), lambda i: (0, 0))
+    half = pl.BlockSpec((2 * rows, features), lambda i: (0, 0))
     whole = pl.BlockSpec((length, features), lambda i: (0, 0))
     tall = lambda k: pl.BlockSpec((features, block), lambda i: (0, i + k * steps))
     out = pl.BlockSpec((length, block), lambda i: (0, i))
     return pl.pallas_call(
         feed_kernel,
         grid=(steps,),
-        in_specs=[whole, whole, tall(0), tall(1), tall(2)],
-        out_specs=[out, out, out, whole],
+        in_specs=[part] * 8 + [tall(0), tall(1), tall(2)],
+        out_specs=[out, out, out, whole, whole, half, half],
         out_shape=[jax.ShapeDtypeStruct((length, width), BF)] * 3
-        + [jax.ShapeDtypeStruct((length, features), BF)],
+        + [jax.ShapeDtypeStruct((length, features), BF)] * 2
+        + [jax.ShapeDtypeStruct((2 * rows, features), BF)] * 2,
         scratch_shapes=[pltpu.VMEM((length, features), F32)],
         compiler_params=pltpu.CompilerParams(vmem_limit_bytes=VMEM_LIMIT),
         cost_estimate=pl.CostEstimate(
             flops=16 * 10**9, bytes_accessed=25 * 10**6, transcendentals=10**6
         ),
         name="feed",
-    )(x, c, w, w, w)
+    )(*xs, *cs, w, w, w)
 
 
 def weight_grad_kernel(steps, left, right, *refs):
@@ -310,22 +370,27 @@
         ),
         name=name,
     )(*lefts, *rights)
-def attend_grads_kernel(x_ref, m_ref, grad_ref, mixed_ref, part_ref, out_ref, gain_ref):
+def attend_grads_kernel(
+    place_ref, x_ref, m_ref, grad_ref, mixed_ref, keep_ref, send_ref, out_ref, gain_ref
+):
     inner = grad_ref.shape[1]
     out_ref[:, :inner] = dotf(x_ref[...], grad_ref[...], TN).astype(BF)
     out_ref[:, inner:] = dotf(m_ref[...], mixed_ref[...], TN).astype(BF)
-    total = jnp.zeros((8, gain_ref.shape[1]), F32)
-    for b in range(0, x_ref.shape[0], 8):
-        rows = slice(b, b + 8)
-        total = total + x_ref[rows, :].astype(F32) * part_ref[rows, :].astype(F32)
-    gain_ref[...] = jnp.broadcast_to(jnp.sum(total, axis=0, keepdims=True), gain_ref.shape)
-
-
-def attend_grads(x, m, grads, mixed, part):
+    block = x_ref.shape[0] // 4
+    total = jnp.zeros((1, gain_ref.shape[1]), F32)
+    for n, at in enumerate(starts(place_ref, block)):
+        part = (send_ref if n >> 1 else keep_ref)[(n & 1) * block : ((n & 1) + 1) * block, :]
+        own = x_ref[pl.ds(at, block), :].astype(F32) * part.astype(F32)
+        total = total + jnp.sum(own, axis=0, keepdims=True)
+    gain_ref[...] = jnp.broadcast_to(total, gain_ref.shape)
+
+
+def attend_grads(place, x, m, grads, mixed, keep, send):
     length, features = x.shape
     columns = grads.shape[1] + mixed.shape[1]
     return pl.pallas_call(
         attend_grads_kernel,
+        in_specs=in_memory(1, 6),
         out_shape=(
             jax.ShapeDtypeStruct((features, columns), BF),
             jax.ShapeDtypeStruct((8, features), F32),
@@ -335,7 +400,7 @@
             flops=2 * length * features * columns, bytes_accessed=2 * 10**7, transcendentals=0
         ),
         name="attend_grads",
-    )(x, m, grads, mixed, part)
+    )(place, x, m, grads, mixed, keep, send)
 
 
 def finish_kernel(widths, odd_ref, low_ref, high_ref, a_ref, b_ref, c_ref, *out_refs):
@@ -361,8 +426,7 @@
     rows = low.shape[0]
     return pl.pallas_call(
         functools.partial(finish_kernel, widths),
-        in_specs=[pl.BlockSpec(memory_space=pltpu.SMEM)]
-        + [pl.BlockSpec(memory_space=pltpu.VMEM)] * 5,
+        in_specs=in_memory(1, 5),
         out_shape=[jax.ShapeDtypeStruct((rows, width), F32) for width in widths],
         compiler_params=pltpu.CompilerParams(vmem_limit_bytes=VMEM_LIMIT),
         cost_estimate=pl.CostEstimate(flops=10**6, bytes_accessed=8 * 10**6, transcendentals=0),
@@ -378,10 +442,7 @@
         flat = lambda d, z: d * tensor + z
         devices = [(d, z) for d in range(dp) for z in range(tensor)]
         away = [(d, z) for d, z in devices if (d & 1) != (z >> 1)]
-        near = [(d, z) for d, z in devices if (d & 1) == (z >> 1)]
         self.move = [(flat(d, z), flat(d ^ 1, z ^ 2)) for d, z in away]
-        self.pair_near = [(flat(d, z), flat(d, z ^ 1)) for d, z in near]
-        self.pair_away = [(flat(d, z), flat(d, z ^ 1)) for d, z in away]
         even = [(d, z) for d, z in devices if d & 1 == 0]
         odd = [(d, z) for d, z in devices if d & 1 == 1]
         self.even_far = [(flat(d, z), flat(d + 1, z ^ 2)) for d, z in even]
@@ -399,11 +460,11 @@
     return lax.optimization_barrier((x, *deps))[0]
 
 
-def swap_weight(lay, w, odd):
+def swap_weight(lay, w, odd, *deps):
     a = lax.ppermute(w, BOTH, lay.even_far)
     b = lax.ppermute(w, BOTH, lay.odd_far)
     c = lax.ppermute(w, BOTH, lay.odd_even)
-    return jnp.where(odd, cat(a, b), cat(w, c))
+    return jnp.where(odd, cat(after(a, *deps), b), cat(w, c))
 
 
 def gather_rows(lay, rows):
@@ -425,46 +486,22 @@
     return finish(odd.astype(jnp.int32).reshape(1), low, high, a, b, c, widths)
 
 
-def gather_pair(lay, x):
+def gather_pair(lay, x, *deps):
+    core = lax.ppermute(x, "dp", lay.core)
     z = lax.ppermute(x, "tensor", lay.pair)
-    near = cat(x, z)
-    return cat(near, lax.ppermute(near, "dp", lay.core))
-
-
-def scatter_pair_first(lay, part):
-    half = part.shape[0] // 2
-    got = lax.ppermute(part[half:], "dp", lay.core)
-    return part[:half].astype(F32) + got.astype(F32)
-
-
-def scatter_pair_second(lay, mine):
-    quarter = mine.shape[0] // 2
-    got = lax.ppermute(mine[quarter:].astype(BF), "tensor", lay.pair)
-    return mine[:quarter] + got.astype(F32)
-
-
-def gather_sequence(lay, x, odd, zodd, away):
-    moved = lax.ppermute(x, BOTH, lay.move)
-    near = lax.ppermute(x, BOTH, lay.pair_near)
-    far = lax.ppermute(moved, BOTH, lay.pair_away)
-    mine = jnp.where(away, moved, x)
-    other = jnp.where(away, far, near)
-    half = jnp.where(zodd, cat(other, mine), cat(mine, other))
-    got = lax.ppermute(half, "dp", lay.core)
-    return jnp.where(odd, cat(got, half), cat(half, got)), moved
-
-
-def scatter_sequence(lay, part, odd, zodd, away):
-    half = part.shape[0] // 2
-    quarter = half // 2
-    first, second = part[:half], part[half:]
-    got = lax.ppermute(jnp.where(odd, first, second), "dp", lay.core)
-    mine = jnp.where(odd, second, first).astype(F32) + got.astype(F32)
-    first, second = mine[:quarter], mine[quarter:]
-    got = lax.ppermute(jnp.where(zodd, first, second).astype(BF), "tensor", lay.pair)
-    mine = jnp.where(zodd, second, first) + got.astype(F32)
-    got = lax.ppermute(mine.astype(BF), BOTH, lay.move)
-    return jnp.where(away, got.astype(F32), mine)
+    return x, z, core, lax.ppermute(after(z, *deps), "dp", lay.core)
+
+
+def scatter_core(lay, keep, send):
+    got = lax.ppermute(send, "dp", lay.core)
+    half = keep.shape[0] // 2
+    mine = keep[:half].astype(F32) + got[:half].astype(F32)
+    other = keep[half:].astype(F32) + got[half:].astype(F32)
+    return mine, other.astype(BF)
+
+
+def scatter_z(lay, mine, other):
+    return mine + lax.ppermute(other, "tensor", lay.pair).astype(F32)
 
 
 def sum_all(x, axis):
@@ -513,84 +550,115 @@
     width = query_weight.shape[1]
     hidden_width = gate_weight.shape[1]
     features = layer_input.shape[1]
+    place = jnp.stack([odd, zodd]).astype(jnp.int32)
+
+    def moved(x):
+        return jnp.where(away, lax.ppermute(x, BOTH, lay.move), x)
+
+    def moved_back(x):
+        low = lax.ppermute(x.astype(BF), BOTH, lay.move)
+        return jnp.where(away, low.astype(F32), x)
+
     forget_pad = jnp.pad(forget_weight, ((0, 0), (0, 128 - heads)))
-
     w_attn_local = jnp.concatenate(
         [query_weight, key_weight, value_weight, forget_pad, output_weight], axis=1
     ).astype(BF)
     attn_rows = swap_weight(lay, w_attn_local, odd)
     w_attn = gather_rows(lay, attn_rows)
-
-    normed = (layer_input * inverse_rms(layer_input) * attn_gain).astype(BF)
-    attn_normed, moved = gather_sequence(lay, after(normed, attn_rows), odd, zodd, away)
-    segment = jnp.where(away, lax.ppermute(segment_ids, "dp", lay.core), segment_ids)
+    w_feed_local = jnp.concatenate([gate_weight, up_weight, down_weight], axis=1).astype(BF)
+    feed_rows = swap_weight(lay, after(w_feed_local, attn_rows), odd)
+    w_feed = gather_rows(lay, feed_rows)
+    segment = jnp.where(
+        away, lax.ppermute(after(segment_ids, attn_rows), "dp", lay.core), segment_ids
+    )
     seg_row = segment[None, :]
     bias = jnp.pad(
         lax.dynamic_slice_in_dim(forget_bias, quarter * heads, heads), (0, 128 - heads)
     )[None, :]
 
-    w_feed_local = jnp.concatenate([gate_weight, up_weight, down_weight], axis=1).astype(BF)
-    feed_rows = swap_weight(lay, after(w_feed_local, moved), odd)
-    w_feed = gather_rows(lay, after(feed_rows, w_attn))
-    cot_low = gather_pair(lay, after(output_cotangent.astype(BF), feed_rows))
-
-    qkv, mixed, branch_part, rows, decay, closed = attend(
-        attn_normed, w_attn, bias, seg_row, heads
-    )
-    branch = scatter_sequence(lay, after(branch_part, cot_low), odd, zodd, away)
-    middle = layer_input + branch
-
-    feed_normed = gather_pair(lay, (middle * inverse_rms(middle) * feed_gain).astype(BF))
-    hidden, gate_back, up_back, feed_part = feed(feed_normed, cot_low, w_feed, 512)
-    feed_sum = scatter_pair_first(lay, feed_part)
-    ready = after(hidden, feed_sum)
+    layer = moved_back(after(layer_input, feed_rows))
+    normed = (layer * inverse_rms(layer) * attn_gain).astype(BF)
+    xs = gather_pair(lay, normed)
+    cot_low = moved(after(output_cotangent.astype(BF), normed))
+    cot_z = lax.ppermute(after(cot_low, xs[1]), "tensor", lay.pair)
+    attn_normed, qkv, mixed, keep, send, rows, decay, closed = attend(
+        place, (*xs[:3], after(xs[3], cot_low)), w_attn, bias, seg_row, heads
+    )
+    mine, other = scatter_core(lay, keep, after(send, cot_z))
+    cots = (
+        cot_low,
+        cot_z,
+        lax.ppermute(after(cot_low, other), "dp", lay.core),
+        lax.ppermute(after(cot_z, other), "dp", lay.core),
+    )
+    branch = scatter_z(lay, mine, other)
+    middle = layer + branch
+
+    feeds = gather_pair(lay, (middle * inverse_rms(middle) * feed_gain).astype(BF))
+    hidden, gate_back, up_back, feed_normed, cot_all, keep, send = feed(feeds, cots, w_feed, 512)
+    feed_keep, feed_send = keep, send
+    mine, other = scatter_core(lay, keep, send)
+    hidden, other = lax.optimization_barrier((hidden, other))
+    got = lax.ppermute(other, "tensor", lay.pair)
     feed_grads = weight_grad(
-        [feed_normed, cot_low],
-        [gate_back, up_back, ready],
+        [feed_normed, cot_all],
+        [gate_back, up_back, hidden],
         [(0, 0), (0, 1), (1, 2)],
         512,
         "feed_grads",
     )
     feed_scattered = scatter_rows(lay, feed_grads)
-    feed_normed_grad = after(scatter_pair_second(lay, feed_sum), feed_grads)
-
-    middle_grad = output_cotangent + norm_back(middle, feed_gain, feed_normed_grad)
-    middle_local = middle_grad.astype(BF)
-    middle_low, _ = gather_sequence(lay, middle_local, odd, zodd, away)
+    feed_normed_grad = after(mine + got.astype(F32), feed_grads)
+
+    middle_part = norm_back(middle, feed_gain, feed_normed_grad)
+    cotangent = jnp.where(away, cot_low.astype(F32), output_cotangent)
+    middle_low = (cotangent + middle_part).astype(BF)
+    ms = gather_pair(lay, middle_low)
     w_down = w_feed[:, 2 * hidden_width :]
-    down_part = dotf(after(hidden, middle_local), w_down, NT).astype(BF)
+    ready = after(hidden, middle_low)
+    half = hidden.shape[0] // 2
+    down_send = dotf(ready[half:], w_down, NT).astype(BF)
+    down_keep = dotf(ready[:half], w_down, NT).astype(BF)
+    near, far = feed_normed[:half].astype(F32), feed_normed[half:].astype(F32)
     feed_gain_part = jnp.sum(
-        after(feed_part, middle_local).astype(F32) * feed_normed.astype(F32), axis=0
+        after(feed_keep, middle_low).astype(F32) * near + feed_send.astype(F32) * far, axis=0
     )
     feed_gain_part = feed_gain_part / feed_gain
-
-    grads, attn_part, bias_part = attend_back(
-        middle_low, w_attn, qkv, mixed, rows, decay, closed, seg_row, heads
-    )
-    down_sum = scatter_pair_first(lay, after(down_part, middle_low))
-    layer_output = middle + scatter_pair_second(lay, down_sum)
+    mine, other = scatter_core(lay, down_keep, down_send)
+    ms = (*ms[:3], after(ms[3], other))
+
+    middle_all, grads, keep, send, bias_part = attend_back(
+        place, ms, w_attn, qkv, mixed, rows, decay, closed, seg_row, heads
+    )
+    down = branch + scatter_z(lay, mine, other)
+    down_back = moved_back(down)
     attn_grads, attn_gain_part = attend_grads(
-        attn_normed, middle_low, after(grads, layer_output), mixed, attn_part
-    )
-    attn_scattered = scatter_rows(lay, after(attn_grads, feed_scattered))
-    attn_gain_part = attn_gain_part[0] / attn_gain
-    attn_normed_grad = scatter_sequence(lay, after(attn_part, attn_grads), odd, zodd, away)
-    input_grad = middle_grad + norm_back(layer_input, attn_gain, attn_normed_grad)
-
+        place, attn_normed, middle_all, after(grads, down), mixed, keep, send
+    )
+    layer_output = layer_input + down_back
     bias_full = lax.dynamic_update_slice_in_dim(
         jnp.zeros(forget_bias.shape, F32), bias_part[0, :heads], quarter * heads, 0
     )
-    packed = cat(attn_gain_part, feed_gain_part, bias_full)
+    packed = cat(attn_gain_part[0] / attn_gain, feed_gain_part, bias_full)
     size = packed.shape[0]
     packed = jnp.pad(packed, (0, -size % 1024)).reshape(-1, 128)
-    packed = after(packed, input_grad)
-    small = sum_all(sum_all(packed, "dp"), "tensor").reshape(-1)
-
+    packed = sum_all(after(packed, down_back), "tensor")
+    attn_scattered = scatter_rows(lay, after(attn_grads, feed_scattered, packed))
     gate_shard, up_shard, down_shard = share_grad(
-        lay, after(feed_scattered, small), odd, [hidden_width] * 3
-    )
+        lay, after(feed_scattered, packed), odd, [hidden_width] * 3
+    )
+    mine, other = scatter_core(lay, keep, after(send, packed))
+    attn_normed_grad = scatter_z(lay, mine, other)
+    input_part = norm_back(layer, attn_gain, attn_normed_grad)
+    input_back = moved_back(after(middle_part + input_part, gate_shard))
+    input_grad = output_cotangent + input_back
+    small = sum_all(after(packed, other), "dp").reshape(-1)
+
     query_shard, key_shard, value_shard, forget_shard, output_shard = share_grad(
-        lay, after(attn_scattered, gate_shard), odd, [width, width, width, 128, width]
+        lay,
+        after(attn_scattered, small, gate_shard, input_back),
+        odd,
+        [width, width, width, 128, width],
     )
     return (
         layer_output,

time: 604 us -> 516 us (0.85)
  waiting for transfers between devices: 216 us -> 175 us
  starting transfers between devices: 171 us -> 139 us
  other arithmetic: 48.6 us -> 29.2 us
    ppermute x21 -> x22, waiting for transfers between devices: 94.1 us -> 53.7 us  [the longest x3 41 us: scatter_z(): return mine + lax.ppermute(other, 'tensor', lay.pair).astype(F32)]
    ppermute x2, starting transfers between devices: 47.3 us -> 21.4 us  [swap_weight(): a = lax.ppermute(w, BOTH, lay.even_far)]
    select_n x13 -> x4, other arithmetic: 23.2 us -> 3.95 us  [the longest x2 3.27 us: swap_weight(): return jnp.where(odd, cat(after(a, *deps), b), cat(w, c))]
    ppermute x5, starting transfers between devices: 24.6 us -> 9.43 us  [sum_all(): x = x + lax.ppermute(x, axis, [(i, i ^ step) for i in range(size)])]
    ppermute x2 -> x3, starting transfers between devices: 18.6 us -> 31.3 us  [gather_pair(): z = lax.ppermute(x, 'tensor', lay.pair)]
    ppermute x2, starting transfers between devices: 23.2 us -> 13.3 us  [share_grad(): c = lax.ppermute(high, BOTH, lay.back_odd_even)]
    ppermute x2, waiting for transfers between devices: 49.1 us -> 40.2 us  [share_grad(): a = lax.ppermute(low, BOTH, lay.back_even_far)]
    ppermute x21 -> x22, starting transfers between devices: 47.5 us -> 54.9 us  [the longest x1 23.5 us: per_device(): lax.ppermute(after(segment_ids, attn_rows), 'dp', lay.core)]
  transfers between devices with their start and end apart: 44 -> 46, of which waited for: 22 -> 18; matrix products, arithmetic and copies ran while one was open for 10% -> 7% of each run, Pallas kernels for 11% -> 17%
where the time goes in v3:
time: 516 us; the launch traced here: 506 us
  waiting for transfers between devices  175 us (34%)
  starting transfers between devices  139 us (27%)
  Pallas kernels  117 us (23%)
  other arithmetic  29.2 us (6%)
  local copies, waits for them, and re-layouts  23.6 us (5%)
  between operations  14.9 us (3%)
  matrix products  8.08 us (2%)
    ppermute x3, waiting for transfers between devices, scatter_z(): return mine + lax.ppermute(other, 'tensor', lay.pair).astype(F32)  41 us
    ppermute x2, waiting for transfers between devices, share_grad(): a = lax.ppermute(low, BOTH, lay.back_even_far)  40.2 us
    ppermute x2, waiting for transfers between devices, swap_weight(): a = lax.ppermute(w, BOTH, lay.even_far)  35.1 us
    ppermute x3, waiting for transfers between devices, gather_pair(): z = lax.ppermute(x, 'tensor', lay.pair)  33.2 us
    ppermute x3, starting transfers between devices, gather_pair(): z = lax.ppermute(x, 'tensor', lay.pair)  31.3 us
    pallas_call x1, Pallas kernels, feed(): pl.pallas_call(feed_kernel, grid=(steps,), in_specs=[part] * 8 + [tall(0)...  28.4 us
    pallas_call x1, Pallas kernels, attend_back(): pl.pallas_call(functools.partial(attend_back_kernel, heads, 256), in_spec...  27.2 us
    pallas_call x1, Pallas kernels, attend(): pl.pallas_call(functools.partial(attend_kernel, heads, 256), in_specs=in_...  23.8 us
  transfers between devices with their start and end apart: 46, of which 18 were waited for; matrix products, arithmetic and copies ran while one was open for 7% of the time, Pallas kernels for 17%

profile of v3, /device:TPU:0, one launch (start us, length us, event | category | flops | bytes accessed | tf_op | source)
XLA Modules:
  0.0 506.1 jit_solution(17470241025788855538)
XLA Ops:
  11.2 5.4 %collective-permute-start = (bf16[192,1664]{1,0:T(8,128)(2,1)S(1)}, bf16[192,1664]{1,0:T(8,128)(2,1)S(1)}, u32[]{:S(2)}, u32[]{:S(2)}) collective-permute-start(bf16[192,1664]{1,0:T(8,128)(2,1)S(1)} %convert_dynamic-update-slice_fusion), channel_id=1, source_target_pairs={{0,6},{1,7},{2,4},{3,5},{8,14},{9,15},{10,12},{11,13},{16,22},{17,... | collective-permute-start | bytes 1916936 | tf_op jit(solution)/shard_map/ppermute | solution.py:464
  17.3 1.3 collective-permute-start.2
  18.6 12.1 %collective-permute-done = bf16[192,1664]{1,0:T(8,128)(2,1)S(1)} collective-permute-done((bf16[192,1664]{1,0:T(8,128)(2,1)S(1)}, bf16[192,1664]{1,0:T(8,128)(2,1)S(1)}, u32[]{:S(2)}, u32[]{:S(2)}) %collective-permute-start) | collective-permute-done | bytes 639008 | tf_op jit(solution)/shard_map/ppermute | solution.py:464
  30.7 1.3 maximum_select_fusion.1
  33.8 16.0 %collective-permute-start.3 = (bf16[192,3072]{1,0:T(8,128)(2,1)S(1)}, bf16[192,3072]{1,0:T(8,128)(2,1)S(1)}, u32[]{:S(2)}, u32[]{:S(2)}) collective-permute-start(bf16[192,3072]{1,0:T(8,128)(2,1)S(1)} %pad_maximum_fusion), channel_id=1, source_target_pairs={{0,6},{1,7},{2,4},{3,5},{8,14},{9,15},{10,12},{11,13},{16,22},{17,... | collective-permute-start | bytes 3538952 | tf_op jit(solution)/shard_map/ppermute | solution.py:464
  50.5 1.3 collective-permute-start.5
  51.8 23.1 %collective-permute-done.3 = bf16[192,3072]{1,0:T(8,128)(2,1)S(1)} collective-permute-done((bf16[192,3072]{1,0:T(8,128)(2,1)S(1)}, bf16[192,3072]{1,0:T(8,128)(2,1)S(1)}, u32[]{:S(2)}, u32[]{:S(2)}) %collective-permute-start.3) | collective-permute-done | bytes 1179680 | tf_op jit(solution)/shard_map/ppermute | solution.py:464
  74.9 1.9 maximum_select_fusion
  76.9 1.3 copy-done.6
  78.3 1.6 collective-permute-start.6
  79.9 1.4 multiply_reduce_fusion.3
  82.5 27.8 %collective-permute-start.7 = (bf16[256,1536]{1,0:T(8,128)(2,1)}, bf16[256,1536]{1,0:T(8,128)(2,1)}, u32[]{:S(2)}, u32[]{:S(2)}) collective-permute-start(bf16[256,1536]{1,0:T(8,128)(2,1)} %multiply_convert_fusion.1.x0_ref), channel_id=1, source_target_pairs={{0,1},{1,0},{2,3},{3,2},{4,5},{5,4},{6,7},{7,6},{8,9},{9,8},{10,11... | collective-permute-start | bytes 2359304 | tf_op jit(solution)/shard_map/ppermute | solution.py:491
  110.4 1.8 collective-permute-start.10
  112.8 23.5 %collective-permute-start.11 = (s32[1024]{0:T(1024)S(1)}, s32[1024]{0:T(1024)S(1)}, u32[]{:S(2)}, u32[]{:S(2)}) collective-permute-start(s32[1024]{0:T(1024)S(1)} %copy-done.53), channel_id=1, source_target_pairs={{0,4},{4,0},{8,12},{12,8},{16,20},{20,16},{24,28},{28,24},{1,5},{5... | collective-permute-start | bytes 12296 | tf_op jit(solution)/shard_map/ppermute | solution.py:572
  136.3 11.9 %collective-permute-start.9 = (bf16[256,1536]{1,0:T(8,128)(2,1)}, bf16[256,1536]{1,0:T(8,128)(2,1)}, u32[]{:S(2)}, u32[]{:S(2)}) collective-permute-start(bf16[256,1536]{1,0:T(8,128)(2,1)} %collective-permute-done.7.x1_ref), channel_id=1, source_target_pairs={{0,4},{4,0},{8,12},{12,8},{16,20},{20,16},{24,28},{28,24},{1,5},{5... | collective-permute-start | bytes 2359304 | tf_op jit(solution)/shard_map/ppermute | solution.py:492
  150.4 23.8 %attend.1 = (bf16[1024,1536]{1,0:T(8,128)(2,1)}, bf16[1024,1152]{1,0:T(8,128)(2,1)}, bf16[1024,384]{1,0:T(8,128)(2,1)}, bf16[512,1536]{1,0:T(8,128)(2,1)}, bf16[...) custom-call(s32[2]{0:T(128)} %add_convert_fusion.5.place_ref, ...), custom_call_target="tpu_custom_call" | custom-call | flops 12000000000 | bytes 20000000 | tf_op jit(solution)/shard_map/attend/pallas_call | solution.py:127
  174.2 6.6 %collective-permute-start.13 = (bf16[512,1536]{1,0:T(8,128)(2,1)}, bf16[512,1536]{1,0:T(8,128)(2,1)S(1)}, u32[]{:S(2)}, u32[]{:S(2)}) collective-permute-start(bf16[512,1536]{1,0:T(8,128)(2,1)} %get-tuple-element.74), channel_id=1, source_target_pairs={{0,4},{4,0},{8,12},{12,8},{16,20},{20,16},{24,28},{28,24},{1,5},{5... | collective-permute-start | bytes 4718600 | tf_op jit(solution)/shard_map/ppermute | solution.py:496
  180.8 3.2 collective-permute-done.13
  184.1 1.9 add_convert_fusion.4
  186.0 1.7 collective-permute-start.14
  187.6 18.2 %collective-permute-done.14 = bf16[256,1536]{1,0:T(8,128)(2,1)S(1)} collective-permute-done((bf16[256,1536]{1,0:T(8,128)(2,1)S(1)}, bf16[256,1536]{1,0:T(8,128)(2,1)S(1)}, u32[]{:S(2)}, u32[]{:S(2)}) %collective-permute-start.14) | collective-permute-done | bytes 786464 | tf_op jit(solution)/shard_map/ppermute | solution.py:504
  207.0 1.6 collective-permute-start.15
  209.5 16.7 %collective-permute-done.15.refs_1_ = bf16[256,1536]{1,0:T(8,128)(2,1)S(1)} collective-permute-done((bf16[256,1536]{1,0:T(8,128)(2,1)S(1)}, bf16[256,1536]{1,0:T(8,128)(2,1)S(1)}, u32[]{:S(2)}, u32[]{:S(2)}) %collective-permute-start.15) | collective-permute-done | bytes 786464 | tf_op jit(solution)/shard_map/ppermute | solution.py:491
  228.6 28.4 %feed.1 = (bf16[1024,1024]{1,0:T(8,128)(2,1)}, bf16[1024,1024]{1,0:T(8,128)(2,1)}, bf16[1024,1024]{1,0:T(8,128)(2,1)}, bf16[1024,1536]{1,0:T(8,128)(2,1)}, bf16[...) custom-call(bf16[256,1536]{1,0:T(8,128)(2,1)} %copy-done.37, ...), custom_call_target="tpu_custom_call" | custom-call | flops 16000000000 | bytes 25000000 | tf_op jit(solution)/shard_map/feed/pallas_call | solution.py:312
  257.4 3.3 collective-permute-done.20
  261.9 2.2 add_convert_fusion.3
  264.1 1.6 collective-permute-start.21
  265.7 16.6 %feed_grads.1 = bf16[1536,3072]{1,0:T(8,128)(2,1)} custom-call(bf16[1024,1536]{1,0:T(8,128)(2,1)} %get-tuple-element.82.refs_0_, bf16[1024,1536]{1,0:T(8,128)(2,1)} %get-tuple-element.83.refs_1_, bf16[1024,1024]{1,0:T(8,128)(2,1)} %get-tuple-element.84.refs_2_, bf16[1024,1024]{1,0:T(8,128)(2,1)} %get-tuple-element.85.refs_3_, ...), custom_call_target="tpu_custom_call" | custom-call | flops 9663676416 | bytes 15728640 | tf_op jit(solution)/shard_map/feed_grads/pallas_call | solution.py:354
  282.3 1.8 collective-permute-done.21
  284.1 1.6 convert_add_fusion
  288.5 1.5 copy-done.65
  290.0 4.1 convolution_convert_fusion
  294.2 1.8 collective-permute-start.25
  297.6 16.6 %collective-permute-done.25.m1_ref = bf16[256,1536]{1,0:T(8,128)(2,1)S(1)} collective-permute-done((bf16[256,1536]{1,0:T(8,128)(2,1)S(1)}, bf16[256,1536]{1,0:T(8,128)(2,1)S(1)}, u32[]{:S(2)}, u32[]{:S(2)}) %collective-permute-start.25) | collective-permute-done | bytes 786464 | tf_op jit(solution)/shard_map/ppermute | solution.py:491
  314.1 4.0 convolution_convert_fusion.1
  318.2 1.2 add_convert_fusion.1
  319.4 1.7 collective-permute-start.23
  322.3 27.2 %attend_back.1 = (bf16[1024,1536]{1,0:T(8,128)(2,1)}, bf16[1024,1280]{1,0:T(8,128)(2,1)}, bf16[512,1536]{1,0:T(8,128)(2,1)}, bf16[512,1536]{1,0:T(8,128)(2,1)}, f32[8,128]{1,0:T(8,128)}) custom-call(s32[2]{0:T(128)} %add_convert_fusion.5.place_ref, bf16[256,1536]{1,0:T(8,128)(2,1)} %copy-done.33, bf16[256,1536]{1,0:T(8,128)(2,1)} %copy-done.57, ...), custom_call_target="tpu_custom_call" | custom-call | flops 149999992832 | bytes 20000000 | tf_op jit(solution)/shard_map/attend_back/pallas_call | solution.py:237
  349.5 3.3 fusion.8
  354.5 13.6 %attend_grads.1 = (bf16[1536,1664]{1,0:T(8,128)(2,1)}, f32[8,1536]{1,0:T(8,128)}) custom-call(s32[2]{0:T(128)} %add_convert_fusion.5.place_ref, bf16[1024,1536]{1,0:T(8,128)(2,1)} %get-tuple-element.96.x_ref, bf16[1024,1536]{1,0:T(8,128)(2,1)} %get-tuple-element.97.m_ref, bf16[1024,1280]{1,0:T(8,128)(2,1)} %get-tuple-element.99.grad_ref, ...), custom_call_target="tpu_custom_call" | custom-call | flops 5234491392 | bytes 20000000 | tf_op jit(solution)/shard_map/attend_grads/pallas_call | solution.py:391
  369.0 1.5 fusion.7
  371.0 5.0 collective-permute-done.28
  376.0 5.5 %collective-permute-start.29 = (f32[32,128]{1,0:T(8,128)S(1)}, f32[32,128]{1,0:T(8,128)S(1)}, u32[]{:S(2)}, u32[]{:S(2)}) collective-permute-start(f32[32,128]{1,0:T(8,128)S(1)} %add.121), channel_id=1, source_target_pairs={{0,2},{1,3},{2,0},{3,1},{4,6},{5,7},{6,4},{7,5},{8,10},{9,11},{10,... | collective-permute-start | bytes 49160 | tf_op jit(solution)/shard_map/ppermute | solution.py:511
  381.6 1.9 collective-permute-done.29
  383.6 1.4 copy-done.54
  385.0 3.3 collective-permute-done.30
  388.5 1.9 collective-permute-start.31
  391.4 6.7 %collective-permute-start.34 = (bf16[192,3072]{1,0:T(8,128)(2,1)S(1)}, bf16[192,3072]{1,0:T(8,128)(2,1)}, u32[]{:S(2)}, u32[]{:S(2)}) collective-permute-start(bf16[192,3072]{1,0:T(8,128)(2,1)S(1)} %get-tuple-element.155.high_ref), channel_id=1, source_target_pairs={{0,4},{1,5},{2,6},{3,7},{8,12},{9,13},{10,14},{11,15},{16,20},{17,... | collective-permute-start | bytes 3538952 | tf_op jit(solution)/shard_map/ppermute | solution.py:485
  398.2 1.6 collective-permute-start.32
  399.8 22.7 %collective-permute-done.31 = bf16[256,1536]{1,0:T(8,128)(2,1)S(1)} collective-permute-done((bf16[256,1536]{1,0:T(8,128)(2,1)S(1)}, bf16[256,1536]{1,0:T(8,128)(2,1)S(1)}, u32[]{:S(2)}, u32[]{:S(2)}) %collective-permute-start.31) | collective-permute-done | bytes 786464 | tf_op jit(solution)/shard_map/ppermute | solution.py:504
  424.0 23.5 %collective-permute-done.32.a_ref = bf16[192,3072]{1,0:T(8,128)(2,1)S(1)} collective-permute-done((bf16[192,3072]{1,0:T(8,128)(2,1)S(1)}, bf16[192,3072]{1,0:T(8,128)(2,1)S(1)}, u32[]{:S(2)}, u32[]{:S(2)}) %collective-permute-start.32) | collective-permute-done | bytes 1179680 | tf_op jit(solution)/shard_map/ppermute | solution.py:483
  449.6 4.3 finish.2
  455.0 1.2 collective-permute-done.36
  456.2 1.7 collective-permute-start.37
  457.8 2.1 collective-permute-done.37
  459.9 1.7 collective-permute-start.38
  461.6 2.1 collective-permute-done.38
  463.7 1.5 fusion.6
  465.2 1.4 fusion.11
  466.6 1.3 collective-permute-start.39
  468.6 6.6 %collective-permute-start.41 = (bf16[192,1664]{1,0:T(8,128)(2,1)S(1)}, bf16[192,1664]{1,0:T(8,128)(2,1)S(1)}, u32[]{:S(2)}, u32[]{:S(2)}) collective-permute-start(bf16[192,1664]{1,0:T(8,128)(2,1)S(1)} %get-tuple-element.157.high_ref), channel_id=1, source_target_pairs={{0,4},{1,5},{2,6},{3,7},{8,12},{9,13},{10,14},{11,15},{16,20},{17,... | collective-permute-start | bytes 1916936 | tf_op jit(solution)/shard_map/ppermute | solution.py:485
  476.3 16.6 %collective-permute-done.39.a_ref = bf16[192,1664]{1,0:T(8,128)(2,1)S(1)} collective-permute-done((bf16[192,1664]{1,0:T(8,128)(2,1)S(1)}, bf16[192,1664]{1,0:T(8,128)(2,1)S(1)}, u32[]{:S(2)}, u32[]{:S(2)}) %collective-permute-start.39) | collective-permute-done | bytes 639008 | tf_op jit(solution)/shard_map/ppermute | solution.py:483
  494.8 3.0 finish.3
  497.8 1.6 copy.30
  (231 shorter events, 35.3 us)
Async XLA Ops:
  7.2 143.2 %all-gather.3.cloned.1.call-start = ((), (), s32[]{:S(2)}) async-start(), calls=%async_computation.2 | async-start | bytes 6389760 | tf_op jit(solution)/shard_map/all_gather | solution.py:471
  11.2 19.5 %collective-permute-start = (bf16[192,1664]{1,0:T(8,128)(2,1)S(1)}, bf16[192,1664]{1,0:T(8,128)(2,1)S(1)}, u32[]{:S(2)}, u32[]{:S(2)}) collective-permute-start(bf16[192,1664]{1,0:T(8,128)(2,1)S(1)} %convert_dynamic-update-slice_fusion), channel_id=1, source_target_pairs={{0,6},{1,7},{2,4},{3,5},{8,14},{9,15},{10,12},{11,13},{16,22},{17,... | collective-permute-start | bytes 1916936 | tf_op jit(solution)/shard_map/ppermute | solution.py:464
  16.6 14.1 %collective-permute-start.1 = (bf16[192,1664]{1,0:T(8,128)(2,1)S(1)}, bf16[192,1664]{1,0:T(8,128)(2,1)S(1)}, u32[]{:S(2)}, u32[]{:S(2)}) collective-permute-start(bf16[192,1664]{1,0:T(8,128)(2,1)S(1)} %convert_dynamic-update-slice_fusion), channel_id=1, source_target_pairs={{4,6},{5,7},{6,4},{7,5},{12,14},{13,15},{14,12},{15,13},{20,22},{2... | collective-permute-start | bytes 1916936 | tf_op jit(solution)/shard_map/ppermute | solution.py:465
  17.3 13.4 %collective-permute-start.2 = (bf16[192,1664]{1,0:T(8,128)(2,1)S(1)}, bf16[192,1664]{1,0:T(8,128)(2,1)S(1)}, u32[]{:S(2)}, u32[]{:S(2)}) collective-permute-start(bf16[192,1664]{1,0:T(8,128)(2,1)S(1)} %convert_dynamic-update-slice_fusion), channel_id=1, source_target_pairs={{4,0},{5,1},{6,2},{7,3},{12,8},{13,9},{14,10},{15,11},{20,16},{21,... | collective-permute-start | bytes 1916936 | tf_op jit(solution)/shard_map/ppermute | solution.py:466
  32.1 196.6 %all-gather.5.cloned.1.call-start = ((), (), s32[]{:S(2)}) async-start(), calls=%async_computation.3 | async-start | bytes 11796480 | tf_op jit(solution)/shard_map/all_gather | solution.py:471
  33.8 41.1 %collective-permute-start.3 = (bf16[192,3072]{1,0:T(8,128)(2,1)S(1)}, bf16[192,3072]{1,0:T(8,128)(2,1)S(1)}, u32[]{:S(2)}, u32[]{:S(2)}) collective-permute-start(bf16[192,3072]{1,0:T(8,128)(2,1)S(1)} %pad_maximum_fusion), channel_id=1, source_target_pairs={{0,6},{1,7},{2,4},{3,5},{8,14},{9,15},{10,12},{11,13},{16,22},{17,... | collective-permute-start | bytes 3538952 | tf_op jit(solution)/shard_map/ppermute | solution.py:464
  49.8 25.1 %collective-permute-start.4 = (bf16[192,3072]{1,0:T(8,128)(2,1)S(1)}, bf16[192,3072]{1,0:T(8,128)(2,1)S(1)}, u32[]{:S(2)}, u32[]{:S(2)}) collective-permute-start(bf16[192,3072]{1,0:T(8,128)(2,1)S(1)} %pad_maximum_fusion), channel_id=1, source_target_pairs={{4,6},{5,7},{6,4},{7,5},{12,14},{13,15},{14,12},{15,13},{20,22},{2... | collective-permute-start | bytes 3538952 | tf_op jit(solution)/shard_map/ppermute | solution.py:465
  50.5 24.4 %collective-permute-start.5 = (bf16[192,3072]{1,0:T(8,128)(2,1)S(1)}, bf16[192,3072]{1,0:T(8,128)(2,1)S(1)}, u32[]{:S(2)}, u32[]{:S(2)}) collective-permute-start(bf16[192,3072]{1,0:T(8,128)(2,1)S(1)} %pad_maximum_fusion), channel_id=1, source_target_pairs={{4,0},{5,1},{6,2},{7,3},{12,8},{13,9},{14,10},{15,11},{20,16},{21,... | collective-permute-start | bytes 3538952 | tf_op jit(solution)/shard_map/ppermute | solution.py:466
  76.8 306.7 %reduce-scatter.3.cloned.1.call-start = ((), (), s32[]{:S(2)}) async-start(), calls=%async_computation.4 | async-start | bytes 11796480 | tf_op jit(solution)/shard_map/reduce_scatter | solution.py:475
  78.3 1.6 collective-permute-start.6
  81.3 124.5 %copy-start = (f32[256,1536]{1,0:T(8,128)}, f32[256,1536]{1,0:T(8,128)S(1)}, u32[]{:S(2)}) copy-start(f32[256,1536]{1,0:T(8,128)S(1)} %get-tuple-element.154) | copy-start | bytes 4718596
  81.4 29.0 %copy-start.8 = (f32[256,1536]{1,0:T(8,128)S(1)}, f32[256,1536]{1,0:T(8,128)}, u32[]{:S(2)}) copy-start(f32[256,1536]{1,0:T(8,128)} %param.27) | copy-start | bytes 4718596
  81.4 29.0 %copy-start.49 = (f32[256]{0:T(256)}, f32[256]{0:T(256)S(1)}, u32[]{:S(2)}) copy-start(f32[256]{0:T(256)S(1)} %add_rsqrt_fusion.1) | copy-start | bytes 3076
  82.5 29.7 %copy-start.64 = (f32[24]{0:T(128)S(1)}, f32[24]{0:T(128)}, u32[]{:S(2)}) copy-start(f32[24]{0:T(128)} %param.21) | copy-start | bytes 292
  82.5 30.3 %copy-start.53 = (s32[1024]{0:T(1024)S(1)}, s32[1024]{0:T(1024)}, u32[]{:S(2)}) copy-start(s32[1024]{0:T(1024)} %param.15) | copy-start | bytes 12292
  82.5 53.8 %collective-permute-start.7 = (bf16[256,1536]{1,0:T(8,128)(2,1)}, bf16[256,1536]{1,0:T(8,128)(2,1)}, u32[]{:S(2)}, u32[]{:S(2)}) collective-permute-start(bf16[256,1536]{1,0:T(8,128)(2,1)} %multiply_convert_fusion.1.x0_ref), channel_id=1, source_target_pairs={{0,1},{1,0},{2,3},{3,2},{4,5},{5,4},{6,7},{7,6},{8,9},{9,8},{10,11... | collective-permute-start | bytes 2359304 | tf_op jit(solution)/shard_map/ppermute | solution.py:491
  110.4 38.9 %collective-permute-start.10 = (bf16[256,1536]{1,0:T(8,128)(2,1)S(1)}, bf16[256,1536]{1,0:T(8,128)(2,1)}, u32[]{:S(2)}, u32[]{:S(2)}) collective-permute-start(bf16[256,1536]{1,0:T(8,128)(2,1)S(1)} %convert_element_type.140), channel_id=1, source_target_pairs={{2,4},{3,5},{4,2},{5,3},{10,12},{11,13},{12,10},{13,11},{18,20},{1... | collective-permute-start | bytes 2359304 | tf_op jit(solution)/shard_map/ppermute | solution.py:556
  112.8 35.9 %collective-permute-start.11 = (s32[1024]{0:T(1024)S(1)}, s32[1024]{0:T(1024)S(1)}, u32[]{:S(2)}, u32[]{:S(2)}) collective-permute-start(s32[1024]{0:T(1024)S(1)} %copy-done.53), channel_id=1, source_target_pairs={{0,4},{4,0},{8,12},{12,8},{16,20},{20,16},{24,28},{28,24},{1,5},{5... | collective-permute-start | bytes 12296 | tf_op jit(solution)/shard_map/ppermute | solution.py:572
  136.3 14.2 %collective-permute-start.8 = (bf16[256,1536]{1,0:T(8,128)(2,1)}, bf16[256,1536]{1,0:T(8,128)(2,1)}, u32[]{:S(2)}, u32[]{:S(2)}) collective-permute-start(bf16[256,1536]{1,0:T(8,128)(2,1)} %multiply_convert_fusion.1.x0_ref), channel_id=1, source_target_pairs={{0,4},{4,0},{8,12},{12,8},{16,20},{20,16},{24,28},{28,24},{1,5},{5... | collective-permute-start | bytes 2359304 | tf_op jit(solution)/shard_map/ppermute | solution.py:490
  136.3 14.1 %collective-permute-start.9 = (bf16[256,1536]{1,0:T(8,128)(2,1)}, bf16[256,1536]{1,0:T(8,128)(2,1)}, u32[]{:S(2)}, u32[]{:S(2)}) collective-permute-start(bf16[256,1536]{1,0:T(8,128)(2,1)} %collective-permute-done.7.x1_ref), channel_id=1, source_target_pairs={{0,4},{4,0},{8,12},{12,8},{16,20},{20,16},{24,28},{28,24},{1,5},{5... | collective-permute-start | bytes 2359304 | tf_op jit(solution)/shard_map/ppermute | solution.py:492
  149.4 24.8 %collective-permute-start.12 = (bf16[256,1536]{1,0:T(8,128)(2,1)S(1)}, bf16[256,1536]{1,0:T(8,128)(2,1)S(1)}, u32[]{:S(2)}, u32[]{:S(2)}) collective-permute-start(bf16[256,1536]{1,0:T(8,128)(2,1)S(1)} %broadcast_select_fusion.refs_4_), channel_id=1, source_target_pairs={{0,1},{1,0},{2,3},{3,2},{4,5},{5,4},{6,7},{7,6},{8,9},{9,8},{10,11... | collective-permute-start | bytes 2359304 | tf_op jit(solution)/shard_map/ppermute | solution.py:583
  174.2 31.7 %copy-start.14 = (bf16[512,1536]{1,0:T(8,128)(2,1)S(1)}, bf16[512,1536]{1,0:T(8,128)(2,1)}, u32[]{:S(2)}) copy-start(bf16[512,1536]{1,0:T(8,128)(2,1)} %get-tuple-element.71) | copy-start | bytes 4718596
  174.2 9.9 %collective-permute-start.13 = (bf16[512,1536]{1,0:T(8,128)(2,1)}, bf16[512,1536]{1,0:T(8,128)(2,1)S(1)}, u32[]{:S(2)}, u32[]{:S(2)}) collective-permute-start(bf16[512,1536]{1,0:T(8,128)(2,1)} %get-tuple-element.74), channel_id=1, source_target_pairs={{0,4},{4,0},{8,12},{12,8},{16,20},{20,16},{24,28},{28,24},{1,5},{5... | collective-permute-start | bytes 4718600 | tf_op jit(solution)/shard_map/ppermute | solution.py:496
  186.0 19.9 %collective-permute-start.14 = (bf16[256,1536]{1,0:T(8,128)(2,1)S(1)}, bf16[256,1536]{1,0:T(8,128)(2,1)S(1)}, u32[]{:S(2)}, u32[]{:S(2)}) collective-permute-start(bf16[256,1536]{1,0:T(8,128)(2,1)S(1)} %add_convert_fusion.4), channel_id=1, source_target_pairs={{0,1},{1,0},{2,3},{3,2},{4,5},{5,4},{6,7},{7,6},{8,9},{9,8},{10,11... | collective-permute-start | bytes 2359304 | tf_op jit(solution)/shard_map/ppermute | solution.py:504
  206.8 79.4 %copy-start.2 = (f32[256,1536]{1,0:T(8,128)}, f32[256,1536]{1,0:T(8,128)S(1)}, u32[]{:S(2)}) copy-start(f32[256,1536]{1,0:T(8,128)S(1)} %get-tuple-element.152) | copy-start | bytes 4718596
  206.8 79.4 %copy-start.47 = (f32[256]{0:T(256)}, f32[256]{0:T(256)S(1)}, u32[]{:S(2)}) copy-start(f32[256]{0:T(256)S(1)} %add_rsqrt_fusion) | copy-start | bytes 3076
  207.0 19.2 %collective-permute-start.15 = (bf16[256,1536]{1,0:T(8,128)(2,1)S(1)}, bf16[256,1536]{1,0:T(8,128)(2,1)S(1)}, u32[]{:S(2)}, u32[]{:S(2)}) collective-permute-start(bf16[256,1536]{1,0:T(8,128)(2,1)S(1)} %multiply_convert_fusion.refs_0_), channel_id=1, source_target_pairs={{0,1},{1,0},{2,3},{3,2},{4,5},{5,4},{6,7},{7,6},{8,9},{9,8},{10,11... | collective-permute-start | bytes 2359304 | tf_op jit(solution)/shard_map/ppermute | solution.py:491
  208.7 17.5 %collective-permute-start.18 = (bf16[256,1536]{1,0:T(8,128)(2,1)S(1)}, bf16[256,1536]{1,0:T(8,128)(2,1)S(1)}, u32[]{:S(2)}, u32[]{:S(2)}) collective-permute-start(bf16[256,1536]{1,0:T(8,128)(2,1)S(1)} %copy-done.19), channel_id=1, source_target_pairs={{0,4},{4,0},{8,12},{12,8},{16,20},{20,16},{24,28},{28,24},{1,5},{5... | collective-permute-start | bytes 2359304 | tf_op jit(solution)/shard_map/ppermute | solution.py:591
  209.0 17.2 %collective-permute-start.19 = (bf16[256,1536]{1,0:T(8,128)(2,1)S(1)}, bf16[256,1536]{1,0:T(8,128)(2,1)S(1)}, u32[]{:S(2)}, u32[]{:S(2)}) collective-permute-start(bf16[256,1536]{1,0:T(8,128)(2,1)S(1)} %copy-done.56), channel_id=1, source_target_pairs={{0,4},{4,0},{8,12},{12,8},{16,20},{20,16},{24,28},{28,24},{1,5},{5... | collective-permute-start | bytes 2359304 | tf_op jit(solution)/shard_map/ppermute | solution.py:592
  209.2 17.1 %collective-permute-start.16 = (bf16[256,1536]{1,0:T(8,128)(2,1)S(1)}, bf16[256,1536]{1,0:T(8,128)(2,1)S(1)}, u32[]{:S(2)}, u32[]{:S(2)}) collective-permute-start(bf16[256,1536]{1,0:T(8,128)(2,1)S(1)} %multiply_convert_fusion.refs_0_), channel_id=1, source_target_pairs={{0,4},{4,0},{8,12},{12,8},{16,20},{20,16},{24,28},{28,24},{1,5},{5... | collective-permute-start | bytes 2359304 | tf_op jit(solution)/shard_map/ppermute | solution.py:490
  226.2 2.4 collective-permute-start.17
  257.0 3.7 collective-permute-start.20
  264.1 20.0 %collective-permute-start.21 = (bf16[256,1536]{1,0:T(8,128)(2,1)}, bf16[256,1536]{1,0:T(8,128)(2,1)}, u32[]{:S(2)}, u32[]{:S(2)}) collective-permute-start(bf16[256,1536]{1,0:T(8,128)(2,1)} %add_convert_fusion.3), channel_id=1, source_target_pairs={{0,1},{1,0},{2,3},{3,2},{4,5},{5,4},{6,7},{7,6},{8,9},{9,8},{10,11... | collective-permute-start | bytes 2359304 | tf_op jit(solution)/shard_map/ppermute | solution.py:602
  282.2 182.9 %reduce-scatter.5.cloned.1.call-start = ((), (), s32[]{:S(2)}) async-start(), calls=%async_computation.5 | async-start | bytes 6389760 | tf_op jit(solution)/shard_map/reduce_scatter | solution.py:475
  294.1 24.1 %collective-permute-start.22 = (bf16[512,1536]{1,0:T(8,128)(2,1)S(1)}, bf16[512,1536]{1,0:T(8,128)(2,1)S(1)}, u32[]{:S(2)}, u32[]{:S(2)}) collective-permute-start(bf16[512,1536]{1,0:T(8,128)(2,1)S(1)} %convolution_convert_fusion), channel_id=1, source_target_pairs={{0,4},{4,0},{8,12},{12,8},{16,20},{20,16},{24,28},{28,24},{1,5},{5... | collective-permute-start | bytes 4718600 | tf_op jit(solution)/shard_map/ppermute | solution.py:496
  294.2 20.0 %collective-permute-start.25 = (bf16[256,1536]{1,0:T(8,128)(2,1)S(1)}, bf16[256,1536]{1,0:T(8,128)(2,1)S(1)}, u32[]{:S(2)}, u32[]{:S(2)}) collective-permute-start(bf16[256,1536]{1,0:T(8,128)(2,1)S(1)} %add_convert_fusion.2.m0_ref), channel_id=1, source_target_pairs={{0,1},{1,0},{2,3},{3,2},{4,5},{5,4},{6,7},{7,6},{8,9},{9,8},{10,11... | collective-permute-start | bytes 2359304 | tf_op jit(solution)/shard_map/ppermute | solution.py:491
  296.0 25.2 %collective-permute-start.26 = (bf16[256,1536]{1,0:T(8,128)(2,1)S(1)}, bf16[256,1536]{1,0:T(8,128)(2,1)S(1)}, u32[]{:S(2)}, u32[]{:S(2)}) collective-permute-start(bf16[256,1536]{1,0:T(8,128)(2,1)S(1)} %add_convert_fusion.2.m0_ref), channel_id=1, source_target_pairs={{0,4},{4,0},{8,12},{12,8},{16,20},{20,16},{24,28},{28,24},{1,5},{5... | collective-permute-start | bytes 2359304 | tf_op jit(solution)/shard_map/ppermute | solution.py:490
  314.1 7.0 %collective-permute-start.27 = (bf16[256,1536]{1,0:T(8,128)(2,1)S(1)}, bf16[256,1536]{1,0:T(8,128)(2,1)S(1)}, u32[]{:S(2)}, u32[]{:S(2)}) collective-permute-start(bf16[256,1536]{1,0:T(8,128)(2,1)S(1)} %collective-permute-done.25.m1_ref), channel_id=1, source_target_pairs={{0,4},{4,0},{8,12},{12,8},{16,20},{20,16},{24,28},{28,24},{1,5},{5... | collective-permute-start | bytes 2359304 | tf_op jit(solution)/shard_map/ppermute | solution.py:492
  319.4 30.1 %collective-permute-start.23 = (bf16[256,1536]{1,0:T(8,128)(2,1)}, bf16[256,1536]{1,0:T(8,128)(2,1)}, u32[]{:S(2)}, u32[]{:S(2)}) collective-permute-start(bf16[256,1536]{1,0:T(8,128)(2,1)} %add_convert_fusion.1), channel_id=1, source_target_pairs={{0,1},{1,0},{2,3},{3,2},{4,5},{5,4},{6,7},{7,6},{8,9},{9,8},{10,11... | collective-permute-start | bytes 2359304 | tf_op jit(solution)/shard_map/ppermute | solution.py:504
  322.3 27.2 %copy-start.15 = (bf16[512,1536]{1,0:T(8,128)(2,1)S(1)}, bf16[512,1536]{1,0:T(8,128)(2,1)}, u32[]{:S(2)}) copy-start(bf16[512,1536]{1,0:T(8,128)(2,1)} %get-tuple-element.71) | copy-start | bytes 4718596
  322.3 27.2 %copy-start.23 = (bf16[256,1536]{1,0:T(8,128)(2,1)S(1)}, bf16[256,1536]{1,0:T(8,128)(2,1)}, u32[]{:S(2)}) copy-start(bf16[256,1536]{1,0:T(8,128)(2,1)} %copy-done.22) | copy-start | bytes 2359300
  352.9 16.1 %collective-permute-start.24 = (bf16[256,1536]{1,0:T(8,128)(2,1)}, bf16[256,1536]{1,0:T(8,128)(2,1)S(1)}, u32[]{:S(2)}, u32[]{:S(2)}) collective-permute-start(bf16[256,1536]{1,0:T(8,128)(2,1)} %get-tuple-element.149), channel_id=1, source_target_pairs={{2,4},{3,5},{4,2},{5,3},{10,12},{11,13},{12,10},{13,11},{18,20},{1... | collective-permute-start | bytes 2359304 | tf_op jit(solution)/shard_map/ppermute | solution.py:559
  370.5 5.5 %collective-permute-start.28 = (f32[32,128]{1,0:T(8,128)S(1)}, f32[32,128]{1,0:T(8,128)S(1)}, u32[]{:S(2)}, u32[]{:S(2)}) collective-permute-start(f32[32,128]{1,0:T(8,128)S(1)} %fusion.5), channel_id=1, source_target_pairs={{0,1},{1,0},{2,3},{3,2},{4,5},{5,4},{6,7},{7,6},{8,9},{9,8},{10,11... | collective-permute-start | bytes 49160 | tf_op jit(solution)/shard_map/ppermute | solution.py:511
  376.0 7.5 %collective-permute-start.29 = (f32[32,128]{1,0:T(8,128)S(1)}, f32[32,128]{1,0:T(8,128)S(1)}, u32[]{:S(2)}, u32[]{:S(2)}) collective-permute-start(f32[32,128]{1,0:T(8,128)S(1)} %add.121), channel_id=1, source_target_pairs={{0,2},{1,3},{2,0},{3,1},{4,6},{5,7},{6,4},{7,5},{8,10},{9,11},{10,... | collective-permute-start | bytes 49160 | tf_op jit(solution)/shard_map/ppermute | solution.py:511
  384.9 3.4 collective-permute-start.30
  388.5 34.0 %collective-permute-start.31 = (bf16[256,1536]{1,0:T(8,128)(2,1)S(1)}, bf16[256,1536]{1,0:T(8,128)(2,1)S(1)}, u32[]{:S(2)}, u32[]{:S(2)}) collective-permute-start(bf16[256,1536]{1,0:T(8,128)(2,1)S(1)} %add_convert_fusion), channel_id=1, source_target_pairs={{0,1},{1,0},{2,3},{3,2},{4,5},{5,4},{6,7},{7,6},{8,9},{9,8},{10,11... | collective-permute-start | bytes 2359304 | tf_op jit(solution)/shard_map/ppermute | solution.py:504
  390.4 32.1 %copy-start.1 = (f32[256,1536]{1,0:T(8,128)S(1)}, f32[256,1536]{1,0:T(8,128)}, u32[]{:S(2)}) copy-start(f32[256,1536]{1,0:T(8,128)} %copy-done) | copy-start | bytes 4718596
  390.4 32.1 %copy-start.50 = (f32[256]{0:T(256)S(1)}, f32[256]{0:T(256)}, u32[]{:S(2)}) copy-start(f32[256]{0:T(256)} %copy-done.49) | copy-start | bytes 3076
  390.6 32.5 %copy-start.12 = (bf16[192,3072]{1,0:T(8,128)(2,1)}, bf16[192,3072]{1,0:T(8,128)(2,1)S(1)}, u32[]{:S(2)}) copy-start(bf16[192,3072]{1,0:T(8,128)(2,1)S(1)} %get-tuple-element.155.high_ref) | copy-start | bytes 3538948
  390.6 32.5 %copy-start.13 = (bf16[192,3072]{1,0:T(8,128)(2,1)}, bf16[192,3072]{1,0:T(8,128)(2,1)S(1)}, u32[]{:S(2)}) copy-start(bf16[192,3072]{1,0:T(8,128)(2,1)S(1)} %get-tuple-element.156.low_ref) | copy-start | bytes 3538948
  390.6 57.0 %collective-permute-start.33 = (bf16[192,3072]{1,0:T(8,128)(2,1)S(1)}, bf16[192,3072]{1,0:T(8,128)(2,1)S(1)}, u32[]{:S(2)}, u32[]{:S(2)}) collective-permute-start(bf16[192,3072]{1,0:T(8,128)(2,1)S(1)} %get-tuple-element.155.high_ref), channel_id=1, source_target_pairs={{4,6},{5,7},{6,4},{7,5},{12,14},{13,15},{14,12},{15,13},{20,22},{2... | collective-permute-start | bytes 3538952 | tf_op jit(solution)/shard_map/ppermute | solution.py:484
  391.4 58.2 %collective-permute-start.34 = (bf16[192,3072]{1,0:T(8,128)(2,1)S(1)}, bf16[192,3072]{1,0:T(8,128)(2,1)}, u32[]{:S(2)}, u32[]{:S(2)}) collective-permute-start(bf16[192,3072]{1,0:T(8,128)(2,1)S(1)} %get-tuple-element.155.high_ref), channel_id=1, source_target_pairs={{0,4},{1,5},{2,6},{3,7},{8,12},{9,13},{10,14},{11,15},{16,20},{17,... | collective-permute-start | bytes 3538952 | tf_op jit(solution)/shard_map/ppermute | solution.py:485
  398.2 24.9 %copy-start.48 = (f32[256]{0:T(256)S(1)}, f32[256]{0:T(256)}, u32[]{:S(2)}) copy-start(f32[256]{0:T(256)} %copy-done.47) | copy-start | bytes 3076
  398.2 24.9 %copy-start.52 = (f32[256]{0:T(256)S(1)}, f32[256]{0:T(256)}, u32[]{:S(2)}) copy-start(f32[256]{0:T(256)} %copy-done.51) | copy-start | bytes 3076
  398.2 49.3 %collective-permute-start.32 = (bf16[192,3072]{1,0:T(8,128)(2,1)S(1)}, bf16[192,3072]{1,0:T(8,128)(2,1)S(1)}, u32[]{:S(2)}, u32[]{:S(2)}) collective-permute-start(bf16[192,3072]{1,0:T(8,128)(2,1)S(1)} %get-tuple-element.156.low_ref), channel_id=1, source_target_pairs={{6,0},{7,1},{4,2},{5,3},{14,8},{15,9},{12,10},{13,11},{22,16},{23,... | collective-permute-start | bytes 3538952 | tf_op jit(solution)/shard_map/ppermute | solution.py:483
  454.1 9.6 %collective-permute-start.35 = (bf16[256,1536]{1,0:T(8,128)(2,1)S(1)}, bf16[256,1536]{1,0:T(8,128)(2,1)S(1)}, u32[]{:S(2)}, u32[]{:S(2)}) collective-permute-start(bf16[256,1536]{1,0:T(8,128)(2,1)S(1)} %convert_element_type.176), channel_id=1, source_target_pairs={{2,4},{3,5},{4,2},{5,3},{10,12},{11,13},{12,10},{13,11},{18,20},{1... | collective-permute-start | bytes 2359304 | tf_op jit(solution)/shard_map/ppermute | solution.py:559
  454.9 1.2 collective-permute-start.36
  456.2 3.7 collective-permute-start.37
  459.9 3.7 collective-permute-start.38
  466.5 26.4 %copy-start.24 = (bf16[192,1664]{1,0:T(8,128)(2,1)}, bf16[192,1664]{1,0:T(8,128)(2,1)S(1)}, u32[]{:S(2)}) copy-start(bf16[192,1664]{1,0:T(8,128)(2,1)S(1)} %get-tuple-element.157.high_ref) | copy-start | bytes 1916932
  466.6 26.4 %copy-start.25 = (bf16[192,1664]{1,0:T(8,128)(2,1)}, bf16[192,1664]{1,0:T(8,128)(2,1)S(1)}, u32[]{:S(2)}) copy-start(bf16[192,1664]{1,0:T(8,128)(2,1)S(1)} %get-tuple-element.158.low_ref) | copy-start | bytes 1916932
  466.6 26.3 %collective-permute-start.39 = (bf16[192,1664]{1,0:T(8,128)(2,1)S(1)}, bf16[192,1664]{1,0:T(8,128)(2,1)S(1)}, u32[]{:S(2)}, u32[]{:S(2)}) collective-permute-start(bf16[192,1664]{1,0:T(8,128)(2,1)S(1)} %get-tuple-element.158.low_ref), channel_id=1, source_target_pairs={{6,0},{7,1},{4,2},{5,3},{14,8},{15,9},{12,10},{13,11},{22,16},{23,... | collective-permute-start | bytes 1916936 | tf_op jit(solution)/shard_map/ppermute | solution.py:483
  467.9 25.0 %collective-permute-start.40 = (bf16[192,1664]{1,0:T(8,128)(2,1)S(1)}, bf16[192,1664]{1,0:T(8,128)(2,1)S(1)}, u32[]{:S(2)}, u32[]{:S(2)}) collective-permute-start(bf16[192,1664]{1,0:T(8,128)(2,1)S(1)} %get-tuple-element.157.high_ref), channel_id=1, source_target_pairs={{4,6},{5,7},{6,4},{7,5},{12,14},{13,15},{14,12},{15,13},{20,22},{2... | collective-permute-start | bytes 1916936 | tf_op jit(solution)/shard_map/ppermute | solution.py:484
  468.6 24.3 %collective-permute-start.41 = (bf16[192,1664]{1,0:T(8,128)(2,1)S(1)}, bf16[192,1664]{1,0:T(8,128)(2,1)S(1)}, u32[]{:S(2)}, u32[]{:S(2)}) collective-permute-start(bf16[192,1664]{1,0:T(8,128)(2,1)S(1)} %get-tuple-element.157.high_ref), channel_id=1, source_target_pairs={{0,4},{1,5},{2,6},{3,7},{8,12},{9,13},{10,14},{11,15},{16,20},{17,... | collective-permute-start | bytes 1916936 | tf_op jit(solution)/shard_map/ppermute | solution.py:485
  (48 other events, 308.8 us)
Sparse Core Ops, SparseCore 0:
  32.2 76.0 all-gather.2
  110.1 96.3 all-gather.4
  282.4 94.5 reduce-scatter.2
  383.7 62.2 reduce-scatter.4

commit v4 on v3

--- a/solution.py
+++ b/solution.py
@@ -20,7 +20,7 @@
     return lax.dot_general(a, b, dn, preferred_element_type=F32)
 
 
-VMEM_LIMIT = 60 * 1024 * 1024
+VMEM_LIMIT = 38 * 1024 * 1024
 
 
 def split3(x):
@@ -260,14 +260,15 @@
 
 
 def feed_kernel(*refs):
-    x_parts, c_parts = refs[:4], refs[4:8]
-    wg_ref, wu_ref, wd_ref, hidden_ref, gb_ref, ub_ref, x_ref, c_ref, keep_ref, send_ref, total_ref = refs[8:]
+    x_parts, c_parts = refs[:2], refs[2:4]
+    wg_ref, wu_ref, wd_ref, hidden_ref, back_ref, x_ref, c_ref, keep_ref, send_ref, total_ref = refs[4:]
     step = pl.program_id(0)
-    block = x_ref.shape[0] // 4
+    block = x_ref.shape[0] // 2
+    columns = wg_ref.shape[1]
 
     @pl.when(step == 0)
     def _():
-        for n in range(4):
+        for n in range(2):
             x_ref[n * block : (n + 1) * block, :] = x_parts[n][...]
             c_ref[n * block : (n + 1) * block, :] = c_parts[n][...]
 
@@ -279,97 +280,149 @@
     sig = 1.0 / (1.0 + jnp.exp(-gate))
     silu = gate * sig
     hidden_ref[...] = (silu * up).astype(BF)
-    gb = (back * up * sig * (1.0 + gate * (1.0 - sig))).astype(BF)
-    ub = (back * silu).astype(BF)
-    gb_ref[...] = gb
-    ub_ref[...] = ub
-    part = dotf(gb, wg, NT) + dotf(ub, wu, NT)
+    back_ref[:, :columns] = (back * up * sig * (1.0 + gate * (1.0 - sig))).astype(BF)
+    back_ref[:, columns:] = (back * silu).astype(BF)
+    part = dotf(back_ref[...], jnp.concatenate([wg, wu], axis=1), NT)
 
     @pl.when(step == 0)
     def _():
         total_ref[...] = part
 
-    @pl.when(step > 0)
+    @pl.when((step > 0) & (step < pl.num_programs(0) - 1))
     def _():
         total_ref[...] += part
 
     @pl.when(step == pl.num_programs(0) - 1)
     def _():
-        keep_ref[...] = total_ref[: 2 * block].astype(BF)
-        send_ref[...] = total_ref[2 * block :].astype(BF)
-
-
-def feed(xs, cs, w, block=256):
+        keep_ref[...] = (total_ref[:block] + part[:block]).astype(BF)
+        send_ref[...] = (total_ref[block:] + part[block:]).astype(BF)
+
+
+def feed(xs, cs, w, columns):
     rows, features = xs[0].shape
-    length = 4 * rows
+    length = 2 * rows
     width = w.shape[1] // 3
-    steps = width // block
+    steps = width // columns
     part = pl.BlockSpec((rows, features), lambda i: (0, 0))
-    half = pl.BlockSpec((2 * rows, features), lambda i: (0, 0))
     whole = pl.BlockSpec((length, features), lambda i: (0, 0))
-    tall = lambda k: pl.BlockSpec((features, block), lambda i: (0, i + k * steps))
-    out = pl.BlockSpec((length, block), lambda i: (0, i))
+    tall = lambda k: pl.BlockSpec((features, columns), lambda i: (0, i + k * steps))
     return pl.pallas_call(
         feed_kernel,
         grid=(steps,),
-        in_specs=[part] * 8 + [tall(0), tall(1), tall(2)],
-        out_specs=[out, out, out, whole, whole, half, half],
-        out_shape=[jax.ShapeDtypeStruct((length, width), BF)] * 3
+        in_specs=[part] * 4 + [tall(0), tall(1), tall(2)],
+        out_specs=[
+            pl.BlockSpec((length, columns), lambda i: (0, i)),
+            pl.BlockSpec((length, 2 * columns), lambda i: (0, i)),
+            whole,
+            whole,
+            part,
+            part,
+        ],
+        out_shape=[
+            jax.ShapeDtypeStruct((length, width), BF),
+            jax.ShapeDtypeStruct((length, 2 * width), BF),
+        ]
         + [jax.ShapeDtypeStruct((length, features), BF)] * 2
-        + [jax.ShapeDtypeStruct((2 * rows, features), BF)] * 2,
+        + [jax.ShapeDtypeStruct((rows, features), BF)] * 2,
         scratch_shapes=[pltpu.VMEM((length, features), F32)],
         compiler_params=pltpu.CompilerParams(vmem_limit_bytes=VMEM_LIMIT),
         cost_estimate=pl.CostEstimate(
-            flops=16 * 10**9, bytes_accessed=25 * 10**6, transcendentals=10**6
+            flops=8 * 10**9, bytes_accessed=18 * 10**6, transcendentals=10**6
         ),
         name="feed",
     )(*xs, *cs, w, w, w)
 
 
-def weight_grad_kernel(steps, left, right, *refs):
-    ins, out_ref = refs[:-1], refs[-1]
+def feed_grads_kernel(steps, xa_ref, xb_ref, ca_ref, cb_ref, ba_ref, bb_ref, ha_ref, hb_ref, out_ref):
     step = pl.program_id(0)
-    begin = 0
-    for lhs, rhs, count in zip(left, right, steps):
-
-        @pl.when((step >= begin) & (step < begin + count))
-        def _():
-            out_ref[...] = dotf(ins[lhs][...], ins[rhs][...], TN).astype(BF)
-
-        begin += count
-
-
-def weight_grad(lefts, rights, uses, block, name):
-    length, features = lefts[0].shape
-    counts = [rights[r].shape[1] // block for _, r in uses]
-    starts = [sum(counts[:n]) for n in range(len(counts))]
-    in_specs = [pl.BlockSpec((length, features), lambda i: (0, 0)) for _ in lefts]
-    for n in range(len(rights)):
-        in_specs.append(
-            pl.BlockSpec(
-                (length, block),
-                lambda i, n=n: (0, jnp.clip(i - starts[n], 0, counts[n] - 1)),
-            )
-        )
+
+    @pl.when(step < 2 * steps)
+    def _():
+        out_ref[...] = (dotf(xa_ref[...], ba_ref[...], TN) + dotf(xb_ref[...], bb_ref[...], TN)).astype(BF)
+
+    @pl.when(step >= 2 * steps)
+    def _():
+        out_ref[...] = (dotf(ca_ref[...], ha_ref[...], TN) + dotf(cb_ref[...], hb_ref[...], TN)).astype(BF)
+
+
+def feed_grads_of(xs, cs, backs, hiddens, columns):
+    length, features = xs[0].shape
+    width = hiddens[0].shape[1]
+    steps = width // columns
+    whole = pl.BlockSpec((length, features), lambda i: (0, 0))
+
+    def back_at(i):
+        i = jnp.minimum(i, 2 * steps - 1)
+        return (0, (i % steps) * 2 + i // steps)
+
+    back = pl.BlockSpec((length, columns), back_at)
+    hidden = pl.BlockSpec((length, columns), lambda i: (0, jnp.maximum(i - 2 * steps, 0)))
     return pl.pallas_call(
-        functools.partial(
-            weight_grad_kernel,
-            counts,
-            [left for left, _ in uses],
-            [len(lefts) + r for _, r in uses],
-        ),
-        grid=(sum(counts),),
-        in_specs=in_specs,
-        out_specs=pl.BlockSpec((features, block), lambda i: (0, i)),
-        out_shape=jax.ShapeDtypeStruct((features, sum(counts) * block), BF),
+        functools.partial(feed_grads_kernel, steps),
+        grid=(3 * steps,),
+        in_specs=[whole] * 4 + [back] * 2 + [hidden] * 2,
+        out_specs=pl.BlockSpec((features, columns), lambda i: (0, i)),
+        out_shape=jax.ShapeDtypeStruct((features, 3 * width), BF),
         compiler_params=pltpu.CompilerParams(vmem_limit_bytes=VMEM_LIMIT),
         cost_estimate=pl.CostEstimate(
-            flops=2 * length * features * sum(counts) * block,
-            bytes_accessed=2 * features * (2 * length + sum(counts) * block),
+            flops=12 * length * features * width,
+            bytes_accessed=25 * 10**6,
             transcendentals=0,
         ),
-        name=name,
-    )(*lefts, *rights)
+        name="feed_grads",
+    )(*xs, *cs, *backs, *hiddens)
+
+
+def down_kernel(ha_ref, hb_ref, w_ref, *outs):
+    rows = outs[0].shape[0]
+    w = w_ref[...]
+    for h_ref, (keep_ref, send_ref) in zip((ha_ref, hb_ref), (outs[:2], outs[2:])):
+        part = dotf(h_ref[...], w, NT)
+        keep_ref[...] = part[:rows].astype(BF)
+        send_ref[...] = part[rows:].astype(BF)
+
+
+def down_product(hiddens, w):
+    length, width = hiddens[0].shape
+    features = w.shape[0]
+    hidden = pl.BlockSpec((length, width), lambda i: (0, 0))
+    part = pl.BlockSpec((length // 2, features), lambda i: (0, 0))
+    return pl.pallas_call(
+        down_kernel,
+        grid=(1,),
+        in_specs=[hidden, hidden, pl.BlockSpec((features, width), lambda i: (0, 2))],
+        out_specs=[part] * 4,
+        out_shape=[jax.ShapeDtypeStruct((length // 2, features), BF)] * 4,
+        compiler_params=pltpu.CompilerParams(vmem_limit_bytes=VMEM_LIMIT),
+        cost_estimate=pl.CostEstimate(
+            flops=4 * length * features * width, bytes_accessed=8 * 10**6, transcendentals=0
+        ),
+        name="down_product",
+    )(*hiddens, w)
+
+
+def pack_kernel(places, *refs):
+    ins, out_ref = refs[:-1], refs[-1]
+    for begin, ref in zip(places, ins):
+        width = ref.shape[1]
+        if width % 128:
+            out_ref[:, begin : begin + 128] = jnp.zeros((out_ref.shape[0], 128), BF)
+        out_ref[:, begin : begin + width] = ref[...].astype(BF)
+
+
+def pack(parts, places, columns):
+    rows = parts[0].shape[0]
+    return pl.pallas_call(
+        functools.partial(pack_kernel, places),
+        out_shape=jax.ShapeDtypeStruct((rows, columns), BF),
+        compiler_params=pltpu.CompilerParams(vmem_limit_bytes=VMEM_LIMIT),
+        cost_estimate=pl.CostEstimate(
+            flops=rows * columns, bytes_accessed=6 * rows * columns, transcendentals=0
+        ),
+        name="pack",
+    )(*parts)
+
+
 def attend_grads_kernel(
     place_ref, x_ref, m_ref, grad_ref, mixed_ref, keep_ref, send_ref, out_ref, gain_ref
 ):
@@ -559,13 +612,18 @@
         low = lax.ppermute(x.astype(BF), BOTH, lay.move)
         return jnp.where(away, low.astype(F32), x)
 
-    forget_pad = jnp.pad(forget_weight, ((0, 0), (0, 128 - heads)))
-    w_attn_local = jnp.concatenate(
-        [query_weight, key_weight, value_weight, forget_pad, output_weight], axis=1
-    ).astype(BF)
+    w_attn_local = pack(
+        [query_weight, key_weight, value_weight, forget_weight, output_weight],
+        [0, width, 2 * width, 3 * width, 3 * width + 128],
+        4 * width + 128,
+    )
     attn_rows = swap_weight(lay, w_attn_local, odd)
     w_attn = gather_rows(lay, attn_rows)
-    w_feed_local = jnp.concatenate([gate_weight, up_weight, down_weight], axis=1).astype(BF)
+    w_feed_local = pack(
+        [gate_weight, up_weight, down_weight],
+        [0, hidden_width, 2 * hidden_width],
+        3 * hidden_width,
+    )
     feed_rows = swap_weight(lay, after(w_feed_local, attn_rows), odd)
     w_feed = gather_rows(lay, feed_rows)
     segment = jnp.where(
@@ -585,52 +643,61 @@
         place, (*xs[:3], after(xs[3], cot_low)), w_attn, bias, seg_row, heads
     )
     mine, other = scatter_core(lay, keep, after(send, cot_z))
-    cots = (
-        cot_low,
-        cot_z,
-        lax.ppermute(after(cot_low, other), "dp", lay.core),
-        lax.ppermute(after(cot_z, other), "dp", lay.core),
-    )
+    cot_core = lax.ppermute(after(cot_low, other), "dp", lay.core)
+    cot_core_z = lax.ppermute(after(cot_z, other), "dp", lay.core)
     branch = scatter_z(lay, mine, other)
     middle = layer + branch
 
-    feeds = gather_pair(lay, (middle * inverse_rms(middle) * feed_gain).astype(BF))
-    hidden, gate_back, up_back, feed_normed, cot_all, keep, send = feed(feeds, cots, w_feed, 512)
-    feed_keep, feed_send = keep, send
-    mine, other = scatter_core(lay, keep, send)
-    hidden, other = lax.optimization_barrier((hidden, other))
-    got = lax.ppermute(other, "tensor", lay.pair)
-    feed_grads = weight_grad(
-        [feed_normed, cot_all],
-        [gate_back, up_back, hidden],
-        [(0, 0), (0, 1), (1, 2)],
-        512,
-        "feed_grads",
+    feed_local = (middle * inverse_rms(middle) * feed_gain).astype(BF)
+    feed_z = lax.ppermute(feed_local, "tensor", lay.pair)
+    feed_core = lax.ppermute(feed_local, "dp", lay.core)
+    hidden_a, back_a, x_a, c_a, keep_a, send_a = feed(
+        (feed_local, feed_core), (cot_low, cot_core), w_feed, 512
+    )
+    feed_z = after(feed_z, keep_a)
+    feed_core_z = lax.ppermute(feed_z, "dp", lay.core)
+    hidden_b, back_b, x_b, c_b, keep_b, send_b = feed(
+        (feed_z, feed_core_z), (cot_z, cot_core_z), w_feed, 512
+    )
+    got_a = lax.ppermute(send_a, "dp", lay.core)
+    got_b = lax.ppermute(send_b, "dp", lay.core)
+    other = (keep_b.astype(F32) + got_b.astype(F32)).astype(BF)
+    got_z = lax.ppermute(other, "tensor", lay.pair)
+    hidden_b, other = lax.optimization_barrier((hidden_b, other))
+    feed_grads = feed_grads_of(
+        (x_a, x_b), (c_a, c_b), (back_a, back_b), (hidden_a, hidden_b), 512
     )
     feed_scattered = scatter_rows(lay, feed_grads)
-    feed_normed_grad = after(mine + got.astype(F32), feed_grads)
+    feed_normed_grad = keep_a.astype(F32) + got_a.astype(F32) + got_z.astype(F32)
+    feed_normed_grad = after(feed_normed_grad, feed_grads)
 
     middle_part = norm_back(middle, feed_gain, feed_normed_grad)
     cotangent = jnp.where(away, cot_low.astype(F32), output_cotangent)
     middle_low = (cotangent + middle_part).astype(BF)
     ms = gather_pair(lay, middle_low)
-    w_down = w_feed[:, 2 * hidden_width :]
-    ready = after(hidden, middle_low)
-    half = hidden.shape[0] // 2
-    down_send = dotf(ready[half:], w_down, NT).astype(BF)
-    down_keep = dotf(ready[:half], w_down, NT).astype(BF)
-    near, far = feed_normed[:half].astype(F32), feed_normed[half:].astype(F32)
-    feed_gain_part = jnp.sum(
-        after(feed_keep, middle_low).astype(F32) * near + feed_send.astype(F32) * far, axis=0
+    down_keep_a, down_send_a, down_keep_b, down_send_b = down_product(
+        (hidden_a, after(hidden_b, middle_low)), w_feed
+    )
+    got_b = lax.ppermute(down_send_b, "dp", lay.core)
+    other = (down_keep_b.astype(F32) + got_b.astype(F32)).astype(BF)
+    got_a = lax.ppermute(down_send_a, "dp", lay.core)
+    ms = (*ms[:3], after(ms[3], other))
+    feed_gain_part = sum(
+        jnp.sum(part.astype(F32) * x.astype(F32), axis=0)
+        for part, x in (
+            (after(keep_a, middle_low), x_a[: keep_a.shape[0]]),
+            (send_a, x_a[keep_a.shape[0] :]),
+            (keep_b, x_b[: keep_b.shape[0]]),
+            (send_b, x_b[keep_b.shape[0] :]),
+        )
     )
     feed_gain_part = feed_gain_part / feed_gain
-    mine, other = scatter_core(lay, down_keep, down_send)
-    ms = (*ms[:3], after(ms[3], other))
 
     middle_all, grads, keep, send, bias_part = attend_back(
         place, ms, w_attn, qkv, mixed, rows, decay, closed, seg_row, heads
     )
-    down = branch + scatter_z(lay, mine, other)
+    down = branch + down_keep_a.astype(F32) + got_a.astype(F32)
+    down = down + after(lax.ppermute(other, "tensor", lay.pair), bias_part).astype(F32)
     down_back = moved_back(down)
     attn_grads, attn_gain_part = attend_grads(
         place, attn_normed, middle_all, after(grads, down), mixed, keep, send
@@ -644,19 +711,19 @@
     packed = jnp.pad(packed, (0, -size % 1024)).reshape(-1, 128)
     packed = sum_all(after(packed, down_back), "tensor")
     attn_scattered = scatter_rows(lay, after(attn_grads, feed_scattered, packed))
+    small = sum_all(after(packed, attn_grads), "dp").reshape(-1)
     gate_shard, up_shard, down_shard = share_grad(
-        lay, after(feed_scattered, packed), odd, [hidden_width] * 3
+        lay, after(feed_scattered, small), odd, [hidden_width] * 3
     )
     mine, other = scatter_core(lay, keep, after(send, packed))
     attn_normed_grad = scatter_z(lay, mine, other)
     input_part = norm_back(layer, attn_gain, attn_normed_grad)
     input_back = moved_back(after(middle_part + input_part, gate_shard))
     input_grad = output_cotangent + input_back
-    small = sum_all(after(packed, other), "dp").reshape(-1)
 
     query_shard, key_shard, value_shard, forget_shard, output_shard = share_grad(
         lay,
-        after(attn_scattered, small, gate_shard, input_back),
+        after(attn_scattered, small, gate_shard),
         odd,
         [width, width, width, 128, width],
     )

time: 516 us -> 481 us (0.932); the launches traced: 506 us -> 477 us
  Pallas kernels: 117 us -> 98.6 us
  matrix products: 8.08 us -> 0 us
  other arithmetic: 29.2 us -> 22 us
  waiting for transfers between devices: 175 us -> 182 us
    ppermute x3 -> x2, waiting for transfers between devices: 33.2 us -> 8.6 us  [gather_pair(): z = lax.ppermute(x, 'tensor', lay.pair)]
    ppermute x2, waiting for transfers between devices: 40.2 us -> 62.1 us  [share_grad(): a = lax.ppermute(low, BOTH, lay.back_even_far)]
    ppermute x3 -> x11, waiting for transfers between devices: 1.84 us -> 10.7 us  [the longest x1 4.67 us: per_device(): got_z = lax.ppermute(other, 'tensor', lay.pair)]
    dot_general x2 -> x0, matrix products: 8.08 us -> none  [dotf(): return lax.dot_general(a, b, dn, preferred_element_type=F32)]
    ppermute x2, starting transfers between devices: 13.3 us -> 6.12 us  [share_grad(): c = lax.ppermute(high, BOTH, lay.back_odd_even)]
    ppermute x4 -> x2, waiting for transfers between devices: 9.89 us -> 3.04 us  [scatter_core(): got = lax.ppermute(send, 'dp', lay.core)]
    reduce_scatter x2, waiting for transfers between devices: 0.01 us -> 6.81 us  [scatter_rows(): lax.psum_scatter(g, 'dp', scatter_dimension=0, tiled=True, axis_index_gro...]
    ppermute x5, waiting for transfers between devices: 12.3 us -> 18.4 us  [sum_all(): x = x + lax.ppermute(x, axis, [(i, i ^ step) for i in range(size)])]
  transfers between devices with their start and end apart: 46 -> 48, of which waited for: 18 -> 19; matrix products, arithmetic and copies ran while one was open for 7% -> 5% of each run, Pallas kernels for 17% -> 18%
where the time goes in v4:
time: 481 us; the launch traced here: 477 us
  waiting for transfers between devices  182 us (38%)
  starting transfers between devices  135 us (28%)
  Pallas kernels  98.6 us (20%)
  local copies, waits for them, and re-layouts  24.3 us (5%)
  other arithmetic  22 us (5%)
  between operations  15.2 us (3%)
    ppermute x2, waiting for transfers between devices, share_grad(): a = lax.ppermute(low, BOTH, lay.back_even_far)  62.1 us
    ppermute x2, waiting for transfers between devices, scatter_z(): return mine + lax.ppermute(other, 'tensor', lay.pair).astype(F32)  36.5 us
    ppermute x2, waiting for transfers between devices, swap_weight(): a = lax.ppermute(w, BOTH, lay.even_far)  35.1 us
    ppermute x2, starting transfers between devices, gather_pair(): z = lax.ppermute(x, 'tensor', lay.pair)  29.8 us
    pallas_call x2, Pallas kernels, feed(): pl.pallas_call(feed_kernel, grid=(steps,), in_specs=[part] * 4 + [tall(0)...  25.7 us
    ppermute x1, starting transfers between devices, per_device(): lax.ppermute(after(segment_ids, attn_rows), 'dp', lay.core)  24.5 us
    pallas_call x1, Pallas kernels, attend_back(): pl.pallas_call(functools.partial(attend_back_kernel, heads, 256), in_spec...  23.3 us
    unnamed x130, local copies, waits for them, and re-layouts  21.5 us
  transfers between devices with their start and end apart: 48, of which 19 were waited for; matrix products, arithmetic and copies ran while one was open for 5% of the time, Pallas kernels for 18%

profile of v4, /device:TPU:0, one launch (start us, length us, event | category | flops | bytes accessed | tf_op | source)
XLA Modules:
  0.0 476.6 jit_solution(11976695620864940750)
XLA Ops:
  12.0 5.4 %collective-permute-start = (bf16[192,1664]{1,0:T(8,128)(2,1)S(1)}, bf16[192,1664]{1,0:T(8,128)(2,1)S(1)}, u32[]{:S(2)}, u32[]{:S(2)}) collective-permute-start(bf16[192,1664]{1,0:T(8,128)(2,1)S(1)} %pack.3), channel_id=1, source_target_pairs={{0,6},{1,7},{2,4},{3,5},{8,14},{9,15},{10,12},{11,13},{16,22},{17,... | collective-permute-start | bytes 1916936 | tf_op jit(solution)/shard_map/ppermute | solution.py:517
  18.1 1.3 collective-permute-start.2
  19.4 12.1 %collective-permute-done = bf16[192,1664]{1,0:T(8,128)(2,1)S(1)} collective-permute-done((bf16[192,1664]{1,0:T(8,128)(2,1)S(1)}, bf16[192,1664]{1,0:T(8,128)(2,1)S(1)}, u32[]{:S(2)}, u32[]{:S(2)}) %collective-permute-start) | collective-permute-done | bytes 639008 | tf_op jit(solution)/shard_map/ppermute | solution.py:517
  31.5 2.5 maximum_select_fusion.1
  34.1 1.0 copy-done.5
  35.3 16.0 %collective-permute-start.3 = (bf16[192,3072]{1,0:T(8,128)(2,1)S(1)}, bf16[192,3072]{1,0:T(8,128)(2,1)S(1)}, u32[]{:S(2)}, u32[]{:S(2)}) collective-permute-start(bf16[192,3072]{1,0:T(8,128)(2,1)S(1)} %pack.2), channel_id=1, source_target_pairs={{0,6},{1,7},{2,4},{3,5},{8,14},{9,15},{10,12},{11,13},{16,22},{17,... | collective-permute-start | bytes 3538952 | tf_op jit(solution)/shard_map/ppermute | solution.py:517
  52.0 1.3 collective-permute-start.5
  53.3 23.1 %collective-permute-done.3 = bf16[192,3072]{1,0:T(8,128)(2,1)S(1)} collective-permute-done((bf16[192,3072]{1,0:T(8,128)(2,1)S(1)}, bf16[192,3072]{1,0:T(8,128)(2,1)S(1)}, u32[]{:S(2)}, u32[]{:S(2)}) %collective-permute-start.3) | collective-permute-done | bytes 1179680 | tf_op jit(solution)/shard_map/ppermute | solution.py:517
  76.4 2.0 maximum_select_fusion
  78.4 1.3 copy-done.40
  81.5 27.9 %collective-permute-start.7 = (bf16[256,1536]{1,0:T(8,128)(2,1)S(1)}, bf16[256,1536]{1,0:T(8,128)(2,1)S(1)}, u32[]{:S(2)}, u32[]{:S(2)}) collective-permute-start(bf16[256,1536]{1,0:T(8,128)(2,1)S(1)} %multiply_convert_fusion.1.x0_ref), channel_id=1, source_target_pairs={{0,1},{1,0},{2,3},{3,2},{4,5},{5,4},{6,7},{7,6},{8,9},{9,8},{10,11... | collective-permute-start | bytes 2359304 | tf_op jit(solution)/shard_map/ppermute | solution.py:544
  109.5 1.7 collective-permute-start.10
  111.4 24.5 %collective-permute-start.11 = (s32[1024]{0:T(1024)S(1)}, s32[1024]{0:T(1024)S(1)}, u32[]{:S(2)}, u32[]{:S(2)}) collective-permute-start(s32[1024]{0:T(1024)S(1)} %copy-done.62), channel_id=1, source_target_pairs={{0,4},{4,0},{8,12},{12,8},{16,20},{20,16},{24,28},{28,24},{1,5},{5... | collective-permute-start | bytes 12296 | tf_op jit(solution)/shard_map/ppermute | solution.py:630
  135.9 10.6 %collective-permute-start.9 = (bf16[256,1536]{1,0:T(8,128)(2,1)S(1)}, bf16[256,1536]{1,0:T(8,128)(2,1)S(1)}, u32[]{:S(2)}, u32[]{:S(2)}) collective-permute-start(bf16[256,1536]{1,0:T(8,128)(2,1)S(1)} %collective-permute-done.7.x1_ref), channel_id=1, source_target_pairs={{0,4},{4,0},{8,12},{12,8},{16,20},{20,16},{24,28},{28,24},{1,5},{5... | collective-permute-start | bytes 2359304 | tf_op jit(solution)/shard_map/ppermute | solution.py:545
  146.6 1.2 broadcast_select_fusion.refs_2_
  149.3 1.1 copy-done.21
  150.4 21.1 %attend.1 = (bf16[1024,1536]{1,0:T(8,128)(2,1)S(1)}, bf16[1024,1152]{1,0:T(8,128)(2,1)S(1)}, bf16[1024,384]{1,0:T(8,128)(2,1)S(1)}, bf16[512,1536]{1,0:T(8,128)(...) custom-call(s32[2]{0:T(128)S(1)} %add_convert_fusion.4.place_ref, ...), custom_call_target="tpu_custom_call" | custom-call | flops 12000000000 | bytes 20000000 | tf_op jit(solution)/shard_map/attend/pallas_call | solution.py:127
  173.2 9.7 %collective-permute-start.13 = (bf16[512,1536]{1,0:T(8,128)(2,1)S(1)}, bf16[512,1536]{1,0:T(8,128)(2,1)S(1)}, u32[]{:S(2)}, u32[]{:S(2)}) collective-permute-start(bf16[512,1536]{1,0:T(8,128)(2,1)S(1)} %get-tuple-element.84), channel_id=1, source_target_pairs={{0,4},{4,0},{8,12},{12,8},{16,20},{20,16},{24,28},{28,24},{1,5},{5... | collective-permute-start | bytes 4718600 | tf_op jit(solution)/shard_map/ppermute | solution.py:549
  182.8 3.0 collective-permute-done.13
  186.1 1.8 collective-permute-start.14
  188.0 18.0 %collective-permute-done.14 = bf16[256,1536]{1,0:T(8,128)(2,1)S(1)} collective-permute-done((bf16[256,1536]{1,0:T(8,128)(2,1)S(1)}, bf16[256,1536]{1,0:T(8,128)(2,1)S(1)}, u32[]{:S(2)}, u32[]{:S(2)}) %collective-permute-start.14) | collective-permute-done | bytes 786464 | tf_op jit(solution)/shard_map/ppermute | solution.py:557
  206.9 1.8 collective-permute-start.17
  210.7 1.1 copy-done.9
  211.8 1.1 copy-done.11
  213.0 12.3 %feed.2 = (bf16[512,1024]{1,0:T(8,128)(2,1)S(1)}, bf16[512,2048]{1,0:T(8,128)(2,1)S(1)}, bf16[512,1536]{1,0:T(8,128)(2,1)S(1)}, bf16[512,1536]{1,0:T(8,128)(2,1)...) custom-call(bf16[256,1536]{1,0:T(8,128)(2,1)S(1)} %multiply_convert_fusion.refs_0_, ...), custom_call_target="tpu_custom_call" | custom-call | flops 8000000000 | bytes 18000000 | tf_op jit(solution)/shard_map/feed/pallas_call | solution.py:309
  225.3 1.7 collective-permute-done.17.refs_0_
  227.0 2.5 collective-permute-done.18.refs_1_
  229.5 13.4 %feed.3 = (bf16[512,1024]{1,0:T(8,128)(2,1)S(1)}, bf16[512,2048]{1,0:T(8,128)(2,1)S(1)}, bf16[512,1536]{1,0:T(8,128)(2,1)S(1)}, bf16[512,1536]{1,0:T(8,128)(2,1)...) custom-call(bf16[256,1536]{1,0:T(8,128)(2,1)} %collective-permute-done.17.refs_0_, ...), custom_call_target="tpu_custom_call" | custom-call | flops 8000000000 | bytes 18000000 | tf_op jit(solution)/shard_map/feed/pallas_call | solution.py:309
  243.5 1.8 collective-permute-done.20
  245.9 1.8 collective-permute-start.22
  247.7 13.0 %feed_grads.1 = bf16[1536,3072]{1,0:T(8,128)(2,1)} custom-call(bf16[512,1536]{1,0:T(8,128)(2,1)S(1)} %get-tuple-element.95.xa_ref, bf16[512,1536]{1,0:T(8,128)(2,1)S(1)} %get-tuple-element.96.xb_ref, bf16[512,1536]{1,0:T(8,128)(2,1)S(1)} %get-tuple-element.97.ca_ref, bf16[512,1536]{1,0:T(8,128)(2,1)S(1)} %get-tuple-element.98.cb_ref, ...), custom_call_target="tpu_custom_call" | custom-call | flops 9663676416 | bytes 25000000 | tf_op jit(solution)/shard_map/feed_grads/pallas_call | solution.py:360
  260.9 4.7 collective-permute-done.22
  265.6 2.0 convert_add_fusion.2
  270.2 1.9 collective-permute-start.26
  272.1 4.0 copy-done
  276.0 3.5 down_product.1
  280.2 8.6 %collective-permute-done.26.m1_ref = bf16[256,1536]{1,0:T(8,128)(2,1)S(1)} collective-permute-done((bf16[256,1536]{1,0:T(8,128)(2,1)S(1)}, bf16[256,1536]{1,0:T(8,128)(2,1)S(1)}, u32[]{:S(2)}, u32[]{:S(2)}) %collective-permute-start.26) | collective-permute-done | bytes 786464 | tf_op jit(solution)/shard_map/ppermute | solution.py:544
  289.9 1.1 add_convert_fusion.1
  290.9 1.7 collective-permute-start.25
  292.7 23.3 %attend_back.1 = (bf16[1024,1536]{1,0:T(8,128)(2,1)S(1)}, bf16[1024,1280]{1,0:T(8,128)(2,1)S(1)}, bf16[512,1536]{1,0:T(8,128)(2,1)S(1)}, bf16[512,1536]{1,0:T(8,128)(2,1)S(1)}, f32[8,128]{1,0:T(8,128)S(1)}) custom-call(s32[2]{0:T(128)S(1)} %add_convert_fusion.4.place_ref, bf16[256,1536]{1,0:T(8,128)(2,1)S(1)} %add_convert_fusion.2.m0_ref, ...), custom_call_target="tpu_custom_call" | custom-call | flops 149999992832 | bytes 20000000 | tf_op jit(solution)/shard_map/attend_back/pallas_call | solution.py:237
  316.1 2.2 fusion.5
  319.3 9.1 %attend_grads.1 = (bf16[1536,1664]{1,0:T(8,128)(2,1)}, f32[8,1536]{1,0:T(8,128)S(1)}) custom-call(s32[2]{0:T(128)S(1)} %add_convert_fusion.4.place_ref, bf16[1024,1536]{1,0:T(8,128)(2,1)S(1)} %copy-done.23, bf16[1024,1536]{1,0:T(8,128)(2,1)S(1)} %get-tuple-element.118.m_ref, bf16[1024,1280]{1,0:T(8,128)(2,1)S(1)} %get-tuple-element.120.grad_ref, ...), custom_call_target="tpu_custom_call" | custom-call | flops 5234491392 | bytes 20000000 | tf_op jit(solution)/shard_map/attend_grads/pallas_call | solution.py:444
  328.6 1.5 fusion.4
  330.5 10.7 %collective-permute-done.30 = f32[32,128]{1,0:T(8,128)S(1)} collective-permute-done((f32[32,128]{1,0:T(8,128)S(1)}, f32[32,128]{1,0:T(8,128)S(1)}, u32[]{:S(2)}, u32[]{:S(2)}) %collective-permute-start.30) | collective-permute-done | bytes 16416 | tf_op jit(solution)/shard_map/ppermute | solution.py:564
  341.3 4.7 collective-permute-start.31
  345.9 1.7 collective-permute-done.31
  347.7 6.8 %reduce-scatter.3.cloned.1.call-done = bf16[384,3072]{1,0:T(8,128)(2,1)} async-done(((bf16[1536,3072]{1,0:T(8,128)(2,1)}), bf16[384,3072]{1,0:T(8,128)(2,1)}) %reduce-scatter.3.cloned.1.call-update) | async-done | bytes 2359312 | tf_op jit(solution)/shard_map/reduce_scatter | solution.py:528
  355.1 2.9 collective-permute-done.34
  358.0 1.4 collective-permute-start.35
  359.6 1.6 collective-permute-start.33
  361.8 1.3 collective-permute-start.36
  363.1 2.4 collective-permute-done.36
  366.6 3.6 collective-permute-start.39
  370.2 1.6 collective-permute-start.37
  371.8 18.5 %collective-permute-done.33 = bf16[256,1536]{1,0:T(8,128)(2,1)S(1)} collective-permute-done((bf16[256,1536]{1,0:T(8,128)(2,1)S(1)}, bf16[256,1536]{1,0:T(8,128)(2,1)S(1)}, u32[]{:S(2)}, u32[]{:S(2)}) %collective-permute-start.33) | collective-permute-done | bytes 786464 | tf_op jit(solution)/shard_map/ppermute | solution.py:557
  391.8 32.1 %collective-permute-done.37.a_ref = bf16[192,3072]{1,0:T(8,128)(2,1)S(1)} collective-permute-done((bf16[192,3072]{1,0:T(8,128)(2,1)S(1)}, bf16[192,3072]{1,0:T(8,128)(2,1)S(1)}, u32[]{:S(2)}, u32[]{:S(2)}) %collective-permute-start.37) | collective-permute-done | bytes 1179680 | tf_op jit(solution)/shard_map/ppermute | solution.py:536
  423.9 1.6 finish.2
  426.5 1.7 collective-permute-start.40
  428.2 1.4 fusion.8
  430.3 2.5 collective-permute-start.43
  432.9 1.3 collective-permute-start.41
  435.3 2.6 select_add_fusion
  437.9 29.9 %collective-permute-done.41.a_ref = bf16[192,1664]{1,0:T(8,128)(2,1)S(1)} collective-permute-done((bf16[192,1664]{1,0:T(8,128)(2,1)S(1)}, bf16[192,1664]{1,0:T(8,128)(2,1)S(1)}, u32[]{:S(2)}, u32[]{:S(2)}) %collective-permute-start.41) | collective-permute-done | bytes 639008 | tf_op jit(solution)/shard_map/ppermute | solution.py:536
  467.8 1.1 finish.3
  (223 shorter events, 29.2 us)
Async XLA Ops:
  7.2 142.1 %all-gather.3.cloned.1.call-start = ((), (), s32[]{:S(2)}) async-start(), calls=%async_computation.2 | async-start | bytes 6389760 | tf_op jit(solution)/shard_map/all_gather | solution.py:524
  12.0 19.5 %collective-permute-start = (bf16[192,1664]{1,0:T(8,128)(2,1)S(1)}, bf16[192,1664]{1,0:T(8,128)(2,1)S(1)}, u32[]{:S(2)}, u32[]{:S(2)}) collective-permute-start(bf16[192,1664]{1,0:T(8,128)(2,1)S(1)} %pack.3), channel_id=1, source_target_pairs={{0,6},{1,7},{2,4},{3,5},{8,14},{9,15},{10,12},{11,13},{16,22},{17,... | collective-permute-start | bytes 1916936 | tf_op jit(solution)/shard_map/ppermute | solution.py:517
  17.4 14.1 %collective-permute-start.1 = (bf16[192,1664]{1,0:T(8,128)(2,1)S(1)}, bf16[192,1664]{1,0:T(8,128)(2,1)S(1)}, u32[]{:S(2)}, u32[]{:S(2)}) collective-permute-start(bf16[192,1664]{1,0:T(8,128)(2,1)S(1)} %pack.3), channel_id=1, source_target_pairs={{4,6},{5,7},{6,4},{7,5},{12,14},{13,15},{14,12},{15,13},{20,22},{2... | collective-permute-start | bytes 1916936 | tf_op jit(solution)/shard_map/ppermute | solution.py:518
  18.1 13.4 %collective-permute-start.2 = (bf16[192,1664]{1,0:T(8,128)(2,1)S(1)}, bf16[192,1664]{1,0:T(8,128)(2,1)}, u32[]{:S(2)}, u32[]{:S(2)}) collective-permute-start(bf16[192,1664]{1,0:T(8,128)(2,1)S(1)} %pack.3), channel_id=1, source_target_pairs={{4,0},{5,1},{6,2},{7,3},{12,8},{13,9},{14,10},{15,11},{20,16},{21,... | collective-permute-start | bytes 1916936 | tf_op jit(solution)/shard_map/ppermute | solution.py:519
  34.1 176.6 %all-gather.5.cloned.1.call-start = ((), (), s32[]{:S(2)}) async-start(), calls=%async_computation.3 | async-start | bytes 11796480 | tf_op jit(solution)/shard_map/all_gather | solution.py:524
  35.3 41.1 %collective-permute-start.3 = (bf16[192,3072]{1,0:T(8,128)(2,1)S(1)}, bf16[192,3072]{1,0:T(8,128)(2,1)S(1)}, u32[]{:S(2)}, u32[]{:S(2)}) collective-permute-start(bf16[192,3072]{1,0:T(8,128)(2,1)S(1)} %pack.2), channel_id=1, source_target_pairs={{0,6},{1,7},{2,4},{3,5},{8,14},{9,15},{10,12},{11,13},{16,22},{17,... | collective-permute-start | bytes 3538952 | tf_op jit(solution)/shard_map/ppermute | solution.py:517
  51.3 25.1 %collective-permute-start.4 = (bf16[192,3072]{1,0:T(8,128)(2,1)S(1)}, bf16[192,3072]{1,0:T(8,128)(2,1)S(1)}, u32[]{:S(2)}, u32[]{:S(2)}) collective-permute-start(bf16[192,3072]{1,0:T(8,128)(2,1)S(1)} %pack.2), channel_id=1, source_target_pairs={{4,6},{5,7},{6,4},{7,5},{12,14},{13,15},{14,12},{15,13},{20,22},{2... | collective-permute-start | bytes 3538952 | tf_op jit(solution)/shard_map/ppermute | solution.py:518
  52.0 24.4 %collective-permute-start.5 = (bf16[192,3072]{1,0:T(8,128)(2,1)S(1)}, bf16[192,3072]{1,0:T(8,128)(2,1)S(1)}, u32[]{:S(2)}, u32[]{:S(2)}) collective-permute-start(bf16[192,3072]{1,0:T(8,128)(2,1)S(1)} %pack.2), channel_id=1, source_target_pairs={{4,0},{5,1},{6,2},{7,3},{12,8},{13,9},{14,10},{15,11},{20,16},{21,... | collective-permute-start | bytes 3538952 | tf_op jit(solution)/shard_map/ppermute | solution.py:519
  78.4 276.1 %reduce-scatter.3.cloned.1.call-start = ((), (), s32[]{:S(2)}) async-start(), calls=%async_computation.4 | async-start | bytes 11796480 | tf_op jit(solution)/shard_map/reduce_scatter | solution.py:528
  79.8 0.7 collective-permute-start.6
  80.9 28.6 %copy-start.32 = (f32[256,1536]{1,0:T(8,128)}, f32[256,1536]{1,0:T(8,128)S(1)}, u32[]{:S(2)}) copy-start(f32[256,1536]{1,0:T(8,128)S(1)} %get-tuple-element.163) | copy-start | bytes 4718596
  80.9 28.5 %copy-start.42 = (f32[256,1536]{1,0:T(8,128)S(1)}, f32[256,1536]{1,0:T(8,128)}, u32[]{:S(2)}) copy-start(f32[256,1536]{1,0:T(8,128)} %param.27) | copy-start | bytes 4718596
  80.9 28.6 %copy-start.58 = (f32[256]{0:T(256)}, f32[256]{0:T(256)S(1)}, u32[]{:S(2)}) copy-start(f32[256]{0:T(256)S(1)} %add_rsqrt_fusion.1) | copy-start | bytes 3076
  81.5 29.8 %copy-start.63 = (f32[24]{0:T(128)S(1)}, f32[24]{0:T(128)}, u32[]{:S(2)}) copy-start(f32[24]{0:T(128)} %param.21) | copy-start | bytes 292
  81.5 29.9 %copy-start.62 = (s32[1024]{0:T(1024)S(1)}, s32[1024]{0:T(1024)}, u32[]{:S(2)}) copy-start(s32[1024]{0:T(1024)} %param.15) | copy-start | bytes 12292
  81.5 54.4 %collective-permute-start.7 = (bf16[256,1536]{1,0:T(8,128)(2,1)S(1)}, bf16[256,1536]{1,0:T(8,128)(2,1)S(1)}, u32[]{:S(2)}, u32[]{:S(2)}) collective-permute-start(bf16[256,1536]{1,0:T(8,128)(2,1)S(1)} %multiply_convert_fusion.1.x0_ref), channel_id=1, source_target_pairs={{0,1},{1,0},{2,3},{3,2},{4,5},{5,4},{6,7},{7,6},{8,9},{9,8},{10,11... | collective-permute-start | bytes 2359304 | tf_op jit(solution)/shard_map/ppermute | solution.py:544
  109.5 37.1 %copy-start.47 = (bf16[256,1536]{1,0:T(8,128)(2,1)}, bf16[256,1536]{1,0:T(8,128)(2,1)S(1)}, u32[]{:S(2)}) copy-start(bf16[256,1536]{1,0:T(8,128)(2,1)S(1)} %convert_element_type.140) | copy-start | bytes 2359300
  109.5 37.1 %collective-permute-start.10 = (bf16[256,1536]{1,0:T(8,128)(2,1)S(1)}, bf16[256,1536]{1,0:T(8,128)(2,1)}, u32[]{:S(2)}, u32[]{:S(2)}) collective-permute-start(bf16[256,1536]{1,0:T(8,128)(2,1)S(1)} %convert_element_type.140), channel_id=1, source_target_pairs={{2,4},{3,5},{4,2},{5,3},{10,12},{11,13},{12,10},{13,11},{18,20},{1... | collective-permute-start | bytes 2359304 | tf_op jit(solution)/shard_map/ppermute | solution.py:609
  111.4 35.2 %collective-permute-start.11 = (s32[1024]{0:T(1024)S(1)}, s32[1024]{0:T(1024)S(1)}, u32[]{:S(2)}, u32[]{:S(2)}) collective-permute-start(s32[1024]{0:T(1024)S(1)} %copy-done.62), channel_id=1, source_target_pairs={{0,4},{4,0},{8,12},{12,8},{16,20},{20,16},{24,28},{28,24},{1,5},{5... | collective-permute-start | bytes 12296 | tf_op jit(solution)/shard_map/ppermute | solution.py:630
  135.8 13.4 %collective-permute-start.8 = (bf16[256,1536]{1,0:T(8,128)(2,1)S(1)}, bf16[256,1536]{1,0:T(8,128)(2,1)S(1)}, u32[]{:S(2)}, u32[]{:S(2)}) collective-permute-start(bf16[256,1536]{1,0:T(8,128)(2,1)S(1)} %multiply_convert_fusion.1.x0_ref), channel_id=1, source_target_pairs={{0,4},{4,0},{8,12},{12,8},{16,20},{20,16},{24,28},{28,24},{1,5},{5... | collective-permute-start | bytes 2359304 | tf_op jit(solution)/shard_map/ppermute | solution.py:543
  135.9 12.5 %collective-permute-start.9 = (bf16[256,1536]{1,0:T(8,128)(2,1)S(1)}, bf16[256,1536]{1,0:T(8,128)(2,1)S(1)}, u32[]{:S(2)}, u32[]{:S(2)}) collective-permute-start(bf16[256,1536]{1,0:T(8,128)(2,1)S(1)} %collective-permute-done.7.x1_ref), channel_id=1, source_target_pairs={{0,4},{4,0},{8,12},{12,8},{16,20},{20,16},{24,28},{28,24},{1,5},{5... | collective-permute-start | bytes 2359304 | tf_op jit(solution)/shard_map/ppermute | solution.py:545
  147.8 25.3 %collective-permute-start.12 = (bf16[256,1536]{1,0:T(8,128)(2,1)S(1)}, bf16[256,1536]{1,0:T(8,128)(2,1)}, u32[]{:S(2)}, u32[]{:S(2)}) collective-permute-start(bf16[256,1536]{1,0:T(8,128)(2,1)S(1)} %broadcast_select_fusion.refs_2_), channel_id=1, source_target_pairs={{0,1},{1,0},{2,3},{3,2},{4,5},{5,4},{6,7},{7,6},{8,9},{9,8},{10,11... | collective-permute-start | bytes 2359304 | tf_op jit(solution)/shard_map/ppermute | solution.py:641
  173.1 33.4 %copy-start.1 = (bf16[512,1536]{1,0:T(8,128)(2,1)}, bf16[512,1536]{1,0:T(8,128)(2,1)S(1)}, u32[]{:S(2)}) copy-start(bf16[512,1536]{1,0:T(8,128)(2,1)S(1)} %get-tuple-element.81) | copy-start | bytes 4718596
  173.1 33.5 %copy-start.22 = (bf16[1024,1536]{1,0:T(8,128)(2,1)}, bf16[1024,1536]{1,0:T(8,128)(2,1)S(1)}, u32[]{:S(2)}) copy-start(bf16[1024,1536]{1,0:T(8,128)(2,1)S(1)} %get-tuple-element.117.x_ref) | copy-start | bytes 9437188
  173.1 33.5 %copy-start.24 = (bf16[1024,384]{1,0:T(8,128)(2,1)}, bf16[1024,384]{1,0:T(8,128)(2,1)S(1)}, u32[]{:S(2)}) copy-start(bf16[1024,384]{1,0:T(8,128)(2,1)S(1)} %get-tuple-element.109.mixed_ref) | copy-start | bytes 2359300
  173.1 33.5 %copy-start.26 = (bf16[1024,1152]{1,0:T(8,128)(2,1)}, bf16[1024,1152]{1,0:T(8,128)(2,1)S(1)}, u32[]{:S(2)}) copy-start(bf16[1024,1152]{1,0:T(8,128)(2,1)S(1)} %get-tuple-element.108.qkv_ref) | copy-start | bytes 7077892
  173.1 32.9 %copy-start.33 = (f32[256,1536]{1,0:T(8,128)S(1)}, f32[256,1536]{1,0:T(8,128)}, u32[]{:S(2)}) copy-start(f32[256,1536]{1,0:T(8,128)} %copy-done.32) | copy-start | bytes 4718596
  173.2 12.7 %collective-permute-start.13 = (bf16[512,1536]{1,0:T(8,128)(2,1)S(1)}, bf16[512,1536]{1,0:T(8,128)(2,1)S(1)}, u32[]{:S(2)}, u32[]{:S(2)}) collective-permute-start(bf16[512,1536]{1,0:T(8,128)(2,1)S(1)} %get-tuple-element.84), channel_id=1, source_target_pairs={{0,4},{4,0},{8,12},{12,8},{16,20},{20,16},{24,28},{28,24},{1,5},{5... | collective-permute-start | bytes 4718600 | tf_op jit(solution)/shard_map/ppermute | solution.py:549
  186.1 19.9 %collective-permute-start.14 = (bf16[256,1536]{1,0:T(8,128)(2,1)S(1)}, bf16[256,1536]{1,0:T(8,128)(2,1)S(1)}, u32[]{:S(2)}, u32[]{:S(2)}) collective-permute-start(bf16[256,1536]{1,0:T(8,128)(2,1)S(1)} %add_convert_fusion.3), channel_id=1, source_target_pairs={{0,1},{1,0},{2,3},{3,2},{4,5},{5,4},{6,7},{7,6},{8,9},{9,8},{10,11... | collective-permute-start | bytes 2359304 | tf_op jit(solution)/shard_map/ppermute | solution.py:557
  187.9 21.0 %collective-permute-start.16 = (bf16[256,1536]{1,0:T(8,128)(2,1)S(1)}, bf16[256,1536]{1,0:T(8,128)(2,1)S(1)}, u32[]{:S(2)}, u32[]{:S(2)}) collective-permute-start(bf16[256,1536]{1,0:T(8,128)(2,1)S(1)} %broadcast_select_fusion.refs_2_), channel_id=1, source_target_pairs={{0,4},{4,0},{8,12},{12,8},{16,20},{20,16},{24,28},{28,24},{1,5},{5... | collective-permute-start | bytes 2359304 | tf_op jit(solution)/shard_map/ppermute | solution.py:646
  206.6 61.4 %copy-start.56 = (f32[256]{0:T(256)}, f32[256]{0:T(256)S(1)}, u32[]{:S(2)}) copy-start(f32[256]{0:T(256)S(1)} %add_rsqrt_fusion) | copy-start | bytes 3076
  206.9 2.9 collective-permute-start.15
  206.9 20.1 %collective-permute-start.17 = (bf16[256,1536]{1,0:T(8,128)(2,1)S(1)}, bf16[256,1536]{1,0:T(8,128)(2,1)}, u32[]{:S(2)}, u32[]{:S(2)}) collective-permute-start(bf16[256,1536]{1,0:T(8,128)(2,1)S(1)} %multiply_convert_fusion.refs_0_), channel_id=1, source_target_pairs={{0,1},{1,0},{2,3},{3,2},{4,5},{5,4},{6,7},{7,6},{8,9},{9,8},{10,11... | collective-permute-start | bytes 2359304 | tf_op jit(solution)/shard_map/ppermute | solution.py:652
  208.7 18.3 %collective-permute-start.19 = (bf16[256,1536]{1,0:T(8,128)(2,1)}, bf16[256,1536]{1,0:T(8,128)(2,1)}, u32[]{:S(2)}, u32[]{:S(2)}) collective-permute-start(bf16[256,1536]{1,0:T(8,128)(2,1)} %collective-permute-done.12.refs_2_), channel_id=1, source_target_pairs={{0,4},{4,0},{8,12},{12,8},{16,20},{20,16},{24,28},{28,24},{1,5},{5... | collective-permute-start | bytes 2359304 | tf_op jit(solution)/shard_map/ppermute | solution.py:647
  227.0 2.5 collective-permute-start.18
  243.0 2.4 collective-permute-start.20
  243.2 17.8 %collective-permute-start.21 = (bf16[256,1536]{1,0:T(8,128)(2,1)S(1)}, bf16[256,1536]{1,0:T(8,128)(2,1)}, u32[]{:S(2)}, u32[]{:S(2)}) collective-permute-start(bf16[256,1536]{1,0:T(8,128)(2,1)S(1)} %get-tuple-element.94), channel_id=1, source_target_pairs={{0,4},{4,0},{8,12},{12,8},{16,20},{20,16},{24,28},{28,24},{1,5},{5... | collective-permute-start | bytes 2359304 | tf_op jit(solution)/shard_map/ppermute | solution.py:662
  245.9 19.8 %collective-permute-start.22 = (bf16[256,1536]{1,0:T(8,128)(2,1)S(1)}, bf16[256,1536]{1,0:T(8,128)(2,1)}, u32[]{:S(2)}, u32[]{:S(2)}) collective-permute-start(bf16[256,1536]{1,0:T(8,128)(2,1)S(1)} %get-tuple-element.168), channel_id=1, source_target_pairs={{0,1},{1,0},{2,3},{3,2},{4,5},{5,4},{6,7},{7,6},{8,9},{9,8},{10,11... | collective-permute-start | bytes 2359304 | tf_op jit(solution)/shard_map/ppermute | solution.py:665
  260.7 167.5 %reduce-scatter.5.cloned.1.call-start = ((), (), s32[]{:S(2)}) async-start(), calls=%async_computation.5 | async-start | bytes 6389760 | tf_op jit(solution)/shard_map/reduce_scatter | solution.py:528
  270.2 18.6 %collective-permute-start.26 = (bf16[256,1536]{1,0:T(8,128)(2,1)S(1)}, bf16[256,1536]{1,0:T(8,128)(2,1)S(1)}, u32[]{:S(2)}, u32[]{:S(2)}) collective-permute-start(bf16[256,1536]{1,0:T(8,128)(2,1)S(1)} %add_convert_fusion.2.m0_ref), channel_id=1, source_target_pairs={{0,1},{1,0},{2,3},{3,2},{4,5},{5,4},{6,7},{7,6},{8,9},{9,8},{10,11... | collective-permute-start | bytes 2359304 | tf_op jit(solution)/shard_map/ppermute | solution.py:544
  279.5 10.3 %collective-permute-start.24 = (bf16[256,1536]{1,0:T(8,128)(2,1)S(1)}, bf16[256,1536]{1,0:T(8,128)(2,1)S(1)}, u32[]{:S(2)}, u32[]{:S(2)}) collective-permute-start(bf16[256,1536]{1,0:T(8,128)(2,1)S(1)} %get-tuple-element.106), channel_id=1, source_target_pairs={{0,4},{4,0},{8,12},{12,8},{16,20},{20,16},{24,28},{28,24},{1,5},{5... | collective-permute-start | bytes 2359304 | tf_op jit(solution)/shard_map/ppermute | solution.py:681
  279.6 13.1 %collective-permute-start.27 = (bf16[256,1536]{1,0:T(8,128)(2,1)S(1)}, bf16[256,1536]{1,0:T(8,128)(2,1)S(1)}, u32[]{:S(2)}, u32[]{:S(2)}) collective-permute-start(bf16[256,1536]{1,0:T(8,128)(2,1)S(1)} %add_convert_fusion.2.m0_ref), channel_id=1, source_target_pairs={{0,4},{4,0},{8,12},{12,8},{16,20},{20,16},{24,28},{28,24},{1,5},{5... | collective-permute-start | bytes 2359304 | tf_op jit(solution)/shard_map/ppermute | solution.py:543
  280.1 36.0 %collective-permute-start.23 = (bf16[256,1536]{1,0:T(8,128)(2,1)}, bf16[256,1536]{1,0:T(8,128)(2,1)}, u32[]{:S(2)}, u32[]{:S(2)}) collective-permute-start(bf16[256,1536]{1,0:T(8,128)(2,1)} %get-tuple-element.104), channel_id=1, source_target_pairs={{0,4},{4,0},{8,12},{12,8},{16,20},{20,16},{24,28},{28,24},{1,5},{5... | collective-permute-start | bytes 2359304 | tf_op jit(solution)/shard_map/ppermute | solution.py:683
  288.8 3.9 collective-permute-start.28
  290.9 25.1 %collective-permute-start.25 = (bf16[256,1536]{1,0:T(8,128)(2,1)}, bf16[256,1536]{1,0:T(8,128)(2,1)}, u32[]{:S(2)}, u32[]{:S(2)}) collective-permute-start(bf16[256,1536]{1,0:T(8,128)(2,1)} %add_convert_fusion.1), channel_id=1, source_target_pairs={{0,1},{1,0},{2,3},{3,2},{4,5},{5,4},{6,7},{7,6},{8,9},{9,8},{10,11... | collective-permute-start | bytes 2359304 | tf_op jit(solution)/shard_map/ppermute | solution.py:700
  292.7 23.3 %copy-start.2 = (bf16[512,1536]{1,0:T(8,128)(2,1)S(1)}, bf16[512,1536]{1,0:T(8,128)(2,1)}, u32[]{:S(2)}) copy-start(bf16[512,1536]{1,0:T(8,128)(2,1)} %copy-done.1) | copy-start | bytes 4718596
  292.7 23.3 %copy-start.46 = (bf16[512,1536]{1,0:T(8,128)(2,1)S(1)}, bf16[512,1536]{1,0:T(8,128)(2,1)}, u32[]{:S(2)}) copy-start(bf16[512,1536]{1,0:T(8,128)(2,1)} %copy-done.45) | copy-start | bytes 4718596
  318.3 10.3 %collective-permute-start.29 = (bf16[256,1536]{1,0:T(8,128)(2,1)S(1)}, bf16[256,1536]{1,0:T(8,128)(2,1)S(1)}, u32[]{:S(2)}, u32[]{:S(2)}) collective-permute-start(bf16[256,1536]{1,0:T(8,128)(2,1)S(1)} %get-tuple-element.158), channel_id=1, source_target_pairs={{2,4},{3,5},{4,2},{5,3},{10,12},{11,13},{12,10},{13,11},{18,20},{1... | collective-permute-start | bytes 2359304 | tf_op jit(solution)/shard_map/ppermute | solution.py:612
  330.2 11.1 %collective-permute-start.30 = (f32[32,128]{1,0:T(8,128)S(1)}, f32[32,128]{1,0:T(8,128)S(1)}, u32[]{:S(2)}, u32[]{:S(2)}) collective-permute-start(f32[32,128]{1,0:T(8,128)S(1)} %fusion.3), channel_id=1, source_target_pairs={{0,1},{1,0},{2,3},{3,2},{4,5},{5,4},{6,7},{7,6},{8,9},{9,8},{10,11... | collective-permute-start | bytes 49160 | tf_op jit(solution)/shard_map/ppermute | solution.py:564
  341.3 6.4 %collective-permute-start.31 = (f32[32,128]{1,0:T(8,128)S(1)}, f32[32,128]{1,0:T(8,128)S(1)}, u32[]{:S(2)}, u32[]{:S(2)}) collective-permute-start(f32[32,128]{1,0:T(8,128)S(1)} %add.127), channel_id=1, source_target_pairs={{0,2},{1,3},{2,0},{3,1},{4,6},{5,7},{6,4},{7,5},{8,10},{9,11},{10,... | collective-permute-start | bytes 49160 | tf_op jit(solution)/shard_map/ppermute | solution.py:564
  354.5 4.9 %collective-permute-start.32 = (bf16[512,1536]{1,0:T(8,128)(2,1)S(1)}, bf16[512,1536]{1,0:T(8,128)(2,1)S(1)}, u32[]{:S(2)}, u32[]{:S(2)}) collective-permute-start(bf16[512,1536]{1,0:T(8,128)(2,1)S(1)} %get-tuple-element.124.send_ref), channel_id=1, source_target_pairs={{0,4},{4,0},{8,12},{12,8},{16,20},{20,16},{24,28},{28,24},{1,5},{5... | collective-permute-start | bytes 4718600 | tf_op jit(solution)/shard_map/ppermute | solution.py:549
  354.6 3.4 collective-permute-start.34
  358.0 3.7 collective-permute-start.35
  359.6 30.7 %collective-permute-start.33 = (bf16[256,1536]{1,0:T(8,128)(2,1)S(1)}, bf16[256,1536]{1,0:T(8,128)(2,1)S(1)}, u32[]{:S(2)}, u32[]{:S(2)}) collective-permute-start(bf16[256,1536]{1,0:T(8,128)(2,1)S(1)} %add_convert_fusion), channel_id=1, source_target_pairs={{0,1},{1,0},{2,3},{3,2},{4,5},{5,4},{6,7},{7,6},{8,9},{9,8},{10,11... | collective-permute-start | bytes 2359304 | tf_op jit(solution)/shard_map/ppermute | solution.py:557
  361.8 3.7 collective-permute-start.36
  365.5 24.8 %copy-start.34 = (f32[256,1536]{1,0:T(8,128)S(1)}, f32[256,1536]{1,0:T(8,128)}, u32[]{:S(2)}) copy-start(f32[256,1536]{1,0:T(8,128)} %copy-done.32) | copy-start | bytes 4718596
  365.5 24.8 %copy-start.59 = (f32[256]{0:T(256)S(1)}, f32[256]{0:T(256)}, u32[]{:S(2)}) copy-start(f32[256]{0:T(256)} %copy-done.58) | copy-start | bytes 3076
  365.7 58.3 %collective-permute-start.38 = (bf16[192,3072]{1,0:T(8,128)(2,1)S(1)}, bf16[192,3072]{1,0:T(8,128)(2,1)S(1)}, u32[]{:S(2)}, u32[]{:S(2)}) collective-permute-start(bf16[192,3072]{1,0:T(8,128)(2,1)S(1)} %get-tuple-element.164.high_ref), channel_id=1, source_target_pairs={{4,6},{5,7},{6,4},{7,5},{12,14},{13,15},{14,12},{15,13},{20,22},{2... | collective-permute-start | bytes 3538952 | tf_op jit(solution)/shard_map/ppermute | solution.py:537
  366.6 57.4 %collective-permute-start.39 = (bf16[192,3072]{1,0:T(8,128)(2,1)S(1)}, bf16[192,3072]{1,0:T(8,128)(2,1)S(1)}, u32[]{:S(2)}, u32[]{:S(2)}) collective-permute-start(bf16[192,3072]{1,0:T(8,128)(2,1)S(1)} %get-tuple-element.164.high_ref), channel_id=1, source_target_pairs={{0,4},{1,5},{2,6},{3,7},{8,12},{9,13},{10,14},{11,15},{16,20},{17,... | collective-permute-start | bytes 3538952 | tf_op jit(solution)/shard_map/ppermute | solution.py:538
  370.2 53.7 %collective-permute-start.37 = (bf16[192,3072]{1,0:T(8,128)(2,1)S(1)}, bf16[192,3072]{1,0:T(8,128)(2,1)S(1)}, u32[]{:S(2)}, u32[]{:S(2)}) collective-permute-start(bf16[192,3072]{1,0:T(8,128)(2,1)S(1)} %get-tuple-element.165.low_ref), channel_id=1, source_target_pairs={{6,0},{7,1},{4,2},{5,3},{14,8},{15,9},{12,10},{13,11},{22,16},{23,... | collective-permute-start | bytes 3538952 | tf_op jit(solution)/shard_map/ppermute | solution.py:536
  426.5 8.7 %collective-permute-start.40 = (bf16[256,1536]{1,0:T(8,128)(2,1)}, bf16[256,1536]{1,0:T(8,128)(2,1)}, u32[]{:S(2)}, u32[]{:S(2)}) collective-permute-start(bf16[256,1536]{1,0:T(8,128)(2,1)} %convert_element_type.177), channel_id=1, source_target_pairs={{2,4},{3,5},{4,2},{5,3},{10,12},{11,13},{12,10},{13,11},{18,20},{1... | collective-permute-start | bytes 2359304 | tf_op jit(solution)/shard_map/ppermute | solution.py:612
  429.6 38.2 %collective-permute-start.42 = (bf16[192,1664]{1,0:T(8,128)(2,1)S(1)}, bf16[192,1664]{1,0:T(8,128)(2,1)S(1)}, u32[]{:S(2)}, u32[]{:S(2)}) collective-permute-start(bf16[192,1664]{1,0:T(8,128)(2,1)S(1)} %get-tuple-element.166.high_ref), channel_id=1, source_target_pairs={{4,6},{5,7},{6,4},{7,5},{12,14},{13,15},{14,12},{15,13},{20,22},{2... | collective-permute-start | bytes 1916936 | tf_op jit(solution)/shard_map/ppermute | solution.py:537
  430.3 37.5 %collective-permute-start.43 = (bf16[192,1664]{1,0:T(8,128)(2,1)S(1)}, bf16[192,1664]{1,0:T(8,128)(2,1)S(1)}, u32[]{:S(2)}, u32[]{:S(2)}) collective-permute-start(bf16[192,1664]{1,0:T(8,128)(2,1)S(1)} %get-tuple-element.166.high_ref), channel_id=1, source_target_pairs={{0,4},{1,5},{2,6},{3,7},{8,12},{9,13},{10,14},{11,15},{16,20},{17,... | collective-permute-start | bytes 1916936 | tf_op jit(solution)/shard_map/ppermute | solution.py:538
  432.9 35.0 %collective-permute-start.41 = (bf16[192,1664]{1,0:T(8,128)(2,1)S(1)}, bf16[192,1664]{1,0:T(8,128)(2,1)S(1)}, u32[]{:S(2)}, u32[]{:S(2)}) collective-permute-start(bf16[192,1664]{1,0:T(8,128)(2,1)S(1)} %get-tuple-element.167.low_ref), channel_id=1, source_target_pairs={{6,0},{7,1},{4,2},{5,3},{14,8},{15,9},{12,10},{13,11},{22,16},{23,... | collective-permute-start | bytes 1916936 | tf_op jit(solution)/shard_map/ppermute | solution.py:536
  (48 other events, 340.5 us)
Sparse Core Ops, SparseCore 0:
  34.2 76.0 all-gather.2
  112.1 96.3 all-gather.4
  260.8 93.5 reduce-scatter.2
  357.4 60.3 reduce-scatter.4

commit v5 on v4

--- a/solution.py
+++ b/solution.py
@@ -20,7 +20,8 @@
     return lax.dot_general(a, b, dn, preferred_element_type=F32)
 
 
-VMEM_LIMIT = 38 * 1024 * 1024
+MIB = 1024 * 1024
+VMEM_LIMIT = 60 * MIB
 
 
 def split3(x):
@@ -142,7 +143,7 @@
             pltpu.VMEM((128, length), F32),
             pltpu.VMEM((length, width), BF),
         ],
-        compiler_params=pltpu.CompilerParams(vmem_limit_bytes=VMEM_LIMIT),
+        compiler_params=pltpu.CompilerParams(vmem_limit_bytes=38 * MIB),
         cost_estimate=pl.CostEstimate(
             flops=12 * 10**9, bytes_accessed=2 * 10**7, transcendentals=5 * 10**6
         ),
@@ -251,7 +252,7 @@
             pltpu.VMEM((8, length), F32),
             pltpu.VMEM((length, 3 * width + 128), BF),
         ],
-        compiler_params=pltpu.CompilerParams(vmem_limit_bytes=VMEM_LIMIT),
+        compiler_params=pltpu.CompilerParams(vmem_limit_bytes=38 * MIB),
         cost_estimate=pl.CostEstimate(
             flops=150 * 10**9, bytes_accessed=2 * 10**7, transcendentals=5 * 10**6
         ),
@@ -325,7 +326,7 @@
         + [jax.ShapeDtypeStruct((length, features), BF)] * 2
         + [jax.ShapeDtypeStruct((rows, features), BF)] * 2,
         scratch_shapes=[pltpu.VMEM((length, features), F32)],
-        compiler_params=pltpu.CompilerParams(vmem_limit_bytes=VMEM_LIMIT),
+        compiler_params=pltpu.CompilerParams(vmem_limit_bytes=38 * MIB),
         cost_estimate=pl.CostEstimate(
             flops=8 * 10**9, bytes_accessed=18 * 10**6, transcendentals=10**6
         ),
@@ -363,7 +364,7 @@
         in_specs=[whole] * 4 + [back] * 2 + [hidden] * 2,
         out_specs=pl.BlockSpec((features, columns), lambda i: (0, i)),
         out_shape=jax.ShapeDtypeStruct((features, 3 * width), BF),
-        compiler_params=pltpu.CompilerParams(vmem_limit_bytes=VMEM_LIMIT),
+        compiler_params=pltpu.CompilerParams(vmem_limit_bytes=38 * MIB),
         cost_estimate=pl.CostEstimate(
             flops=12 * length * features * width,
             bytes_accessed=25 * 10**6,
@@ -393,25 +394,32 @@
         in_specs=[hidden, hidden, pl.BlockSpec((features, width), lambda i: (0, 2))],
         out_specs=[part] * 4,
         out_shape=[jax.ShapeDtypeStruct((length // 2, features), BF)] * 4,
-        compiler_params=pltpu.CompilerParams(vmem_limit_bytes=VMEM_LIMIT),
+        compiler_params=pltpu.CompilerParams(vmem_limit_bytes=38 * MIB),
         cost_estimate=pl.CostEstimate(
             flops=4 * length * features * width, bytes_accessed=8 * 10**6, transcendentals=0
         ),
         name="down_product",
     )(*hiddens, w)
+
+
+def unit(rows, columns):
+    i = lax.broadcasted_iota(jnp.int32, (rows, columns), 0)
+    j = lax.broadcasted_iota(jnp.int32, (rows, columns), 1)
+    return (i == j).astype(BF)
 
 
 def pack_kernel(places, *refs):
     ins, out_ref = refs[:-1], refs[-1]
     for begin, ref in zip(places, ins):
-        width = ref.shape[1]
-        if width % 128:
-            out_ref[:, begin : begin + 128] = jnp.zeros((out_ref.shape[0], 128), BF)
-        out_ref[:, begin : begin + width] = ref[...].astype(BF)
+        if ref.shape[0] == out_ref.shape[0]:
+            out_ref[:, begin : begin + ref.shape[1]] = ref[...].astype(BF)
+        else:
+            turned = dotf(ref[...].astype(BF), unit(ref.shape[0], 128), TN)
+            out_ref[:, begin : begin + 128] = turned.astype(BF)
 
 
 def pack(parts, places, columns):
-    rows = parts[0].shape[0]
+    rows = parts[-1].shape[0]
     return pl.pallas_call(
         functools.partial(pack_kernel, places),
         out_shape=jax.ShapeDtypeStruct((rows, columns), BF),
@@ -448,7 +456,7 @@
             jax.ShapeDtypeStruct((features, columns), BF),
             jax.ShapeDtypeStruct((8, features), F32),
         ),
-        compiler_params=pltpu.CompilerParams(vmem_limit_bytes=VMEM_LIMIT),
+        compiler_params=pltpu.CompilerParams(vmem_limit_bytes=38 * MIB),
         cost_estimate=pl.CostEstimate(
             flops=2 * length * features * columns, bytes_accessed=2 * 10**7, transcendentals=0
         ),
@@ -462,8 +470,15 @@
     def put(first_ref, second_ref):
         begin = 0
         for width, out_ref in zip(widths, out_refs):
-            first = first_ref[:, begin : begin + width].astype(F32)
-            out_ref[...] = first + second_ref[:, begin : begin + width].astype(F32)
+            if width > 0:
+                first = first_ref[:, begin : begin + width].astype(F32)
+                out_ref[...] = first + second_ref[:, begin : begin + width].astype(F32)
+            else:
+                width = 128
+                pick = unit(out_ref.shape[0], 128)
+                out_ref[...] = dotf(pick, first_ref[:, begin : begin + 128], NT) + dotf(
+                    pick, second_ref[:, begin : begin + 128], NT
+                )
             begin += width
 
     @pl.when(odd)
@@ -480,8 +495,11 @@
     return pl.pallas_call(
         functools.partial(finish_kernel, widths),
         in_specs=in_memory(1, 5),
-        out_shape=[jax.ShapeDtypeStruct((rows, width), F32) for width in widths],
-        compiler_params=pltpu.CompilerParams(vmem_limit_bytes=VMEM_LIMIT),
+        out_shape=[
+            jax.ShapeDtypeStruct((rows, width) if width > 0 else (-width, rows), F32)
+            for width in widths
+        ],
+        compiler_params=pltpu.CompilerParams(vmem_limit_bytes=38 * MIB),
         cost_estimate=pl.CostEstimate(flops=10**6, bytes_accessed=8 * 10**6, transcendentals=0),
         name="finish",
     )(odd, low, high, a, b, c)
@@ -613,7 +631,7 @@
         return jnp.where(away, low.astype(F32), x)
 
     w_attn_local = pack(
-        [query_weight, key_weight, value_weight, forget_weight, output_weight],
+        [query_weight, key_weight, value_weight, forget_weight.T, output_weight],
         [0, width, 2 * width, 3 * width, 3 * width + 128],
         4 * width + 128,
     )
@@ -709,23 +727,23 @@
     packed = cat(attn_gain_part[0] / attn_gain, feed_gain_part, bias_full)
     size = packed.shape[0]
     packed = jnp.pad(packed, (0, -size % 1024)).reshape(-1, 128)
-    packed = sum_all(after(packed, down_back), "tensor")
-    attn_scattered = scatter_rows(lay, after(attn_grads, feed_scattered, packed))
-    small = sum_all(after(packed, attn_grads), "dp").reshape(-1)
+    small = sum_all(sum_all(packed, "dp"), "tensor")
+    attn_scattered = scatter_rows(lay, after(attn_grads, feed_scattered, small, down_back))
     gate_shard, up_shard, down_shard = share_grad(
         lay, after(feed_scattered, small), odd, [hidden_width] * 3
     )
-    mine, other = scatter_core(lay, keep, after(send, packed))
+    mine, other = scatter_core(lay, keep, after(send, small))
     attn_normed_grad = scatter_z(lay, mine, other)
     input_part = norm_back(layer, attn_gain, attn_normed_grad)
     input_back = moved_back(after(middle_part + input_part, gate_shard))
     input_grad = output_cotangent + input_back
 
+    small = small.reshape(-1)
     query_shard, key_shard, value_shard, forget_shard, output_shard = share_grad(
         lay,
         after(attn_scattered, small, gate_shard),
         odd,
-        [width, width, width, 128, width],
+        [width, width, width, -heads, width],
     )
     return (
         layer_output,
@@ -734,7 +752,7 @@
         query_shard,
         key_shard,
         value_shard,
-        forget_shard[:, :heads],
+        forget_shard.T,
         small[2 * features : size],
         output_shard,
         small[features : 2 * features],

time: 481 us -> 477 us (level)
  local copies, waits for them, and re-layouts: 24.3 us -> 18.2 us
  Pallas kernels: 98.6 us -> 104 us
    ppermute x2, waiting for transfers between devices: 36.5 us -> 43.9 us  [scatter_z(): return mine + lax.ppermute(other, 'tensor', lay.pair).astype(F32)]
    reduce_scatter x2, waiting for transfers between devices: 6.81 us -> 0.01 us  [scatter_rows(): lax.psum_scatter(g, 'dp', scatter_dimension=0, tiled=True, axis_index_gro...]
    ppermute x2, waiting for transfers between devices: 62.1 us -> 55.7 us  [share_grad(): a = lax.ppermute(low, BOTH, lay.back_even_far)]
    unnamed x130 -> x114, local copies, waits for them, and re-layouts: 21.5 us -> 15.4 us
    pallas_call x2, Pallas kernels: 0.19 us -> 5.01 us  [pack(): pl.pallas_call(functools.partial(pack_kernel, places), out_shape=jax.Shap...]
where the time goes in v5:
time: 477 us; the launch traced here: 473 us
  waiting for transfers between devices  182 us (38%)
  starting transfers between devices  132 us (28%)
  Pallas kernels  104 us (22%)
  other arithmetic  22.9 us (5%)
  local copies, waits for them, and re-layouts  18.2 us (4%)
  between operations  15.2 us (3%)
    ppermute x2, waiting for transfers between devices, share_grad(): a = lax.ppermute(low, BOTH, lay.back_even_far)  55.7 us
    ppermute x2, waiting for transfers between devices, scatter_z(): return mine + lax.ppermute(other, 'tensor', lay.pair).astype(F32)  43.9 us
    ppermute x2, waiting for transfers between devices, swap_weight(): a = lax.ppermute(w, BOTH, lay.even_far)  35.9 us
    ppermute x2, starting transfers between devices, gather_pair(): z = lax.ppermute(x, 'tensor', lay.pair)  29.6 us
    pallas_call x2, Pallas kernels, feed(): pl.pallas_call(feed_kernel, grid=(steps,), in_specs=[part] * 4 + [tall(0)...  25.7 us
    ppermute x1, starting transfers between devices, per_device(): lax.ppermute(after(segment_ids, attn_rows), 'dp', lay.core)  24.4 us
    pallas_call x1, Pallas kernels, attend_back(): pl.pallas_call(functools.partial(attend_back_kernel, heads, 256), in_spec...  23.2 us
    ppermute x2, starting transfers between devices, swap_weight(): a = lax.ppermute(w, BOTH, lay.even_far)  21.4 us
  transfers between devices with their start and end apart: 48, of which 19 were waited for; matrix products, arithmetic and copies ran while one was open for 5% of the time, Pallas kernels for 18%

profile of v5, /device:TPU:0, one launch (start us, length us, event | category | flops | bytes accessed | tf_op | source)
XLA Modules:
  0.0 473.5 jit_solution(16217582304854242456)
XLA Ops:
  7.2 2.3 pack.3
  9.5 5.4 %collective-permute-start = (bf16[192,1664]{1,0:T(8,128)(2,1)}, bf16[192,1664]{1,0:T(8,128)(2,1)S(1)}, u32[]{:S(2)}, u32[]{:S(2)}) collective-permute-start(bf16[192,1664]{1,0:T(8,128)(2,1)} %pack.3), channel_id=1, source_target_pairs={{0,6},{1,7},{2,4},{3,5},{8,14},{9,15},{10,12},{11,13},{16,22},{17,... | collective-permute-start | bytes 1916936 | tf_op jit(solution)/shard_map/ppermute | solution.py:535
  15.6 1.3 collective-permute-start.2
  16.9 12.4 %collective-permute-done = bf16[192,1664]{1,0:T(8,128)(2,1)S(1)} collective-permute-done((bf16[192,1664]{1,0:T(8,128)(2,1)}, bf16[192,1664]{1,0:T(8,128)(2,1)S(1)}, u32[]{:S(2)}, u32[]{:S(2)}) %collective-permute-start) | collective-permute-done | bytes 639008 | tf_op jit(solution)/shard_map/ppermute | solution.py:535
  29.3 2.4 maximum_select_fusion.1
  31.8 2.7 pack.2
  34.5 16.0 %collective-permute-start.3 = (bf16[192,3072]{1,0:T(8,128)(2,1)}, bf16[192,3072]{1,0:T(8,128)(2,1)S(1)}, u32[]{:S(2)}, u32[]{:S(2)}) collective-permute-start(bf16[192,3072]{1,0:T(8,128)(2,1)} %pack.2), channel_id=1, source_target_pairs={{0,6},{1,7},{2,4},{3,5},{8,14},{9,15},{10,12},{11,13},{16,22},{17,... | collective-permute-start | bytes 3538952 | tf_op jit(solution)/shard_map/ppermute | solution.py:535
  51.3 1.3 collective-permute-start.5
  52.6 23.5 %collective-permute-done.3 = bf16[192,3072]{1,0:T(8,128)(2,1)S(1)} collective-permute-done((bf16[192,3072]{1,0:T(8,128)(2,1)}, bf16[192,3072]{1,0:T(8,128)(2,1)S(1)}, u32[]{:S(2)}, u32[]{:S(2)}) %collective-permute-start.3) | collective-permute-done | bytes 1179680 | tf_op jit(solution)/shard_map/ppermute | solution.py:535
  76.1 3.0 maximum_select_fusion
  79.2 1.3 copy-done.33
  82.2 27.7 %collective-permute-start.7 = (bf16[256,1536]{1,0:T(8,128)(2,1)S(1)}, bf16[256,1536]{1,0:T(8,128)(2,1)S(1)}, u32[]{:S(2)}, u32[]{:S(2)}) collective-permute-start(bf16[256,1536]{1,0:T(8,128)(2,1)S(1)} %multiply_convert_fusion.1.x0_ref), channel_id=1, source_target_pairs={{0,1},{1,0},{2,3},{3,2},{4,5},{5,4},{6,7},{7,6},{8,9},{9,8},{10,11... | collective-permute-start | bytes 2359304 | tf_op jit(solution)/shard_map/ppermute | solution.py:562
  110.1 1.7 collective-permute-start.10
  111.9 24.4 %collective-permute-start.11 = (s32[1024]{0:T(1024)S(1)}, s32[1024]{0:T(1024)S(1)}, u32[]{:S(2)}, u32[]{:S(2)}) collective-permute-start(s32[1024]{0:T(1024)S(1)} %copy-done.55), channel_id=1, source_target_pairs={{0,4},{4,0},{8,12},{12,8},{16,20},{20,16},{24,28},{28,24},{1,5},{5... | collective-permute-start | bytes 12296 | tf_op jit(solution)/shard_map/ppermute | solution.py:648
  136.4 10.6 %collective-permute-start.9 = (bf16[256,1536]{1,0:T(8,128)(2,1)S(1)}, bf16[256,1536]{1,0:T(8,128)(2,1)S(1)}, u32[]{:S(2)}, u32[]{:S(2)}) collective-permute-start(bf16[256,1536]{1,0:T(8,128)(2,1)S(1)} %collective-permute-done.7.x1_ref), channel_id=1, source_target_pairs={{0,4},{4,0},{8,12},{12,8},{16,20},{20,16},{24,28},{28,24},{1,5},{5... | collective-permute-start | bytes 2359304 | tf_op jit(solution)/shard_map/ppermute | solution.py:563
  147.0 1.2 broadcast_select_fusion.refs_2_
  149.7 1.1 copy-done.14
  150.9 21.1 %attend.1 = (bf16[1024,1536]{1,0:T(8,128)(2,1)S(1)}, bf16[1024,1152]{1,0:T(8,128)(2,1)S(1)}, bf16[1024,384]{1,0:T(8,128)(2,1)S(1)}, bf16[512,1536]{1,0:T(8,128)(...) custom-call(s32[2]{0:T(128)S(1)} %add_convert_fusion.4.place_ref, ...), custom_call_target="tpu_custom_call" | custom-call | flops 12000000000 | bytes 20000000 | tf_op jit(solution)/shard_map/attend/pallas_call | solution.py:128
  173.6 9.4 %collective-permute-start.13 = (bf16[512,1536]{1,0:T(8,128)(2,1)S(1)}, bf16[512,1536]{1,0:T(8,128)(2,1)S(1)}, u32[]{:S(2)}, u32[]{:S(2)}) collective-permute-start(bf16[512,1536]{1,0:T(8,128)(2,1)S(1)} %get-tuple-element.82), channel_id=1, source_target_pairs={{0,4},{4,0},{8,12},{12,8},{16,20},{20,16},{24,28},{28,24},{1,5},{5... | collective-permute-start | bytes 4718600 | tf_op jit(solution)/shard_map/ppermute | solution.py:567
  183.1 3.0 collective-permute-done.13
  186.3 1.8 collective-permute-start.14
  188.2 18.0 %collective-permute-done.14 = bf16[256,1536]{1,0:T(8,128)(2,1)S(1)} collective-permute-done((bf16[256,1536]{1,0:T(8,128)(2,1)S(1)}, bf16[256,1536]{1,0:T(8,128)(2,1)S(1)}, u32[]{:S(2)}, u32[]{:S(2)}) %collective-permute-start.14) | collective-permute-done | bytes 786464 | tf_op jit(solution)/shard_map/ppermute | solution.py:575
  207.2 1.8 collective-permute-start.17
  210.9 1.1 copy-done.6
  212.0 1.1 copy-done.8
  213.2 12.3 %feed.2 = (bf16[512,1024]{1,0:T(8,128)(2,1)S(1)}, bf16[512,2048]{1,0:T(8,128)(2,1)S(1)}, bf16[512,1536]{1,0:T(8,128)(2,1)S(1)}, bf16[512,1536]{1,0:T(8,128)(2,1)...) custom-call(bf16[256,1536]{1,0:T(8,128)(2,1)S(1)} %multiply_convert_fusion.refs_0_, ...), custom_call_target="tpu_custom_call" | custom-call | flops 8000000000 | bytes 18000000 | tf_op jit(solution)/shard_map/feed/pallas_call | solution.py:310
  225.5 1.7 collective-permute-done.17.refs_0_
  227.2 2.5 collective-permute-done.18.refs_1_
  229.7 13.4 %feed.3 = (bf16[512,1024]{1,0:T(8,128)(2,1)S(1)}, bf16[512,2048]{1,0:T(8,128)(2,1)S(1)}, bf16[512,1536]{1,0:T(8,128)(2,1)S(1)}, bf16[512,1536]{1,0:T(8,128)(2,1)...) custom-call(bf16[256,1536]{1,0:T(8,128)(2,1)} %collective-permute-done.17.refs_0_, ...), custom_call_target="tpu_custom_call" | custom-call | flops 8000000000 | bytes 18000000 | tf_op jit(solution)/shard_map/feed/pallas_call | solution.py:310
  243.8 1.8 collective-permute-done.20
  246.1 1.8 collective-permute-start.22
  247.9 13.0 %feed_grads.1 = bf16[1536,3072]{1,0:T(8,128)(2,1)} custom-call(bf16[512,1536]{1,0:T(8,128)(2,1)S(1)} %get-tuple-element.93.xa_ref, bf16[512,1536]{1,0:T(8,128)(2,1)S(1)} %get-tuple-element.94.xb_ref, bf16[512,1536]{1,0:T(8,128)(2,1)S(1)} %get-tuple-element.95.ca_ref, bf16[512,1536]{1,0:T(8,128)(2,1)S(1)} %get-tuple-element.96.cb_ref, ...), custom_call_target="tpu_custom_call" | custom-call | flops 9663676416 | bytes 25000000 | tf_op jit(solution)/shard_map/feed_grads/pallas_call | solution.py:361
  261.2 4.7 collective-permute-done.22
  265.8 2.0 convert_add_fusion.2
  270.4 1.9 collective-permute-start.26
  272.3 4.0 copy-done
  276.3 3.5 down_product.1
  280.4 8.5 %collective-permute-done.26.m1_ref = bf16[256,1536]{1,0:T(8,128)(2,1)S(1)} collective-permute-done((bf16[256,1536]{1,0:T(8,128)(2,1)S(1)}, bf16[256,1536]{1,0:T(8,128)(2,1)S(1)}, u32[]{:S(2)}, u32[]{:S(2)}) %collective-permute-start.26) | collective-permute-done | bytes 786464 | tf_op jit(solution)/shard_map/ppermute | solution.py:562
  290.0 1.1 add_convert_fusion.1
  291.1 1.7 collective-permute-start.25
  292.9 23.2 %attend_back.1 = (bf16[1024,1536]{1,0:T(8,128)(2,1)S(1)}, bf16[1024,1280]{1,0:T(8,128)(2,1)S(1)}, bf16[512,1536]{1,0:T(8,128)(2,1)S(1)}, bf16[512,1536]{1,0:T(8,128)(2,1)S(1)}, f32[8,128]{1,0:T(8,128)S(1)}) custom-call(s32[2]{0:T(128)S(1)} %add_convert_fusion.4.place_ref, bf16[256,1536]{1,0:T(8,128)(2,1)S(1)} %add_convert_fusion.2.m0_ref, ...), custom_call_target="tpu_custom_call" | custom-call | flops 149999992832 | bytes 20000000 | tf_op jit(solution)/shard_map/attend_back/pallas_call | solution.py:238
  316.2 2.2 fusion.5
  318.7 9.4 %attend_grads.1 = (bf16[1536,1664]{1,0:T(8,128)(2,1)}, f32[8,1536]{1,0:T(8,128)S(1)}) custom-call(s32[2]{0:T(128)S(1)} %add_convert_fusion.4.place_ref, bf16[1024,1536]{1,0:T(8,128)(2,1)S(1)} %copy-done.16, bf16[1024,1536]{1,0:T(8,128)(2,1)S(1)} %get-tuple-element.116.m_ref, bf16[1024,1280]{1,0:T(8,128)(2,1)S(1)} %get-tuple-element.118.grad_ref, ...), custom_call_target="tpu_custom_call" | custom-call | flops 5234491392 | bytes 20000000 | tf_op jit(solution)/shard_map/attend_grads/pallas_call | solution.py:452
  329.0 1.7 collective-permute-start.30
  331.6 2.2 collective-permute-start.31
  333.7 2.1 collective-permute-done.31
  335.8 2.1 collective-permute-start.32
  337.9 2.1 collective-permute-done.32
  340.9 10.2 %collective-permute-done.33 = f32[32,128]{1,0:T(8,128)S(1)} collective-permute-done((f32[32,128]{1,0:T(8,128)S(1)}, f32[32,128]{1,0:T(8,128)S(1)}, u32[]{:S(2)}, u32[]{:S(2)}) %collective-permute-start.33) | collective-permute-done | bytes 16416 | tf_op jit(solution)/shard_map/ppermute | solution.py:582
  351.0 4.6 collective-permute-done.34
  355.7 1.5 fusion.4
  357.3 3.4 collective-permute-done.35
  362.1 4.4 collective-permute-start.39
  366.6 1.6 collective-permute-start.37
  368.2 25.9 %collective-permute-done.36 = bf16[256,1536]{1,0:T(8,128)(2,1)S(1)} collective-permute-done((bf16[256,1536]{1,0:T(8,128)(2,1)S(1)}, bf16[256,1536]{1,0:T(8,128)(2,1)S(1)}, u32[]{:S(2)}, u32[]{:S(2)}) %collective-permute-start.36) | collective-permute-done | bytes 786464 | tf_op jit(solution)/shard_map/ppermute | solution.py:575
  395.6 25.8 %collective-permute-done.37.a_ref = bf16[192,3072]{1,0:T(8,128)(2,1)S(1)} collective-permute-done((bf16[192,3072]{1,0:T(8,128)(2,1)S(1)}, bf16[192,3072]{1,0:T(8,128)(2,1)S(1)}, u32[]{:S(2)}, u32[]{:S(2)}) %collective-permute-start.37) | collective-permute-done | bytes 1179680 | tf_op jit(solution)/shard_map/ppermute | solution.py:554
  421.4 1.6 finish.2
  423.9 1.7 collective-permute-start.40
  425.6 1.4 fusion.8
  427.7 2.5 collective-permute-start.43
  430.3 1.3 collective-permute-start.41
  432.7 2.6 select_add_fusion
  435.3 29.9 %collective-permute-done.41.a_ref = bf16[192,1664]{1,0:T(8,128)(2,1)S(1)} collective-permute-done((bf16[192,1664]{1,0:T(8,128)(2,1)S(1)}, bf16[192,1664]{1,0:T(8,128)(2,1)S(1)}, u32[]{:S(2)}, u32[]{:S(2)}) %collective-permute-start.41) | collective-permute-done | bytes 639008 | tf_op jit(solution)/shard_map/ppermute | solution.py:554
  465.2 1.2 finish.3
  (207 shorter events, 24.0 us)
Async XLA Ops:
  7.2 142.5 %all-gather.3.cloned.1.call-start = ((), (), s32[]{:S(2)}) async-start(), calls=%async_computation.2 | async-start | bytes 6389760 | tf_op jit(solution)/shard_map/all_gather | solution.py:542
  9.5 19.8 %collective-permute-start = (bf16[192,1664]{1,0:T(8,128)(2,1)}, bf16[192,1664]{1,0:T(8,128)(2,1)S(1)}, u32[]{:S(2)}, u32[]{:S(2)}) collective-permute-start(bf16[192,1664]{1,0:T(8,128)(2,1)} %pack.3), channel_id=1, source_target_pairs={{0,6},{1,7},{2,4},{3,5},{8,14},{9,15},{10,12},{11,13},{16,22},{17,... | collective-permute-start | bytes 1916936 | tf_op jit(solution)/shard_map/ppermute | solution.py:535
  14.9 14.4 %collective-permute-start.1 = (bf16[192,1664]{1,0:T(8,128)(2,1)}, bf16[192,1664]{1,0:T(8,128)(2,1)S(1)}, u32[]{:S(2)}, u32[]{:S(2)}) collective-permute-start(bf16[192,1664]{1,0:T(8,128)(2,1)} %pack.3), channel_id=1, source_target_pairs={{4,6},{5,7},{6,4},{7,5},{12,14},{13,15},{14,12},{15,13},{20,22},{2... | collective-permute-start | bytes 1916936 | tf_op jit(solution)/shard_map/ppermute | solution.py:536
  15.6 13.7 %collective-permute-start.2 = (bf16[192,1664]{1,0:T(8,128)(2,1)}, bf16[192,1664]{1,0:T(8,128)(2,1)S(1)}, u32[]{:S(2)}, u32[]{:S(2)}) collective-permute-start(bf16[192,1664]{1,0:T(8,128)(2,1)} %pack.3), channel_id=1, source_target_pairs={{4,0},{5,1},{6,2},{7,3},{12,8},{13,9},{14,10},{15,11},{20,16},{21,... | collective-permute-start | bytes 1916936 | tf_op jit(solution)/shard_map/ppermute | solution.py:537
  31.8 179.1 %all-gather.5.cloned.1.call-start = ((), (), s32[]{:S(2)}) async-start(), calls=%async_computation.3 | async-start | bytes 11796480 | tf_op jit(solution)/shard_map/all_gather | solution.py:542
  34.5 41.5 %collective-permute-start.3 = (bf16[192,3072]{1,0:T(8,128)(2,1)}, bf16[192,3072]{1,0:T(8,128)(2,1)S(1)}, u32[]{:S(2)}, u32[]{:S(2)}) collective-permute-start(bf16[192,3072]{1,0:T(8,128)(2,1)} %pack.2), channel_id=1, source_target_pairs={{0,6},{1,7},{2,4},{3,5},{8,14},{9,15},{10,12},{11,13},{16,22},{17,... | collective-permute-start | bytes 3538952 | tf_op jit(solution)/shard_map/ppermute | solution.py:535
  50.5 25.6 %collective-permute-start.4 = (bf16[192,3072]{1,0:T(8,128)(2,1)}, bf16[192,3072]{1,0:T(8,128)(2,1)S(1)}, u32[]{:S(2)}, u32[]{:S(2)}) collective-permute-start(bf16[192,3072]{1,0:T(8,128)(2,1)} %pack.2), channel_id=1, source_target_pairs={{4,6},{5,7},{6,4},{7,5},{12,14},{13,15},{14,12},{15,13},{20,22},{2... | collective-permute-start | bytes 3538952 | tf_op jit(solution)/shard_map/ppermute | solution.py:536
  51.3 24.8 %collective-permute-start.5 = (bf16[192,3072]{1,0:T(8,128)(2,1)}, bf16[192,3072]{1,0:T(8,128)(2,1)S(1)}, u32[]{:S(2)}, u32[]{:S(2)}) collective-permute-start(bf16[192,3072]{1,0:T(8,128)(2,1)} %pack.2), channel_id=1, source_target_pairs={{4,0},{5,1},{6,2},{7,3},{12,8},{13,9},{14,10},{15,11},{20,16},{21,... | collective-permute-start | bytes 3538952 | tf_op jit(solution)/shard_map/ppermute | solution.py:537
  79.1 278.1 %reduce-scatter.3.cloned.1.call-start = ((), (), s32[]{:S(2)}) async-start(), calls=%async_computation.4 | async-start | bytes 11796480 | tf_op jit(solution)/shard_map/reduce_scatter | solution.py:546
  80.6 0.7 collective-permute-start.6
  81.6 28.4 %copy-start.25 = (f32[256,1536]{1,0:T(8,128)}, f32[256,1536]{1,0:T(8,128)S(1)}, u32[]{:S(2)}) copy-start(f32[256,1536]{1,0:T(8,128)S(1)} %get-tuple-element.146) | copy-start | bytes 4718596
  81.6 28.3 %copy-start.35 = (f32[256,1536]{1,0:T(8,128)S(1)}, f32[256,1536]{1,0:T(8,128)}, u32[]{:S(2)}) copy-start(f32[256,1536]{1,0:T(8,128)} %param.27) | copy-start | bytes 4718596
  81.6 28.4 %copy-start.51 = (f32[256]{0:T(256)}, f32[256]{0:T(256)S(1)}, u32[]{:S(2)}) copy-start(f32[256]{0:T(256)S(1)} %add_rsqrt_fusion.1) | copy-start | bytes 3076
  82.2 29.6 %copy-start.56 = (f32[24]{0:T(128)S(1)}, f32[24]{0:T(128)}, u32[]{:S(2)}) copy-start(f32[24]{0:T(128)} %param.21) | copy-start | bytes 292
  82.2 29.7 %copy-start.55 = (s32[1024]{0:T(1024)S(1)}, s32[1024]{0:T(1024)}, u32[]{:S(2)}) copy-start(s32[1024]{0:T(1024)} %param.15) | copy-start | bytes 12292
  82.2 54.1 %collective-permute-start.7 = (bf16[256,1536]{1,0:T(8,128)(2,1)S(1)}, bf16[256,1536]{1,0:T(8,128)(2,1)S(1)}, u32[]{:S(2)}, u32[]{:S(2)}) collective-permute-start(bf16[256,1536]{1,0:T(8,128)(2,1)S(1)} %multiply_convert_fusion.1.x0_ref), channel_id=1, source_target_pairs={{0,1},{1,0},{2,3},{3,2},{4,5},{5,4},{6,7},{7,6},{8,9},{9,8},{10,11... | collective-permute-start | bytes 2359304 | tf_op jit(solution)/shard_map/ppermute | solution.py:562
  110.0 37.0 %copy-start.40 = (bf16[256,1536]{1,0:T(8,128)(2,1)}, bf16[256,1536]{1,0:T(8,128)(2,1)S(1)}, u32[]{:S(2)}) copy-start(bf16[256,1536]{1,0:T(8,128)(2,1)S(1)} %convert_element_type.140) | copy-start | bytes 2359300
  110.1 37.0 %collective-permute-start.10 = (bf16[256,1536]{1,0:T(8,128)(2,1)S(1)}, bf16[256,1536]{1,0:T(8,128)(2,1)}, u32[]{:S(2)}, u32[]{:S(2)}) collective-permute-start(bf16[256,1536]{1,0:T(8,128)(2,1)S(1)} %convert_element_type.140), channel_id=1, source_target_pairs={{2,4},{3,5},{4,2},{5,3},{10,12},{11,13},{12,10},{13,11},{18,20},{1... | collective-permute-start | bytes 2359304 | tf_op jit(solution)/shard_map/ppermute | solution.py:627
  111.9 35.1 %collective-permute-start.11 = (s32[1024]{0:T(1024)S(1)}, s32[1024]{0:T(1024)S(1)}, u32[]{:S(2)}, u32[]{:S(2)}) collective-permute-start(s32[1024]{0:T(1024)S(1)} %copy-done.55), channel_id=1, source_target_pairs={{0,4},{4,0},{8,12},{12,8},{16,20},{20,16},{24,28},{28,24},{1,5},{5... | collective-permute-start | bytes 12296 | tf_op jit(solution)/shard_map/ppermute | solution.py:648
  136.3 13.4 %collective-permute-start.8 = (bf16[256,1536]{1,0:T(8,128)(2,1)S(1)}, bf16[256,1536]{1,0:T(8,128)(2,1)S(1)}, u32[]{:S(2)}, u32[]{:S(2)}) collective-permute-start(bf16[256,1536]{1,0:T(8,128)(2,1)S(1)} %multiply_convert_fusion.1.x0_ref), channel_id=1, source_target_pairs={{0,4},{4,0},{8,12},{12,8},{16,20},{20,16},{24,28},{28,24},{1,5},{5... | collective-permute-start | bytes 2359304 | tf_op jit(solution)/shard_map/ppermute | solution.py:561
  136.4 12.5 %collective-permute-start.9 = (bf16[256,1536]{1,0:T(8,128)(2,1)S(1)}, bf16[256,1536]{1,0:T(8,128)(2,1)S(1)}, u32[]{:S(2)}, u32[]{:S(2)}) collective-permute-start(bf16[256,1536]{1,0:T(8,128)(2,1)S(1)} %collective-permute-done.7.x1_ref), channel_id=1, source_target_pairs={{0,4},{4,0},{8,12},{12,8},{16,20},{20,16},{24,28},{28,24},{1,5},{5... | collective-permute-start | bytes 2359304 | tf_op jit(solution)/shard_map/ppermute | solution.py:563
  148.3 25.4 %collective-permute-start.12 = (bf16[256,1536]{1,0:T(8,128)(2,1)S(1)}, bf16[256,1536]{1,0:T(8,128)(2,1)}, u32[]{:S(2)}, u32[]{:S(2)}) collective-permute-start(bf16[256,1536]{1,0:T(8,128)(2,1)S(1)} %broadcast_select_fusion.refs_2_), channel_id=1, source_target_pairs={{0,1},{1,0},{2,3},{3,2},{4,5},{5,4},{6,7},{7,6},{8,9},{9,8},{10,11... | collective-permute-start | bytes 2359304 | tf_op jit(solution)/shard_map/ppermute | solution.py:659
  173.6 33.2 %copy-start.1 = (bf16[512,1536]{1,0:T(8,128)(2,1)}, bf16[512,1536]{1,0:T(8,128)(2,1)S(1)}, u32[]{:S(2)}) copy-start(bf16[512,1536]{1,0:T(8,128)(2,1)S(1)} %get-tuple-element.79) | copy-start | bytes 4718596
  173.6 33.2 %copy-start.15 = (bf16[1024,1536]{1,0:T(8,128)(2,1)}, bf16[1024,1536]{1,0:T(8,128)(2,1)S(1)}, u32[]{:S(2)}) copy-start(bf16[1024,1536]{1,0:T(8,128)(2,1)S(1)} %get-tuple-element.115.x_ref) | copy-start | bytes 9437188
  173.6 33.2 %copy-start.17 = (bf16[1024,384]{1,0:T(8,128)(2,1)}, bf16[1024,384]{1,0:T(8,128)(2,1)S(1)}, u32[]{:S(2)}) copy-start(bf16[1024,384]{1,0:T(8,128)(2,1)S(1)} %get-tuple-element.107.mixed_ref) | copy-start | bytes 2359300
  173.6 33.2 %copy-start.19 = (bf16[1024,1152]{1,0:T(8,128)(2,1)}, bf16[1024,1152]{1,0:T(8,128)(2,1)S(1)}, u32[]{:S(2)}) copy-start(bf16[1024,1152]{1,0:T(8,128)(2,1)S(1)} %get-tuple-element.106.qkv_ref) | copy-start | bytes 7077892
  173.6 32.6 %copy-start.26 = (f32[256,1536]{1,0:T(8,128)S(1)}, f32[256,1536]{1,0:T(8,128)}, u32[]{:S(2)}) copy-start(f32[256,1536]{1,0:T(8,128)} %copy-done.25) | copy-start | bytes 4718596
  173.6 12.5 %collective-permute-start.13 = (bf16[512,1536]{1,0:T(8,128)(2,1)S(1)}, bf16[512,1536]{1,0:T(8,128)(2,1)S(1)}, u32[]{:S(2)}, u32[]{:S(2)}) collective-permute-start(bf16[512,1536]{1,0:T(8,128)(2,1)S(1)} %get-tuple-element.82), channel_id=1, source_target_pairs={{0,4},{4,0},{8,12},{12,8},{16,20},{20,16},{24,28},{28,24},{1,5},{5... | collective-permute-start | bytes 4718600 | tf_op jit(solution)/shard_map/ppermute | solution.py:567
  186.3 19.9 %collective-permute-start.14 = (bf16[256,1536]{1,0:T(8,128)(2,1)S(1)}, bf16[256,1536]{1,0:T(8,128)(2,1)S(1)}, u32[]{:S(2)}, u32[]{:S(2)}) collective-permute-start(bf16[256,1536]{1,0:T(8,128)(2,1)S(1)} %add_convert_fusion.3), channel_id=1, source_target_pairs={{0,1},{1,0},{2,3},{3,2},{4,5},{5,4},{6,7},{7,6},{8,9},{9,8},{10,11... | collective-permute-start | bytes 2359304 | tf_op jit(solution)/shard_map/ppermute | solution.py:575
  188.1 21.0 %collective-permute-start.16 = (bf16[256,1536]{1,0:T(8,128)(2,1)S(1)}, bf16[256,1536]{1,0:T(8,128)(2,1)S(1)}, u32[]{:S(2)}, u32[]{:S(2)}) collective-permute-start(bf16[256,1536]{1,0:T(8,128)(2,1)S(1)} %broadcast_select_fusion.refs_2_), channel_id=1, source_target_pairs={{0,4},{4,0},{8,12},{12,8},{16,20},{20,16},{24,28},{28,24},{1,5},{5... | collective-permute-start | bytes 2359304 | tf_op jit(solution)/shard_map/ppermute | solution.py:664
  206.8 61.4 %copy-start.49 = (f32[256]{0:T(256)}, f32[256]{0:T(256)S(1)}, u32[]{:S(2)}) copy-start(f32[256]{0:T(256)S(1)} %add_rsqrt_fusion) | copy-start | bytes 3076
  207.1 2.9 collective-permute-start.15
  207.2 20.1 %collective-permute-start.17 = (bf16[256,1536]{1,0:T(8,128)(2,1)S(1)}, bf16[256,1536]{1,0:T(8,128)(2,1)}, u32[]{:S(2)}, u32[]{:S(2)}) collective-permute-start(bf16[256,1536]{1,0:T(8,128)(2,1)S(1)} %multiply_convert_fusion.refs_0_), channel_id=1, source_target_pairs={{0,1},{1,0},{2,3},{3,2},{4,5},{5,4},{6,7},{7,6},{8,9},{9,8},{10,11... | collective-permute-start | bytes 2359304 | tf_op jit(solution)/shard_map/ppermute | solution.py:670
  208.9 18.3 %collective-permute-start.19 = (bf16[256,1536]{1,0:T(8,128)(2,1)}, bf16[256,1536]{1,0:T(8,128)(2,1)}, u32[]{:S(2)}, u32[]{:S(2)}) collective-permute-start(bf16[256,1536]{1,0:T(8,128)(2,1)} %collective-permute-done.12.refs_2_), channel_id=1, source_target_pairs={{0,4},{4,0},{8,12},{12,8},{16,20},{20,16},{24,28},{28,24},{1,5},{5... | collective-permute-start | bytes 2359304 | tf_op jit(solution)/shard_map/ppermute | solution.py:665
  227.2 2.5 collective-permute-start.18
  243.2 2.4 collective-permute-start.20
  243.4 17.8 %collective-permute-start.21 = (bf16[256,1536]{1,0:T(8,128)(2,1)S(1)}, bf16[256,1536]{1,0:T(8,128)(2,1)}, u32[]{:S(2)}, u32[]{:S(2)}) collective-permute-start(bf16[256,1536]{1,0:T(8,128)(2,1)S(1)} %get-tuple-element.92), channel_id=1, source_target_pairs={{0,4},{4,0},{8,12},{12,8},{16,20},{20,16},{24,28},{28,24},{1,5},{5... | collective-permute-start | bytes 2359304 | tf_op jit(solution)/shard_map/ppermute | solution.py:680
  246.1 19.8 %collective-permute-start.22 = (bf16[256,1536]{1,0:T(8,128)(2,1)S(1)}, bf16[256,1536]{1,0:T(8,128)(2,1)}, u32[]{:S(2)}, u32[]{:S(2)}) collective-permute-start(bf16[256,1536]{1,0:T(8,128)(2,1)S(1)} %get-tuple-element.151), channel_id=1, source_target_pairs={{0,1},{1,0},{2,3},{3,2},{4,5},{5,4},{6,7},{7,6},{8,9},{9,8},{10,11... | collective-permute-start | bytes 2359304 | tf_op jit(solution)/shard_map/ppermute | solution.py:683
  260.9 164.7 %reduce-scatter.5.cloned.1.call-start = ((), (), s32[]{:S(2)}) async-start(), calls=%async_computation.5 | async-start | bytes 6389760 | tf_op jit(solution)/shard_map/reduce_scatter | solution.py:546
  270.4 18.5 %collective-permute-start.26 = (bf16[256,1536]{1,0:T(8,128)(2,1)S(1)}, bf16[256,1536]{1,0:T(8,128)(2,1)S(1)}, u32[]{:S(2)}, u32[]{:S(2)}) collective-permute-start(bf16[256,1536]{1,0:T(8,128)(2,1)S(1)} %add_convert_fusion.2.m0_ref), channel_id=1, source_target_pairs={{0,1},{1,0},{2,3},{3,2},{4,5},{5,4},{6,7},{7,6},{8,9},{9,8},{10,11... | collective-permute-start | bytes 2359304 | tf_op jit(solution)/shard_map/ppermute | solution.py:562
  279.8 10.3 %collective-permute-start.24 = (bf16[256,1536]{1,0:T(8,128)(2,1)S(1)}, bf16[256,1536]{1,0:T(8,128)(2,1)S(1)}, u32[]{:S(2)}, u32[]{:S(2)}) collective-permute-start(bf16[256,1536]{1,0:T(8,128)(2,1)S(1)} %get-tuple-element.104), channel_id=1, source_target_pairs={{0,4},{4,0},{8,12},{12,8},{16,20},{20,16},{24,28},{28,24},{1,5},{5... | collective-permute-start | bytes 2359304 | tf_op jit(solution)/shard_map/ppermute | solution.py:699
  279.8 13.0 %collective-permute-start.27 = (bf16[256,1536]{1,0:T(8,128)(2,1)S(1)}, bf16[256,1536]{1,0:T(8,128)(2,1)S(1)}, u32[]{:S(2)}, u32[]{:S(2)}) collective-permute-start(bf16[256,1536]{1,0:T(8,128)(2,1)S(1)} %add_convert_fusion.2.m0_ref), channel_id=1, source_target_pairs={{0,4},{4,0},{8,12},{12,8},{16,20},{20,16},{24,28},{28,24},{1,5},{5... | collective-permute-start | bytes 2359304 | tf_op jit(solution)/shard_map/ppermute | solution.py:561
  280.3 35.8 %collective-permute-start.23 = (bf16[256,1536]{1,0:T(8,128)(2,1)}, bf16[256,1536]{1,0:T(8,128)(2,1)}, u32[]{:S(2)}, u32[]{:S(2)}) collective-permute-start(bf16[256,1536]{1,0:T(8,128)(2,1)} %get-tuple-element.102), channel_id=1, source_target_pairs={{0,4},{4,0},{8,12},{12,8},{16,20},{20,16},{24,28},{28,24},{1,5},{5... | collective-permute-start | bytes 2359304 | tf_op jit(solution)/shard_map/ppermute | solution.py:701
  288.9 3.9 collective-permute-start.28
  291.1 25.0 %collective-permute-start.25 = (bf16[256,1536]{1,0:T(8,128)(2,1)}, bf16[256,1536]{1,0:T(8,128)(2,1)}, u32[]{:S(2)}, u32[]{:S(2)}) collective-permute-start(bf16[256,1536]{1,0:T(8,128)(2,1)} %add_convert_fusion.1), channel_id=1, source_target_pairs={{0,1},{1,0},{2,3},{3,2},{4,5},{5,4},{6,7},{7,6},{8,9},{9,8},{10,11... | collective-permute-start | bytes 2359304 | tf_op jit(solution)/shard_map/ppermute | solution.py:718
  318.7 37.0 %copy-start.34 = (f32[256,1536]{1,0:T(8,128)S(1)}, f32[256,1536]{1,0:T(8,128)}, u32[]{:S(2)}) copy-start(f32[256,1536]{1,0:T(8,128)} %param.14) | copy-start | bytes 4718596
  328.1 27.6 %collective-permute-start.29 = (bf16[256,1536]{1,0:T(8,128)(2,1)S(1)}, bf16[256,1536]{1,0:T(8,128)(2,1)S(1)}, u32[]{:S(2)}, u32[]{:S(2)}) collective-permute-start(bf16[256,1536]{1,0:T(8,128)(2,1)S(1)} %get-tuple-element.141), channel_id=1, source_target_pairs={{2,4},{3,5},{4,2},{5,3},{10,12},{11,13},{12,10},{13,11},{18,20},{1... | collective-permute-start | bytes 2359304 | tf_op jit(solution)/shard_map/ppermute | solution.py:630
  329.0 2.6 collective-permute-start.30
  331.6 4.3 collective-permute-start.31
  335.8 4.1 collective-permute-start.32
  340.0 11.1 %collective-permute-start.33 = (f32[32,128]{1,0:T(8,128)S(1)}, f32[32,128]{1,0:T(8,128)S(1)}, u32[]{:S(2)}, u32[]{:S(2)}) collective-permute-start(f32[32,128]{1,0:T(8,128)S(1)} %add.129), channel_id=1, source_target_pairs={{0,1},{1,0},{2,3},{3,2},{4,5},{5,4},{6,7},{7,6},{8,9},{9,8},{10,11... | collective-permute-start | bytes 49160 | tf_op jit(solution)/shard_map/ppermute | solution.py:582
  351.0 4.6 collective-permute-start.34
  357.2 3.5 collective-permute-start.35
  360.9 33.1 %collective-permute-start.36 = (bf16[256,1536]{1,0:T(8,128)(2,1)S(1)}, bf16[256,1536]{1,0:T(8,128)(2,1)S(1)}, u32[]{:S(2)}, u32[]{:S(2)}) collective-permute-start(bf16[256,1536]{1,0:T(8,128)(2,1)S(1)} %add_convert_fusion), channel_id=1, source_target_pairs={{0,1},{1,0},{2,3},{3,2},{4,5},{5,4},{6,7},{7,6},{8,9},{9,8},{10,11... | collective-permute-start | bytes 2359304 | tf_op jit(solution)/shard_map/ppermute | solution.py:575
  361.0 33.1 %copy-start.27 = (f32[256,1536]{1,0:T(8,128)S(1)}, f32[256,1536]{1,0:T(8,128)}, u32[]{:S(2)}) copy-start(f32[256,1536]{1,0:T(8,128)} %copy-done.25) | copy-start | bytes 4718596
  361.0 33.0 %copy-start.52 = (f32[256]{0:T(256)S(1)}, f32[256]{0:T(256)}, u32[]{:S(2)}) copy-start(f32[256]{0:T(256)} %copy-done.51) | copy-start | bytes 3076
  361.2 60.1 %collective-permute-start.38 = (bf16[192,3072]{1,0:T(8,128)(2,1)S(1)}, bf16[192,3072]{1,0:T(8,128)(2,1)S(1)}, u32[]{:S(2)}, u32[]{:S(2)}) collective-permute-start(bf16[192,3072]{1,0:T(8,128)(2,1)S(1)} %get-tuple-element.147.high_ref), channel_id=1, source_target_pairs={{4,6},{5,7},{6,4},{7,5},{12,14},{13,15},{14,12},{15,13},{20,22},{2... | collective-permute-start | bytes 3538952 | tf_op jit(solution)/shard_map/ppermute | solution.py:555
  362.1 59.3 %collective-permute-start.39 = (bf16[192,3072]{1,0:T(8,128)(2,1)S(1)}, bf16[192,3072]{1,0:T(8,128)(2,1)S(1)}, u32[]{:S(2)}, u32[]{:S(2)}) collective-permute-start(bf16[192,3072]{1,0:T(8,128)(2,1)S(1)} %get-tuple-element.147.high_ref), channel_id=1, source_target_pairs={{0,4},{1,5},{2,6},{3,7},{8,12},{9,13},{10,14},{11,15},{16,20},{17,... | collective-permute-start | bytes 3538952 | tf_op jit(solution)/shard_map/ppermute | solution.py:556
  366.5 28.1 %copy-start.30 = (f32[256,1536]{1,0:T(8,128)S(1)}, f32[256,1536]{1,0:T(8,128)}, u32[]{:S(2)}) copy-start(f32[256,1536]{1,0:T(8,128)} %copy-done.28) | copy-start | bytes 4718596
  366.6 54.8 %collective-permute-start.37 = (bf16[192,3072]{1,0:T(8,128)(2,1)S(1)}, bf16[192,3072]{1,0:T(8,128)(2,1)S(1)}, u32[]{:S(2)}, u32[]{:S(2)}) collective-permute-start(bf16[192,3072]{1,0:T(8,128)(2,1)S(1)} %get-tuple-element.148.low_ref), channel_id=1, source_target_pairs={{6,0},{7,1},{4,2},{5,3},{14,8},{15,9},{12,10},{13,11},{22,16},{23,... | collective-permute-start | bytes 3538952 | tf_op jit(solution)/shard_map/ppermute | solution.py:554
  423.9 8.7 %collective-permute-start.40 = (bf16[256,1536]{1,0:T(8,128)(2,1)}, bf16[256,1536]{1,0:T(8,128)(2,1)}, u32[]{:S(2)}, u32[]{:S(2)}) collective-permute-start(bf16[256,1536]{1,0:T(8,128)(2,1)} %convert_element_type.177), channel_id=1, source_target_pairs={{2,4},{3,5},{4,2},{5,3},{10,12},{11,13},{12,10},{13,11},{18,20},{1... | collective-permute-start | bytes 2359304 | tf_op jit(solution)/shard_map/ppermute | solution.py:630
  427.0 38.2 %collective-permute-start.42 = (bf16[192,1664]{1,0:T(8,128)(2,1)S(1)}, bf16[192,1664]{1,0:T(8,128)(2,1)S(1)}, u32[]{:S(2)}, u32[]{:S(2)}) collective-permute-start(bf16[192,1664]{1,0:T(8,128)(2,1)S(1)} %get-tuple-element.149.high_ref), channel_id=1, source_target_pairs={{4,6},{5,7},{6,4},{7,5},{12,14},{13,15},{14,12},{15,13},{20,22},{2... | collective-permute-start | bytes 1916936 | tf_op jit(solution)/shard_map/ppermute | solution.py:555
  427.7 37.5 %collective-permute-start.43 = (bf16[192,1664]{1,0:T(8,128)(2,1)S(1)}, bf16[192,1664]{1,0:T(8,128)(2,1)S(1)}, u32[]{:S(2)}, u32[]{:S(2)}) collective-permute-start(bf16[192,1664]{1,0:T(8,128)(2,1)S(1)} %get-tuple-element.149.high_ref), channel_id=1, source_target_pairs={{0,4},{1,5},{2,6},{3,7},{8,12},{9,13},{10,14},{11,15},{16,20},{17,... | collective-permute-start | bytes 1916936 | tf_op jit(solution)/shard_map/ppermute | solution.py:556
  430.3 35.0 %collective-permute-start.41 = (bf16[192,1664]{1,0:T(8,128)(2,1)S(1)}, bf16[192,1664]{1,0:T(8,128)(2,1)S(1)}, u32[]{:S(2)}, u32[]{:S(2)}) collective-permute-start(bf16[192,1664]{1,0:T(8,128)(2,1)S(1)} %get-tuple-element.150.low_ref), channel_id=1, source_target_pairs={{6,0},{7,1},{4,2},{5,3},{14,8},{15,9},{12,10},{13,11},{22,16},{23,... | collective-permute-start | bytes 1916936 | tf_op jit(solution)/shard_map/ppermute | solution.py:554
  (41 other events, 369.3 us)
Sparse Core Ops, SparseCore 0:
  31.9 75.9 all-gather.2
  109.7 96.3 all-gather.4
  261.0 93.9 reduce-scatter.2
  358.0 60.2 reduce-scatter.4

commit v6 on v5

--- a/solution.py
+++ b/solution.py
@@ -728,7 +728,7 @@
     size = packed.shape[0]
     packed = jnp.pad(packed, (0, -size % 1024)).reshape(-1, 128)
     small = sum_all(sum_all(packed, "dp"), "tensor")
-    attn_scattered = scatter_rows(lay, after(attn_grads, feed_scattered, small, down_back))
+    attn_scattered = scatter_rows(lay, after(attn_grads, feed_scattered, down_back))
     gate_shard, up_shard, down_shard = share_grad(
         lay, after(feed_scattered, small), odd, [hidden_width] * 3
     )

time: 477 us -> 500 us (1.048)
  waiting for transfers between devices: 182 us -> 198 us
    reduce_scatter x2, waiting for transfers between devices: 0.01 us -> 23.8 us  [scatter_rows(): lax.psum_scatter(g, 'dp', scatter_dimension=0, tiled=True, axis_index_gro...]
    ppermute x5, waiting for transfers between devices: 19.8 us -> 10.4 us  [sum_all(): x = x + lax.ppermute(x, axis, [(i, i ^ step) for i in range(size)])]
    unnamed x114 -> x132, local copies, waits for them, and re-layouts: 15.4 us -> 19.8 us
  transfers between devices with their start and end apart: 48 -> 48, of which waited for: 19 -> 21; matrix products, arithmetic and copies ran while one was open for 5% -> 5% of each run, Pallas kernels for 18% -> 18%
where the time goes in v6:
time: 500 us; the launch traced here: 496 us
  waiting for transfers between devices  198 us (40%)
  starting transfers between devices  133 us (27%)
  Pallas kernels  104 us (21%)
  other arithmetic  23.6 us (5%)
  local copies, waits for them, and re-layouts  22.6 us (5%)
  between operations  15.2 us (3%)
    ppermute x2, waiting for transfers between devices, share_grad(): a = lax.ppermute(low, BOTH, lay.back_even_far)  55.7 us
    ppermute x2, waiting for transfers between devices, scatter_z(): return mine + lax.ppermute(other, 'tensor', lay.pair).astype(F32)  42.7 us
    ppermute x2, waiting for transfers between devices, swap_weight(): a = lax.ppermute(w, BOTH, lay.even_far)  35.9 us
    ppermute x2, starting transfers between devices, gather_pair(): z = lax.ppermute(x, 'tensor', lay.pair)  29.6 us
    pallas_call x2, Pallas kernels, feed(): pl.pallas_call(feed_kernel, grid=(steps,), in_specs=[part] * 4 + [tall(0)...  25.7 us
    ppermute x1, starting transfers between devices, per_device(): lax.ppermute(after(segment_ids, attn_rows), 'dp', lay.core)  24.3 us
    reduce_scatter x2, waiting for transfers between devices, scatter_rows(): lax.psum_scatter(g, 'dp', scatter_dimension=0, tiled=True, axis_index_gro...  23.8 us
    pallas_call x1, Pallas kernels, attend_back(): pl.pallas_call(functools.partial(attend_back_kernel, heads, 256), in_spec...  23.2 us
  transfers between devices with their start and end apart: 48, of which 21 were waited for; matrix products, arithmetic and copies ran while one was open for 5% of the time, Pallas kernels for 18%

profile of v6, /device:TPU:0, one launch (start us, length us, event | category | flops | bytes accessed | tf_op | source)
XLA Modules:
  0.0 496.4 jit_solution(1272592237570604729)
XLA Ops:
  7.2 2.3 pack.3
  9.5 5.4 %collective-permute-start = (bf16[192,1664]{1,0:T(8,128)(2,1)}, bf16[192,1664]{1,0:T(8,128)(2,1)S(1)}, u32[]{:S(2)}, u32[]{:S(2)}) collective-permute-start(bf16[192,1664]{1,0:T(8,128)(2,1)} %pack.3), channel_id=1, source_target_pairs={{0,6},{1,7},{2,4},{3,5},{8,14},{9,15},{10,12},{11,13},{16,22},{17,... | collective-permute-start | bytes 1916936 | tf_op jit(solution)/shard_map/ppermute | solution.py:535
  15.6 1.3 collective-permute-start.2
  16.9 12.4 %collective-permute-done = bf16[192,1664]{1,0:T(8,128)(2,1)S(1)} collective-permute-done((bf16[192,1664]{1,0:T(8,128)(2,1)}, bf16[192,1664]{1,0:T(8,128)(2,1)S(1)}, u32[]{:S(2)}, u32[]{:S(2)}) %collective-permute-start) | collective-permute-done | bytes 639008 | tf_op jit(solution)/shard_map/ppermute | solution.py:535
  29.3 2.4 maximum_select_fusion.1
  31.8 2.7 pack.2
  34.5 16.0 %collective-permute-start.3 = (bf16[192,3072]{1,0:T(8,128)(2,1)}, bf16[192,3072]{1,0:T(8,128)(2,1)S(1)}, u32[]{:S(2)}, u32[]{:S(2)}) collective-permute-start(bf16[192,3072]{1,0:T(8,128)(2,1)} %pack.2), channel_id=1, source_target_pairs={{0,6},{1,7},{2,4},{3,5},{8,14},{9,15},{10,12},{11,13},{16,22},{17,... | collective-permute-start | bytes 3538952 | tf_op jit(solution)/shard_map/ppermute | solution.py:535
  51.3 1.3 collective-permute-start.5
  52.6 23.5 %collective-permute-done.3 = bf16[192,3072]{1,0:T(8,128)(2,1)S(1)} collective-permute-done((bf16[192,3072]{1,0:T(8,128)(2,1)}, bf16[192,3072]{1,0:T(8,128)(2,1)S(1)}, u32[]{:S(2)}, u32[]{:S(2)}) %collective-permute-start.3) | collective-permute-done | bytes 1179680 | tf_op jit(solution)/shard_map/ppermute | solution.py:535
  76.1 3.0 maximum_select_fusion
  79.2 1.3 copy-done.42
  82.2 27.7 %collective-permute-start.7 = (bf16[256,1536]{1,0:T(8,128)(2,1)S(1)}, bf16[256,1536]{1,0:T(8,128)(2,1)S(1)}, u32[]{:S(2)}, u32[]{:S(2)}) collective-permute-start(bf16[256,1536]{1,0:T(8,128)(2,1)S(1)} %multiply_convert_fusion.1.x0_ref), channel_id=1, source_target_pairs={{0,1},{1,0},{2,3},{3,2},{4,5},{5,4},{6,7},{7,6},{8,9},{9,8},{10,11... | collective-permute-start | bytes 2359304 | tf_op jit(solution)/shard_map/ppermute | solution.py:562
  110.0 1.8 collective-permute-start.10
  112.0 24.3 %collective-permute-start.11 = (s32[1024]{0:T(1024)S(1)}, s32[1024]{0:T(1024)S(1)}, u32[]{:S(2)}, u32[]{:S(2)}) collective-permute-start(s32[1024]{0:T(1024)S(1)} %copy-done.64), channel_id=1, source_target_pairs={{0,4},{4,0},{8,12},{12,8},{16,20},{20,16},{24,28},{28,24},{1,5},{5... | collective-permute-start | bytes 12296 | tf_op jit(solution)/shard_map/ppermute | solution.py:648
  136.4 10.6 %collective-permute-start.9 = (bf16[256,1536]{1,0:T(8,128)(2,1)S(1)}, bf16[256,1536]{1,0:T(8,128)(2,1)S(1)}, u32[]{:S(2)}, u32[]{:S(2)}) collective-permute-start(bf16[256,1536]{1,0:T(8,128)(2,1)S(1)} %collective-permute-done.7.x1_ref), channel_id=1, source_target_pairs={{0,4},{4,0},{8,12},{12,8},{16,20},{20,16},{24,28},{28,24},{1,5},{5... | collective-permute-start | bytes 2359304 | tf_op jit(solution)/shard_map/ppermute | solution.py:563
  147.2 1.6 collective-permute-done.9.x3_ref
  152.9 1.4 copy-done.23
  154.3 21.7 %attend.1 = (bf16[1024,1536]{1,0:T(8,128)(2,1)S(1)}, bf16[1024,1152]{1,0:T(8,128)(2,1)S(1)}, bf16[1024,384]{1,0:T(8,128)(2,1)S(1)}, bf16[512,1536]{1,0:T(8,128)(...) custom-call(s32[2]{0:T(128)S(1)} %add_convert_fusion.4.place_ref, ...), custom_call_target="tpu_custom_call" | custom-call | flops 12000000000 | bytes 20000000 | tf_op jit(solution)/shard_map/attend/pallas_call | solution.py:128
  177.6 8.6 %collective-permute-start.13 = (bf16[512,1536]{1,0:T(8,128)(2,1)S(1)}, bf16[512,1536]{1,0:T(8,128)(2,1)S(1)}, u32[]{:S(2)}, u32[]{:S(2)}) collective-permute-start(bf16[512,1536]{1,0:T(8,128)(2,1)S(1)} %get-tuple-element.82), channel_id=1, source_target_pairs={{0,4},{4,0},{8,12},{12,8},{16,20},{20,16},{24,28},{28,24},{1,5},{5... | collective-permute-start | bytes 4718600 | tf_op jit(solution)/shard_map/ppermute | solution.py:567
  186.1 3.0 collective-permute-done.13
  189.4 1.8 collective-permute-start.14
  191.3 18.0 %collective-permute-done.14 = bf16[256,1536]{1,0:T(8,128)(2,1)S(1)} collective-permute-done((bf16[256,1536]{1,0:T(8,128)(2,1)S(1)}, bf16[256,1536]{1,0:T(8,128)(2,1)S(1)}, u32[]{:S(2)}, u32[]{:S(2)}) %collective-permute-start.14) | collective-permute-done | bytes 786464 | tf_op jit(solution)/shard_map/ppermute | solution.py:575
  210.2 1.8 collective-permute-start.17
  216.2 12.3 %feed.2 = (bf16[512,1024]{1,0:T(8,128)(2,1)S(1)}, bf16[512,2048]{1,0:T(8,128)(2,1)S(1)}, bf16[512,1536]{1,0:T(8,128)(2,1)S(1)}, bf16[512,1536]{1,0:T(8,128)(2,1)...) custom-call(bf16[256,1536]{1,0:T(8,128)(2,1)S(1)} %multiply_convert_fusion.refs_0_, ...), custom_call_target="tpu_custom_call" | custom-call | flops 8000000000 | bytes 18000000 | tf_op jit(solution)/shard_map/feed/pallas_call | solution.py:310
  228.6 1.7 collective-permute-done.17.refs_0_
  230.3 2.5 collective-permute-done.18.refs_1_
  232.8 13.4 %feed.3 = (bf16[512,1024]{1,0:T(8,128)(2,1)S(1)}, bf16[512,2048]{1,0:T(8,128)(2,1)S(1)}, bf16[512,1536]{1,0:T(8,128)(2,1)S(1)}, bf16[512,1536]{1,0:T(8,128)(2,1)...) custom-call(bf16[256,1536]{1,0:T(8,128)(2,1)} %collective-permute-done.17.refs_0_, ...), custom_call_target="tpu_custom_call" | custom-call | flops 8000000000 | bytes 18000000 | tf_op jit(solution)/shard_map/feed/pallas_call | solution.py:310
  246.8 1.8 collective-permute-done.20
  249.7 1.7 collective-permute-start.22
  251.5 13.0 %feed_grads.1 = bf16[1536,3072]{1,0:T(8,128)(2,1)} custom-call(bf16[512,1536]{1,0:T(8,128)(2,1)S(1)} %get-tuple-element.93.xa_ref, bf16[512,1536]{1,0:T(8,128)(2,1)S(1)} %get-tuple-element.94.xb_ref, bf16[512,1536]{1,0:T(8,128)(2,1)S(1)} %get-tuple-element.95.ca_ref, bf16[512,1536]{1,0:T(8,128)(2,1)S(1)} %get-tuple-element.96.cb_ref, ...), custom_call_target="tpu_custom_call" | custom-call | flops 9663676416 | bytes 25000000 | tf_op jit(solution)/shard_map/feed_grads/pallas_call | solution.py:361
  264.8 4.7 collective-permute-done.22
  269.4 2.0 convert_add_fusion.2
  274.0 1.9 collective-permute-start.26
  275.9 4.0 copy-done
  279.9 3.5 down_product.1
  283.4 9.1 %collective-permute-done.26.m1_ref = bf16[256,1536]{1,0:T(8,128)(2,1)S(1)} collective-permute-done((bf16[256,1536]{1,0:T(8,128)(2,1)S(1)}, bf16[256,1536]{1,0:T(8,128)(2,1)S(1)}, u32[]{:S(2)}, u32[]{:S(2)}) %collective-permute-start.26) | collective-permute-done | bytes 786464 | tf_op jit(solution)/shard_map/ppermute | solution.py:562
  294.1 1.7 collective-permute-start.25
  297.2 23.2 %attend_back.1 = (bf16[1024,1536]{1,0:T(8,128)(2,1)S(1)}, bf16[1024,1280]{1,0:T(8,128)(2,1)S(1)}, bf16[512,1536]{1,0:T(8,128)(2,1)S(1)}, bf16[512,1536]{1,0:T(8,128)(2,1)S(1)}, f32[8,128]{1,0:T(8,128)S(1)}) custom-call(s32[2]{0:T(128)S(1)} %add_convert_fusion.4.place_ref, bf16[256,1536]{1,0:T(8,128)(2,1)S(1)} %add_convert_fusion.2.m0_ref, ...), custom_call_target="tpu_custom_call" | custom-call | flops 149999992832 | bytes 20000000 | tf_op jit(solution)/shard_map/attend_back/pallas_call | solution.py:238
  320.5 2.5 fusion.5
  324.0 9.0 %attend_grads.1 = (bf16[1536,1664]{1,0:T(8,128)(2,1)}, f32[8,1536]{1,0:T(8,128)S(1)}) custom-call(s32[2]{0:T(128)S(1)} %add_convert_fusion.4.place_ref, bf16[1024,1536]{1,0:T(8,128)(2,1)S(1)} %copy-done.25, bf16[1024,1536]{1,0:T(8,128)(2,1)S(1)} %get-tuple-element.116.m_ref, bf16[1024,1280]{1,0:T(8,128)(2,1)S(1)} %get-tuple-element.118.grad_ref, ...), custom_call_target="tpu_custom_call" | custom-call | flops 5234491392 | bytes 20000000 | tf_op jit(solution)/shard_map/attend_grads/pallas_call | solution.py:452
  333.0 1.5 fusion.4
  334.5 23.8 %reduce-scatter.3.cloned.1.call-done = bf16[384,3072]{1,0:T(8,128)(2,1)} async-done(((bf16[1536,3072]{1,0:T(8,128)(2,1)}), bf16[384,3072]{1,0:T(8,128)(2,1)}) %reduce-scatter.3.cloned.1.call-update) | async-done | bytes 2359312 | tf_op jit(solution)/shard_map/reduce_scatter | solution.py:546
  359.7 1.9 multiply_reduce_fusion.2
  363.1 1.4 collective-permute-start.31
  364.5 2.4 collective-permute-done.31
  366.9 1.4 collective-permute-start.32
  368.3 2.4 collective-permute-done.32
  370.7 1.5 collective-permute-start.33
  372.2 2.3 collective-permute-done.33
  374.5 2.4 collective-permute-start.34
  376.9 2.2 collective-permute-done.34
  379.2 3.4 collective-permute-done.35
  382.8 1.6 collective-permute-start.36
  385.4 5.3 %collective-permute-start.39 = (bf16[192,3072]{1,0:T(8,128)(2,1)S(1)}, bf16[192,3072]{1,0:T(8,128)(2,1)S(1)}, u32[]{:S(2)}, u32[]{:S(2)}) collective-permute-start(bf16[192,3072]{1,0:T(8,128)(2,1)S(1)} %get-tuple-element.147.high_ref), channel_id=1, source_target_pairs={{0,4},{1,5},{2,6},{3,7},{8,12},{9,13},{10,14},{11,15},{16,20},{17,... | collective-permute-start | bytes 3538952 | tf_op jit(solution)/shard_map/ppermute | solution.py:556
  390.8 1.6 collective-permute-start.37
  392.3 24.7 %collective-permute-done.36 = bf16[256,1536]{1,0:T(8,128)(2,1)S(1)} collective-permute-done((bf16[256,1536]{1,0:T(8,128)(2,1)S(1)}, bf16[256,1536]{1,0:T(8,128)(2,1)S(1)}, u32[]{:S(2)}, u32[]{:S(2)}) %collective-permute-start.36) | collective-permute-done | bytes 786464 | tf_op jit(solution)/shard_map/ppermute | solution.py:575
  418.5 25.8 %collective-permute-done.37.a_ref = bf16[192,3072]{1,0:T(8,128)(2,1)S(1)} collective-permute-done((bf16[192,3072]{1,0:T(8,128)(2,1)S(1)}, bf16[192,3072]{1,0:T(8,128)(2,1)S(1)}, u32[]{:S(2)}, u32[]{:S(2)}) %collective-permute-start.37) | collective-permute-done | bytes 1179680 | tf_op jit(solution)/shard_map/ppermute | solution.py:554
  444.3 1.6 finish.2
  446.9 1.7 collective-permute-start.40
  448.6 1.4 fusion.8
  450.7 2.5 collective-permute-start.43
  453.2 1.3 collective-permute-start.41
  455.7 2.6 select_add_fusion
  458.3 29.9 %collective-permute-done.41.a_ref = bf16[192,1664]{1,0:T(8,128)(2,1)S(1)} collective-permute-done((bf16[192,1664]{1,0:T(8,128)(2,1)S(1)}, bf16[192,1664]{1,0:T(8,128)(2,1)S(1)}, u32[]{:S(2)}, u32[]{:S(2)}) %collective-permute-start.41) | collective-permute-done | bytes 639008 | tf_op jit(solution)/shard_map/ppermute | solution.py:554
  (225 shorter events, 32.8 us)
Async XLA Ops:
  7.2 143.4 %all-gather.3.cloned.1.call-start = ((), (), s32[]{:S(2)}) async-start(), calls=%async_computation.2 | async-start | bytes 6389760 | tf_op jit(solution)/shard_map/all_gather | solution.py:542
  9.5 19.8 %collective-permute-start = (bf16[192,1664]{1,0:T(8,128)(2,1)}, bf16[192,1664]{1,0:T(8,128)(2,1)S(1)}, u32[]{:S(2)}, u32[]{:S(2)}) collective-permute-start(bf16[192,1664]{1,0:T(8,128)(2,1)} %pack.3), channel_id=1, source_target_pairs={{0,6},{1,7},{2,4},{3,5},{8,14},{9,15},{10,12},{11,13},{16,22},{17,... | collective-permute-start | bytes 1916936 | tf_op jit(solution)/shard_map/ppermute | solution.py:535
  14.9 14.4 %collective-permute-start.1 = (bf16[192,1664]{1,0:T(8,128)(2,1)}, bf16[192,1664]{1,0:T(8,128)(2,1)S(1)}, u32[]{:S(2)}, u32[]{:S(2)}) collective-permute-start(bf16[192,1664]{1,0:T(8,128)(2,1)} %pack.3), channel_id=1, source_target_pairs={{4,6},{5,7},{6,4},{7,5},{12,14},{13,15},{14,12},{15,13},{20,22},{2... | collective-permute-start | bytes 1916936 | tf_op jit(solution)/shard_map/ppermute | solution.py:536
  15.6 13.7 %collective-permute-start.2 = (bf16[192,1664]{1,0:T(8,128)(2,1)}, bf16[192,1664]{1,0:T(8,128)(2,1)S(1)}, u32[]{:S(2)}, u32[]{:S(2)}) collective-permute-start(bf16[192,1664]{1,0:T(8,128)(2,1)} %pack.3), channel_id=1, source_target_pairs={{4,0},{5,1},{6,2},{7,3},{12,8},{13,9},{14,10},{15,11},{20,16},{21,... | collective-permute-start | bytes 1916936 | tf_op jit(solution)/shard_map/ppermute | solution.py:537
  31.8 182.2 %all-gather.5.cloned.1.call-start = ((), (), s32[]{:S(2)}) async-start(), calls=%async_computation.3 | async-start | bytes 11796480 | tf_op jit(solution)/shard_map/all_gather | solution.py:542
  34.5 41.5 %collective-permute-start.3 = (bf16[192,3072]{1,0:T(8,128)(2,1)}, bf16[192,3072]{1,0:T(8,128)(2,1)S(1)}, u32[]{:S(2)}, u32[]{:S(2)}) collective-permute-start(bf16[192,3072]{1,0:T(8,128)(2,1)} %pack.2), channel_id=1, source_target_pairs={{0,6},{1,7},{2,4},{3,5},{8,14},{9,15},{10,12},{11,13},{16,22},{17,... | collective-permute-start | bytes 3538952 | tf_op jit(solution)/shard_map/ppermute | solution.py:535
  50.5 25.6 %collective-permute-start.4 = (bf16[192,3072]{1,0:T(8,128)(2,1)}, bf16[192,3072]{1,0:T(8,128)(2,1)S(1)}, u32[]{:S(2)}, u32[]{:S(2)}) collective-permute-start(bf16[192,3072]{1,0:T(8,128)(2,1)} %pack.2), channel_id=1, source_target_pairs={{4,6},{5,7},{6,4},{7,5},{12,14},{13,15},{14,12},{15,13},{20,22},{2... | collective-permute-start | bytes 3538952 | tf_op jit(solution)/shard_map/ppermute | solution.py:536
  51.3 24.8 %collective-permute-start.5 = (bf16[192,3072]{1,0:T(8,128)(2,1)}, bf16[192,3072]{1,0:T(8,128)(2,1)S(1)}, u32[]{:S(2)}, u32[]{:S(2)}) collective-permute-start(bf16[192,3072]{1,0:T(8,128)(2,1)} %pack.2), channel_id=1, source_target_pairs={{4,0},{5,1},{6,2},{7,3},{12,8},{13,9},{14,10},{15,11},{20,16},{21,... | collective-permute-start | bytes 3538952 | tf_op jit(solution)/shard_map/ppermute | solution.py:537
  79.1 279.2 %reduce-scatter.3.cloned.1.call-start = ((), (), s32[]{:S(2)}) async-start(), calls=%async_computation.4 | async-start | bytes 11796480 | tf_op jit(solution)/shard_map/reduce_scatter | solution.py:546
  80.6 0.7 collective-permute-start.6
  81.6 28.4 %copy-start.34 = (f32[256,1536]{1,0:T(8,128)}, f32[256,1536]{1,0:T(8,128)S(1)}, u32[]{:S(2)}) copy-start(f32[256,1536]{1,0:T(8,128)S(1)} %get-tuple-element.146) | copy-start | bytes 4718596
  81.6 28.3 %copy-start.44 = (f32[256,1536]{1,0:T(8,128)S(1)}, f32[256,1536]{1,0:T(8,128)}, u32[]{:S(2)}) copy-start(f32[256,1536]{1,0:T(8,128)} %param.27) | copy-start | bytes 4718596
  81.6 28.4 %copy-start.60 = (f32[256]{0:T(256)}, f32[256]{0:T(256)S(1)}, u32[]{:S(2)}) copy-start(f32[256]{0:T(256)S(1)} %add_rsqrt_fusion.1) | copy-start | bytes 3076
  82.2 29.7 %copy-start.65 = (f32[24]{0:T(128)S(1)}, f32[24]{0:T(128)}, u32[]{:S(2)}) copy-start(f32[24]{0:T(128)} %param.21) | copy-start | bytes 292
  82.2 29.7 %copy-start.64 = (s32[1024]{0:T(1024)S(1)}, s32[1024]{0:T(1024)}, u32[]{:S(2)}) copy-start(s32[1024]{0:T(1024)} %param.15) | copy-start | bytes 12292
  82.2 54.1 %collective-permute-start.7 = (bf16[256,1536]{1,0:T(8,128)(2,1)S(1)}, bf16[256,1536]{1,0:T(8,128)(2,1)S(1)}, u32[]{:S(2)}, u32[]{:S(2)}) collective-permute-start(bf16[256,1536]{1,0:T(8,128)(2,1)S(1)} %multiply_convert_fusion.1.x0_ref), channel_id=1, source_target_pairs={{0,1},{1,0},{2,3},{3,2},{4,5},{5,4},{6,7},{7,6},{8,9},{9,8},{10,11... | collective-permute-start | bytes 2359304 | tf_op jit(solution)/shard_map/ppermute | solution.py:562
  110.0 37.0 %collective-permute-start.10 = (bf16[256,1536]{1,0:T(8,128)(2,1)S(1)}, bf16[256,1536]{1,0:T(8,128)(2,1)}, u32[]{:S(2)}, u32[]{:S(2)}) collective-permute-start(bf16[256,1536]{1,0:T(8,128)(2,1)S(1)} %convert_element_type.140), channel_id=1, source_target_pairs={{2,4},{3,5},{4,2},{5,3},{10,12},{11,13},{12,10},{13,11},{18,20},{1... | collective-permute-start | bytes 2359304 | tf_op jit(solution)/shard_map/ppermute | solution.py:627
  112.0 35.1 %collective-permute-start.11 = (s32[1024]{0:T(1024)S(1)}, s32[1024]{0:T(1024)S(1)}, u32[]{:S(2)}, u32[]{:S(2)}) collective-permute-start(s32[1024]{0:T(1024)S(1)} %copy-done.64), channel_id=1, source_target_pairs={{0,4},{4,0},{8,12},{12,8},{16,20},{20,16},{24,28},{28,24},{1,5},{5... | collective-permute-start | bytes 12296 | tf_op jit(solution)/shard_map/ppermute | solution.py:648
  136.3 13.5 %collective-permute-start.8 = (bf16[256,1536]{1,0:T(8,128)(2,1)S(1)}, bf16[256,1536]{1,0:T(8,128)(2,1)S(1)}, u32[]{:S(2)}, u32[]{:S(2)}) collective-permute-start(bf16[256,1536]{1,0:T(8,128)(2,1)S(1)} %multiply_convert_fusion.1.x0_ref), channel_id=1, source_target_pairs={{0,4},{4,0},{8,12},{12,8},{16,20},{20,16},{24,28},{28,24},{1,5},{5... | collective-permute-start | bytes 2359304 | tf_op jit(solution)/shard_map/ppermute | solution.py:561
  136.4 12.5 %collective-permute-start.9 = (bf16[256,1536]{1,0:T(8,128)(2,1)S(1)}, bf16[256,1536]{1,0:T(8,128)(2,1)S(1)}, u32[]{:S(2)}, u32[]{:S(2)}) collective-permute-start(bf16[256,1536]{1,0:T(8,128)(2,1)S(1)} %collective-permute-done.7.x1_ref), channel_id=1, source_target_pairs={{0,4},{4,0},{8,12},{12,8},{16,20},{20,16},{24,28},{28,24},{1,5},{5... | collective-permute-start | bytes 2359304 | tf_op jit(solution)/shard_map/ppermute | solution.py:563
  147.2 30.4 %collective-permute-start.12 = (bf16[256,1536]{1,0:T(8,128)(2,1)S(1)}, bf16[256,1536]{1,0:T(8,128)(2,1)}, u32[]{:S(2)}, u32[]{:S(2)}) collective-permute-start(bf16[256,1536]{1,0:T(8,128)(2,1)S(1)} %broadcast_select_fusion.refs_2_), channel_id=1, source_target_pairs={{0,1},{1,0},{2,3},{3,2},{4,5},{5,4},{6,7},{7,6},{8,9},{9,8},{10,11... | collective-permute-start | bytes 2359304 | tf_op jit(solution)/shard_map/ppermute | solution.py:659
  177.5 32.3 %copy-start.1 = (bf16[512,1536]{1,0:T(8,128)(2,1)}, bf16[512,1536]{1,0:T(8,128)(2,1)S(1)}, u32[]{:S(2)}) copy-start(bf16[512,1536]{1,0:T(8,128)(2,1)S(1)} %get-tuple-element.79) | copy-start | bytes 4718596
  177.5 32.3 %copy-start.24 = (bf16[1024,1536]{1,0:T(8,128)(2,1)}, bf16[1024,1536]{1,0:T(8,128)(2,1)S(1)}, u32[]{:S(2)}) copy-start(bf16[1024,1536]{1,0:T(8,128)(2,1)S(1)} %get-tuple-element.115.x_ref) | copy-start | bytes 9437188
  177.5 32.3 %copy-start.26 = (bf16[1024,384]{1,0:T(8,128)(2,1)}, bf16[1024,384]{1,0:T(8,128)(2,1)S(1)}, u32[]{:S(2)}) copy-start(bf16[1024,384]{1,0:T(8,128)(2,1)S(1)} %get-tuple-element.107.mixed_ref) | copy-start | bytes 2359300
  177.6 32.3 %copy-start.28 = (bf16[1024,1152]{1,0:T(8,128)(2,1)}, bf16[1024,1152]{1,0:T(8,128)(2,1)S(1)}, u32[]{:S(2)}) copy-start(bf16[1024,1152]{1,0:T(8,128)(2,1)S(1)} %get-tuple-element.106.qkv_ref) | copy-start | bytes 7077892
  177.6 31.7 %copy-start.35 = (f32[256,1536]{1,0:T(8,128)S(1)}, f32[256,1536]{1,0:T(8,128)}, u32[]{:S(2)}) copy-start(f32[256,1536]{1,0:T(8,128)} %copy-done.34) | copy-start | bytes 4718596
  177.6 11.6 %collective-permute-start.13 = (bf16[512,1536]{1,0:T(8,128)(2,1)S(1)}, bf16[512,1536]{1,0:T(8,128)(2,1)S(1)}, u32[]{:S(2)}, u32[]{:S(2)}) collective-permute-start(bf16[512,1536]{1,0:T(8,128)(2,1)S(1)} %get-tuple-element.82), channel_id=1, source_target_pairs={{0,4},{4,0},{8,12},{12,8},{16,20},{20,16},{24,28},{28,24},{1,5},{5... | collective-permute-start | bytes 4718600 | tf_op jit(solution)/shard_map/ppermute | solution.py:567
  189.4 19.9 %collective-permute-start.14 = (bf16[256,1536]{1,0:T(8,128)(2,1)S(1)}, bf16[256,1536]{1,0:T(8,128)(2,1)S(1)}, u32[]{:S(2)}, u32[]{:S(2)}) collective-permute-start(bf16[256,1536]{1,0:T(8,128)(2,1)S(1)} %add_convert_fusion.3), channel_id=1, source_target_pairs={{0,1},{1,0},{2,3},{3,2},{4,5},{5,4},{6,7},{7,6},{8,9},{9,8},{10,11... | collective-permute-start | bytes 2359304 | tf_op jit(solution)/shard_map/ppermute | solution.py:575
  191.2 21.0 %collective-permute-start.16 = (bf16[256,1536]{1,0:T(8,128)(2,1)S(1)}, bf16[256,1536]{1,0:T(8,128)(2,1)S(1)}, u32[]{:S(2)}, u32[]{:S(2)}) collective-permute-start(bf16[256,1536]{1,0:T(8,128)(2,1)S(1)} %broadcast_select_fusion.refs_2_), channel_id=1, source_target_pairs={{0,4},{4,0},{8,12},{12,8},{16,20},{20,16},{24,28},{28,24},{1,5},{5... | collective-permute-start | bytes 2359304 | tf_op jit(solution)/shard_map/ppermute | solution.py:664
  209.9 61.9 %copy-start.58 = (f32[256]{0:T(256)}, f32[256]{0:T(256)S(1)}, u32[]{:S(2)}) copy-start(f32[256]{0:T(256)S(1)} %add_rsqrt_fusion) | copy-start | bytes 3076
  210.1 2.9 collective-permute-start.15
  210.2 20.1 %collective-permute-start.17 = (bf16[256,1536]{1,0:T(8,128)(2,1)S(1)}, bf16[256,1536]{1,0:T(8,128)(2,1)}, u32[]{:S(2)}, u32[]{:S(2)}) collective-permute-start(bf16[256,1536]{1,0:T(8,128)(2,1)S(1)} %multiply_convert_fusion.refs_0_), channel_id=1, source_target_pairs={{0,1},{1,0},{2,3},{3,2},{4,5},{5,4},{6,7},{7,6},{8,9},{9,8},{10,11... | collective-permute-start | bytes 2359304 | tf_op jit(solution)/shard_map/ppermute | solution.py:670
  212.0 18.3 %collective-permute-start.19 = (bf16[256,1536]{1,0:T(8,128)(2,1)}, bf16[256,1536]{1,0:T(8,128)(2,1)}, u32[]{:S(2)}, u32[]{:S(2)}) collective-permute-start(bf16[256,1536]{1,0:T(8,128)(2,1)} %collective-permute-done.12.refs_2_), channel_id=1, source_target_pairs={{0,4},{4,0},{8,12},{12,8},{16,20},{20,16},{24,28},{28,24},{1,5},{5... | collective-permute-start | bytes 2359304 | tf_op jit(solution)/shard_map/ppermute | solution.py:665
  228.6 40.9 %copy-start.3 = (bf16[256,1536]{1,0:T(8,128)(2,1)}, bf16[256,1536]{1,0:T(8,128)(2,1)S(1)}, u32[]{:S(2)}) copy-start(bf16[256,1536]{1,0:T(8,128)(2,1)S(1)} %get-tuple-element.120) | copy-start | bytes 2359300
  230.3 2.5 collective-permute-start.18
  246.2 2.4 collective-permute-start.20
  246.4 18.3 %collective-permute-start.21 = (bf16[256,1536]{1,0:T(8,128)(2,1)S(1)}, bf16[256,1536]{1,0:T(8,128)(2,1)}, u32[]{:S(2)}, u32[]{:S(2)}) collective-permute-start(bf16[256,1536]{1,0:T(8,128)(2,1)S(1)} %get-tuple-element.92), channel_id=1, source_target_pairs={{0,4},{4,0},{8,12},{12,8},{16,20},{20,16},{24,28},{28,24},{1,5},{5... | collective-permute-start | bytes 2359304 | tf_op jit(solution)/shard_map/ppermute | solution.py:680
  249.7 19.7 %collective-permute-start.22 = (bf16[256,1536]{1,0:T(8,128)(2,1)S(1)}, bf16[256,1536]{1,0:T(8,128)(2,1)}, u32[]{:S(2)}, u32[]{:S(2)}) collective-permute-start(bf16[256,1536]{1,0:T(8,128)(2,1)S(1)} %get-tuple-element.151), channel_id=1, source_target_pairs={{0,1},{1,0},{2,3},{3,2},{4,5},{5,4},{6,7},{7,6},{8,9},{9,8},{10,11... | collective-permute-start | bytes 2359304 | tf_op jit(solution)/shard_map/ppermute | solution.py:683
  264.5 184.1 %reduce-scatter.5.cloned.1.call-start = ((), (), s32[]{:S(2)}) async-start(), calls=%async_computation.5 | async-start | bytes 6389760 | tf_op jit(solution)/shard_map/reduce_scatter | solution.py:546
  274.0 18.6 %collective-permute-start.26 = (bf16[256,1536]{1,0:T(8,128)(2,1)S(1)}, bf16[256,1536]{1,0:T(8,128)(2,1)S(1)}, u32[]{:S(2)}, u32[]{:S(2)}) collective-permute-start(bf16[256,1536]{1,0:T(8,128)(2,1)S(1)} %add_convert_fusion.2.m0_ref), channel_id=1, source_target_pairs={{0,1},{1,0},{2,3},{3,2},{4,5},{5,4},{6,7},{7,6},{8,9},{9,8},{10,11... | collective-permute-start | bytes 2359304 | tf_op jit(solution)/shard_map/ppermute | solution.py:562
  283.4 9.7 %collective-permute-start.24 = (bf16[256,1536]{1,0:T(8,128)(2,1)S(1)}, bf16[256,1536]{1,0:T(8,128)(2,1)S(1)}, u32[]{:S(2)}, u32[]{:S(2)}) collective-permute-start(bf16[256,1536]{1,0:T(8,128)(2,1)S(1)} %get-tuple-element.104), channel_id=1, source_target_pairs={{0,4},{4,0},{8,12},{12,8},{16,20},{20,16},{24,28},{28,24},{1,5},{5... | collective-permute-start | bytes 2359304 | tf_op jit(solution)/shard_map/ppermute | solution.py:699
  292.6 3.3 collective-permute-start.28
  292.6 4.5 collective-permute-start.27
  293.1 27.4 %collective-permute-start.23 = (bf16[256,1536]{1,0:T(8,128)(2,1)}, bf16[256,1536]{1,0:T(8,128)(2,1)}, u32[]{:S(2)}, u32[]{:S(2)}) collective-permute-start(bf16[256,1536]{1,0:T(8,128)(2,1)} %get-tuple-element.102), channel_id=1, source_target_pairs={{0,4},{4,0},{8,12},{12,8},{16,20},{20,16},{24,28},{28,24},{1,5},{5... | collective-permute-start | bytes 2359304 | tf_op jit(solution)/shard_map/ppermute | solution.py:701
  294.1 26.3 %collective-permute-start.25 = (bf16[256,1536]{1,0:T(8,128)(2,1)}, bf16[256,1536]{1,0:T(8,128)(2,1)}, u32[]{:S(2)}, u32[]{:S(2)}) collective-permute-start(bf16[256,1536]{1,0:T(8,128)(2,1)} %add_convert_fusion.1), channel_id=1, source_target_pairs={{0,1},{1,0},{2,3},{3,2},{4,5},{5,4},{6,7},{7,6},{8,9},{9,8},{10,11... | collective-permute-start | bytes 2359304 | tf_op jit(solution)/shard_map/ppermute | solution.py:718
  323.0 10.0 %collective-permute-start.29 = (bf16[256,1536]{1,0:T(8,128)(2,1)S(1)}, bf16[256,1536]{1,0:T(8,128)(2,1)S(1)}, u32[]{:S(2)}, u32[]{:S(2)}) collective-permute-start(bf16[256,1536]{1,0:T(8,128)(2,1)S(1)} %get-tuple-element.141), channel_id=1, source_target_pairs={{2,4},{3,5},{4,2},{5,3},{10,12},{11,13},{12,10},{13,11},{18,20},{1... | collective-permute-start | bytes 2359304 | tf_op jit(solution)/shard_map/ppermute | solution.py:630
  361.8 1.2 collective-permute-start.30
  363.1 3.8 collective-permute-start.31
  366.9 3.8 collective-permute-start.32
  370.7 3.7 collective-permute-start.33
  374.5 4.6 collective-permute-start.34
  379.1 3.5 collective-permute-start.35
  382.8 34.2 %collective-permute-start.36 = (bf16[256,1536]{1,0:T(8,128)(2,1)S(1)}, bf16[256,1536]{1,0:T(8,128)(2,1)S(1)}, u32[]{:S(2)}, u32[]{:S(2)}) collective-permute-start(bf16[256,1536]{1,0:T(8,128)(2,1)S(1)} %add_convert_fusion), channel_id=1, source_target_pairs={{0,1},{1,0},{2,3},{3,2},{4,5},{5,4},{6,7},{7,6},{8,9},{9,8},{10,11... | collective-permute-start | bytes 2359304 | tf_op jit(solution)/shard_map/ppermute | solution.py:575
  384.4 32.7 %copy-start.36 = (f32[256,1536]{1,0:T(8,128)S(1)}, f32[256,1536]{1,0:T(8,128)}, u32[]{:S(2)}) copy-start(f32[256,1536]{1,0:T(8,128)} %copy-done.34) | copy-start | bytes 4718596
  384.4 32.7 %copy-start.61 = (f32[256]{0:T(256)S(1)}, f32[256]{0:T(256)}, u32[]{:S(2)}) copy-start(f32[256]{0:T(256)} %copy-done.60) | copy-start | bytes 3076
  384.5 59.8 %collective-permute-start.38 = (bf16[192,3072]{1,0:T(8,128)(2,1)S(1)}, bf16[192,3072]{1,0:T(8,128)(2,1)S(1)}, u32[]{:S(2)}, u32[]{:S(2)}) collective-permute-start(bf16[192,3072]{1,0:T(8,128)(2,1)S(1)} %get-tuple-element.147.high_ref), channel_id=1, source_target_pairs={{4,6},{5,7},{6,4},{7,5},{12,14},{13,15},{14,12},{15,13},{20,22},{2... | collective-permute-start | bytes 3538952 | tf_op jit(solution)/shard_map/ppermute | solution.py:555
  385.4 58.9 %collective-permute-start.39 = (bf16[192,3072]{1,0:T(8,128)(2,1)S(1)}, bf16[192,3072]{1,0:T(8,128)(2,1)S(1)}, u32[]{:S(2)}, u32[]{:S(2)}) collective-permute-start(bf16[192,3072]{1,0:T(8,128)(2,1)S(1)} %get-tuple-element.147.high_ref), channel_id=1, source_target_pairs={{0,4},{1,5},{2,6},{3,7},{8,12},{9,13},{10,14},{11,15},{16,20},{17,... | collective-permute-start | bytes 3538952 | tf_op jit(solution)/shard_map/ppermute | solution.py:556
  390.7 26.9 %copy-start.39 = (f32[256,1536]{1,0:T(8,128)S(1)}, f32[256,1536]{1,0:T(8,128)}, u32[]{:S(2)}) copy-start(f32[256,1536]{1,0:T(8,128)} %copy-done.37) | copy-start | bytes 4718596
  390.7 26.9 %copy-start.41 = (f32[256,1536]{1,0:T(8,128)S(1)}, f32[256,1536]{1,0:T(8,128)}, u32[]{:S(2)}) copy-start(f32[256,1536]{1,0:T(8,128)} %copy-done.40) | copy-start | bytes 4718596
  390.8 53.6 %collective-permute-start.37 = (bf16[192,3072]{1,0:T(8,128)(2,1)S(1)}, bf16[192,3072]{1,0:T(8,128)(2,1)S(1)}, u32[]{:S(2)}, u32[]{:S(2)}) collective-permute-start(bf16[192,3072]{1,0:T(8,128)(2,1)S(1)} %get-tuple-element.148.low_ref), channel_id=1, source_target_pairs={{6,0},{7,1},{4,2},{5,3},{14,8},{15,9},{12,10},{13,11},{22,16},{23,... | collective-permute-start | bytes 3538952 | tf_op jit(solution)/shard_map/ppermute | solution.py:554
  446.9 8.7 %collective-permute-start.40 = (bf16[256,1536]{1,0:T(8,128)(2,1)}, bf16[256,1536]{1,0:T(8,128)(2,1)}, u32[]{:S(2)}, u32[]{:S(2)}) collective-permute-start(bf16[256,1536]{1,0:T(8,128)(2,1)} %convert_element_type.177), channel_id=1, source_target_pairs={{2,4},{3,5},{4,2},{5,3},{10,12},{11,13},{12,10},{13,11},{18,20},{1... | collective-permute-start | bytes 2359304 | tf_op jit(solution)/shard_map/ppermute | solution.py:630
  450.0 38.2 %collective-permute-start.42 = (bf16[192,1664]{1,0:T(8,128)(2,1)S(1)}, bf16[192,1664]{1,0:T(8,128)(2,1)S(1)}, u32[]{:S(2)}, u32[]{:S(2)}) collective-permute-start(bf16[192,1664]{1,0:T(8,128)(2,1)S(1)} %get-tuple-element.149.high_ref), channel_id=1, source_target_pairs={{4,6},{5,7},{6,4},{7,5},{12,14},{13,15},{14,12},{15,13},{20,22},{2... | collective-permute-start | bytes 1916936 | tf_op jit(solution)/shard_map/ppermute | solution.py:555
  450.7 37.5 %collective-permute-start.43 = (bf16[192,1664]{1,0:T(8,128)(2,1)S(1)}, bf16[192,1664]{1,0:T(8,128)(2,1)S(1)}, u32[]{:S(2)}, u32[]{:S(2)}) collective-permute-start(bf16[192,1664]{1,0:T(8,128)(2,1)S(1)} %get-tuple-element.149.high_ref), channel_id=1, source_target_pairs={{0,4},{1,5},{2,6},{3,7},{8,12},{9,13},{10,14},{11,15},{16,20},{17,... | collective-permute-start | bytes 1916936 | tf_op jit(solution)/shard_map/ppermute | solution.py:556
  453.2 35.0 %collective-permute-start.41 = (bf16[192,1664]{1,0:T(8,128)(2,1)S(1)}, bf16[192,1664]{1,0:T(8,128)(2,1)S(1)}, u32[]{:S(2)}, u32[]{:S(2)}) collective-permute-start(bf16[192,1664]{1,0:T(8,128)(2,1)S(1)} %get-tuple-element.150.low_ref), channel_id=1, source_target_pairs={{6,0},{7,1},{4,2},{5,3},{14,8},{15,9},{12,10},{13,11},{22,16},{23,... | collective-permute-start | bytes 1916936 | tf_op jit(solution)/shard_map/ppermute | solution.py:554
  (50 other events, 422.2 us)
Sparse Core Ops, SparseCore 0:
  31.9 75.9 all-gather.2
  109.7 96.3 all-gather.4
  264.6 93.5 reduce-scatter.2
  361.2 60.4 reduce-scatter.4
